TPU v7x, 256 devices: a whole 4x4x8 slice. The times are simulated.
256 devices in a mesh: cell: 8 (over x, z_hi), dom: 32 (over y, z_lo, core).
Axes of the slice: x: 4, y: 4, z: 8 (z_hi: 2, z_lo: 4; z = z_hi * 4 + z_lo), core: 2. Of those that a mesh axis runs over, the one named last changes fastest.
Arguments:
- feats: bfloat16 [8, 4096, 128], P('cell', 'dom'), may hold values from -6 to 6
- positions: float32 [8, 3, 4096], P('cell', None, 'dom'), may hold values from 0 to 1
- species: int32 [8, 4096], P('cell', 'dom'), may hold values from 0 to 7
- wave_vectors: int32 [3, 2048], replicated, may hold values from -8 to 8, as said below
- smearing: float32 [128], replicated, may hold values from 0.001 to 0.03
- species_gain: float32 [8, 128], replicated, may hold values from 0.5 to 1.5
- w_charge: bfloat16 [128, 128], replicated, may hold values from -0.5 to 0.5
- w_message: bfloat16 [128, 128], replicated, may hold values from -0.5 to 0.5
- w_radial: float32 [8, 128], replicated, may hold values from -2 to 2
- w_out: bfloat16 [128, 128], replicated, may hold values from -0.5 to 0.5
- edge_sender: int32 [8, 393216], P('cell', 'dom'), may hold values from 0 to 191
- edge_receiver: int32 [8, 393216], P('cell', 'dom'), may hold values from 0 to 127
- edge_mask: int32 [8, 393216], P('cell', 'dom'), may hold values 0 or 1
- edge_length: float32 [8, 393216], P('cell', 'dom'), may hold values from 0.8 to 5.8
- ghost_down: int32 [8, 1024], P('cell', 'dom'), may hold values from 0 to 127
- ghost_up: int32 [8, 1024], P('cell', 'dom'), may hold values from 0 to 127
- cotangent: bfloat16 [8, 4096, 128], P('cell', 'dom'), may hold values from -6 to 6
Outputs:
- updated: bfloat16 [8, 4096, 128], P('cell', 'dom')
- feat_grad: bfloat16 [8, 4096, 128], P('cell', 'dom')
- grad_charge: float32 [128, 128], replicated
- grad_message: float32 [128, 128], replicated
- grad_radial: float32 [8, 128], replicated
- grad_out: float32 [128, 128], replicated
Inputs may be any that keep to these rules, and one draw needn't show every extreme that they name: `wave_vectors`: every column is a nonzero integer triple. `edge_sender`: rows below 128 are the domain's own atoms, then 32 rows from below, then 32 from above. `edge_receiver`: local row within the domain. `ghost_down`: local row within the sending domain; rows may repeat. `ghost_up`: local row within the sending domain; rows may repeat.
All inputs are finite; a program needn't handle non-finite values. No bound on the sum of `edge_mask` on one device may be relied on, other than what follows from the above.
Results may differ from a plain program's by a relative error of at most 0.01.
Values may be sent and summed in bfloat16 or wider, within the bound.
No kernel may reach another device: no remote copies, remote signals or barrier semaphores. Data moves between devices by JAX's collectives and lax.ppermute only.
A program may use at most 64 MiB of HBM per device.

v0:
```python
import math

import jax
import jax.numpy as jnp
from jax import lax
from jax.sharding import PartitionSpec as P

cutoff_radius = 6.0
basis_width = 0.75
edge_scale = 0.25
filter_factor = 12.0


def extended_2(block, sides, width):
    for axis, dim in sides:
        count = lax.axis_size(axis)
        forward = [(i, i + 1) for i in range(count - 1)]
        forward.append((count - 1, 0))
        backward = [(target, source) for source, target in forward]
        low = lax.ppermute(
            lax.slice_in_dim(block, block.shape[dim] - width, None, axis=dim), axis, forward
        )
        high = lax.ppermute(lax.slice_in_dim(block, 0, width, axis=dim), axis, backward)
        block = jnp.concatenate([low, block, high], axis=dim)
    return block


def phase_tables(coords, wave_vectors):
    waves = wave_vectors.astype(jnp.float32)
    theta = (
        coords[0][:, None] * waves[0][None, :]
        + coords[1][:, None] * waves[1][None, :]
        + coords[2][:, None] * waves[2][None, :]
    )
    theta = 2.0 * math.pi * theta
    return (jnp.cos(theta).astype(jnp.bfloat16), jnp.sin(theta).astype(jnp.bfloat16))


def filter_table(wave_vectors, smearing):
    waves = wave_vectors.astype(jnp.float32)
    squared = jnp.sum(waves * waves, axis=0)
    return (
        filter_factor * jnp.exp(-squared[:, None] * smearing[None, :]) / jnp.sqrt(squared)[:, None]
    )


def radial_terms(lengths, w_radial):
    centers = 0.5 + basis_width * jnp.arange(w_radial.shape[0]).astype(jnp.float32)
    basis = jnp.exp(-jnp.square((lengths[:, None] - centers[None, :]) / basis_width))
    envelope = 0.5 * (jnp.cos(math.pi * lengths / cutoff_radius) + 1.0)
    radial = envelope[:, None] * jnp.dot(basis, w_radial, precision=lax.Precision.HIGHEST)
    return (basis, envelope, radial)


def contract_rows(left, right):
    return lax.dot_general(
        left, right, (((0,), (0,)), ((), ())), preferred_element_type=jnp.float32
    )


def reduced_field(local_re, local_im, filt, scale):
    total_re, total_im = lax.psum((local_re, local_im), "dom")
    return (
        (filt * total_re * scale).astype(jnp.bfloat16),
        (filt * total_im * scale).astype(jnp.bfloat16),
    )


def per_device(
    feats,
    positions,
    species,
    wave_vectors,
    smearing,
    species_gain,
    w_charge,
    w_message,
    w_radial,
    w_out,
    edge_sender,
    edge_receiver,
    edge_mask,
    edge_length,
    ghost_down,
    ghost_up,
    cotangent,
):
    own_rows = feats[0]
    coords = positions[0]
    senders = edge_sender[0]
    receivers = edge_receiver[0]
    live = edge_mask[0].astype(jnp.float32)[:, None]
    lengths = edge_length[0]
    downs = ghost_down[0]
    ups = ghost_up[0]
    upstream_cot = cotangent[0]
    atoms = own_rows.shape[0]
    ghosts = downs.shape[0]
    domains = lax.axis_size("dom")
    cells = lax.axis_size("cell")
    inv_waves = 1.0 / math.sqrt(wave_vectors.shape[1])
    inv_atoms = 1.0 / math.sqrt(atoms * domains)
    grad_scale = 1.0 / math.sqrt(cells * atoms * domains)
    labels = jnp.arange(species_gain.shape[0], dtype=jnp.int32)
    onehot = (species[0][:, None] == labels[None, :]).astype(jnp.float32)
    gain = jnp.dot(onehot, species_gain, precision=lax.Precision.HIGHEST)
    charges = (jnp.dot(own_rows, w_charge, preferred_element_type=jnp.float32) * gain).astype(
        jnp.bfloat16
    )
    outgoing = jnp.concatenate([own_rows[downs], own_rows[ups]], axis=0)
    padded = extended_2(outgoing, (("dom", 0),), ghosts)
    extended = jnp.concatenate([own_rows, padded[:ghosts], padded[3 * ghosts :]], axis=0)
    cos_table, sin_table = phase_tables(coords, wave_vectors)
    filt = filter_table(wave_vectors, smearing)
    field_re, field_im = reduced_field(
        contract_rows(cos_table, charges), contract_rows(sin_table, charges), filt, inv_atoms
    )
    potential = (
        jnp.dot(cos_table, field_re, preferred_element_type=jnp.float32)
        + jnp.dot(sin_table, field_im, preferred_element_type=jnp.float32)
    ) * inv_waves
    message_rows = jnp.dot(extended, w_message, preferred_element_type=jnp.float32).astype(
        jnp.bfloat16
    )
    basis, envelope, radial = radial_terms(lengths, w_radial)
    picked = message_rows[senders].astype(jnp.float32)
    messages = live * radial * picked
    aggregate = (
        jnp.zeros((atoms, message_rows.shape[1]), jnp.float32).at[receivers].add(messages)
        * edge_scale
    )
    preact = aggregate + potential
    act = jax.nn.silu(preact).astype(jnp.bfloat16)
    updated = (
        own_rows.astype(jnp.float32) + jnp.dot(act, w_out, preferred_element_type=jnp.float32)
    ).astype(jnp.bfloat16)
    grad_act = jnp.dot(upstream_cot, w_out.T, preferred_element_type=jnp.float32)
    sig = jax.nn.sigmoid(preact)
    grad_pre = grad_act * sig * (1.0 + preact * (1.0 - sig))
    grad_pre_b = grad_pre.astype(jnp.bfloat16)
    grad_out = contract_rows(act, upstream_cot)
    dfield_re, dfield_im = reduced_field(
        contract_rows(cos_table, grad_pre_b),
        contract_rows(sin_table, grad_pre_b),
        filt,
        inv_waves * inv_atoms,
    )
    grad_charges = jnp.dot(cos_table, dfield_re, preferred_element_type=jnp.float32) + jnp.dot(
        sin_table, dfield_im, preferred_element_type=jnp.float32
    )
    grad_raw = (grad_charges * gain).astype(jnp.bfloat16)
    grad_charge = contract_rows(own_rows, grad_raw)
    feat_from_charge = jnp.dot(grad_raw, w_charge.T, preferred_element_type=jnp.float32)
    upstream = grad_pre[receivers] * edge_scale
    grad_picked = live * radial * upstream
    grad_radial_edge = live * picked * upstream
    grad_msg = (
        jnp.zeros(message_rows.shape, jnp.float32).at[senders].add(grad_picked).astype(jnp.bfloat16)
    )
    grad_message = contract_rows(extended, grad_msg)
    grad_rows = jnp.dot(grad_msg, w_message.T, preferred_element_type=jnp.float32)
    grad_radial = jnp.dot(
        basis.T, envelope[:, None] * grad_radial_edge, precision=lax.Precision.HIGHEST
    )
    returning = grad_rows[atoms:]
    padded_back = extended_2(returning, (("dom", 0),), ghosts)
    own_total = upstream_cot.astype(jnp.float32) + feat_from_charge + grad_rows[:atoms]
    own_total = own_total.at[downs].add(padded_back[:ghosts]).at[ups].add(padded_back[3 * ghosts :])
    feat_grad = own_total.astype(jnp.bfloat16)
    partials = (grad_charge, grad_message, grad_radial, grad_out)
    totals = lax.psum((partials[0], partials[1], partials[2], partials[3]), ("cell", "dom"))
    return (
        updated[None],
        feat_grad[None],
        totals[0] * grad_scale,
        totals[1] * grad_scale,
        totals[2] * grad_scale,
        totals[3] * grad_scale,
    )


def solution(mesh):
    placed = (
        P("cell", "dom", None),
        P("cell", None, "dom"),
        P("cell", "dom"),
        P(),
        P(),
        P(),
        P(),
        P(),
        P(),
        P(),
        P("cell", "dom"),
        P("cell", "dom"),
        P("cell", "dom"),
        P("cell", "dom"),
        P("cell", "dom"),
        P("cell", "dom"),
        P("cell", "dom", None),
    )
    return jax.shard_map(
        per_device,
        mesh=mesh,
        in_specs=placed,
        out_specs=(P("cell", "dom", None), P("cell", "dom", None), P(), P(), P(), P()),
        check_vma=False,
    )
```

profile of v0, /device:TPU:1, one launch (start us, length us, event | category | flops | bytes accessed | tf_op | source)
XLA Modules:
  0.0 887.6 jit_solution(7845488237856659214)
XLA Ops:
  8.0 1.3 gather_fusion.1
  9.3 3.3 collective-permute-start.1
  13.8 1.3 gather_fusion
  16.7 0.9 fusion.35
  18.3 0.9 fusion.19
  19.2 4.8 fusion.67
  24.0 4.9 fusion.68
  29.0 11.8 %all-reduce.9.cloned.1.call-start = ((), (), s32[]{:S(2)}) async-start(), calls=%async_computation.1 | async-start | bytes 4194304 | tf_op jit(solution)/shard_map/psum | solution.py:62
  41.2 19.4 %fusion = f32[12288,128]{1,0:T(8,128)} fusion(f32[8,128]{1,0:T(8,128)S(1)} %copy-done.30, f32[12288]{0:T(1024)S(1)} %add_multiply_fusion.1, f32[12288]{0:T(1024)S(1)} %bitcast.60, f32[8]{0:T(128)S(1)} %multiply_add_fusion, f32[12288]{0:T(1024)S(1)} %bitcast.63), kind=kOutput, calls=%fused_computation.9 | convolution fusion | flops 154533888 | bytes 6443040 | tf_op jit(solution)/shard_map/dot_general | solution.py:51
  62.7 35.9 %gather_fusion.2 = bf16[12288,128]{1,0:T(8,128)(2,1)S(1)} fusion(bf16[192,128]{1,0:T(8,128)(2,1)S(1)} %convolution_convert_fusion, s32[12288]{0:T(1024)S(1)} %broadcast_clamp_fusion.1), kind=kCustom, calls=%fused_computation.2 | custom fusion | bytes 6340608 | tf_op jit(solution)/shard_map/gather | solution.py:126
  98.6 67.1 %scatter_custom_fusion = f32[128,128]{1,0:T(8,128)} fusion(s32[12288]{0:T(1024)S(1)} %bitcast.67, f32[12288,128]{1,0:T(8,128)} %fusion, bf16[12288,128]{1,0:T(8,128)(2,1)S(1)} %gather_fusion.2, f32[]{:T(128)} %constant.16.clone.1), kind=kCustom, calls=%fused_computation.12 | custom fusion | flops 4718592 | bytes 9502724 | tf_op jit(solution)/shard_map/scatter-add | solution.py:129
  165.8 150.6 %all-reduce.11.cloned.1.call-done = (f32[2048,128]{1,0:T(8,128)}, f32[2048,128]{1,0:T(8,128)}) async-done(((f32[2048,128]{1,0:T(8,128)}, f32[2048,128]{1,0:T(8,128)}), (f32[2048,128]{1,0:T(8,128)}, f32[2048,128]{1,0:T(8,128)})) %all-reduce.11.cloned.1.call-update) | async-done | bytes 2097168 | tf_op jit(solution)/shard_map/psum | solution.py:62
  316.4 5.5 fusion.23
  322.0 4.9 fusion.18
  327.5 5.3 fusion.48
  332.8 4.9 fusion.46
  337.7 0.8 broadcast_clamp_fusion
  338.5 41.0 %gather_fusion.3 = f32[12288,128]{1,0:T(8,128)} fusion(f32[128,128]{1,0:T(8,128)S(1)} %fusion.16, s32[12288]{0:T(1024)S(1)} %broadcast_clamp_fusion), kind=kCustom, calls=%fused_computation.3 | custom fusion | bytes 12632064 | tf_op jit(solution)/shard_map/gather | solution.py:154
  379.5 66.7 %scatter_custom_fusion.1 = f32[192,128]{1,0:T(8,128)S(1)} fusion(s32[12288]{0:T(1024)S(1)} %bitcast.66, f32[12288,128]{1,0:T(8,128)} %fusion, f32[12288,128]{1,0:T(8,128)} %gather_fusion.3, f32[]{:T(128)} %constant.25.clone.1, f32[]{:T(128)} %constant.16.clone.1), kind=kCustom, calls=%fused_computation.16 | custom fusion | flops 4718592 | bytes 12681224 | tf_op jit(solution)/shard_map/scatter-add | solution.py:158
  447.6 13.3 %fusion.4 = f32[8,128]{1,0:T(8,128)} fusion(bf16[12288,128]{1,0:T(8,128)(2,1)S(1)} %gather_fusion.2, f32[12288,128]{1,0:T(8,128)} %gather_fusion.3, f32[12288]{0:T(1024)S(1)} %add_multiply_fusion.1, f32[12288]{0:T(1024)S(1)} %bitcast.61, f32[8]{0:T(128)} %copy-done.31, f32[12288]{0:T(1024)S(1)} %bitcast.64), kind=kOutput, calls=%fused_computation.15 | convolution fusion | flops 159252480 | bytes 9588768 | tf_op jit(solution)/shard_map/dot_general | solution.py:162
  461.0 81.0 %psum.62 = f32[8,128]{1,0:T(8,128)S(1)} all-reduce(f32[8,128]{1,0:T(8,128)} %fusion.4), channel_id=1, replica_groups=mesh['cell'=8,'dom'=32] {'cell','dom'}, use_global_device_ids=true, to_apply=%region_11.12 | all-reduce | flops 1024 | bytes 8192 | tf_op jit(solution)/shard_map/psum | solution.py:171
  542.0 1.6 fusion.22
  544.2 1.7 fusion.37
  545.9 1.6 fusion.42
  547.4 72.4 %all-reduce.9.cloned.1.call-done = (f32[2048,128]{1,0:T(8,128)}, f32[2048,128]{1,0:T(8,128)}) async-done(((f32[2048,128]{1,0:T(8,128)}, f32[2048,128]{1,0:T(8,128)}), (f32[2048,128]{1,0:T(8,128)}, f32[2048,128]{1,0:T(8,128)})) %all-reduce.9.cloned.1.call-update) | async-done | bytes 2097168 | tf_op jit(solution)/shard_map/psum | solution.py:62
  619.9 5.5 fusion.24
  625.4 4.2 fusion.21
  629.8 0.8 convolution_bitcast_fusion
  631.5 0.8 scatter_fusion.1
  632.9 244.1 %all-reduce.7.cloned.1.call-done = (f32[128,128]{0,1:T(8,128)}, f32[128,128]{0,1:T(8,128)}, f32[128,128]{0,1:T(8,128)}) async-done(((f32[128,128]{0,1:T(8,128)}, f32[128,128]{0,1:T(8,128)}, f32[128,128]{0,1:T(8,128)}), (f32[128,128]{0,1:T(8,128)}, f32[128,128]{0,1:T(8,128)}, f32[128,128]{0,1:T(8,128)})) %all-reduce.7.cloned.1.call-update) | async-done | bytes 196624 | tf_op jit(solution)/shard_map/psum | solution.py:171
  877.0 0.8 broadcast_multiply_fusion.2
  878.6 0.9 broadcast_multiply_fusion
  (138 shorter events, 12.9 us)
Async XLA Ops:
  7.2 55.4 %copy-start = (bf16[128,128]{1,0:T(8,128)(2,1)S(1)}, bf16[128,128]{1,0:T(8,128)(2,1)}, u32[]{:S(2)}) copy-start(bf16[128,128]{1,0:T(8,128)(2,1)} %param.24) | copy-start | bytes 98308
  7.2 33.6 %copy-start.9 = (s32[3,2048]{1,0:T(4,128)S(1)}, s32[3,2048]{1,0:T(4,128)}, u32[]{:S(2)}) copy-start(s32[3,2048]{1,0:T(4,128)} %param.20) | copy-start | bytes 73732
  7.2 33.7 %copy-start.2 = (f32[1,12288]{1,0:T(1,128)S(1)}, f32[1,12288]{1,0:T(1,128)}, u32[]{:S(2)}) copy-start(f32[1,12288]{1,0:T(1,128)} %param.30) | copy-start | bytes 147460
  7.2 33.9 %copy-start.11 = (s32[1,12288]{1,0:T(1,128)S(1)}, s32[1,12288]{1,0:T(1,128)}, u32[]{:S(2)}) copy-start(s32[1,12288]{1,0:T(1,128)} %param.29) | copy-start | bytes 147460
  7.2 33.9 %copy-start.12 = (s32[1,12288]{1,0:T(1,128)S(1)}, s32[1,12288]{1,0:T(1,128)}, u32[]{:S(2)}) copy-start(s32[1,12288]{1,0:T(1,128)} %param.27) | copy-start | bytes 147460
  7.2 34.0 %copy-start.30 = (f32[8,128]{1,0:T(8,128)S(1)}, f32[8,128]{1,0:T(8,128)}, u32[]{:S(2)}) copy-start(f32[8,128]{1,0:T(8,128)} %param.25) | copy-start | bytes 12292
  7.2 309.2 %all-reduce.11.cloned.1.call-start = ((), (), s32[]{:S(2)}) async-start(), calls=%async_computation.2 | async-start | bytes 4194304 | tf_op jit(solution)/shard_map/psum | solution.py:62
  9.3 52.0 %collective-permute-start.1 = (bf16[32,128]{1,0:T(8,128)(2,1)S(1)}, bf16[32,128]{1,0:T(8,128)(2,1)S(1)}, u32[]{:S(2)}, u32[]{:S(2)}) collective-permute-start(bf16[32,128]{1,0:T(8,128)(2,1)S(1)} %gather_fusion.1), channel_id=1, source_target_pairs={{1,0},{2,1},{3,2},{4,3},{5,4},{6,5},{7,6},{8,7},{9,8},{10,9},{11,1... | collective-permute-start | bytes 24584 | tf_op jit(solution)/shard_map/ppermute | solution.py:23
  15.1 46.2 %collective-permute-start = (bf16[32,128]{1,0:T(8,128)(2,1)S(1)}, bf16[32,128]{1,0:T(8,128)(2,1)S(1)}, u32[]{:S(2)}, u32[]{:S(2)}) collective-permute-start(bf16[32,128]{1,0:T(8,128)(2,1)S(1)} %gather_fusion), channel_id=1, source_target_pairs={{0,1},{1,2},{2,3},{3,4},{4,5},{5,6},{6,7},{7,8},{8,9},{9,10},{10,1... | collective-permute-start | bytes 24584 | tf_op jit(solution)/shard_map/ppermute | solution.py:20
  29.0 590.9 %all-reduce.9.cloned.1.call-start = ((), (), s32[]{:S(2)}) async-start(), calls=%async_computation.1 | async-start | bytes 4194304 | tf_op jit(solution)/shard_map/psum | solution.py:62
  60.7 37.9 %copy-start.7 = (s32[12288,1]{0,1:T(1,128)}, s32[12288,1]{0,1:T(1,128)S(1)}, u32[]{:S(2)}) copy-start(s32[12288,1]{0,1:T(1,128)S(1)} %compare_select_fusion.1) | copy-start | bytes 147460
  98.6 217.8 %copy-start.15 = (f32[2048]{0:T(1024)S(1)}, f32[2048]{0:T(1024)}, u32[]{:S(2)}) copy-start(f32[2048]{0:T(1024)} %get-tuple-element.36) | copy-start | bytes 24580
  98.6 217.8 %copy-start.17 = (f32[2048]{0:T(1024)S(1)}, f32[2048]{0:T(1024)}, u32[]{:S(2)}) copy-start(f32[2048]{0:T(1024)} %get-tuple-element.37) | copy-start | bytes 24580
  165.8 156.1 %copy-start.10 = (f32[128,128]{1,0:T(8,128)S(1)}, f32[128,128]{1,0:T(8,128)}, u32[]{:S(2)}) copy-start(f32[128,128]{1,0:T(8,128)} %scatter_custom_fusion) | copy-start | bytes 196612
  165.8 156.1 %copy-start.20 = (f32[1,2048]{1,0:T(1,128)S(1)}, f32[1,2048]{1,0:T(1,128)}, u32[]{:S(2)}) copy-start(f32[1,2048]{1,0:T(1,128)} %copy-done.19) | copy-start | bytes 24580
  165.8 156.2 %copy-start.23 = (f32[1,2048]{1,0:T(1,128)S(1)}, f32[1,2048]{1,0:T(1,128)}, u32[]{:S(2)}) copy-start(f32[1,2048]{1,0:T(1,128)} %copy-done.22) | copy-start | bytes 24580
  165.8 156.2 %copy-start.26 = (f32[1,2048]{1,0:T(1,128)S(1)}, f32[1,2048]{1,0:T(1,128)}, u32[]{:S(2)}) copy-start(f32[1,2048]{1,0:T(1,128)} %copy-done.25) | copy-start | bytes 24580
  165.8 156.2 %copy-start.37 = (f32[128]{0:T(128)S(1)}, f32[128]{0:T(128)}, u32[]{:S(2)}) copy-start(f32[128]{0:T(128)} %copy-done.36) | copy-start | bytes 1540
  165.8 156.2 %copy-start.40 = (f32[128]{0:T(128)S(1)}, f32[128]{0:T(128)}, u32[]{:S(2)}) copy-start(f32[128]{0:T(128)} %copy-done.39) | copy-start | bytes 1540
  337.7 539.3 %all-reduce.7.cloned.1.call-start = ((), (), s32[]{:S(2)}) async-start(), calls=%async_computation | async-start | bytes 393216 | tf_op jit(solution)/shard_map/psum | solution.py:171
  447.1 183.5 %collective-permute-start.2 = (f32[32,128]{1,0:T(8,128)S(1)}, f32[32,128]{1,0:T(8,128)S(1)}, u32[]{:S(2)}, u32[]{:S(2)}) collective-permute-start(f32[32,128]{1,0:T(8,128)S(1)} %get-tuple-element.32), channel_id=1, source_target_pairs={{0,1},{1,2},{2,3},{3,4},{4,5},{5,6},{6,7},{7,8},{8,9},{9,10},{10,1... | collective-permute-start | bytes 49160 | tf_op jit(solution)/shard_map/ppermute | solution.py:20
  447.1 184.3 %collective-permute-start.3 = (f32[32,128]{1,0:T(8,128)S(1)}, f32[32,128]{1,0:T(8,128)S(1)}, u32[]{:S(2)}, u32[]{:S(2)}) collective-permute-start(f32[32,128]{1,0:T(8,128)S(1)} %get-tuple-element.31), channel_id=1, source_target_pairs={{1,0},{2,1},{3,2},{4,3},{5,4},{6,5},{7,6},{8,7},{9,8},{10,9},{11,1... | collective-permute-start | bytes 49160 | tf_op jit(solution)/shard_map/ppermute | solution.py:23
  460.9 164.4 %copy-start.6 = (f32[128,128]{1,0:T(8,128)S(1)}, f32[128,128]{1,0:T(8,128)}, u32[]{:S(2)}) copy-start(f32[128,128]{1,0:T(8,128)} %copy-done.5) | copy-start | bytes 196612
  460.9 164.4 %copy-start.16 = (f32[2048]{0:T(1024)S(1)}, f32[2048]{0:T(1024)}, u32[]{:S(2)}) copy-start(f32[2048]{0:T(1024)} %get-tuple-element.36) | copy-start | bytes 24580
  460.9 164.4 %copy-start.18 = (f32[2048]{0:T(1024)S(1)}, f32[2048]{0:T(1024)}, u32[]{:S(2)}) copy-start(f32[2048]{0:T(1024)} %get-tuple-element.37) | copy-start | bytes 24580
  460.9 164.4 %copy-start.21 = (f32[1,2048]{1,0:T(1,128)S(1)}, f32[1,2048]{1,0:T(1,128)}, u32[]{:S(2)}) copy-start(f32[1,2048]{1,0:T(1,128)} %copy-done.19) | copy-start | bytes 24580
  460.9 164.4 %copy-start.24 = (f32[1,2048]{1,0:T(1,128)S(1)}, f32[1,2048]{1,0:T(1,128)}, u32[]{:S(2)}) copy-start(f32[1,2048]{1,0:T(1,128)} %copy-done.22) | copy-start | bytes 24580
  461.0 164.4 %copy-start.27 = (f32[1,2048]{1,0:T(1,128)S(1)}, f32[1,2048]{1,0:T(1,128)}, u32[]{:S(2)}) copy-start(f32[1,2048]{1,0:T(1,128)} %copy-done.25) | copy-start | bytes 24580
  461.0 164.4 %copy-start.38 = (f32[128]{0:T(128)S(1)}, f32[128]{0:T(128)}, u32[]{:S(2)}) copy-start(f32[128]{0:T(128)} %copy-done.36) | copy-start | bytes 1540
  461.0 164.4 %copy-start.41 = (f32[128]{0:T(128)S(1)}, f32[128]{0:T(128)}, u32[]{:S(2)}) copy-start(f32[128]{0:T(128)} %copy-done.39) | copy-start | bytes 1540
  461.0 164.4 %copy-start.44 = (f32[128]{0:T(128)S(1)}, f32[128]{0:T(128)}, u32[]{:S(2)}) copy-start(f32[128]{0:T(128)} %copy-done.42) | copy-start | bytes 1540
  461.0 164.4 %copy-start.48 = (f32[128]{0:T(128)S(1)}, f32[128]{0:T(128)}, u32[]{:S(2)}) copy-start(f32[128]{0:T(128)} %param.21) | copy-start | bytes 1540
  (25 other events, 258.4 us)
Sparse Core Ops, SparseCore 0:
  29.1 287.2 all-reduce.10
  337.8 282.0 all-reduce.8
  630.7 246.2 all-reduce.6
where the time goes:
time: 896 us; the launch traced here: 888 us
  waiting for transfers between devices  467 us (52%)
  other arithmetic  142 us (16%)
  local copies, waits for them, and re-layouts  86.2 us (10%)
  blocking collectives  81 us (9%)
  matrix products  80.6 us (9%)
  starting transfers between devices  15.8 us (2%)
  between operations  14.6 us (2%)
    psum x1, waiting for transfers between devices, per_device(): lax.psum((partials[0], partials[1], partials[2], partials[3]), ('cell', '...  244 us
    psum x2, waiting for transfers between devices, reduced_field(): total_re, total_im = lax.psum((local_re, local_im), 'dom')  223 us
    psum x1, blocking collectives, per_device(): lax.psum((partials[0], partials[1], partials[2], partials[3]), ('cell', '...  81 us
    scatter-add x1, other arithmetic, per_device(): jnp.zeros((atoms, message_rows.shape[1]), jnp.float32).at[receivers]  67.1 us
    scatter-add x1, other arithmetic, per_device(): jnp.zeros(message_rows.shape, jnp.float32).at[senders].add(grad_picked)  66.7 us
    gather x1, local copies, waits for them, and re-layouts, per_device(): upstream = grad_pre[receivers] * edge_scale  41 us
    gather x1, local copies, waits for them, and re-layouts, per_device(): picked = message_rows[senders].astype(jnp.float32)  35.9 us
    dot_general x7, matrix products, contract_rows(): lax.dot_general(left, right, (((0,), (0,)), ((), ())), preferred_element_...  23.9 us
  transfers between devices with their start and end apart: 7, of which 3 were waited for; matrix products, arithmetic and copies ran while one was open for 31% of the time, Pallas kernels for 0%

commit v1 on v0

v1 whole, which is shorter than its diff:
```python
import functools
import math

import jax
import jax.numpy as jnp
from jax import lax
from jax.experimental import pallas as pl
from jax.experimental.pallas import tpu as pltpu
from jax.sharding import PartitionSpec as P

bf16 = jnp.bfloat16
f32 = jnp.float32

C = 128
K = 2048
NB = 8
ATOMS = 128
GHOST = 32
EXT = ATOMS + 2 * GHOST
EDGES = 12288
DOMS = 32
CELLS = 8
ROW = 8
KB = K // ROW
PACK = ATOMS + 16
GROWS = 3 * C + 16
CHUNK = 1024

cutoff_radius = 6.0
basis_width = 0.75
edge_scale = 0.25
filter_factor = 12.0
inv_waves = 1.0 / math.sqrt(K)
inv_atoms = 1.0 / math.sqrt(ATOMS * DOMS)
grad_scale = 1.0 / math.sqrt(CELLS * ATOMS * DOMS)

COS_TURN = (
    0.9999999890754399,
    -19.73920450099313,
    64.93911749956553,
    -85.45013994347214,
    60.16763282514798,
    -25.967602441408868,
    6.528658639370483,
)
SIN_TURN = (
    6.283184916984331,
    -41.34158926418157,
    81.59994386455666,
    -76.61447586020026,
    41.342889428722025,
    -12.471244745942547,
)


def horner(coefficients, x):
    total = jnp.full_like(x, coefficients[-1])
    for value in coefficients[-2::-1]:
        total = total * x + value
    return total


def iota(shape, axis):
    return lax.broadcasted_iota(jnp.int32, shape, axis)


def dot(left, right):
    return jnp.dot(left, right, preferred_element_type=f32)


def dot_rows(left, right):
    return lax.dot_general(left, right, (((0,), (0,)), ((), ())), preferred_element_type=f32)


def dot_lanes(left, right):
    return lax.dot_general(left, right, (((1,), (1,)), ((), ())), preferred_element_type=f32)


def split(values):
    high = values.astype(bf16)
    return high, (values - high.astype(f32)).astype(bf16)


def call(kernel, outs, *args, scratch=(), flops=0, grid=None, in_specs=None, out_specs=None, name=None):
    more = {}
    if grid is not None:
        more = {"grid": grid, "in_specs": in_specs, "out_specs": out_specs}
    return pl.pallas_call(
        kernel,
        out_shape=[jax.ShapeDtypeStruct(shape, dtype) for shape, dtype in outs],
        scratch_shapes=list(scratch),
        compiler_params=pltpu.CompilerParams(vmem_limit_bytes=40 * 1024 * 1024),
        name=name,
        **more,
    )(*args)


def pack_kernel(feats, coords, kinds, downs, ups, packed, sent_up, sent_down):
    rows = feats[...]
    packed[0:ATOMS, :] = rows
    place = coords[...]
    high = place.astype(bf16).astype(f32)
    rest = place - high
    middle = rest.astype(bf16).astype(f32)
    low = rest - middle
    at = iota((16, ATOMS), 0)
    tail = jnp.zeros((16, ATOMS), f32)
    for part, values in enumerate((high, middle, low)):
        for axis in range(3):
            tail = jnp.where(at == 3 * part + axis, values[axis : axis + 1, :], tail)
    tail = jnp.where(at == 9, kinds[...].astype(f32), tail)
    packed[ATOMS:PACK, :] = tail.astype(bf16)
    atom = iota((ATOMS, GHOST), 0)
    sent_up[...] = dot_rows((atom == ups[...]).astype(f32).astype(bf16), rows).astype(bf16)
    sent_down[...] = dot_rows((atom == downs[...]).astype(f32).astype(bf16), rows).astype(bf16)


def structure_kernel(packed, waves, smearing, species_gain, w_charge, table, sums, filt, gain, charges):
    block = lax.rem(lax.axis_index("dom"), ROW)
    mine = waves[:, pl.ds(pl.multiple_of(block * KB, KB), KB)].astype(f32)
    at = iota((16, KB), 0)
    stacked = jnp.zeros((16, KB), f32)
    for axis in range(3):
        stacked = jnp.where(at == axis, mine[axis : axis + 1, :], stacked)
    stacked = stacked.astype(bf16)
    axis_at = iota((16, C), 0)
    lanes = [
        dot_rows(stacked, (axis_at == axis).astype(f32).astype(bf16)) for axis in range(3)
    ]
    squared = lanes[0] * lanes[0] + lanes[1] * lanes[1] + lanes[2] * lanes[2]
    filt[...] = filter_factor * jnp.exp(-squared * smearing[...]) / jnp.sqrt(squared)
    kind_at = iota((8, ATOMS), 0).astype(f32)
    for j in range(ROW):
        rows = packed[PACK * j : PACK * j + ATOMS, :]
        tail = packed[PACK * j + ATOMS : PACK * (j + 1), :].astype(f32)
        onehot = (tail[9:10, :] == kind_at).astype(f32)
        own_gain = lax.dot_general(
            onehot,
            species_gain[...],
            (((0,), (0,)), ((), ())),
            precision=lax.Precision.HIGHEST,
            preferred_element_type=f32,
        )
        span = slice(ATOMS * j, ATOMS * (j + 1))
        gain[span, :] = own_gain
        charges[span, :] = (dot(rows, w_charge[...]) * own_gain).astype(bf16)
        turns = jnp.zeros((KB, ATOMS), f32)
        for axis in range(3):
            place = tail[axis : axis + 1, :] + tail[axis + 3 : axis + 4, :] + tail[axis + 6 : axis + 7, :]
            turns = turns + place * lanes[axis]
        turns = turns - jnp.round(turns)
        square = turns * turns
        table[0:KB, span] = horner(COS_TURN, square).astype(bf16)
        table[KB : 2 * KB, span] = (turns * horner(SIN_TURN, square)).astype(bf16)
    sums[...] = dot(table[...], charges[...]).astype(bf16)


def field_of(parts, filt, scale):
    total = parts[0][...].astype(f32)
    for part in parts[1:]:
        total = total + part[...].astype(f32)
    weight = filt[...]
    return jnp.concatenate(
        [
            (weight * total[0:KB] * scale).astype(bf16),
            (weight * total[KB : 2 * KB] * scale).astype(bf16),
        ],
        axis=0,
    )


def potential_kernel(s0, s1, s2, s3, filt, table, send, keep):
    field = field_of((s0, s1, s2, s3), filt, inv_atoms)
    values = dot_rows(table[...], field) * inv_waves
    half = ROW * ATOMS // 2
    keep[...] = values[:half]
    send[...] = values[half:].astype(bf16)


def halve_kernel(held, received, send, keep):
    half = keep.shape[0]
    keep[...] = held[0:half, :] + received[0:half, :].astype(f32)
    send[...] = (held[half : 2 * half, :] + received[half : 2 * half, :].astype(f32)).astype(bf16)


def edge_kernel(senders, receivers, live, lengths, total, left, right):
    step = pl.program_id(0)
    reach = lengths[...]
    turn = reach * (0.5 / cutoff_radius)
    envelope = 0.5 * (horner(COS_TURN, turn * turn) + 1.0) * live[...].astype(f32)
    centers = 0.5 + basis_width * iota((NB, CHUNK), 0).astype(f32)
    offset = (reach - centers) * (1.0 / basis_width)
    weights = (jnp.exp(-offset * offset) * envelope).astype(bf16)
    atom = iota((ATOMS, CHUNK), 0)
    onehot = (atom == receivers[...]).astype(f32).astype(bf16)
    for b in range(NB):
        left[ATOMS * b : ATOMS * (b + 1), :] = onehot * weights[b : b + 1, :]
    source = iota((EXT, CHUNK), 0)
    right[...] = (source == senders[...]).astype(f32).astype(bf16)

    @pl.when(step == 0)
    def _():
        total[...] = jnp.zeros_like(total)

    total[...] += dot_lanes(left[...], right[...])


def aggregate_kernel(feats, below, above, w_message, operator, w_radial, aggregate, radial_rows):
    extended = jnp.concatenate([feats[...], below[...], above[...]], axis=0)
    rows = dot(extended, w_message[...]).astype(bf16)
    high, low = split(operator[...])
    products = dot(high, rows) + dot(low, rows)
    radial_rows[...] = products
    total = jnp.zeros((ATOMS, C), f32)
    for b in range(NB):
        total = total + w_radial[b : b + 1, :] * products[ATOMS * b : ATOMS * (b + 1)]
    aggregate[...] = total * edge_scale


def update_kernel(held, received, aggregate, feats, cotangent, w_out, updated, act_out, grad_pre, grad_pre_b):
    preact = aggregate[...] + held[...] + received[...].astype(f32)
    sig = jax.nn.sigmoid(preact)
    grad_act = dot_lanes(cotangent[...], w_out[...])
    grad = grad_act * sig * (1.0 + preact * (1.0 - sig))
    grad_pre[...] = grad
    grad_pre_b[...] = grad.astype(bf16)
    act = (preact * sig).astype(bf16)
    act_out[...] = act
    updated[...] = (feats[...].astype(f32) + dot(act, w_out[...])).astype(bf16)


def message_back_kernel(
    grad_pre, act, cotangent, feats, below, above, w_message, operator, radial_rows, w_radial,
    own, back_below, back_above, grads,
):
    grad = grad_pre[...] * edge_scale
    stacked = jnp.concatenate([w_radial[b : b + 1, :] * grad for b in range(NB)], axis=0).astype(bf16)
    high, low = split(operator[...])
    grad_msg = (dot_rows(high, stacked) + dot_rows(low, stacked)).astype(bf16)
    grad_rows = dot_lanes(grad_msg, w_message[...])
    own[...] = cotangent[...].astype(f32) + grad_rows[:ATOMS]
    back_below[...] = grad_rows[ATOMS : ATOMS + GHOST]
    back_above[...] = grad_rows[ATOMS + GHOST :]
    extended = jnp.concatenate([feats[...], below[...], above[...]], axis=0)
    grads[0:C, :] = dot_rows(extended, grad_msg).astype(bf16)
    grads[C : 2 * C, :] = dot_rows(act[...], cotangent[...]).astype(bf16)
    at = iota((16, C), 0)
    tail = jnp.zeros((16, C), f32)
    for b in range(NB):
        part = jnp.sum(grad * radial_rows[ATOMS * b : ATOMS * (b + 1), :], axis=0, keepdims=True)
        tail = jnp.where(at == b, part, tail)
    grads[2 * C :, :] = tail.astype(bf16)


def back_structure_kernel(table, grad_pre_b, sums):
    sums[...] = dot(table[...], grad_pre_b[...]).astype(bf16)


def charge_back_kernel(s0, s1, s2, s3, filt, table, gain, packed, grads, send, keep, partial, rounded):
    field = field_of((s0, s1, s2, s3), filt, inv_waves * inv_atoms)
    half = ROW * ATOMS // 2
    values = dot_rows(table[...], field) * gain[...]
    rounded[...] = values.astype(bf16)
    keep[...] = values[:half]
    send[0:half, :] = rounded[half:, :]
    total = jnp.zeros((C, C), f32)
    for j in range(ROW):
        total = total + dot_rows(
            packed[PACK * j : PACK * j + ATOMS, :], rounded[ATOMS * j : ATOMS * (j + 1), :]
        )
    partial[0:C, :] = total.astype(bf16)
    partial[C:, :] = grads[...]
    send[half:, :] = partial[...]


def tail_kernel(held, held_grads, received, send, keep, partial):
    whole = held.shape[0]
    half = whole // 2
    values = held[...] + received[0:whole, :].astype(f32)
    total = (held_grads[...].astype(f32) + received[whole:, :].astype(f32)).astype(bf16)
    keep[...] = values[:half]
    partial[...] = total
    send[0:half, :] = values[half:].astype(bf16)
    send[half:, :] = total


def raw_kernel(held, held_grads, received, raw, partial):
    raw[...] = (held[...] + received[0:ATOMS, :].astype(f32)).astype(bf16)
    partial[...] = (held_grads[...].astype(f32) + received[ATOMS:, :].astype(f32)).astype(bf16)


def feature_kernel(raw, w_charge, own, downs, ups, back_down, back_up, out):
    total = own[...] + dot_lanes(raw[...], w_charge[...])
    atom = iota((ATOMS, GHOST), 0)
    for index, rows in ((downs, back_down), (ups, back_up)):
        onehot = (atom == index[...]).astype(f32).astype(bf16)
        high, low = split(rows[...])
        total = total + dot(onehot, high) + dot(onehot, low)
    out[...] = total.astype(bf16)


def add_kernel(held, received, out):
    out[...] = (held[...].astype(f32) + received[...].astype(f32)).astype(bf16)


def weights_kernel(held, received, charge, message, radial, out):
    total = (held[...].astype(f32) + received[...].astype(f32)) * grad_scale
    charge[...] = total[0:C]
    message[...] = total[C : 2 * C]
    out[...] = total[2 * C : 3 * C]
    radial[...] = total[3 * C : 3 * C + NB]


def swap(values, axis, mask):
    count = lax.axis_size(axis)
    return lax.ppermute(values, axis, [(i, i ^ mask) for i in range(count)])


def shift(values, by):
    return lax.ppermute(values, "dom", [(i, (i + by) % DOMS) for i in range(DOMS)])


def gather_row(values):
    for mask in (4, 2, 1):
        values = jnp.concatenate([values, swap(values, "dom", mask)], axis=0)
    return values


def column_parts(values):
    return [values] + [swap(values, "dom", mask) for mask in (8, 16, 24)]


def per_device(
    feats,
    positions,
    species,
    wave_vectors,
    smearing,
    species_gain,
    w_charge,
    w_message,
    w_radial,
    w_out,
    edge_sender,
    edge_receiver,
    edge_mask,
    edge_length,
    ghost_down,
    ghost_up,
    cotangent,
):
    own_rows = feats[0]
    cot = cotangent[0]
    packed, sent_up, sent_down = call(
        pack_kernel,
        [((PACK, C), bf16), ((GHOST, C), bf16), ((GHOST, C), bf16)],
        own_rows, positions[0], species, ghost_down, ghost_up,
        name="pack",
    )
    gathered = gather_row(packed)
    below = shift(sent_up, 1)
    above = shift(sent_down, -1)

    edge_spec = pl.BlockSpec((1, CHUNK), lambda e: (0, e))
    (operator,) = call(
        edge_kernel,
        [((NB * ATOMS, EXT), f32)],
        edge_sender, edge_receiver, edge_mask, edge_length,
        scratch=[pltpu.VMEM((NB * ATOMS, CHUNK), bf16), pltpu.VMEM((EXT, CHUNK), bf16)],
        grid=(EDGES // CHUNK,),
        in_specs=[edge_spec] * 4,
        out_specs=[pl.BlockSpec((NB * ATOMS, EXT), lambda e: (0, 0))],
        name="edges",
    )
    table, sums, filt, gain = call(
        structure_kernel,
        [((2 * KB, ROW * ATOMS), bf16), ((2 * KB, C), bf16), ((KB, C), f32), ((ROW * ATOMS, C), f32)],
        gathered, wave_vectors, smearing[None], species_gain, w_charge,
        scratch=[pltpu.VMEM((ROW * ATOMS, C), bf16)],
        name="structure",
    )
    parts = column_parts(sums)
    half = ROW * ATOMS // 2
    send, keep = call(
        potential_kernel, [((half, C), bf16), ((half, C), f32)], *parts, filt, table, name="potential"
    )
    for mask in (1, 2):
        received = swap(send, "dom", mask)
        half //= 2
        send, keep = call(
            halve_kernel, [((half, C), bf16), ((half, C), f32)], keep, received, name="halve"
        )
    received = swap(send, "dom", 4)
    aggregate, radial_rows = call(
        aggregate_kernel,
        [((ATOMS, C), f32), ((NB * ATOMS, C), f32)],
        own_rows, below, above, w_message, operator, w_radial,
        name="aggregate",
    )
    updated, act, grad_pre, grad_pre_b = call(
        update_kernel,
        [((ATOMS, C), bf16), ((ATOMS, C), bf16), ((ATOMS, C), f32), ((ATOMS, C), bf16)],
        keep, received, aggregate, own_rows, cot, w_out,
        name="update",
    )
    all_grad_pre = gather_row(grad_pre_b)
    own, back_below, back_above, grads = call(
        message_back_kernel,
        [((ATOMS, C), f32), ((GHOST, C), f32), ((GHOST, C), f32), ((2 * C + 16, C), bf16)],
        grad_pre, act, cot, own_rows, below, above, w_message, operator, radial_rows, w_radial,
        name="message_back",
    )
    back_down = shift(back_above, 1)
    back_up = shift(back_below, -1)
    (back_sums,) = call(
        back_structure_kernel, [((2 * KB, C), bf16)], table, all_grad_pre, name="back_structure"
    )
    parts = column_parts(back_sums)
    half = ROW * ATOMS // 2
    send, keep, partial = call(
        charge_back_kernel,
        [((half + GROWS, C), bf16), ((half, C), f32), ((GROWS, C), bf16)],
        *parts, filt, table, gain, gathered, grads,
        scratch=[pltpu.VMEM((ROW * ATOMS, C), bf16)],
        name="charge_back",
    )
    for mask in (1, 2):
        received = swap(send, "dom", mask)
        half //= 2
        send, keep, partial = call(
            tail_kernel,
            [((half + GROWS, C), bf16), ((half, C), f32), ((GROWS, C), bf16)],
            keep, partial, received,
            name="tail",
        )
    received = swap(send, "dom", 4)
    raw, partial = call(
        raw_kernel, [((ATOMS, C), bf16), ((GROWS, C), bf16)], keep, partial, received, name="raw"
    )
    for axis, mask in (("dom", 8), ("dom", 24), ("cell", 2), ("cell", 6)):
        received = swap(partial, axis, mask)
        (partial,) = call(add_kernel, [((GROWS, C), bf16)], partial, received, name="add")
    received = swap(partial, "cell", 1)
    (feat_grad,) = call(
        feature_kernel,
        [((ATOMS, C), bf16)],
        raw, w_charge, own, ghost_down, ghost_up, back_down, back_up,
        name="feature",
    )
    charge, message, radial, out = call(
        weights_kernel,
        [((C, C), f32), ((C, C), f32), ((NB, C), f32), ((C, C), f32)],
        partial, received,
        name="weights",
    )
    return updated[None], feat_grad[None], charge, message, radial, out


def solution(mesh):
    placed = (
        P("cell", "dom", None),
        P("cell", None, "dom"),
        P("cell", "dom"),
        P(),
        P(),
        P(),
        P(),
        P(),
        P(),
        P(),
        P("cell", "dom"),
        P("cell", "dom"),
        P("cell", "dom"),
        P("cell", "dom"),
        P("cell", "dom"),
        P("cell", "dom"),
        P("cell", "dom", None),
    )
    return jax.shard_map(
        per_device,
        mesh=mesh,
        in_specs=placed,
        out_specs=(P("cell", "dom", None), P("cell", "dom", None), P(), P(), P(), P()),
        check_vma=False,
    )
```

time: 896 us -> 130 us (0.15)
  the two profiles are of different devices: /device:TPU:1 before, /device:TPU:6 now
where the time goes in v1:
time: 130 us
  waiting for transfers between devices  62.6 us (48%)
  starting transfers between devices  43 us (33%)
  Pallas kernels  20.5 us (16%)
  local copies, waits for them, and re-layouts  2.97 us (2%)
    ppermute x23, waiting for transfers between devices, swap(): return lax.ppermute(values, axis, [(i, i ^ mask) for i in range(count)])  61 us
    ppermute x23, starting transfers between devices, swap(): return lax.ppermute(values, axis, [(i, i ^ mask) for i in range(count)])  36.8 us
    pallas_call x20, Pallas kernels, call(): pl.pallas_call(kernel, out_shape=[jax.ShapeDtypeStruct(shape, dtype) for...  20.5 us
    ppermute x4, starting transfers between devices, shift(): lax.ppermute(values, 'dom', [(i, (i + by) % DOMS) for i in range(DOMS)])  6.16 us
    unnamed x38, local copies, waits for them, and re-layouts  2.95 us
  transfers between devices with their start and end apart: 27, of which 22 were waited for; matrix products, arithmetic and copies ran while one was open for 0% of the time, Pallas kernels for 11%

profile of v1, /device:TPU:6, one launch (start us, length us, event | category | flops | bytes accessed | tf_op | source)
XLA Modules:
  0.0 129.9 jit_solution(5934324658396722595)
XLA Ops:
  2.9 3.3 %collective-permute-start = (bf16[144,128]{1,0:T(8,128)(2,1)S(1)}, bf16[144,128]{1,0:T(8,128)(2,1)S(1)}, u32[]{:S(2)}, u32[]{:S(2)}) collective-permute-start(bf16[144,128]{1,0:T(8,128)(2,1)S(1)} %get-tuple-element.44), channel_id=1, source_target_pairs={{0,4},{1,5},{2,6},{3,7},{4,0},{5,1},{6,2},{7,3},{8,12},{9,13},{10,... | collective-permute-start | bytes 110600 | tf_op jit(solution)/shard_map/ppermute | solution.py:316
  6.2 1.9 %collective-permute-done = bf16[144,128]{1,0:T(8,128)(2,1)S(1)} collective-permute-done((bf16[144,128]{1,0:T(8,128)(2,1)S(1)}, bf16[144,128]{1,0:T(8,128)(2,1)S(1)}, u32[]{:S(2)}, u32[]{:S(2)}) %collective-permute-start) | collective-permute-done | bytes 36896 | tf_op jit(solution)/shard_map/ppermute | solution.py:316
  8.2 1.9 %collective-permute-start.1 = (bf16[288,128]{1,0:T(8,128)(2,1)S(1)}, bf16[288,128]{1,0:T(8,128)(2,1)S(1)}, u32[]{:S(2)}, u32[]{:S(2)}) collective-permute-start(bf16[288,128]{1,0:T(8,128)(2,1)S(1)} %pad_maximum_fusion.3), channel_id=1, source_target_pairs={{0,2},{1,3},{2,0},{3,1},{4,6},{5,7},{6,4},{7,5},{8,10},{9,11},{10,... | collective-permute-start | bytes 221192 | tf_op jit(solution)/shard_map/ppermute | solution.py:316
  10.1 2.4 %collective-permute-done.1 = bf16[288,128]{1,0:T(8,128)(2,1)S(1)} collective-permute-done((bf16[288,128]{1,0:T(8,128)(2,1)S(1)}, bf16[288,128]{1,0:T(8,128)(2,1)S(1)}, u32[]{:S(2)}, u32[]{:S(2)}) %collective-permute-start.1) | collective-permute-done | bytes 73760 | tf_op jit(solution)/shard_map/ppermute | solution.py:316
  14.7 2.0 %structure.1 = (bf16[512,1024]{1,0:T(8,128)(2,1)S(1)}, bf16[512,128]{1,0:T(8,128)(2,1)S(1)}, f32[256,128]{1,0:T(8,128)S(1)}, f32[1024,128]{1,0:T(8,128)S(1)}) custom-call(bf16[1152,128]{1,0:T(8,128)(2,1)S(1)} %constant_dynamic-update-slice_fusion.packed, s32[3,2048]{1,0:T(4,128)S(1)} %copy-done.9, f32[1,128]{1,0:T(1,128)S(1)} %bitcast.15, ...), custom_call_target="tpu_custom_call" | custom-call | tf_op jit(solution)/shard_map/structure/pallas_call | solution.py:88
  16.6 1.7 %collective-permute-start.3 = (bf16[512,128]{1,0:T(8,128)(2,1)S(1)}, bf16[512,128]{1,0:T(8,128)(2,1)S(1)}, u32[]{:S(2)}, u32[]{:S(2)}) collective-permute-start(bf16[512,128]{1,0:T(8,128)(2,1)S(1)} %get-tuple-element.45.s0), channel_id=1, source_target_pairs={{0,8},{1,9},{2,10},{3,11},{4,12},{5,13},{6,14},{7,15},{8,0},{9,1},... | collective-permute-start | bytes 393224 | tf_op jit(solution)/shard_map/ppermute | solution.py:316
  18.3 2.9 %collective-permute-start.4 = (bf16[512,128]{1,0:T(8,128)(2,1)S(1)}, bf16[512,128]{1,0:T(8,128)(2,1)S(1)}, u32[]{:S(2)}, u32[]{:S(2)}) collective-permute-start(bf16[512,128]{1,0:T(8,128)(2,1)S(1)} %get-tuple-element.45.s0), channel_id=1, source_target_pairs={{0,16},{1,17},{2,18},{3,19},{4,20},{5,21},{6,22},{7,23},{8,24},{9,... | collective-permute-start | bytes 393224 | tf_op jit(solution)/shard_map/ppermute | solution.py:316
  22.7 4.9 %collective-permute-done.4.s2 = bf16[512,128]{1,0:T(8,128)(2,1)S(1)} collective-permute-done((bf16[512,128]{1,0:T(8,128)(2,1)S(1)}, bf16[512,128]{1,0:T(8,128)(2,1)S(1)}, u32[]{:S(2)}, u32[]{:S(2)}) %collective-permute-start.4) | collective-permute-done | bytes 131104 | tf_op jit(solution)/shard_map/ppermute | solution.py:316
  27.6 2.2 %collective-permute-done.5.s3 = bf16[512,128]{1,0:T(8,128)(2,1)S(1)} collective-permute-done((bf16[512,128]{1,0:T(8,128)(2,1)S(1)}, bf16[512,128]{1,0:T(8,128)(2,1)S(1)}, u32[]{:S(2)}, u32[]{:S(2)}) %collective-permute-start.5) | collective-permute-done | bytes 131104 | tf_op jit(solution)/shard_map/ppermute | solution.py:316
  31.9 2.0 %collective-permute-start.7 = (bf16[256,128]{1,0:T(8,128)(2,1)S(1)}, bf16[256,128]{1,0:T(8,128)(2,1)S(1)}, u32[]{:S(2)}, u32[]{:S(2)}) collective-permute-start(bf16[256,128]{1,0:T(8,128)(2,1)S(1)} %get-tuple-element.51), channel_id=1, source_target_pairs={{0,2},{1,3},{2,0},{3,1},{4,6},{5,7},{6,4},{7,5},{8,10},{9,11},{10,... | collective-permute-start | bytes 196616 | tf_op jit(solution)/shard_map/ppermute | solution.py:316
  33.9 2.4 %collective-permute-done.7.received = bf16[256,128]{1,0:T(8,128)(2,1)S(1)} collective-permute-done((bf16[256,128]{1,0:T(8,128)(2,1)S(1)}, bf16[256,128]{1,0:T(8,128)(2,1)S(1)}, u32[]{:S(2)}, u32[]{:S(2)}) %collective-permute-start.7) | collective-permute-done | bytes 65568 | tf_op jit(solution)/shard_map/ppermute | solution.py:316
  36.3 3.0 %collective-permute-start.8 = (bf16[128,128]{1,0:T(8,128)(2,1)S(1)}, bf16[128,128]{1,0:T(8,128)(2,1)S(1)}, u32[]{:S(2)}, u32[]{:S(2)}) collective-permute-start(bf16[128,128]{1,0:T(8,128)(2,1)S(1)} %get-tuple-element.53), channel_id=1, source_target_pairs={{0,4},{1,5},{2,6},{3,7},{4,0},{5,1},{6,2},{7,3},{8,12},{9,13},{10,... | collective-permute-start | bytes 98312 | tf_op jit(solution)/shard_map/ppermute | solution.py:316
  39.9 12.8 %edges.1.operator = f32[1024,192]{1,0:T(8,128)S(1)} custom-call(s32[1,12288]{1,0:T(1,128)S(1)} %copy-done.5, s32[1,12288]{1,0:T(1,128)S(1)} %copy-done.6, s32[1,12288]{1,0:T(1,128)S(1)} %copy-done.7, f32[1,12288]{1,0:T(1,128)S(1)} %copy-done.8), custom_call_target="tpu_custom_call" | custom-call | tf_op jit(solution)/shard_map/edges/pallas_call | solution.py:88
  55.4 3.6 %collective-permute-done.11 = bf16[128,128]{1,0:T(8,128)(2,1)S(1)} collective-permute-done((bf16[128,128]{1,0:T(8,128)(2,1)S(1)}, bf16[128,128]{1,0:T(8,128)(2,1)S(1)}, u32[]{:S(2)}, u32[]{:S(2)}) %collective-permute-start.11) | collective-permute-done | bytes 32800 | tf_op jit(solution)/shard_map/ppermute | solution.py:316
  59.1 1.9 %collective-permute-start.12 = (bf16[256,128]{1,0:T(8,128)(2,1)S(1)}, bf16[256,128]{1,0:T(8,128)(2,1)S(1)}, u32[]{:S(2)}, u32[]{:S(2)}) collective-permute-start(bf16[256,128]{1,0:T(8,128)(2,1)S(1)} %pad_maximum_fusion.4), channel_id=1, source_target_pairs={{0,2},{1,3},{2,0},{3,1},{4,6},{5,7},{6,4},{7,5},{8,10},{9,11},{10,... | collective-permute-start | bytes 196616 | tf_op jit(solution)/shard_map/ppermute | solution.py:316
  60.9 2.9 %collective-permute-done.12 = bf16[256,128]{1,0:T(8,128)(2,1)S(1)} collective-permute-done((bf16[256,128]{1,0:T(8,128)(2,1)S(1)}, bf16[256,128]{1,0:T(8,128)(2,1)S(1)}, u32[]{:S(2)}, u32[]{:S(2)}) %collective-permute-start.12) | collective-permute-done | bytes 65568 | tf_op jit(solution)/shard_map/ppermute | solution.py:316
  68.0 2.7 %collective-permute-start.16 = (bf16[512,128]{1,0:T(8,128)(2,1)S(1)}, bf16[512,128]{1,0:T(8,128)(2,1)S(1)}, u32[]{:S(2)}, u32[]{:S(2)}) collective-permute-start(bf16[512,128]{1,0:T(8,128)(2,1)S(1)} %back_structure.1.s0), channel_id=1, source_target_pairs={{0,24},{1,25},{2,26},{3,27},{4,28},{5,29},{6,30},{7,31},{8,16},{9,... | collective-permute-start | bytes 393224 | tf_op jit(solution)/shard_map/ppermute | solution.py:316
  72.4 2.0 %collective-permute-done.15.s2 = bf16[512,128]{1,0:T(8,128)(2,1)S(1)} collective-permute-done((bf16[512,128]{1,0:T(8,128)(2,1)S(1)}, bf16[512,128]{1,0:T(8,128)(2,1)S(1)}, u32[]{:S(2)}, u32[]{:S(2)}) %collective-permute-start.15) | collective-permute-done | bytes 131104 | tf_op jit(solution)/shard_map/ppermute | solution.py:316
  74.4 2.2 %collective-permute-done.16.s3 = bf16[512,128]{1,0:T(8,128)(2,1)S(1)} collective-permute-done((bf16[512,128]{1,0:T(8,128)(2,1)S(1)}, bf16[512,128]{1,0:T(8,128)(2,1)S(1)}, u32[]{:S(2)}, u32[]{:S(2)}) %collective-permute-start.16) | collective-permute-done | bytes 131104 | tf_op jit(solution)/shard_map/ppermute | solution.py:316
  77.5 1.5 %collective-permute-done.17.received = bf16[912,128]{1,0:T(8,128)(2,1)S(1)} collective-permute-done((bf16[912,128]{1,0:T(8,128)(2,1)S(1)}, bf16[912,128]{1,0:T(8,128)(2,1)S(1)}, u32[]{:S(2)}, u32[]{:S(2)}) %collective-permute-start.17) | collective-permute-done | bytes 233504 | tf_op jit(solution)/shard_map/ppermute | solution.py:316
  79.1 1.8 %collective-permute-start.18 = (bf16[656,128]{1,0:T(8,128)(2,1)S(1)}, bf16[656,128]{1,0:T(8,128)(2,1)S(1)}, u32[]{:S(2)}, u32[]{:S(2)}) collective-permute-start(bf16[656,128]{1,0:T(8,128)(2,1)S(1)} %get-tuple-element.69), channel_id=1, source_target_pairs={{0,2},{1,3},{2,0},{3,1},{4,6},{5,7},{6,4},{7,5},{8,10},{9,11},{10,... | collective-permute-start | bytes 503816 | tf_op jit(solution)/shard_map/ppermute | solution.py:316
  80.9 4.6 %collective-permute-done.18.received = bf16[656,128]{1,0:T(8,128)(2,1)S(1)} collective-permute-done((bf16[656,128]{1,0:T(8,128)(2,1)S(1)}, bf16[656,128]{1,0:T(8,128)(2,1)S(1)}, u32[]{:S(2)}, u32[]{:S(2)}) %collective-permute-start.18) | collective-permute-done | bytes 167968 | tf_op jit(solution)/shard_map/ppermute | solution.py:316
  85.5 1.8 %collective-permute-start.19 = (bf16[528,128]{1,0:T(8,128)(2,1)S(1)}, bf16[528,128]{1,0:T(8,128)(2,1)S(1)}, u32[]{:S(2)}, u32[]{:S(2)}) collective-permute-start(bf16[528,128]{1,0:T(8,128)(2,1)S(1)} %get-tuple-element.72), channel_id=1, source_target_pairs={{0,4},{1,5},{2,6},{3,7},{4,0},{5,1},{6,2},{7,3},{8,12},{9,13},{10,... | collective-permute-start | bytes 405512 | tf_op jit(solution)/shard_map/ppermute | solution.py:316
  87.3 6.9 %collective-permute-done.19.received = bf16[528,128]{1,0:T(8,128)(2,1)S(1)} collective-permute-done((bf16[528,128]{1,0:T(8,128)(2,1)S(1)}, bf16[528,128]{1,0:T(8,128)(2,1)S(1)}, u32[]{:S(2)}, u32[]{:S(2)}) %collective-permute-start.19) | collective-permute-done | bytes 135200 | tf_op jit(solution)/shard_map/ppermute | solution.py:316
  94.3 4.6 %collective-permute-done.22.received = bf16[400,128]{1,0:T(8,128)(2,1)S(1)} collective-permute-done((bf16[400,128]{1,0:T(8,128)(2,1)S(1)}, bf16[400,128]{1,0:T(8,128)(2,1)S(1)}, u32[]{:S(2)}, u32[]{:S(2)}) %collective-permute-start.22) | collective-permute-done | bytes 102432 | tf_op jit(solution)/shard_map/ppermute | solution.py:316
  99.0 2.8 %collective-permute-start.23 = (bf16[400,128]{1,0:T(8,128)(2,1)S(1)}, bf16[400,128]{1,0:T(8,128)(2,1)S(1)}, u32[]{:S(2)}, u32[]{:S(2)}) collective-permute-start(bf16[400,128]{1,0:T(8,128)(2,1)S(1)} %add.4.held), channel_id=1, source_target_pairs={{0,24},{1,25},{2,26},{3,27},{4,28},{5,29},{6,30},{7,31},{8,16},{9,... | collective-permute-start | bytes 307208 | tf_op jit(solution)/shard_map/ppermute | solution.py:316
  101.9 3.1 %collective-permute-done.23.received = bf16[400,128]{1,0:T(8,128)(2,1)S(1)} collective-permute-done((bf16[400,128]{1,0:T(8,128)(2,1)S(1)}, bf16[400,128]{1,0:T(8,128)(2,1)S(1)}, u32[]{:S(2)}, u32[]{:S(2)}) %collective-permute-start.23) | collective-permute-done | bytes 102432 | tf_op jit(solution)/shard_map/ppermute | solution.py:316
  105.9 3.9 %collective-permute-done.24.received = bf16[400,128]{1,0:T(8,128)(2,1)S(1)} collective-permute-done((bf16[400,128]{1,0:T(8,128)(2,1)S(1)}, bf16[400,128]{1,0:T(8,128)(2,1)S(1)}, u32[]{:S(2)}, u32[]{:S(2)}) %collective-permute-start.24) | collective-permute-done | bytes 102432 | tf_op jit(solution)/shard_map/ppermute | solution.py:316
  110.3 5.4 %collective-permute-done.25.received = bf16[400,128]{1,0:T(8,128)(2,1)S(1)} collective-permute-done((bf16[400,128]{1,0:T(8,128)(2,1)S(1)}, bf16[400,128]{1,0:T(8,128)(2,1)S(1)}, u32[]{:S(2)}, u32[]{:S(2)}) %collective-permute-start.25) | collective-permute-done | bytes 102432 | tf_op jit(solution)/shard_map/ppermute | solution.py:316
  115.8 5.4 %collective-permute-start.26 = (bf16[400,128]{1,0:T(8,128)(2,1)S(1)}, bf16[400,128]{1,0:T(8,128)(2,1)S(1)}, u32[]{:S(2)}, u32[]{:S(2)}) collective-permute-start(bf16[400,128]{1,0:T(8,128)(2,1)S(1)} %add.7.held), channel_id=1, source_target_pairs={{0,32},{32,0},{64,96},{96,64},{128,160},{160,128},{192,224},{224,1... | collective-permute-start | bytes 307208 | tf_op jit(solution)/shard_map/ppermute | solution.py:316
  121.2 5.7 %collective-permute-start.21 = (f32[32,128]{1,0:T(8,128)S(1)}, f32[32,128]{1,0:T(8,128)S(1)}, u32[]{:S(2)}, u32[]{:S(2)}) collective-permute-start(f32[32,128]{1,0:T(8,128)S(1)} %get-tuple-element.76), channel_id=1, source_target_pairs={{0,31},{1,0},{2,1},{3,2},{4,3},{5,4},{6,5},{7,6},{8,7},{9,8},{10,9... | collective-permute-start | bytes 49160 | tf_op jit(solution)/shard_map/ppermute | solution.py:320
  126.9 1.6 %collective-permute-done.20.back_down = f32[32,128]{1,0:T(8,128)S(1)} collective-permute-done((f32[32,128]{1,0:T(8,128)S(1)}, f32[32,128]{1,0:T(8,128)S(1)}, u32[]{:S(2)}, u32[]{:S(2)}) %collective-permute-start.20) | collective-permute-done | bytes 16416 | tf_op jit(solution)/shard_map/ppermute | solution.py:320
  (86 shorter events, 21.0 us)
Async XLA Ops:
  2.9 5.2 %collective-permute-start = (bf16[144,128]{1,0:T(8,128)(2,1)S(1)}, bf16[144,128]{1,0:T(8,128)(2,1)S(1)}, u32[]{:S(2)}, u32[]{:S(2)}) collective-permute-start(bf16[144,128]{1,0:T(8,128)(2,1)S(1)} %get-tuple-element.44), channel_id=1, source_target_pairs={{0,4},{1,5},{2,6},{3,7},{4,0},{5,1},{6,2},{7,3},{8,12},{9,13},{10,... | collective-permute-start | bytes 110600 | tf_op jit(solution)/shard_map/ppermute | solution.py:316
  8.2 4.4 %collective-permute-start.1 = (bf16[288,128]{1,0:T(8,128)(2,1)S(1)}, bf16[288,128]{1,0:T(8,128)(2,1)S(1)}, u32[]{:S(2)}, u32[]{:S(2)}) collective-permute-start(bf16[288,128]{1,0:T(8,128)(2,1)S(1)} %pad_maximum_fusion.3), channel_id=1, source_target_pairs={{0,2},{1,3},{2,0},{3,1},{4,6},{5,7},{6,4},{7,5},{8,10},{9,11},{10,... | collective-permute-start | bytes 221192 | tf_op jit(solution)/shard_map/ppermute | solution.py:316
  12.5 1.5 %collective-permute-start.2 = (bf16[576,128]{1,0:T(8,128)(2,1)S(1)}, bf16[576,128]{1,0:T(8,128)(2,1)S(1)}, u32[]{:S(2)}, u32[]{:S(2)}) collective-permute-start(bf16[576,128]{1,0:T(8,128)(2,1)S(1)} %pad_maximum_fusion.1), channel_id=1, source_target_pairs={{0,1},{1,0},{2,3},{3,2},{4,5},{5,4},{6,7},{7,6},{8,9},{9,8},{10,11... | collective-permute-start | bytes 442376 | tf_op jit(solution)/shard_map/ppermute | solution.py:316
  16.6 6.1 %collective-permute-start.3 = (bf16[512,128]{1,0:T(8,128)(2,1)S(1)}, bf16[512,128]{1,0:T(8,128)(2,1)S(1)}, u32[]{:S(2)}, u32[]{:S(2)}) collective-permute-start(bf16[512,128]{1,0:T(8,128)(2,1)S(1)} %get-tuple-element.45.s0), channel_id=1, source_target_pairs={{0,8},{1,9},{2,10},{3,11},{4,12},{5,13},{6,14},{7,15},{8,0},{9,1},... | collective-permute-start | bytes 393224 | tf_op jit(solution)/shard_map/ppermute | solution.py:316
  18.3 9.3 %collective-permute-start.4 = (bf16[512,128]{1,0:T(8,128)(2,1)S(1)}, bf16[512,128]{1,0:T(8,128)(2,1)S(1)}, u32[]{:S(2)}, u32[]{:S(2)}) collective-permute-start(bf16[512,128]{1,0:T(8,128)(2,1)S(1)} %get-tuple-element.45.s0), channel_id=1, source_target_pairs={{0,16},{1,17},{2,18},{3,19},{4,20},{5,21},{6,22},{7,23},{8,24},{9,... | collective-permute-start | bytes 393224 | tf_op jit(solution)/shard_map/ppermute | solution.py:316
  21.2 8.7 %collective-permute-start.5 = (bf16[512,128]{1,0:T(8,128)(2,1)S(1)}, bf16[512,128]{1,0:T(8,128)(2,1)S(1)}, u32[]{:S(2)}, u32[]{:S(2)}) collective-permute-start(bf16[512,128]{1,0:T(8,128)(2,1)S(1)} %get-tuple-element.45.s0), channel_id=1, source_target_pairs={{0,24},{1,25},{2,26},{3,27},{4,28},{5,29},{6,30},{7,31},{8,16},{9,... | collective-permute-start | bytes 393224 | tf_op jit(solution)/shard_map/ppermute | solution.py:316
  30.4 1.4 %collective-permute-start.6 = (bf16[512,128]{1,0:T(8,128)(2,1)S(1)}, bf16[512,128]{1,0:T(8,128)(2,1)S(1)}, u32[]{:S(2)}, u32[]{:S(2)}) collective-permute-start(bf16[512,128]{1,0:T(8,128)(2,1)S(1)} %get-tuple-element.49), channel_id=1, source_target_pairs={{0,1},{1,0},{2,3},{3,2},{4,5},{5,4},{6,7},{7,6},{8,9},{9,8},{10,11... | collective-permute-start | bytes 393224 | tf_op jit(solution)/shard_map/ppermute | solution.py:316
  31.9 4.4 %collective-permute-start.7 = (bf16[256,128]{1,0:T(8,128)(2,1)S(1)}, bf16[256,128]{1,0:T(8,128)(2,1)S(1)}, u32[]{:S(2)}, u32[]{:S(2)}) collective-permute-start(bf16[256,128]{1,0:T(8,128)(2,1)S(1)} %get-tuple-element.51), channel_id=1, source_target_pairs={{0,2},{1,3},{2,0},{3,1},{4,6},{5,7},{6,4},{7,5},{8,10},{9,11},{10,... | collective-permute-start | bytes 196616 | tf_op jit(solution)/shard_map/ppermute | solution.py:316
  36.3 3.6 %copy-start.7 = (s32[1,12288]{1,0:T(1,128)S(1)}, s32[1,12288]{1,0:T(1,128)}, u32[]{:S(2)}) copy-start(s32[1,12288]{1,0:T(1,128)} %live.1) | copy-start | bytes 147460
  36.3 3.6 %copy-start.8 = (f32[1,12288]{1,0:T(1,128)S(1)}, f32[1,12288]{1,0:T(1,128)}, u32[]{:S(2)}) copy-start(f32[1,12288]{1,0:T(1,128)} %lengths.1) | copy-start | bytes 147460
  36.3 17.0 %collective-permute-start.8 = (bf16[128,128]{1,0:T(8,128)(2,1)S(1)}, bf16[128,128]{1,0:T(8,128)(2,1)S(1)}, u32[]{:S(2)}, u32[]{:S(2)}) collective-permute-start(bf16[128,128]{1,0:T(8,128)(2,1)S(1)} %get-tuple-element.53), channel_id=1, source_target_pairs={{0,4},{1,5},{2,6},{3,7},{4,0},{5,1},{6,2},{7,3},{8,12},{9,13},{10,... | collective-permute-start | bytes 98312 | tf_op jit(solution)/shard_map/ppermute | solution.py:316
  39.3 13.4 %collective-permute-start.10 = (bf16[32,128]{1,0:T(8,128)(2,1)S(1)}, bf16[32,128]{1,0:T(8,128)(2,1)S(1)}, u32[]{:S(2)}, u32[]{:S(2)}) collective-permute-start(bf16[32,128]{1,0:T(8,128)(2,1)S(1)} %get-tuple-element.55), channel_id=1, source_target_pairs={{0,31},{1,0},{2,1},{3,2},{4,3},{5,4},{6,5},{7,6},{8,7},{9,8},{10,9... | collective-permute-start | bytes 24584 | tf_op jit(solution)/shard_map/ppermute | solution.py:320
  39.3 13.4 %copy-start.1 = (bf16[1,128,128]{2,1,0:T(8,128)(2,1)S(1)}, bf16[1,128,128]{2,1,0:T(8,128)(2,1)}, u32[]{:S(2)}) copy-start(bf16[1,128,128]{2,1,0:T(8,128)(2,1)} %param.17) | copy-start | bytes 98308
  39.3 13.4 %copy-start.2 = (bf16[128,128]{1,0:T(8,128)(2,1)S(1)}, bf16[128,128]{1,0:T(8,128)(2,1)}, u32[]{:S(2)}) copy-start(bf16[128,128]{1,0:T(8,128)(2,1)} %w_message.3) | copy-start | bytes 98308
  39.3 13.4 %copy-start.11 = (f32[8,128]{1,0:T(8,128)S(1)}, f32[8,128]{1,0:T(8,128)}, u32[]{:S(2)}) copy-start(f32[8,128]{1,0:T(8,128)} %w_radial.3) | copy-start | bytes 12292
  39.4 13.4 %collective-permute-start.9 = (bf16[32,128]{1,0:T(8,128)(2,1)S(1)}, bf16[32,128]{1,0:T(8,128)(2,1)S(1)}, u32[]{:S(2)}, u32[]{:S(2)}) collective-permute-start(bf16[32,128]{1,0:T(8,128)(2,1)S(1)} %get-tuple-element.54), channel_id=1, source_target_pairs={{0,1},{1,2},{2,3},{3,4},{4,5},{5,6},{6,7},{7,8},{8,9},{9,10},{10,1... | collective-permute-start | bytes 24584 | tf_op jit(solution)/shard_map/ppermute | solution.py:320
  54.3 4.8 %collective-permute-start.11 = (bf16[128,128]{1,0:T(8,128)(2,1)S(1)}, bf16[128,128]{1,0:T(8,128)(2,1)S(1)}, u32[]{:S(2)}, u32[]{:S(2)}) collective-permute-start(bf16[128,128]{1,0:T(8,128)(2,1)S(1)} %get-tuple-element.58), channel_id=1, source_target_pairs={{0,4},{1,5},{2,6},{3,7},{4,0},{5,1},{6,2},{7,3},{8,12},{9,13},{10,... | collective-permute-start | bytes 98312 | tf_op jit(solution)/shard_map/ppermute | solution.py:316
  59.1 4.7 %collective-permute-start.12 = (bf16[256,128]{1,0:T(8,128)(2,1)S(1)}, bf16[256,128]{1,0:T(8,128)(2,1)S(1)}, u32[]{:S(2)}, u32[]{:S(2)}) collective-permute-start(bf16[256,128]{1,0:T(8,128)(2,1)S(1)} %pad_maximum_fusion.4), channel_id=1, source_target_pairs={{0,2},{1,3},{2,0},{3,1},{4,6},{5,7},{6,4},{7,5},{8,10},{9,11},{10,... | collective-permute-start | bytes 196616 | tf_op jit(solution)/shard_map/ppermute | solution.py:316
  63.8 1.6 %collective-permute-start.13 = (bf16[512,128]{1,0:T(8,128)(2,1)S(1)}, bf16[512,128]{1,0:T(8,128)(2,1)S(1)}, u32[]{:S(2)}, u32[]{:S(2)}) collective-permute-start(bf16[512,128]{1,0:T(8,128)(2,1)S(1)} %pad_maximum_fusion.2), channel_id=1, source_target_pairs={{0,1},{1,0},{2,3},{3,2},{4,5},{5,4},{6,7},{7,6},{8,9},{9,8},{10,11... | collective-permute-start | bytes 393224 | tf_op jit(solution)/shard_map/ppermute | solution.py:316
  65.9 6.4 %collective-permute-start.14 = (bf16[512,128]{1,0:T(8,128)(2,1)S(1)}, bf16[512,128]{1,0:T(8,128)(2,1)S(1)}, u32[]{:S(2)}, u32[]{:S(2)}) collective-permute-start(bf16[512,128]{1,0:T(8,128)(2,1)S(1)} %back_structure.1.s0), channel_id=1, source_target_pairs={{0,8},{1,9},{2,10},{3,11},{4,12},{5,13},{6,14},{7,15},{8,0},{9,1},... | collective-permute-start | bytes 393224 | tf_op jit(solution)/shard_map/ppermute | solution.py:316
  66.5 7.9 %collective-permute-start.15 = (bf16[512,128]{1,0:T(8,128)(2,1)S(1)}, bf16[512,128]{1,0:T(8,128)(2,1)S(1)}, u32[]{:S(2)}, u32[]{:S(2)}) collective-permute-start(bf16[512,128]{1,0:T(8,128)(2,1)S(1)} %back_structure.1.s0), channel_id=1, source_target_pairs={{0,16},{1,17},{2,18},{3,19},{4,20},{5,21},{6,22},{7,23},{8,24},{9,... | collective-permute-start | bytes 393224 | tf_op jit(solution)/shard_map/ppermute | solution.py:316
  68.0 8.7 %collective-permute-start.16 = (bf16[512,128]{1,0:T(8,128)(2,1)S(1)}, bf16[512,128]{1,0:T(8,128)(2,1)S(1)}, u32[]{:S(2)}, u32[]{:S(2)}) collective-permute-start(bf16[512,128]{1,0:T(8,128)(2,1)S(1)} %back_structure.1.s0), channel_id=1, source_target_pairs={{0,24},{1,25},{2,26},{3,27},{4,28},{5,29},{6,30},{7,31},{8,16},{9,... | collective-permute-start | bytes 393224 | tf_op jit(solution)/shard_map/ppermute | solution.py:316
  77.4 1.6 %collective-permute-start.17 = (bf16[912,128]{1,0:T(8,128)(2,1)S(1)}, bf16[912,128]{1,0:T(8,128)(2,1)S(1)}, u32[]{:S(2)}, u32[]{:S(2)}) collective-permute-start(bf16[912,128]{1,0:T(8,128)(2,1)S(1)} %get-tuple-element.66), channel_id=1, source_target_pairs={{0,1},{1,0},{2,3},{3,2},{4,5},{5,4},{6,7},{7,6},{8,9},{9,8},{10,11... | collective-permute-start | bytes 700424 | tf_op jit(solution)/shard_map/ppermute | solution.py:316
  79.1 6.4 %collective-permute-start.18 = (bf16[656,128]{1,0:T(8,128)(2,1)S(1)}, bf16[656,128]{1,0:T(8,128)(2,1)S(1)}, u32[]{:S(2)}, u32[]{:S(2)}) collective-permute-start(bf16[656,128]{1,0:T(8,128)(2,1)S(1)} %get-tuple-element.69), channel_id=1, source_target_pairs={{0,2},{1,3},{2,0},{3,1},{4,6},{5,7},{6,4},{7,5},{8,10},{9,11},{10,... | collective-permute-start | bytes 503816 | tf_op jit(solution)/shard_map/ppermute | solution.py:316
  85.5 8.7 %collective-permute-start.19 = (bf16[528,128]{1,0:T(8,128)(2,1)S(1)}, bf16[528,128]{1,0:T(8,128)(2,1)S(1)}, u32[]{:S(2)}, u32[]{:S(2)}) collective-permute-start(bf16[528,128]{1,0:T(8,128)(2,1)S(1)} %get-tuple-element.72), channel_id=1, source_target_pairs={{0,4},{1,5},{2,6},{3,7},{4,0},{5,1},{6,2},{7,3},{8,12},{9,13},{10,... | collective-permute-start | bytes 405512 | tf_op jit(solution)/shard_map/ppermute | solution.py:316
  94.2 4.7 %collective-permute-start.22 = (bf16[400,128]{1,0:T(8,128)(2,1)S(1)}, bf16[400,128]{1,0:T(8,128)(2,1)S(1)}, u32[]{:S(2)}, u32[]{:S(2)}) collective-permute-start(bf16[400,128]{1,0:T(8,128)(2,1)S(1)} %get-tuple-element.77.held), channel_id=1, source_target_pairs={{0,8},{1,9},{2,10},{3,11},{4,12},{5,13},{6,14},{7,15},{8,0},{9,1},... | collective-permute-start | bytes 307208 | tf_op jit(solution)/shard_map/ppermute | solution.py:316
  99.0 6.0 %collective-permute-start.23 = (bf16[400,128]{1,0:T(8,128)(2,1)S(1)}, bf16[400,128]{1,0:T(8,128)(2,1)S(1)}, u32[]{:S(2)}, u32[]{:S(2)}) collective-permute-start(bf16[400,128]{1,0:T(8,128)(2,1)S(1)} %add.4.held), channel_id=1, source_target_pairs={{0,24},{1,25},{2,26},{3,27},{4,28},{5,29},{6,30},{7,31},{8,16},{9,... | collective-permute-start | bytes 307208 | tf_op jit(solution)/shard_map/ppermute | solution.py:316
  105.0 4.7 %collective-permute-start.24 = (bf16[400,128]{1,0:T(8,128)(2,1)S(1)}, bf16[400,128]{1,0:T(8,128)(2,1)S(1)}, u32[]{:S(2)}, u32[]{:S(2)}) collective-permute-start(bf16[400,128]{1,0:T(8,128)(2,1)S(1)} %add.5.held), channel_id=1, source_target_pairs={{0,64},{32,96},{64,0},{96,32},{128,192},{160,224},{192,128},{224,1... | collective-permute-start | bytes 307208 | tf_op jit(solution)/shard_map/ppermute | solution.py:316
  109.8 6.0 %collective-permute-start.25 = (bf16[400,128]{1,0:T(8,128)(2,1)S(1)}, bf16[400,128]{1,0:T(8,128)(2,1)S(1)}, u32[]{:S(2)}, u32[]{:S(2)}) collective-permute-start(bf16[400,128]{1,0:T(8,128)(2,1)S(1)} %add.6.held), channel_id=1, source_target_pairs={{0,192},{32,224},{64,128},{96,160},{128,64},{160,96},{192,0},{224,... | collective-permute-start | bytes 307208 | tf_op jit(solution)/shard_map/ppermute | solution.py:316
  115.8 13.5 %collective-permute-start.26 = (bf16[400,128]{1,0:T(8,128)(2,1)S(1)}, bf16[400,128]{1,0:T(8,128)(2,1)S(1)}, u32[]{:S(2)}, u32[]{:S(2)}) collective-permute-start(bf16[400,128]{1,0:T(8,128)(2,1)S(1)} %add.7.held), channel_id=1, source_target_pairs={{0,32},{32,0},{64,96},{96,64},{128,160},{160,128},{192,224},{224,1... | collective-permute-start | bytes 307208 | tf_op jit(solution)/shard_map/ppermute | solution.py:316
  121.2 7.2 %collective-permute-start.20 = (f32[32,128]{1,0:T(8,128)S(1)}, f32[32,128]{1,0:T(8,128)S(1)}, u32[]{:S(2)}, u32[]{:S(2)}) collective-permute-start(f32[32,128]{1,0:T(8,128)S(1)} %get-tuple-element.75), channel_id=1, source_target_pairs={{0,1},{1,2},{2,3},{3,4},{4,5},{5,6},{6,7},{7,8},{8,9},{9,10},{10,1... | collective-permute-start | bytes 49160 | tf_op jit(solution)/shard_map/ppermute | solution.py:320
  121.2 7.2 %collective-permute-start.21 = (f32[32,128]{1,0:T(8,128)S(1)}, f32[32,128]{1,0:T(8,128)S(1)}, u32[]{:S(2)}, u32[]{:S(2)}) collective-permute-start(f32[32,128]{1,0:T(8,128)S(1)} %get-tuple-element.76), channel_id=1, source_target_pairs={{0,31},{1,0},{2,1},{3,2},{4,3},{5,4},{6,5},{7,6},{8,7},{9,8},{10,9... | collective-permute-start | bytes 49160 | tf_op jit(solution)/shard_map/ppermute | solution.py:320
  (12 other events, 15.5 us)

commit v2 on v1

v2 whole, which is shorter than its diff:
```python
import math

import jax
import jax.numpy as jnp
from jax import lax
from jax.experimental import pallas as pl
from jax.experimental.pallas import tpu as pltpu
from jax.sharding import PartitionSpec as P

bf16 = jnp.bfloat16
f32 = jnp.float32

C = 128
K = 2048
NB = 8
ATOMS = 128
GHOST = 32
EXT = ATOMS + 2 * GHOST
EDGES = 12288
DOMS = 32
CELLS = 8
ROW = 8
KB = K // ROW
PACK = ATOMS + 16
QUARTER = 80
HALF = ROW * ATOMS // 2
CHUNK = 1024
EDGE_STEPS = (3, 5, 1, 3)

cutoff_radius = 6.0
basis_width = 0.75
edge_scale = 0.25
filter_factor = 12.0
inv_waves = 1.0 / math.sqrt(K)
inv_atoms = 1.0 / math.sqrt(ATOMS * DOMS)
grad_scale = 1.0 / math.sqrt(CELLS * ATOMS * DOMS)

COS_TURN = (
    0.9999999890754399,
    -19.73920450099313,
    64.93911749956553,
    -85.45013994347214,
    60.16763282514798,
    -25.967602441408868,
    6.528658639370483,
)
SIN_TURN = (
    6.283184916984331,
    -41.34158926418157,
    81.59994386455666,
    -76.61447586020026,
    41.342889428722025,
    -12.471244745942547,
)


def horner(coefficients, x):
    total = jnp.full_like(x, coefficients[-1])
    for value in coefficients[-2::-1]:
        total = total * x + value
    return total


def iota(shape, axis):
    return lax.broadcasted_iota(jnp.int32, shape, axis)


def dot(left, right):
    return jnp.dot(left, right, preferred_element_type=f32)


def dot_rows(left, right):
    return lax.dot_general(left, right, (((0,), (0,)), ((), ())), preferred_element_type=f32)


def dot_lanes(left, right):
    return lax.dot_general(left, right, (((1,), (1,)), ((), ())), preferred_element_type=f32)


def split(values):
    high = values.astype(bf16)
    return high, (values - high.astype(f32)).astype(bf16)


def call(kernel, outs, *args, scratch=(), flops=0, after=(), name=None, **more):
    def run(*refs):
        kernel(*refs[: len(args)], *refs[len(args) + len(after) :])

    if "in_specs" not in more:
        more["in_specs"] = [pl.BlockSpec(memory_space=pltpu.VMEM)] * len(args)
        more["out_specs"] = [pl.BlockSpec(memory_space=pltpu.VMEM)] * len(outs)
    more["in_specs"] = more["in_specs"] + [pl.BlockSpec(memory_space=pl.ANY)] * len(after)
    return pl.pallas_call(
        run,
        out_shape=[jax.ShapeDtypeStruct(shape, dtype) for shape, dtype in outs],
        scratch_shapes=list(scratch),
        compiler_params=pltpu.CompilerParams(vmem_limit_bytes=40 * 1024 * 1024),
        cost_estimate=pl.CostEstimate(flops=flops, bytes_accessed=1 << 18, transcendentals=0),
        name=name,
        **more,
    )(*args, *after)


def place_in_row():
    return lax.rem(lax.axis_index("dom"), ROW)


def at_block(mask, rows):
    return pl.multiple_of((mask // 2 + (mask % 2) * (ROW // 2)) * rows, rows)


def quarter_at(part):
    return pl.ds(pl.multiple_of(((place_in_row() // 2) ^ part) * QUARTER, QUARTER), QUARTER)


def pack_kernel(feats, coords, kinds, downs, ups, packed, tail):
    packed[0:ATOMS, :] = feats[...]
    place = coords[...]
    high = place.astype(bf16).astype(f32)
    rest = place - high
    middle = rest.astype(bf16).astype(f32)
    low = rest - middle
    at = iota((16, ATOMS), 0)
    values = jnp.zeros((16, ATOMS), f32)
    for part, piece in enumerate((high, middle, low)):
        for axis in range(3):
            values = jnp.where(at == 3 * part + axis, piece[axis : axis + 1, :], values)
    tail[...] = jnp.where(at == 9, kinds[...].astype(f32), values)
    tail[10:11, 0:GHOST] = ups[...].astype(f32)
    tail[11:12, 0:GHOST] = downs[...].astype(f32)
    packed[ATOMS:PACK, :] = tail[...].astype(bf16)


def wave_lanes(waves):
    mine = waves[:, pl.ds(pl.multiple_of(place_in_row() * KB, KB), KB)].astype(f32)
    at = iota((16, KB), 0)
    stacked = jnp.zeros((16, KB), f32)
    for axis in range(3):
        stacked = jnp.where(at == axis, mine[axis : axis + 1, :], stacked)
    stacked = stacked.astype(bf16)
    axis_at = iota((16, C), 0)
    return [dot_rows(stacked, (axis_at == axis).astype(f32).astype(bf16)) for axis in range(3)]


def tables_of(packed, lanes, species_gain, w_charge, table, gain, charges):
    kind_at = iota((8, ATOMS), 0).astype(f32)
    for j in range(ROW // 2):
        rows = packed[PACK * j : PACK * j + ATOMS, :]
        tail = packed[PACK * j + ATOMS : PACK * (j + 1), :].astype(f32)
        onehot = (tail[9:10, :] == kind_at).astype(f32)
        own_gain = lax.dot_general(
            onehot,
            species_gain[...],
            (((0,), (0,)), ((), ())),
            precision=lax.Precision.HIGHEST,
            preferred_element_type=f32,
        )
        span = slice(ATOMS * j, ATOMS * (j + 1))
        gain[span, :] = own_gain
        charges[span, :] = (dot(rows, w_charge[...]) * own_gain).astype(bf16)
        turns = jnp.zeros((KB, ATOMS), f32)
        for axis in range(3):
            place = tail[axis : axis + 1, :] + tail[axis + 3 : axis + 4, :] + tail[axis + 6 : axis + 7, :]
            turns = turns + place * lanes[axis]
        turns = turns - jnp.round(turns)
        square = turns * turns
        table[0:KB, span] = horner(COS_TURN, square).astype(bf16)
        table[KB : 2 * KB, span] = (turns * horner(SIN_TURN, square)).astype(bf16)


def structure_near_kernel(packed, waves, smearing, species_gain, w_charge, table, sums, filt, gain, charges):
    lanes = wave_lanes(waves)
    squared = lanes[0] * lanes[0] + lanes[1] * lanes[1] + lanes[2] * lanes[2]
    filt[...] = filter_factor * jnp.exp(-squared * smearing[...]) / jnp.sqrt(squared)
    tables_of(packed, lanes, species_gain, w_charge, table, gain, charges)
    sums[...] = dot(table[...], charges[...])


def structure_far_kernel(
    packed, near, near_sums, waves, species_gain, w_charge,
    table, sums, message, gain, below, above, charges, joined,
):
    tables_of(packed, wave_lanes(waves), species_gain, w_charge, table, gain, charges)
    total = (near_sums[...] + dot(table[...], charges[...])).astype(bf16)
    sums[...] = total
    message[0 : 2 * KB, :] = total
    joined[0 : PACK * ROW // 2, :] = near[...]
    joined[PACK * ROW // 2 :, :] = packed[...]
    place = place_in_row()
    atom = iota((ATOMS, GHOST), 0).astype(f32)

    def ghosts(owner, row):
        start = at_block(place ^ owner, PACK)
        rows = joined[pl.ds(start, ATOMS), :]
        tail = joined[pl.ds(pl.multiple_of(start + ATOMS, 16), 16), :].astype(f32)
        return dot_rows((atom == tail[row : row + 1, 0:GHOST]).astype(f32).astype(bf16), rows).astype(bf16)

    below[...] = ghosts((place + ROW - 1) % ROW, 10)
    above[...] = ghosts((place + 1) % ROW, 11)
    message[2 * KB : 2 * KB + GHOST, :] = ghosts(ROW - 1, 10)
    message[2 * KB + GHOST :, :] = ghosts(0, 11)


def column_sum(own, up, down, over, span):
    return (own[span, :].astype(f32) + over[span, :].astype(f32)) + (
        up[span, :].astype(f32) + down[span, :].astype(f32)
    )


def field_of(sums, filt, scale):
    weight = filt[...] * scale
    return jnp.concatenate(
        [(weight * sums[0:KB]).astype(bf16), (weight * sums[KB : 2 * KB]).astype(bf16)], axis=0
    )


def potential_kernel(own, up, down, over, filt, near, far, send, keep):
    field = field_of(column_sum(own, up, down, over, slice(0, 2 * KB)), filt, inv_atoms)
    send[...] = (dot_rows(far[...], field) * inv_waves).astype(bf16)
    keep[...] = dot_rows(near[...], field) * inv_waves


def spread_kernel(held, received, own, *sends):
    values = held[...] + received[...].astype(f32)
    own[...] = values[0:ATOMS]
    for part, send in enumerate(sends):
        send[...] = values[ATOMS * (part + 1) : ATOMS * (part + 2)].astype(bf16)


def edge_kernel(first, *refs):
    senders, receivers, live, lengths = refs[:4]
    total, left, right = refs[-3:]
    step = pl.program_id(0)
    reach = lengths[...]
    turn = reach * (0.5 / cutoff_radius)
    envelope = 0.5 * (horner(COS_TURN, turn * turn) + 1.0) * live[...].astype(f32)
    centers = 0.5 + basis_width * iota((NB, CHUNK), 0).astype(f32)
    offset = (reach - centers) * (1.0 / basis_width)
    weights = (jnp.exp(-offset * offset) * envelope).astype(bf16)
    atom = iota((ATOMS, CHUNK), 0)
    onehot = (atom == receivers[...]).astype(f32).astype(bf16)
    for b in range(NB):
        left[ATOMS * b : ATOMS * (b + 1), :] = onehot * weights[b : b + 1, :]
    source = iota((EXT, CHUNK), 0)
    right[...] = (source == senders[...]).astype(f32).astype(bf16)

    @pl.when(step == 0)
    def _():
        total[...] = jnp.zeros_like(total) if first else refs[4][...]

    total[...] += dot_lanes(left[...], right[...])


def aggregate_kernel(feats, below, above, up, down, w_message, operator, w_radial, aggregate, radial_rows, extended):
    place = place_in_row()
    extended[0:ATOMS, :] = feats[...]
    first, last = 2 * KB, 2 * KB + GHOST
    extended[ATOMS : ATOMS + GHOST, :] = jnp.where(place == 0, up[first:last, :], below[...])
    extended[ATOMS + GHOST :, :] = jnp.where(place == ROW - 1, down[last:, :], above[...])
    rows = dot(extended[...], w_message[...]).astype(bf16)
    high, low = split(operator[...])
    products = dot(high, rows) + dot(low, rows)
    radial_rows[...] = products
    total = jnp.zeros((ATOMS, C), f32)
    for b in range(NB):
        total = total + w_radial[b : b + 1, :] * products[ATOMS * b : ATOMS * (b + 1)]
    aggregate[...] = total * edge_scale


def update_kernel(
    held, near, across, corner, aggregate, feats, cotangent, w_out, extended, w_message, operator, radial_rows,
    w_radial, updated, own_total, own_rows, own_quarter, send_near, send_across, send_corner, grads,
):
    preact = aggregate[...] + (
        (held[...] + near[...].astype(f32)) + (across[...].astype(f32) + corner[...].astype(f32))
    )
    sig = jax.nn.sigmoid(preact)
    grad_act = dot_lanes(cotangent[...], w_out[...])
    grad = grad_act * sig * (1.0 + preact * (1.0 - sig))
    rounded = grad.astype(bf16)
    grad = grad * edge_scale
    stacked = jnp.concatenate([w_radial[b : b + 1, :] * grad for b in range(NB)], axis=0).astype(bf16)
    high, low = split(operator[...])
    grad_msg = (dot_rows(high, stacked) + dot_rows(low, stacked)).astype(bf16)
    grad_rows = dot_lanes(grad_msg, w_message[...])
    own_total[...] = cotangent[...].astype(f32) + grad_rows[:ATOMS]
    own_rows[0:ATOMS, :] = rounded
    own_rows[ATOMS:, :] = grad_rows[ATOMS:].astype(bf16)
    act = (preact * sig).astype(bf16)
    updated[...] = (feats[...].astype(f32) + dot(act, w_out[...])).astype(bf16)
    grads[0:C, :] = dot_rows(extended[...], grad_msg)
    grads[C : 2 * C, :] = dot_rows(act, cotangent[...])
    at = iota((4 * QUARTER - 2 * C, C), 0)
    tail = jnp.zeros((4 * QUARTER - 2 * C, C), f32)
    for b in range(NB):
        part = jnp.sum(grad * radial_rows[ATOMS * b : ATOMS * (b + 1), :], axis=0, keepdims=True)
        tail = jnp.where(at == b, part, tail)
    grads[2 * C :, :] = tail
    own_quarter[...] = grads[quarter_at(0), :]
    for part, send in ((1, send_near), (2, send_across), (3, send_corner)):
        send[0:EXT, :] = own_rows[...]
        send[EXT:, :] = grads[quarter_at(part), :].astype(bf16)


def join_kernel(own_rows, own_quarter, near, across, corner, joined):
    quarter = own_quarter[...]
    for part, rows in enumerate((own_rows, near, across, corner)):
        joined[ATOMS * part : ATOMS * (part + 1), :] = rows[0:ATOMS, :]
        start = HALF + 2 * GHOST * part
        joined[start : start + 2 * GHOST, :] = rows[ATOMS:EXT, :]
        if part:
            quarter = quarter + rows[EXT:, :].astype(f32)
    joined[HALF + 8 * GHOST :, :] = quarter.astype(bf16)


def back_near_kernel(table, joined, sums):
    sums[...] = dot(table[...], joined[0:HALF, :])


def back_far_kernel(table, received, joined, near_sums, message, over, back_down, back_up, ghosts):
    total = (near_sums[...] + dot(table[...], received[0:HALF, :])).astype(bf16)
    ends = HALF + 8 * GHOST
    quarter = (joined[ends:, :].astype(f32) + received[ends:, :].astype(f32)).astype(bf16)
    for target in (message, over):
        target[0 : 2 * KB, :] = total
        target[2 * KB : 2 * KB + QUARTER, :] = quarter
    ghosts[0 : 8 * GHOST, :] = joined[HALF:ends, :]
    ghosts[8 * GHOST :, :] = received[HALF:ends, :]
    place = place_in_row()

    def returned(owner, above):
        start = at_block(place ^ owner, 2 * GHOST) + above * GHOST
        return ghosts[pl.ds(pl.multiple_of(start, GHOST), GHOST), :]

    back_down[...] = returned((place + ROW - 1) % ROW, 1)
    back_up[...] = returned((place + 1) % ROW, 0)
    message[2 * KB + QUARTER : 2 * KB + QUARTER + GHOST, :] = returned(ROW - 1, 1)
    message[2 * KB + QUARTER + GHOST :, :] = returned(0, 0)


def charge_back_kernel(
    own, up, down, over, filt, near, far, near_gain, far_gain, near_rows, far_rows,
    send, keep, charge, quarter, rounded,
):
    field = field_of(column_sum(own, up, down, over, slice(0, 2 * KB)), filt, inv_waves * inv_atoms)
    quarter[...] = column_sum(own, up, down, over, slice(2 * KB, 2 * KB + QUARTER)).astype(bf16)
    send[0:HALF, :] = (dot_rows(far[...], field) * far_gain[...]).astype(bf16)
    values = dot_rows(near[...], field) * near_gain[...]
    keep[...] = values
    rounded[...] = values.astype(bf16)
    total = jnp.zeros((C, C), f32)
    for j in range(ROW // 2):
        rows, atoms = slice(PACK * j, PACK * j + ATOMS), slice(ATOMS * j, ATOMS * (j + 1))
        total = total + dot_rows(near_rows[rows, :], rounded[atoms, :])
        total = total + dot_rows(far_rows[rows, :], send[atoms, :])
    charge[...] = total.astype(bf16)
    send[HALF:, :] = charge[...]


def tail_spread_kernel(held, charge, quarter, received, own, charge_out, *sends):
    values = held[...] + received[0:HALF, :].astype(f32)
    total = (charge[...].astype(f32) + received[HALF:, :].astype(f32)).astype(bf16)
    own[...] = values[0:ATOMS]
    charge_out[...] = total
    for part, send in enumerate(sends):
        send[0:ATOMS, :] = values[ATOMS * (part + 1) : ATOMS * (part + 2)].astype(bf16)
        send[ATOMS : ATOMS + C, :] = total
        send[ATOMS + C :, :] = quarter[...]


def raw_kernel(held, charge, quarter, near, across, corner, raw, charge_out, grads):
    rows = slice(0, ATOMS)
    raw[...] = (
        (held[...] + near[rows, :].astype(f32)) + (across[rows, :].astype(f32) + corner[rows, :].astype(f32))
    ).astype(bf16)
    rows = slice(ATOMS, ATOMS + C)
    charge_out[...] = (
        (charge[...].astype(f32) + near[rows, :].astype(f32))
        + (across[rows, :].astype(f32) + corner[rows, :].astype(f32))
    ).astype(bf16)
    grads[quarter_at(0), :] = quarter[...]
    for part, received in ((1, near), (2, across), (3, corner)):
        grads[quarter_at(part), :] = received[ATOMS + C :, :]


def charge_sum_kernel(own, up, down, over, grads, out):
    out[0:C, :] = column_sum(own, up, down, over, slice(0, C)).astype(bf16)
    out[C:, :] = grads[...]


def cell_sum_kernel(own, near, across, corner, out):
    out[...] = (
        (own[...].astype(f32) + near[...].astype(f32)) + (across[...].astype(f32) + corner[...].astype(f32))
    ).astype(bf16)


def feature_kernel(raw, w_charge, own, downs, ups, back_down, back_up, up, down, out):
    place = place_in_row()
    first, last = 2 * KB + QUARTER, 2 * KB + QUARTER + GHOST
    returned = jnp.where(place == 0, up[first:last, :], back_down[...])
    total = own[...] + dot_lanes(raw[...], w_charge[...])
    atom = iota((ATOMS, GHOST), 0)
    total = total + dot((atom == downs[...]).astype(f32).astype(bf16), returned)
    returned = jnp.where(place == ROW - 1, down[last:, :], back_up[...])
    total = total + dot((atom == ups[...]).astype(f32).astype(bf16), returned)
    out[...] = total.astype(bf16)


def weights_kernel(held, received, charge, message, radial, out):
    total = (held[...].astype(f32) + received[...].astype(f32)) * grad_scale
    charge[...] = total[0:C]
    message[...] = total[C : 2 * C]
    out[...] = total[2 * C : 3 * C]
    radial[...] = total[3 * C : 3 * C + NB]


def swap(values, axis, mask):
    count = lax.axis_size(axis)
    return lax.ppermute(values, axis, [(i, i ^ mask) for i in range(count)])


def from_y(values, by):
    return lax.ppermute(values, "dom", [(i, (i + ROW * by) % DOMS) for i in range(DOMS)])


def per_device(
    feats,
    positions,
    species,
    wave_vectors,
    smearing,
    species_gain,
    w_charge,
    w_message,
    w_radial,
    w_out,
    edge_sender,
    edge_receiver,
    edge_mask,
    edge_length,
    ghost_down,
    ghost_up,
    cotangent,
):
    own_rows = feats[0]
    cot = cotangent[0]

    def edges(first, count, total, after):
        spec = pl.BlockSpec((1, CHUNK), lambda e: (0, first + e))
        whole = pl.BlockSpec((NB * ATOMS, EXT), lambda e: (0, 0))
        held = [] if total is None else [total]
        (out,) = call(
            lambda *refs: edge_kernel(total is None, *refs),
            [((NB * ATOMS, EXT), f32)],
            edge_sender, edge_receiver, edge_mask, edge_length, *held,
            scratch=[pltpu.VMEM((NB * ATOMS, CHUNK), bf16), pltpu.VMEM((EXT, CHUNK), bf16)],
            flops=count * 2 * NB * ATOMS * CHUNK * 256,
            grid=(count,),
            in_specs=[spec] * 4 + [whole] * len(held),
            out_specs=[whole],
            after=after,
            name="edges",
        )
        return out

    (packed,) = call(
        pack_kernel,
        [((PACK, C), bf16)],
        own_rows, positions[0], species, ghost_down, ghost_up,
        scratch=[pltpu.VMEM((16, C), f32)],
        name="pack",
    )
    operator = edges(0, EDGE_STEPS[0], None, [packed])
    near_rows = jnp.concatenate([packed] + [swap(packed, "dom", mask) for mask in (2, 4, 6)], axis=0)
    far_rows = swap(near_rows, "dom", 1)
    near, near_sums, filt, near_gain = call(
        structure_near_kernel,
        [((2 * KB, HALF), bf16), ((2 * KB, C), f32), ((KB, C), f32), ((HALF, C), f32)],
        near_rows, wave_vectors, smearing[None], species_gain, w_charge,
        scratch=[pltpu.VMEM((HALF, C), bf16)],
        after=[operator],
        name="structure_near",
    )
    far, sums, message, far_gain, below, above = call(
        structure_far_kernel,
        [
            ((2 * KB, HALF), bf16), ((2 * KB, C), bf16), ((2 * KB + 2 * GHOST, C), bf16), ((HALF, C), f32),
            ((GHOST, C), bf16), ((GHOST, C), bf16),
        ],
        far_rows, near_rows, near_sums, wave_vectors, species_gain, w_charge,
        scratch=[pltpu.VMEM((HALF, C), bf16), pltpu.VMEM((ROW * PACK, C), bf16)],
        name="structure_far",
    )
    up, down, over = from_y(message, 1), from_y(message, -1), from_y(sums, 2)
    operator = edges(EDGE_STEPS[0], EDGE_STEPS[1], operator, [message])
    send, keep = call(
        potential_kernel,
        [((HALF, C), bf16), ((HALF, C), f32)],
        sums, up, down, over, filt, near, far,
        after=[operator],
        name="potential",
    )
    received = swap(send, "dom", 1)
    operator = edges(EDGE_STEPS[0] + EDGE_STEPS[1], EDGE_STEPS[2], operator, [send])
    held, *sends = call(
        spread_kernel, [((ATOMS, C), f32)] + [((ATOMS, C), bf16)] * 3, keep, received, after=[operator], name="spread"
    )
    parts = [swap(values, "dom", 2 * (part + 1)) for part, values in enumerate(sends)]
    operator = edges(sum(EDGE_STEPS[:3]), EDGE_STEPS[3], operator, [held])
    aggregate, radial_rows, extended = call(
        aggregate_kernel,
        [((ATOMS, C), f32), ((NB * ATOMS, C), f32), ((EXT, C), bf16)],
        own_rows, below, above, up, down, w_message, operator, w_radial,
        name="aggregate",
    )
    updated, own_total, back_rows, quarter, *sends = call(
        update_kernel,
        [((ATOMS, C), bf16), ((ATOMS, C), f32), ((EXT, C), bf16), ((QUARTER, C), f32)]
        + [((EXT + QUARTER, C), bf16)] * 3,
        held, *parts, aggregate, own_rows, cot, w_out, extended, w_message, operator, radial_rows, w_radial,
        scratch=[pltpu.VMEM((4 * QUARTER, C), f32)],
        name="update",
    )
    parts = [swap(values, "dom", 2 * (part + 1)) for part, values in enumerate(sends)]
    (joined,) = call(
        join_kernel, [((HALF + 8 * GHOST + QUARTER, C), bf16)], back_rows, quarter, *parts, name="join"
    )
    received = swap(joined, "dom", 1)
    (near_sums,) = call(back_near_kernel, [((2 * KB, C), f32)], near, joined, name="back_near")
    message, over, back_down, back_up = call(
        back_far_kernel,
        [
            ((2 * KB + QUARTER + 2 * GHOST, C), bf16), ((2 * KB + QUARTER, C), bf16),
            ((GHOST, C), bf16), ((GHOST, C), bf16),
        ],
        far, received, joined, near_sums,
        scratch=[pltpu.VMEM((16 * GHOST, C), bf16)],
        name="back_far",
    )
    up, down, over = from_y(message, 1), from_y(message, -1), from_y(over, 2)
    send, keep, charge, quarter = call(
        charge_back_kernel,
        [((HALF + C, C), bf16), ((HALF, C), f32), ((C, C), bf16), ((QUARTER, C), bf16)],
        message, up, down, over, filt, near, far, near_gain, far_gain, near_rows, far_rows,
        scratch=[pltpu.VMEM((HALF, C), bf16)],
        name="charge_back",
    )
    received = swap(send, "dom", 1)
    held, charge, *sends = call(
        tail_spread_kernel,
        [((ATOMS, C), f32), ((C, C), bf16)] + [((ATOMS + C + QUARTER, C), bf16)] * 3,
        keep, charge, quarter, received,
        name="tail_spread",
    )
    parts = [swap(values, "dom", 2 * (part + 1)) for part, values in enumerate(sends)]
    raw, charge, grads = call(
        raw_kernel,
        [((ATOMS, C), bf16), ((C, C), bf16), ((4 * QUARTER, C), bf16)],
        held, charge, quarter, *parts,
        name="raw",
    )
    parts = [from_y(charge, by) for by in (1, -1, 2)]
    (feat_grad,) = call(
        feature_kernel,
        [((ATOMS, C), bf16)],
        raw, w_charge, own_total, ghost_down, ghost_up, back_down, back_up, up, down,
        name="feature",
    )
    (total,) = call(
        charge_sum_kernel, [((C + 4 * QUARTER, C), bf16)], charge, *parts, grads, after=[feat_grad], name="charge_sum"
    )
    parts = [swap(total, "cell", mask) for mask in (2, 4, 6)]
    (total,) = call(cell_sum_kernel, [((C + 4 * QUARTER, C), bf16)], total, *parts, name="cell_sum")
    received = swap(total, "cell", 1)
    charge, message, radial, out = call(
        weights_kernel,
        [((C, C), f32), ((C, C), f32), ((NB, C), f32), ((C, C), f32)],
        total, received,
        name="weights",
    )
    return updated[None], feat_grad[None], charge, message, radial, out


def solution(mesh):
    placed = (
        P("cell", "dom", None),
        P("cell", None, "dom"),
        P("cell", "dom"),
        P(),
        P(),
        P(),
        P(),
        P(),
        P(),
        P(),
        P("cell", "dom"),
        P("cell", "dom"),
        P("cell", "dom"),
        P("cell", "dom"),
        P("cell", "dom"),
        P("cell", "dom"),
        P("cell", "dom", None),
    )
    return jax.shard_map(
        per_device,
        mesh=mesh,
        in_specs=placed,
        out_specs=(P("cell", "dom", None), P("cell", "dom", None), P(), P(), P(), P()),
        check_vma=False,
    )
```

time: 130 us -> 106 us (0.82)
  the two profiles are of different devices: /device:TPU:6 before, /device:TPU:32 now
where the time goes in v2:
time: 106 us
  waiting for transfers between devices  44 us (42%)
  starting transfers between devices  36.9 us (35%)
  Pallas kernels  20.3 us (19%)
  local copies, waits for them, and re-layouts  3.69 us (3%)
    ppermute x20, waiting for transfers between devices, swap(): return lax.ppermute(values, axis, [(i, i ^ mask) for i in range(count)])  31 us
    ppermute x20, starting transfers between devices, swap(): return lax.ppermute(values, axis, [(i, i ^ mask) for i in range(count)])  25.6 us
    pallas_call x21, Pallas kernels, call(): pl.pallas_call(run, out_shape=[jax.ShapeDtypeStruct(shape, dtype) for sha...  20.3 us
    ppermute x9, waiting for transfers between devices, from_y(): lax.ppermute(values, 'dom', [(i, (i + ROW * by) % DOMS) for i in range(DO...  13 us
    ppermute x9, starting transfers between devices, from_y(): lax.ppermute(values, 'dom', [(i, (i + ROW * by) % DOMS) for i in range(DO...  11.4 us
    unnamed x37, local copies, waits for them, and re-layouts  3.69 us
  transfers between devices with their start and end apart: 29, of which 21 were waited for; matrix products, arithmetic and copies ran while one was open for 0% of the time, Pallas kernels for 15%

profile of v2, /device:TPU:32, one launch (start us, length us, event | category | flops | bytes accessed | tf_op | source)
XLA Modules:
  0.0 105.9 jit_solution(13970294885260193107)
XLA Ops:
  2.8 2.0 %collective-permute-start.2 = (bf16[144,128]{1,0:T(8,128)(2,1)S(1)}, bf16[144,128]{1,0:T(8,128)(2,1)S(1)}, u32[]{:S(2)}, u32[]{:S(2)}) collective-permute-start(bf16[144,128]{1,0:T(8,128)(2,1)S(1)} %pack.1.refs_4_), channel_id=1, source_target_pairs={{0,6},{1,7},{2,4},{3,5},{4,2},{5,3},{6,0},{7,1},{8,14},{9,15},{10,... | collective-permute-start | bytes 110600 | tf_op jit(solution)/shard_map/ppermute | solution.py:419
  4.8 2.3 %collective-permute-start.1 = (bf16[144,128]{1,0:T(8,128)(2,1)S(1)}, bf16[144,128]{1,0:T(8,128)(2,1)S(1)}, u32[]{:S(2)}, u32[]{:S(2)}) collective-permute-start(bf16[144,128]{1,0:T(8,128)(2,1)S(1)} %pack.1.refs_4_), channel_id=1, source_target_pairs={{0,4},{1,5},{2,6},{3,7},{4,0},{5,1},{6,2},{7,3},{8,12},{9,13},{10,... | collective-permute-start | bytes 110600 | tf_op jit(solution)/shard_map/ppermute | solution.py:419
  7.7 2.1 %collective-permute-done.1 = bf16[144,128]{1,0:T(8,128)(2,1)S(1)} collective-permute-done((bf16[144,128]{1,0:T(8,128)(2,1)S(1)}, bf16[144,128]{1,0:T(8,128)(2,1)S(1)}, u32[]{:S(2)}, u32[]{:S(2)}) %collective-permute-start.1) | collective-permute-done | bytes 36896 | tf_op jit(solution)/shard_map/ppermute | solution.py:419
  9.8 1.3 %collective-permute-done = bf16[144,128]{1,0:T(8,128)(2,1)S(1)} collective-permute-done((bf16[144,128]{1,0:T(8,128)(2,1)S(1)}, bf16[144,128]{1,0:T(8,128)(2,1)S(1)}, u32[]{:S(2)}, u32[]{:S(2)}) %collective-permute-start) | collective-permute-done | bytes 36896 | tf_op jit(solution)/shard_map/ppermute | solution.py:419
  11.3 3.2 %edges.4.refs_5_.refs_4_ = f32[1024,192]{1,0:T(8,128)S(1)} custom-call(s32[1,12288]{1,0:T(1,128)S(1)} %copy-done.6, s32[1,12288]{1,0:T(1,128)S(1)} %copy-done.7, s32[1,12288]{1,0:T(1,128)S(1)} %copy-done.8, f32[1,12288]{1,0:T(1,128)S(1)} %copy-done.9, bf16[144,128]{1,0:T(8,128)(2,1)S(1)} %pack.1.refs_4_), custom_call_target="tpu_custom_call" | custom-call | flops 1610612736 | bytes 262144 | tf_op jit(solution)/shard_map/edges/pallas_call | solution.py:93
  17.5 2.4 %collective-permute-start.5 = (bf16[576,128]{1,0:T(8,128)(2,1)S(1)}, bf16[576,128]{1,0:T(8,128)(2,1)S(1)}, u32[]{:S(2)}, u32[]{:S(2)}) collective-permute-start(bf16[576,128]{1,0:T(8,128)(2,1)S(1)} %get-tuple-element.54.refs_5_), channel_id=1, source_target_pairs={{0,24},{1,25},{2,26},{3,27},{4,28},{5,29},{6,30},{7,31},{8,0},{9,1... | collective-permute-start | bytes 442376 | tf_op jit(solution)/shard_map/ppermute | solution.py:423
  19.9 2.2 %collective-permute-start.6 = (bf16[512,128]{1,0:T(8,128)(2,1)S(1)}, bf16[512,128]{1,0:T(8,128)(2,1)S(1)}, u32[]{:S(2)}, u32[]{:S(2)}) collective-permute-start(bf16[512,128]{1,0:T(8,128)(2,1)S(1)} %get-tuple-element.53.refs_0_), channel_id=1, source_target_pairs={{0,16},{1,17},{2,18},{3,19},{4,20},{5,21},{6,22},{7,23},{8,24},{9,... | collective-permute-start | bytes 393224 | tf_op jit(solution)/shard_map/ppermute | solution.py:423
  22.1 5.3 %edges.5.refs_7_.refs_4_ = f32[1024,192]{1,0:T(8,128)S(1)} custom-call(s32[1,12288]{1,0:T(1,128)S(1)} %copy-done.6, s32[1,12288]{1,0:T(1,128)S(1)} %copy-done.7, s32[1,12288]{1,0:T(1,128)S(1)} %copy-done.8, f32[1,12288]{1,0:T(1,128)S(1)} %copy-done.9, f32[1024,192]{1,0:T(8,128)S(1)} %edges.4.refs_5_.refs_4_, bf16[576,128]{1,0:T(8,128)(2,1)S(1)} %get-tuple-element.54.refs_5_), custom_call_target="tpu_custom_call" | custom-call | flops 2684354560 | bytes 262144 | tf_op jit(solution)/shard_map/edges/pallas_call | solution.py:93
  27.4 1.5 %collective-permute-done.6.refs_3_ = bf16[512,128]{1,0:T(8,128)(2,1)S(1)} collective-permute-done((bf16[512,128]{1,0:T(8,128)(2,1)S(1)}, bf16[512,128]{1,0:T(8,128)(2,1)S(1)}, u32[]{:S(2)}, u32[]{:S(2)}) %collective-permute-start.6) | collective-permute-done | bytes 131104 | tf_op jit(solution)/shard_map/ppermute | solution.py:423
  31.8 2.2 %collective-permute-start.8 = (bf16[128,128]{1,0:T(8,128)(2,1)S(1)}, bf16[128,128]{1,0:T(8,128)(2,1)S(1)}, u32[]{:S(2)}, u32[]{:S(2)}) collective-permute-start(bf16[128,128]{1,0:T(8,128)(2,1)S(1)} %get-tuple-element.61), channel_id=1, source_target_pairs={{0,2},{1,3},{2,0},{3,1},{4,6},{5,7},{6,4},{7,5},{8,10},{9,11},{10,... | collective-permute-start | bytes 98312 | tf_op jit(solution)/shard_map/ppermute | solution.py:419
  34.0 2.0 %collective-permute-start.9 = (bf16[128,128]{1,0:T(8,128)(2,1)S(1)}, bf16[128,128]{1,0:T(8,128)(2,1)S(1)}, u32[]{:S(2)}, u32[]{:S(2)}) collective-permute-start(bf16[128,128]{1,0:T(8,128)(2,1)S(1)} %get-tuple-element.62), channel_id=1, source_target_pairs={{0,4},{1,5},{2,6},{3,7},{4,0},{5,1},{6,2},{7,3},{8,12},{9,13},{10,... | collective-permute-start | bytes 98312 | tf_op jit(solution)/shard_map/ppermute | solution.py:419
  36.0 3.2 %edges.7.refs_6_.refs_10_ = f32[1024,192]{1,0:T(8,128)S(1)} custom-call(s32[1,12288]{1,0:T(1,128)S(1)} %copy-done.6, s32[1,12288]{1,0:T(1,128)S(1)} %copy-done.7, s32[1,12288]{1,0:T(1,128)S(1)} %copy-done.8, f32[1,12288]{1,0:T(1,128)S(1)} %copy-done.9, f32[1024,192]{1,0:T(8,128)S(1)} %edges.6.refs_2_.refs_4_, f32[128,128]{1,0:T(8,128)S(1)} %get-tuple-element.60.refs_5_.refs_0_), custom_call_target="tpu_custom_call" | custom-call | flops 1610612736 | bytes 262144 | tf_op jit(solution)/shard_map/edges/pallas_call | solution.py:93
  40.1 1.4 %update.1 = (bf16[128,128]{1,0:T(8,128)(2,1)}, f32[128,128]{1,0:T(8,128)S(1)}, bf16[192,128]{1,0:T(8,128)(2,1)S(1)}, f32[80,128]{1,0:T(8,128)S(1)}, bf16[272,128...) custom-call(f32[128,128]{1,0:T(8,128)S(1)} %get-tuple-element.60.refs_5_.refs_0_, ...), custom_call_target="tpu_custom_call" | custom-call | bytes 262144 | tf_op jit(solution)/shard_map/update/pallas_call | solution.py:93
  41.4 2.3 %collective-permute-start.11 = (bf16[272,128]{1,0:T(8,128)(2,1)S(1)}, bf16[272,128]{1,0:T(8,128)(2,1)S(1)}, u32[]{:S(2)}, u32[]{:S(2)}) collective-permute-start(bf16[272,128]{1,0:T(8,128)(2,1)S(1)} %get-tuple-element.72), channel_id=1, source_target_pairs={{0,2},{1,3},{2,0},{3,1},{4,6},{5,7},{6,4},{7,5},{8,10},{9,11},{10,... | collective-permute-start | bytes 208904 | tf_op jit(solution)/shard_map/ppermute | solution.py:419
  45.2 1.2 %collective-permute-done.11.refs_2_ = bf16[272,128]{1,0:T(8,128)(2,1)S(1)} collective-permute-done((bf16[272,128]{1,0:T(8,128)(2,1)S(1)}, bf16[272,128]{1,0:T(8,128)(2,1)S(1)}, u32[]{:S(2)}, u32[]{:S(2)}) %collective-permute-start.11) | collective-permute-done | bytes 69664 | tf_op jit(solution)/shard_map/ppermute | solution.py:419
  46.4 2.9 %collective-permute-done.12.refs_3_ = bf16[272,128]{1,0:T(8,128)(2,1)S(1)} collective-permute-done((bf16[272,128]{1,0:T(8,128)(2,1)S(1)}, bf16[272,128]{1,0:T(8,128)(2,1)S(1)}, u32[]{:S(2)}, u32[]{:S(2)}) %collective-permute-start.12) | collective-permute-done | bytes 69664 | tf_op jit(solution)/shard_map/ppermute | solution.py:419
  49.3 2.1 %collective-permute-done.13.refs_4_ = bf16[272,128]{1,0:T(8,128)(2,1)S(1)} collective-permute-done((bf16[272,128]{1,0:T(8,128)(2,1)S(1)}, bf16[272,128]{1,0:T(8,128)(2,1)S(1)}, u32[]{:S(2)}, u32[]{:S(2)}) %collective-permute-start.13) | collective-permute-done | bytes 69664 | tf_op jit(solution)/shard_map/ppermute | solution.py:419
  53.7 1.7 %collective-permute-start.15 = (bf16[656,128]{1,0:T(8,128)(2,1)S(1)}, bf16[656,128]{1,0:T(8,128)(2,1)S(1)}, u32[]{:S(2)}, u32[]{:S(2)}) collective-permute-start(bf16[656,128]{1,0:T(8,128)(2,1)S(1)} %get-tuple-element.75.refs_0_), channel_id=1, source_target_pairs={{0,8},{1,9},{2,10},{3,11},{4,12},{5,13},{6,14},{7,15},{8,16},{9,17... | collective-permute-start | bytes 503816 | tf_op jit(solution)/shard_map/ppermute | solution.py:423
  56.0 7.4 %collective-permute-done.17.refs_3_ = bf16[592,128]{1,0:T(8,128)(2,1)S(1)} collective-permute-done((bf16[592,128]{1,0:T(8,128)(2,1)S(1)}, bf16[592,128]{1,0:T(8,128)(2,1)S(1)}, u32[]{:S(2)}, u32[]{:S(2)}) %collective-permute-start.17) | collective-permute-done | bytes 151584 | tf_op jit(solution)/shard_map/ppermute | solution.py:423
  65.2 1.4 %collective-permute-done.18.refs_3_ = bf16[640,128]{1,0:T(8,128)(2,1)S(1)} collective-permute-done((bf16[640,128]{1,0:T(8,128)(2,1)S(1)}, bf16[640,128]{1,0:T(8,128)(2,1)S(1)}, u32[]{:S(2)}, u32[]{:S(2)}) %collective-permute-start.18) | collective-permute-done | bytes 163872 | tf_op jit(solution)/shard_map/ppermute | solution.py:419
  67.4 1.7 %collective-permute-start.20 = (bf16[336,128]{1,0:T(8,128)(2,1)S(1)}, bf16[336,128]{1,0:T(8,128)(2,1)S(1)}, u32[]{:S(2)}, u32[]{:S(2)}) collective-permute-start(bf16[336,128]{1,0:T(8,128)(2,1)S(1)} %get-tuple-element.86), channel_id=1, source_target_pairs={{0,4},{1,5},{2,6},{3,7},{4,0},{5,1},{6,2},{7,3},{8,12},{9,13},{10,... | collective-permute-start | bytes 258056 | tf_op jit(solution)/shard_map/ppermute | solution.py:419
  70.2 1.7 %collective-permute-done.19.refs_3_ = bf16[336,128]{1,0:T(8,128)(2,1)S(1)} collective-permute-done((bf16[336,128]{1,0:T(8,128)(2,1)S(1)}, bf16[336,128]{1,0:T(8,128)(2,1)S(1)}, u32[]{:S(2)}, u32[]{:S(2)}) %collective-permute-start.19) | collective-permute-done | bytes 86048 | tf_op jit(solution)/shard_map/ppermute | solution.py:419
  71.9 3.5 %collective-permute-done.20.refs_4_ = bf16[336,128]{1,0:T(8,128)(2,1)S(1)} collective-permute-done((bf16[336,128]{1,0:T(8,128)(2,1)S(1)}, bf16[336,128]{1,0:T(8,128)(2,1)S(1)}, u32[]{:S(2)}, u32[]{:S(2)}) %collective-permute-start.20) | collective-permute-done | bytes 86048 | tf_op jit(solution)/shard_map/ppermute | solution.py:419
  75.4 2.5 %collective-permute-done.21.refs_5_ = bf16[336,128]{1,0:T(8,128)(2,1)S(1)} collective-permute-done((bf16[336,128]{1,0:T(8,128)(2,1)S(1)}, bf16[336,128]{1,0:T(8,128)(2,1)S(1)}, u32[]{:S(2)}, u32[]{:S(2)}) %collective-permute-start.21) | collective-permute-done | bytes 86048 | tf_op jit(solution)/shard_map/ppermute | solution.py:419
  78.0 2.0 %collective-permute-start.24 = (bf16[128,128]{1,0:T(8,128)(2,1)S(1)}, bf16[128,128]{1,0:T(8,128)(2,1)S(1)}, u32[]{:S(2)}, u32[]{:S(2)}) collective-permute-start(bf16[128,128]{1,0:T(8,128)(2,1)S(1)} %get-tuple-element.92.refs_0_), channel_id=1, source_target_pairs={{0,16},{1,17},{2,18},{3,19},{4,20},{5,21},{6,22},{7,23},{8,24},{9,... | collective-permute-start | bytes 98312 | tf_op jit(solution)/shard_map/ppermute | solution.py:423
  80.1 2.0 %collective-permute-start.22 = (bf16[128,128]{1,0:T(8,128)(2,1)S(1)}, bf16[128,128]{1,0:T(8,128)(2,1)S(1)}, u32[]{:S(2)}, u32[]{:S(2)}) collective-permute-start(bf16[128,128]{1,0:T(8,128)(2,1)S(1)} %get-tuple-element.92.refs_0_), channel_id=1, source_target_pairs={{0,8},{1,9},{2,10},{3,11},{4,12},{5,13},{6,14},{7,15},{8,16},{9,17... | collective-permute-start | bytes 98312 | tf_op jit(solution)/shard_map/ppermute | solution.py:423
  84.0 1.2 %collective-permute-done.22.refs_1_ = bf16[128,128]{1,0:T(8,128)(2,1)S(1)} collective-permute-done((bf16[128,128]{1,0:T(8,128)(2,1)S(1)}, bf16[128,128]{1,0:T(8,128)(2,1)S(1)}, u32[]{:S(2)}, u32[]{:S(2)}) %collective-permute-start.22) | collective-permute-done | bytes 32800 | tf_op jit(solution)/shard_map/ppermute | solution.py:423
  86.0 2.8 %collective-permute-start.27 = (bf16[448,128]{1,0:T(8,128)(2,1)S(1)}, bf16[448,128]{1,0:T(8,128)(2,1)S(1)}, u32[]{:S(2)}, u32[]{:S(2)}) collective-permute-start(bf16[448,128]{1,0:T(8,128)(2,1)S(1)} %charge_sum.1.refs_0_), channel_id=1, source_target_pairs={{0,192},{32,224},{64,128},{96,160},{128,64},{160,96},{192,0},{224,... | collective-permute-start | bytes 344072 | tf_op jit(solution)/shard_map/ppermute | solution.py:419
  90.1 3.1 %collective-permute-done.27.refs_3_ = bf16[448,128]{1,0:T(8,128)(2,1)S(1)} collective-permute-done((bf16[448,128]{1,0:T(8,128)(2,1)S(1)}, bf16[448,128]{1,0:T(8,128)(2,1)S(1)}, u32[]{:S(2)}, u32[]{:S(2)}) %collective-permute-start.27) | collective-permute-done | bytes 114720 | tf_op jit(solution)/shard_map/ppermute | solution.py:419
  93.3 1.8 %collective-permute-done.26.refs_2_ = bf16[448,128]{1,0:T(8,128)(2,1)S(1)} collective-permute-done((bf16[448,128]{1,0:T(8,128)(2,1)S(1)}, bf16[448,128]{1,0:T(8,128)(2,1)S(1)}, u32[]{:S(2)}, u32[]{:S(2)}) %collective-permute-start.26) | collective-permute-done | bytes 114720 | tf_op jit(solution)/shard_map/ppermute | solution.py:419
  95.2 4.6 %collective-permute-start.28 = (bf16[448,128]{1,0:T(8,128)(2,1)S(1)}, bf16[448,128]{1,0:T(8,128)(2,1)S(1)}, u32[]{:S(2)}, u32[]{:S(2)}) collective-permute-start(bf16[448,128]{1,0:T(8,128)(2,1)S(1)} %cell_sum.1.refs_0_), channel_id=1, source_target_pairs={{0,32},{32,0},{64,96},{96,64},{128,160},{160,128},{192,224},{224,1... | collective-permute-start | bytes 344072 | tf_op jit(solution)/shard_map/ppermute | solution.py:419
  99.7 5.4 %collective-permute-done.28.refs_1_ = bf16[448,128]{1,0:T(8,128)(2,1)S(1)} collective-permute-done((bf16[448,128]{1,0:T(8,128)(2,1)S(1)}, bf16[448,128]{1,0:T(8,128)(2,1)S(1)}, u32[]{:S(2)}, u32[]{:S(2)}) %collective-permute-start.28) | collective-permute-done | bytes 114720 | tf_op jit(solution)/shard_map/ppermute | solution.py:419
  (85 shorter events, 22.0 us)
Async XLA Ops:
  2.8 8.4 %copy-start.6 = (s32[1,12288]{1,0:T(1,128)S(1)}, s32[1,12288]{1,0:T(1,128)}, u32[]{:S(2)}) copy-start(s32[1,12288]{1,0:T(1,128)} %refs_0_.7) | copy-start | bytes 147460
  2.8 8.4 %copy-start.7 = (s32[1,12288]{1,0:T(1,128)S(1)}, s32[1,12288]{1,0:T(1,128)}, u32[]{:S(2)}) copy-start(s32[1,12288]{1,0:T(1,128)} %refs_1_.10) | copy-start | bytes 147460
  2.8 8.4 %copy-start.8 = (s32[1,12288]{1,0:T(1,128)S(1)}, s32[1,12288]{1,0:T(1,128)}, u32[]{:S(2)}) copy-start(s32[1,12288]{1,0:T(1,128)} %refs_2_.9) | copy-start | bytes 147460
  2.8 4.8 %collective-permute-start.2 = (bf16[144,128]{1,0:T(8,128)(2,1)S(1)}, bf16[144,128]{1,0:T(8,128)(2,1)S(1)}, u32[]{:S(2)}, u32[]{:S(2)}) collective-permute-start(bf16[144,128]{1,0:T(8,128)(2,1)S(1)} %pack.1.refs_4_), channel_id=1, source_target_pairs={{0,6},{1,7},{2,4},{3,5},{4,2},{5,3},{6,0},{7,1},{8,14},{9,15},{10,... | collective-permute-start | bytes 110600 | tf_op jit(solution)/shard_map/ppermute | solution.py:419
  4.8 5.0 %collective-permute-start.1 = (bf16[144,128]{1,0:T(8,128)(2,1)S(1)}, bf16[144,128]{1,0:T(8,128)(2,1)S(1)}, u32[]{:S(2)}, u32[]{:S(2)}) collective-permute-start(bf16[144,128]{1,0:T(8,128)(2,1)S(1)} %pack.1.refs_4_), channel_id=1, source_target_pairs={{0,4},{1,5},{2,6},{3,7},{4,0},{5,1},{6,2},{7,3},{8,12},{9,13},{10,... | collective-permute-start | bytes 110600 | tf_op jit(solution)/shard_map/ppermute | solution.py:419
  7.1 4.0 %collective-permute-start = (bf16[144,128]{1,0:T(8,128)(2,1)S(1)}, bf16[144,128]{1,0:T(8,128)(2,1)S(1)}, u32[]{:S(2)}, u32[]{:S(2)}) collective-permute-start(bf16[144,128]{1,0:T(8,128)(2,1)S(1)} %pack.1.refs_4_), channel_id=1, source_target_pairs={{0,2},{1,3},{2,0},{3,1},{4,6},{5,7},{6,4},{7,5},{8,10},{9,11},{10,... | collective-permute-start | bytes 110600 | tf_op jit(solution)/shard_map/ppermute | solution.py:419
  11.1 5.2 %collective-permute-start.3 = (bf16[576,128]{1,0:T(8,128)(2,1)S(1)}, bf16[576,128]{1,0:T(8,128)(2,1)S(1)}, u32[]{:S(2)}, u32[]{:S(2)}) collective-permute-start(bf16[576,128]{1,0:T(8,128)(2,1)S(1)} %pad_maximum_fusion.refs_0_.refs_1_.refs_9_), channel_id=1, source_target_pairs={{0,1},{1,0},{2,3},{3,2},{4,5},{5,4},{6,7},{7,6},{8,9},{9,8},{10,11... | collective-permute-start | bytes 442376 | tf_op jit(solution)/shard_map/ppermute | solution.py:419
  17.5 11.5 %collective-permute-start.5 = (bf16[576,128]{1,0:T(8,128)(2,1)S(1)}, bf16[576,128]{1,0:T(8,128)(2,1)S(1)}, u32[]{:S(2)}, u32[]{:S(2)}) collective-permute-start(bf16[576,128]{1,0:T(8,128)(2,1)S(1)} %get-tuple-element.54.refs_5_), channel_id=1, source_target_pairs={{0,24},{1,25},{2,26},{3,27},{4,28},{5,29},{6,30},{7,31},{8,0},{9,1... | collective-permute-start | bytes 442376 | tf_op jit(solution)/shard_map/ppermute | solution.py:423
  19.9 10.0 %collective-permute-start.4 = (bf16[576,128]{1,0:T(8,128)(2,1)S(1)}, bf16[576,128]{1,0:T(8,128)(2,1)S(1)}, u32[]{:S(2)}, u32[]{:S(2)}) collective-permute-start(bf16[576,128]{1,0:T(8,128)(2,1)S(1)} %get-tuple-element.54.refs_5_), channel_id=1, source_target_pairs={{0,8},{1,9},{2,10},{3,11},{4,12},{5,13},{6,14},{7,15},{8,16},{9,17... | collective-permute-start | bytes 442376 | tf_op jit(solution)/shard_map/ppermute | solution.py:423
  19.9 9.0 %collective-permute-start.6 = (bf16[512,128]{1,0:T(8,128)(2,1)S(1)}, bf16[512,128]{1,0:T(8,128)(2,1)S(1)}, u32[]{:S(2)}, u32[]{:S(2)}) collective-permute-start(bf16[512,128]{1,0:T(8,128)(2,1)S(1)} %get-tuple-element.53.refs_0_), channel_id=1, source_target_pairs={{0,16},{1,17},{2,18},{3,19},{4,20},{5,21},{6,22},{7,23},{8,24},{9,... | collective-permute-start | bytes 393224 | tf_op jit(solution)/shard_map/ppermute | solution.py:423
  30.3 1.4 %collective-permute-start.7 = (bf16[512,128]{1,0:T(8,128)(2,1)S(1)}, bf16[512,128]{1,0:T(8,128)(2,1)S(1)}, u32[]{:S(2)}, u32[]{:S(2)}) collective-permute-start(bf16[512,128]{1,0:T(8,128)(2,1)S(1)} %get-tuple-element.59.refs_5_), channel_id=1, source_target_pairs={{0,1},{1,0},{2,3},{3,2},{4,5},{5,4},{6,7},{7,6},{8,9},{9,8},{10,11... | collective-permute-start | bytes 393224 | tf_op jit(solution)/shard_map/ppermute | solution.py:419
  31.8 8.1 %collective-permute-start.8 = (bf16[128,128]{1,0:T(8,128)(2,1)S(1)}, bf16[128,128]{1,0:T(8,128)(2,1)S(1)}, u32[]{:S(2)}, u32[]{:S(2)}) collective-permute-start(bf16[128,128]{1,0:T(8,128)(2,1)S(1)} %get-tuple-element.61), channel_id=1, source_target_pairs={{0,2},{1,3},{2,0},{3,1},{4,6},{5,7},{6,4},{7,5},{8,10},{9,11},{10,... | collective-permute-start | bytes 98312 | tf_op jit(solution)/shard_map/ppermute | solution.py:419
  34.0 6.0 %collective-permute-start.9 = (bf16[128,128]{1,0:T(8,128)(2,1)S(1)}, bf16[128,128]{1,0:T(8,128)(2,1)S(1)}, u32[]{:S(2)}, u32[]{:S(2)}) collective-permute-start(bf16[128,128]{1,0:T(8,128)(2,1)S(1)} %get-tuple-element.62), channel_id=1, source_target_pairs={{0,4},{1,5},{2,6},{3,7},{4,0},{5,1},{6,2},{7,3},{8,12},{9,13},{10,... | collective-permute-start | bytes 98312 | tf_op jit(solution)/shard_map/ppermute | solution.py:419
  36.0 3.9 %collective-permute-start.10 = (bf16[128,128]{1,0:T(8,128)(2,1)S(1)}, bf16[128,128]{1,0:T(8,128)(2,1)S(1)}, u32[]{:S(2)}, u32[]{:S(2)}) collective-permute-start(bf16[128,128]{1,0:T(8,128)(2,1)S(1)} %get-tuple-element.63), channel_id=1, source_target_pairs={{0,6},{1,7},{2,4},{3,5},{4,2},{5,3},{6,0},{7,1},{8,14},{9,15},{10,... | collective-permute-start | bytes 98312 | tf_op jit(solution)/shard_map/ppermute | solution.py:419
  41.4 5.0 %collective-permute-start.11 = (bf16[272,128]{1,0:T(8,128)(2,1)S(1)}, bf16[272,128]{1,0:T(8,128)(2,1)S(1)}, u32[]{:S(2)}, u32[]{:S(2)}) collective-permute-start(bf16[272,128]{1,0:T(8,128)(2,1)S(1)} %get-tuple-element.72), channel_id=1, source_target_pairs={{0,2},{1,3},{2,0},{3,1},{4,6},{5,7},{6,4},{7,5},{8,10},{9,11},{10,... | collective-permute-start | bytes 208904 | tf_op jit(solution)/shard_map/ppermute | solution.py:419
  43.8 5.6 %collective-permute-start.12 = (bf16[272,128]{1,0:T(8,128)(2,1)S(1)}, bf16[272,128]{1,0:T(8,128)(2,1)S(1)}, u32[]{:S(2)}, u32[]{:S(2)}) collective-permute-start(bf16[272,128]{1,0:T(8,128)(2,1)S(1)} %get-tuple-element.73), channel_id=1, source_target_pairs={{0,4},{1,5},{2,6},{3,7},{4,0},{5,1},{6,2},{7,3},{8,12},{9,13},{10,... | collective-permute-start | bytes 208904 | tf_op jit(solution)/shard_map/ppermute | solution.py:419
  44.9 6.6 %collective-permute-start.13 = (bf16[272,128]{1,0:T(8,128)(2,1)S(1)}, bf16[272,128]{1,0:T(8,128)(2,1)S(1)}, u32[]{:S(2)}, u32[]{:S(2)}) collective-permute-start(bf16[272,128]{1,0:T(8,128)(2,1)S(1)} %get-tuple-element.74), channel_id=1, source_target_pairs={{0,6},{1,7},{2,4},{3,5},{4,2},{5,3},{6,0},{7,1},{8,14},{9,15},{10,... | collective-permute-start | bytes 208904 | tf_op jit(solution)/shard_map/ppermute | solution.py:419
  51.5 1.6 %collective-permute-start.14 = (bf16[848,128]{1,0:T(8,128)(2,1)S(1)}, bf16[848,128]{1,0:T(8,128)(2,1)S(1)}, u32[]{:S(2)}, u32[]{:S(2)}) collective-permute-start(bf16[848,128]{1,0:T(8,128)(2,1)S(1)} %join.1.refs_1_.refs_2_), channel_id=1, source_target_pairs={{0,1},{1,0},{2,3},{3,2},{4,5},{5,4},{6,7},{7,6},{8,9},{9,8},{10,11... | collective-permute-start | bytes 651272 | tf_op jit(solution)/shard_map/ppermute | solution.py:419
  53.3 10.1 %collective-permute-start.16 = (bf16[656,128]{1,0:T(8,128)(2,1)S(1)}, bf16[656,128]{1,0:T(8,128)(2,1)S(1)}, u32[]{:S(2)}, u32[]{:S(2)}) collective-permute-start(bf16[656,128]{1,0:T(8,128)(2,1)S(1)} %get-tuple-element.75.refs_0_), channel_id=1, source_target_pairs={{0,24},{1,25},{2,26},{3,27},{4,28},{5,29},{6,30},{7,31},{8,0},{9,1... | collective-permute-start | bytes 503816 | tf_op jit(solution)/shard_map/ppermute | solution.py:423
  53.7 10.6 %collective-permute-start.15 = (bf16[656,128]{1,0:T(8,128)(2,1)S(1)}, bf16[656,128]{1,0:T(8,128)(2,1)S(1)}, u32[]{:S(2)}, u32[]{:S(2)}) collective-permute-start(bf16[656,128]{1,0:T(8,128)(2,1)S(1)} %get-tuple-element.75.refs_0_), channel_id=1, source_target_pairs={{0,8},{1,9},{2,10},{3,11},{4,12},{5,13},{6,14},{7,15},{8,16},{9,17... | collective-permute-start | bytes 503816 | tf_op jit(solution)/shard_map/ppermute | solution.py:423
  55.4 8.0 %collective-permute-start.17 = (bf16[592,128]{1,0:T(8,128)(2,1)S(1)}, bf16[592,128]{1,0:T(8,128)(2,1)S(1)}, u32[]{:S(2)}, u32[]{:S(2)}) collective-permute-start(bf16[592,128]{1,0:T(8,128)(2,1)S(1)} %get-tuple-element.76), channel_id=1, source_target_pairs={{0,16},{1,17},{2,18},{3,19},{4,20},{5,21},{6,22},{7,23},{8,24},{9,... | collective-permute-start | bytes 454664 | tf_op jit(solution)/shard_map/ppermute | solution.py:423
  65.1 1.5 %collective-permute-start.18 = (bf16[640,128]{1,0:T(8,128)(2,1)S(1)}, bf16[640,128]{1,0:T(8,128)(2,1)S(1)}, u32[]{:S(2)}, u32[]{:S(2)}) collective-permute-start(bf16[640,128]{1,0:T(8,128)(2,1)S(1)} %get-tuple-element.82), channel_id=1, source_target_pairs={{0,1},{1,0},{2,3},{3,2},{4,5},{5,4},{6,7},{7,6},{8,9},{9,8},{10,11... | collective-permute-start | bytes 491528 | tf_op jit(solution)/shard_map/ppermute | solution.py:419
  66.6 5.3 %collective-permute-start.19 = (bf16[336,128]{1,0:T(8,128)(2,1)S(1)}, bf16[336,128]{1,0:T(8,128)(2,1)S(1)}, u32[]{:S(2)}, u32[]{:S(2)}) collective-permute-start(bf16[336,128]{1,0:T(8,128)(2,1)S(1)} %get-tuple-element.85), channel_id=1, source_target_pairs={{0,2},{1,3},{2,0},{3,1},{4,6},{5,7},{6,4},{7,5},{8,10},{9,11},{10,... | collective-permute-start | bytes 258056 | tf_op jit(solution)/shard_map/ppermute | solution.py:419
  67.4 8.0 %collective-permute-start.20 = (bf16[336,128]{1,0:T(8,128)(2,1)S(1)}, bf16[336,128]{1,0:T(8,128)(2,1)S(1)}, u32[]{:S(2)}, u32[]{:S(2)}) collective-permute-start(bf16[336,128]{1,0:T(8,128)(2,1)S(1)} %get-tuple-element.86), channel_id=1, source_target_pairs={{0,4},{1,5},{2,6},{3,7},{4,0},{5,1},{6,2},{7,3},{8,12},{9,13},{10,... | collective-permute-start | bytes 258056 | tf_op jit(solution)/shard_map/ppermute | solution.py:419
  69.1 8.8 %collective-permute-start.21 = (bf16[336,128]{1,0:T(8,128)(2,1)S(1)}, bf16[336,128]{1,0:T(8,128)(2,1)S(1)}, u32[]{:S(2)}, u32[]{:S(2)}) collective-permute-start(bf16[336,128]{1,0:T(8,128)(2,1)S(1)} %get-tuple-element.87), channel_id=1, source_target_pairs={{0,6},{1,7},{2,4},{3,5},{4,2},{5,3},{6,0},{7,1},{8,14},{9,15},{10,... | collective-permute-start | bytes 258056 | tf_op jit(solution)/shard_map/ppermute | solution.py:419
  78.0 5.7 %collective-permute-start.24 = (bf16[128,128]{1,0:T(8,128)(2,1)S(1)}, bf16[128,128]{1,0:T(8,128)(2,1)S(1)}, u32[]{:S(2)}, u32[]{:S(2)}) collective-permute-start(bf16[128,128]{1,0:T(8,128)(2,1)S(1)} %get-tuple-element.92.refs_0_), channel_id=1, source_target_pairs={{0,16},{1,17},{2,18},{3,19},{4,20},{5,21},{6,22},{7,23},{8,24},{9,... | collective-permute-start | bytes 98312 | tf_op jit(solution)/shard_map/ppermute | solution.py:423
  80.0 3.9 %collective-permute-start.23 = (bf16[128,128]{1,0:T(8,128)(2,1)S(1)}, bf16[128,128]{1,0:T(8,128)(2,1)S(1)}, u32[]{:S(2)}, u32[]{:S(2)}) collective-permute-start(bf16[128,128]{1,0:T(8,128)(2,1)S(1)} %get-tuple-element.92.refs_0_), channel_id=1, source_target_pairs={{0,24},{1,25},{2,26},{3,27},{4,28},{5,29},{6,30},{7,31},{8,0},{9,1... | collective-permute-start | bytes 98312 | tf_op jit(solution)/shard_map/ppermute | solution.py:423
  80.1 5.1 %collective-permute-start.22 = (bf16[128,128]{1,0:T(8,128)(2,1)S(1)}, bf16[128,128]{1,0:T(8,128)(2,1)S(1)}, u32[]{:S(2)}, u32[]{:S(2)}) collective-permute-start(bf16[128,128]{1,0:T(8,128)(2,1)S(1)} %get-tuple-element.92.refs_0_), channel_id=1, source_target_pairs={{0,8},{1,9},{2,10},{3,11},{4,12},{5,13},{6,14},{7,15},{8,16},{9,17... | collective-permute-start | bytes 98312 | tf_op jit(solution)/shard_map/ppermute | solution.py:423
  86.0 7.3 %collective-permute-start.27 = (bf16[448,128]{1,0:T(8,128)(2,1)S(1)}, bf16[448,128]{1,0:T(8,128)(2,1)S(1)}, u32[]{:S(2)}, u32[]{:S(2)}) collective-permute-start(bf16[448,128]{1,0:T(8,128)(2,1)S(1)} %charge_sum.1.refs_0_), channel_id=1, source_target_pairs={{0,192},{32,224},{64,128},{96,160},{128,64},{160,96},{192,0},{224,... | collective-permute-start | bytes 344072 | tf_op jit(solution)/shard_map/ppermute | solution.py:419
  88.8 6.3 %collective-permute-start.26 = (bf16[448,128]{1,0:T(8,128)(2,1)S(1)}, bf16[448,128]{1,0:T(8,128)(2,1)S(1)}, u32[]{:S(2)}, u32[]{:S(2)}) collective-permute-start(bf16[448,128]{1,0:T(8,128)(2,1)S(1)} %charge_sum.1.refs_0_), channel_id=1, source_target_pairs={{0,128},{32,160},{64,192},{96,224},{128,0},{160,32},{192,64},{224,... | collective-permute-start | bytes 344072 | tf_op jit(solution)/shard_map/ppermute | solution.py:419
  89.6 5.5 %collective-permute-start.25 = (bf16[448,128]{1,0:T(8,128)(2,1)S(1)}, bf16[448,128]{1,0:T(8,128)(2,1)S(1)}, u32[]{:S(2)}, u32[]{:S(2)}) collective-permute-start(bf16[448,128]{1,0:T(8,128)(2,1)S(1)} %charge_sum.1.refs_0_), channel_id=1, source_target_pairs={{0,64},{32,96},{64,0},{96,32},{128,192},{160,224},{192,128},{224,1... | collective-permute-start | bytes 344072 | tf_op jit(solution)/shard_map/ppermute | solution.py:419
  95.2 10.0 %collective-permute-start.28 = (bf16[448,128]{1,0:T(8,128)(2,1)S(1)}, bf16[448,128]{1,0:T(8,128)(2,1)S(1)}, u32[]{:S(2)}, u32[]{:S(2)}) collective-permute-start(bf16[448,128]{1,0:T(8,128)(2,1)S(1)} %cell_sum.1.refs_0_), channel_id=1, source_target_pairs={{0,32},{32,0},{64,96},{96,64},{128,160},{160,128},{192,224},{224,1... | collective-permute-start | bytes 344072 | tf_op jit(solution)/shard_map/ppermute | solution.py:419
  (15 other events, 34.1 us)

commit v3 on v2

--- a/solution.py
+++ b/solution.py
@@ -22,10 +22,12 @@
 ROW = 8
 KB = K // ROW
 PACK = ATOMS + 16
-QUARTER = 80
+QUARTER = 64
+PART = QUARTER // 2
+LOW = C // 2
 HALF = ROW * ATOMS // 2
 CHUNK = 1024
-EDGE_STEPS = (3, 5, 1, 3)
+EDGE_STEPS = (3, 6, 1, 2)
 
 cutoff_radius = 6.0
 basis_width = 0.75
@@ -109,26 +111,53 @@
     return pl.multiple_of((mask // 2 + (mask % 2) * (ROW // 2)) * rows, rows)
 
 
-def quarter_at(part):
-    return pl.ds(pl.multiple_of(((place_in_row() // 2) ^ part) * QUARTER, QUARTER), QUARTER)
-
-
-def pack_kernel(feats, coords, kinds, downs, ups, packed, tail):
-    packed[0:ATOMS, :] = feats[...]
-    place = coords[...]
-    high = place.astype(bf16).astype(f32)
-    rest = place - high
-    middle = rest.astype(bf16).astype(f32)
-    low = rest - middle
+def rows_at(index, count):
+    return pl.ds(pl.multiple_of(index * count, count), count)
+
+
+def z_at(part, count):
+    return rows_at((place_in_row() // 2) ^ part, count)
+
+
+def core():
+    return lax.rem(lax.axis_index("dom"), 2)
+
+
+def tree(own, near, across, corner):
+    return (own.astype(f32) + near.astype(f32)) + (across.astype(f32) + corner.astype(f32))
+
+
+def pack_kernel(
+    feats, coords, kinds, downs, ups, sent, got, live, reach,
+    packed, senders, receivers, mask, lengths, tail, whole, places, labels, indices, sems,
+):
+    near = [(feats, whole), (coords, places), (kinds, labels), (ups, indices.at[0]), (downs, indices.at[1])]
+    edges = [(sent, senders), (got, receivers), (live, mask), (reach, lengths)]
+    copies = [
+        pltpu.make_async_copy(source, target, sems.at[i]) for i, (source, target) in enumerate(near + edges)
+    ]
+    for copy in copies:
+        copy.start()
+    for copy in copies:
+        copy.wait()
+    packed[0:ATOMS, :] = whole[...]
     at = iota((16, ATOMS), 0)
-    values = jnp.zeros((16, ATOMS), f32)
-    for part, piece in enumerate((high, middle, low)):
-        for axis in range(3):
-            values = jnp.where(at == 3 * part + axis, piece[axis : axis + 1, :], values)
-    tail[...] = jnp.where(at == 9, kinds[...].astype(f32), values)
-    tail[10:11, 0:GHOST] = ups[...].astype(f32)
-    tail[11:12, 0:GHOST] = downs[...].astype(f32)
+    values = jnp.where(at == 9, labels[...].astype(f32), 0.0)
+    for axis in range(3):
+        place = places[axis]
+        for part in range(3):
+            piece = place.astype(bf16).astype(f32)
+            values = jnp.where(at == 3 * part + axis, piece, values)
+            place = place - piece
+    tail[...] = values
+    tail[10:11, 0:GHOST] = indices[0].astype(f32)
+    tail[11:12, 0:GHOST] = indices[1].astype(f32)
     packed[ATOMS:PACK, :] = tail[...].astype(bf16)
+
+
+def gather_kernel(own, near, across, corner, out):
+    for part, rows in enumerate((own, near, across, corner)):
+        out[PACK * part : PACK * (part + 1), :] = rows[...]
 
 
 def wave_lanes(waves):
@@ -202,9 +231,7 @@
 
 
 def column_sum(own, up, down, over, span):
-    return (own[span, :].astype(f32) + over[span, :].astype(f32)) + (
-        up[span, :].astype(f32) + down[span, :].astype(f32)
-    )
+    return tree(own[span, :], over[span, :], up[span, :], down[span, :])
 
 
 def field_of(sums, filt, scale):
@@ -268,12 +295,10 @@
 
 
 def update_kernel(
-    held, near, across, corner, aggregate, feats, cotangent, w_out, extended, w_message, operator, radial_rows,
-    w_radial, updated, own_total, own_rows, own_quarter, send_near, send_across, send_corner, grads,
+    held, near, across, corner, aggregate, cotangent, w_out, extended, w_message, operator, radial_rows, w_radial,
+    act_out, own_total, own_rows, own_quarter, own_radial, send_near, send_across, send_corner, grads,
 ):
-    preact = aggregate[...] + (
-        (held[...] + near[...].astype(f32)) + (across[...].astype(f32) + corner[...].astype(f32))
-    )
+    preact = aggregate[...] + tree(held[...], near[...], across[...], corner[...])
     sig = jax.nn.sigmoid(preact)
     grad_act = dot_lanes(cotangent[...], w_out[...])
     grad = grad_act * sig * (1.0 + preact * (1.0 - sig))
@@ -287,43 +312,61 @@
     own_rows[0:ATOMS, :] = rounded
     own_rows[ATOMS:, :] = grad_rows[ATOMS:].astype(bf16)
     act = (preact * sig).astype(bf16)
-    updated[...] = (feats[...].astype(f32) + dot(act, w_out[...])).astype(bf16)
-    grads[0:C, :] = dot_rows(extended[...], grad_msg)
-    grads[C : 2 * C, :] = dot_rows(act, cotangent[...])
-    at = iota((4 * QUARTER - 2 * C, C), 0)
-    tail = jnp.zeros((4 * QUARTER - 2 * C, C), f32)
+    act_out[...] = act
+    grad_message = dot_rows(extended[...], grad_msg)
+    grad_out = dot_rows(act, cotangent[...])
+    for t in range(ROW):
+        grads[PART * t : PART * t + 16, :] = grad_message[16 * t : 16 * (t + 1)]
+        grads[PART * t + 16 : PART * (t + 1), :] = grad_out[16 * t : 16 * (t + 1)]
+    at = iota((16, C), 0)
+    tail = jnp.zeros((16, C), f32)
     for b in range(NB):
         part = jnp.sum(grad * radial_rows[ATOMS * b : ATOMS * (b + 1), :], axis=0, keepdims=True)
         tail = jnp.where(at == b, part, tail)
-    grads[2 * C :, :] = tail
-    own_quarter[...] = grads[quarter_at(0), :]
+    tail = tail.astype(bf16)
+    own_radial[...] = tail
+    own_quarter[...] = grads[z_at(0, QUARTER), :]
     for part, send in ((1, send_near), (2, send_across), (3, send_corner)):
         send[0:EXT, :] = own_rows[...]
-        send[EXT:, :] = grads[quarter_at(part), :].astype(bf16)
-
-
-def join_kernel(own_rows, own_quarter, near, across, corner, joined):
+        send[EXT : EXT + QUARTER, :] = grads[z_at(part, QUARTER), :].astype(bf16)
+        send[EXT + QUARTER :, :] = tail
+
+
+def updated_kernel(feats, act, w_out, updated, token):
+    total = feats[...].astype(f32) + dot(act[...], w_out[...])
+    updated[...] = total.astype(bf16)
+    token[...] = total[0:8]
+
+
+def join_kernel(own_rows, own_quarter, own_radial, near, across, corner, joined, kept, sums):
     quarter = own_quarter[...]
     for part, rows in enumerate((own_rows, near, across, corner)):
         joined[ATOMS * part : ATOMS * (part + 1), :] = rows[0:ATOMS, :]
         start = HALF + 2 * GHOST * part
         joined[start : start + 2 * GHOST, :] = rows[ATOMS:EXT, :]
         if part:
-            quarter = quarter + rows[EXT:, :].astype(f32)
-    joined[HALF + 8 * GHOST :, :] = quarter.astype(bf16)
+            quarter = quarter + rows[EXT : EXT + QUARTER, :].astype(f32)
+    sums[...] = quarter
+    kept[...] = sums[rows_at(core(), PART), :]
+    ends = HALF + 8 * GHOST
+    joined[ends : ends + PART, :] = sums[rows_at(1 - core(), PART), :].astype(bf16)
+    last = slice(EXT + QUARTER, EXT + QUARTER + 16)
+    joined[ends + PART :, :] = tree(own_radial[...], near[last, :], across[last, :], corner[last, :]).astype(bf16)
 
 
 def back_near_kernel(table, joined, sums):
     sums[...] = dot(table[...], joined[0:HALF, :])
 
 
-def back_far_kernel(table, received, joined, near_sums, message, over, back_down, back_up, ghosts):
+def back_far_kernel(table, received, joined, kept, near_sums, message, over, back_down, back_up, ghosts):
     total = (near_sums[...] + dot(table[...], received[0:HALF, :])).astype(bf16)
     ends = HALF + 8 * GHOST
-    quarter = (joined[ends:, :].astype(f32) + received[ends:, :].astype(f32)).astype(bf16)
+    part = (kept[...] + received[ends : ends + PART, :].astype(f32)).astype(bf16)
+    radial = (joined[ends + PART :, :].astype(f32) + received[ends + PART :, :].astype(f32)).astype(bf16)
     for target in (message, over):
         target[0 : 2 * KB, :] = total
-        target[2 * KB : 2 * KB + QUARTER, :] = quarter
+        target[2 * KB : 2 * KB + PART, :] = part
+        target[2 * KB + PART : 2 * KB + PART + 16, :] = radial
     ghosts[0 : 8 * GHOST, :] = joined[HALF:ends, :]
     ghosts[8 * GHOST :, :] = received[HALF:ends, :]
     place = place_in_row()
@@ -334,16 +377,17 @@
 
     back_down[...] = returned((place + ROW - 1) % ROW, 1)
     back_up[...] = returned((place + 1) % ROW, 0)
-    message[2 * KB + QUARTER : 2 * KB + QUARTER + GHOST, :] = returned(ROW - 1, 1)
-    message[2 * KB + QUARTER + GHOST :, :] = returned(0, 0)
+    first = 2 * KB + PART + 16
+    message[first : first + GHOST, :] = returned(ROW - 1, 1)
+    message[first + GHOST :, :] = returned(0, 0)
 
 
 def charge_back_kernel(
     own, up, down, over, filt, near, far, near_gain, far_gain, near_rows, far_rows,
-    send, keep, charge, quarter, rounded,
+    send, keep, charge, early, rounded, sums,
 ):
     field = field_of(column_sum(own, up, down, over, slice(0, 2 * KB)), filt, inv_waves * inv_atoms)
-    quarter[...] = column_sum(own, up, down, over, slice(2 * KB, 2 * KB + QUARTER)).astype(bf16)
+    early[...] = column_sum(own, up, down, over, slice(2 * KB, 2 * KB + PART + 16)).astype(bf16)
     send[0:HALF, :] = (dot_rows(far[...], field) * far_gain[...]).astype(bf16)
     values = dot_rows(near[...], field) * near_gain[...]
     keep[...] = values
@@ -353,50 +397,45 @@
         rows, atoms = slice(PACK * j, PACK * j + ATOMS), slice(ATOMS * j, ATOMS * (j + 1))
         total = total + dot_rows(near_rows[rows, :], rounded[atoms, :])
         total = total + dot_rows(far_rows[rows, :], send[atoms, :])
-    charge[...] = total.astype(bf16)
-    send[HALF:, :] = charge[...]
-
-
-def tail_spread_kernel(held, charge, quarter, received, own, charge_out, *sends):
+    sums[...] = total
+    charge[...] = sums[rows_at(core(), LOW), :]
+    send[HALF:, :] = sums[rows_at(1 - core(), LOW), :].astype(bf16)
+
+
+def tail_spread_kernel(held, charge, early, received, own, charge_out, *sends):
     values = held[...] + received[0:HALF, :].astype(f32)
-    total = (charge[...].astype(f32) + received[HALF:, :].astype(f32)).astype(bf16)
+    total = (charge[...] + received[HALF:, :].astype(f32)).astype(bf16)
     own[...] = values[0:ATOMS]
     charge_out[...] = total
     for part, send in enumerate(sends):
         send[0:ATOMS, :] = values[ATOMS * (part + 1) : ATOMS * (part + 2)].astype(bf16)
-        send[ATOMS : ATOMS + C, :] = total
-        send[ATOMS + C :, :] = quarter[...]
-
-
-def raw_kernel(held, charge, quarter, near, across, corner, raw, charge_out, grads):
+        send[ATOMS : ATOMS + LOW, :] = total
+        send[ATOMS + LOW :, :] = early[0:PART, :]
+
+
+def raw_kernel(held, charge, early, near, across, corner, raw, charge_out, grads):
     rows = slice(0, ATOMS)
-    raw[...] = (
-        (held[...] + near[rows, :].astype(f32)) + (across[rows, :].astype(f32) + corner[rows, :].astype(f32))
-    ).astype(bf16)
-    rows = slice(ATOMS, ATOMS + C)
-    charge_out[...] = (
-        (charge[...].astype(f32) + near[rows, :].astype(f32))
-        + (across[rows, :].astype(f32) + corner[rows, :].astype(f32))
-    ).astype(bf16)
-    grads[quarter_at(0), :] = quarter[...]
+    raw[...] = tree(held[...], near[rows, :], across[rows, :], corner[rows, :]).astype(bf16)
+    rows = slice(ATOMS, ATOMS + LOW)
+    charge_out[...] = tree(charge[...], near[rows, :], across[rows, :], corner[rows, :]).astype(bf16)
+    grads[z_at(0, PART), :] = early[0:PART, :]
     for part, received in ((1, near), (2, across), (3, corner)):
-        grads[quarter_at(part), :] = received[ATOMS + C :, :]
-
-
-def charge_sum_kernel(own, up, down, over, grads, out):
-    out[0:C, :] = column_sum(own, up, down, over, slice(0, C)).astype(bf16)
-    out[C:, :] = grads[...]
+        grads[z_at(part, PART), :] = received[ATOMS + LOW :, :]
+
+
+def charge_sum_kernel(own, up, down, over, grads, early, out):
+    out[0:LOW, :] = column_sum(own, up, down, over, slice(0, LOW)).astype(bf16)
+    out[LOW : LOW + C, :] = grads[...]
+    out[LOW + C :, :] = early[PART:, :]
 
 
 def cell_sum_kernel(own, near, across, corner, out):
-    out[...] = (
-        (own[...].astype(f32) + near[...].astype(f32)) + (across[...].astype(f32) + corner[...].astype(f32))
-    ).astype(bf16)
-
-
-def feature_kernel(raw, w_charge, own, downs, ups, back_down, back_up, up, down, out):
+    out[...] = tree(own[...], near[...], across[...], corner[...]).astype(bf16)
+
+
+def feature_kernel(raw, w_charge, own, downs, ups, back_down, back_up, up, down, out, token):
     place = place_in_row()
-    first, last = 2 * KB + QUARTER, 2 * KB + QUARTER + GHOST
+    first, last = 2 * KB + PART + 16, 2 * KB + PART + 16 + GHOST
     returned = jnp.where(place == 0, up[first:last, :], back_down[...])
     total = own[...] + dot_lanes(raw[...], w_charge[...])
     atom = iota((ATOMS, GHOST), 0)
@@ -404,14 +443,18 @@
     returned = jnp.where(place == ROW - 1, down[last:, :], back_up[...])
     total = total + dot((atom == ups[...]).astype(f32).astype(bf16), returned)
     out[...] = total.astype(bf16)
-
-
-def weights_kernel(held, received, charge, message, radial, out):
-    total = (held[...].astype(f32) + received[...].astype(f32)) * grad_scale
-    charge[...] = total[0:C]
-    message[...] = total[C : 2 * C]
-    out[...] = total[2 * C : 3 * C]
-    radial[...] = total[3 * C : 3 * C + NB]
+    token[...] = total[0:8]
+
+
+def weights_kernel(own, other, own_cell, other_cell, charge, message, radial, out):
+    for first, second, at in ((own, own_cell, core()), (other, other_cell, 1 - core())):
+        total = (first[...].astype(f32) + second[...].astype(f32)) * grad_scale
+        charge[rows_at(at, LOW), :] = total[0:LOW]
+        for z in range(4):
+            start = LOW + PART * z
+            message[rows_at(2 * z + at, 16), :] = total[start : start + 16]
+            out[rows_at(2 * z + at, 16), :] = total[start + 16 : start + PART]
+        radial[...] = total[LOW + C : LOW + C + NB]
 
 
 def swap(values, axis, mask):
@@ -452,7 +495,7 @@
         (out,) = call(
             lambda *refs: edge_kernel(total is None, *refs),
             [((NB * ATOMS, EXT), f32)],
-            edge_sender, edge_receiver, edge_mask, edge_length, *held,
+            *edge_arrays, *held,
             scratch=[pltpu.VMEM((NB * ATOMS, CHUNK), bf16), pltpu.VMEM((EXT, CHUNK), bf16)],
             flops=count * 2 * NB * ATOMS * CHUNK * 256,
             grid=(count,),
@@ -463,22 +506,37 @@
         )
         return out
 
-    (packed,) = call(
+    in_place = pl.BlockSpec(memory_space=pltpu.HBM)
+    arrays = (
+        own_rows, positions.transpose(1, 0, 2), species, ghost_down, ghost_up,
+        edge_sender, edge_receiver, edge_mask, edge_length,
+    )
+    packed, *edge_arrays = call(
         pack_kernel,
-        [((PACK, C), bf16)],
-        own_rows, positions[0], species, ghost_down, ghost_up,
-        scratch=[pltpu.VMEM((16, C), f32)],
+        [((PACK, C), bf16)] + [((1, EDGES), jnp.int32)] * 3 + [((1, EDGES), f32)],
+        *[pltpu.with_memory_space_constraint(values, pltpu.HBM) for values in arrays],
+        scratch=[
+            pltpu.VMEM((16, C), f32), pltpu.VMEM((ATOMS, C), bf16), pltpu.VMEM((3, 1, ATOMS), f32),
+            pltpu.VMEM((1, ATOMS), jnp.int32), pltpu.VMEM((2, 1, GHOST), jnp.int32), pltpu.SemaphoreType.DMA((9,)),
+        ],
+        in_specs=[in_place] * 9,
+        out_specs=[pl.BlockSpec(memory_space=pltpu.VMEM)] * 5,
         name="pack",
     )
     operator = edges(0, EDGE_STEPS[0], None, [packed])
-    near_rows = jnp.concatenate([packed] + [swap(packed, "dom", mask) for mask in (2, 4, 6)], axis=0)
+    (near_rows,) = call(
+        gather_kernel,
+        [((ROW // 2 * PACK, C), bf16)],
+        packed, *[swap(packed, "dom", mask) for mask in (2, 4, 6)],
+        after=[operator],
+        name="gather",
+    )
     far_rows = swap(near_rows, "dom", 1)
     near, near_sums, filt, near_gain = call(
         structure_near_kernel,
         [((2 * KB, HALF), bf16), ((2 * KB, C), f32), ((KB, C), f32), ((HALF, C), f32)],
         near_rows, wave_vectors, smearing[None], species_gain, w_charge,
         scratch=[pltpu.VMEM((HALF, C), bf16)],
-        after=[operator],
         name="structure_near",
     )
     far, sums, message, far_gain, below, above = call(
@@ -513,69 +571,77 @@
         own_rows, below, above, up, down, w_message, operator, w_radial,
         name="aggregate",
     )
-    updated, own_total, back_rows, quarter, *sends = call(
+    act, own_total, back_rows, quarter, radial, *sends = call(
         update_kernel,
-        [((ATOMS, C), bf16), ((ATOMS, C), f32), ((EXT, C), bf16), ((QUARTER, C), f32)]
-        + [((EXT + QUARTER, C), bf16)] * 3,
-        held, *parts, aggregate, own_rows, cot, w_out, extended, w_message, operator, radial_rows, w_radial,
-        scratch=[pltpu.VMEM((4 * QUARTER, C), f32)],
+        [((ATOMS, C), bf16), ((ATOMS, C), f32), ((EXT, C), bf16), ((QUARTER, C), f32), ((16, C), bf16)]
+        + [((EXT + QUARTER + 16, C), bf16)] * 3,
+        held, *parts, aggregate, cot, w_out, extended, w_message, operator, radial_rows, w_radial,
+        scratch=[pltpu.VMEM((2 * C, C), f32)],
         name="update",
     )
     parts = [swap(values, "dom", 2 * (part + 1)) for part, values in enumerate(sends)]
-    (joined,) = call(
-        join_kernel, [((HALF + 8 * GHOST + QUARTER, C), bf16)], back_rows, quarter, *parts, name="join"
+    updated, token = call(
+        updated_kernel, [((ATOMS, C), bf16), ((8, C), f32)], own_rows, act, w_out, after=[sends[0]], name="updated"
+    )
+    joined, kept = call(
+        join_kernel,
+        [((HALF + 8 * GHOST + PART + 16, C), bf16), ((PART, C), f32)],
+        back_rows, quarter, radial, *parts,
+        scratch=[pltpu.VMEM((QUARTER, C), f32)],
+        after=[token],
+        name="join",
     )
     received = swap(joined, "dom", 1)
     (near_sums,) = call(back_near_kernel, [((2 * KB, C), f32)], near, joined, name="back_near")
     message, over, back_down, back_up = call(
         back_far_kernel,
         [
-            ((2 * KB + QUARTER + 2 * GHOST, C), bf16), ((2 * KB + QUARTER, C), bf16),
+            ((2 * KB + PART + 16 + 2 * GHOST, C), bf16), ((2 * KB + PART + 16, C), bf16),
             ((GHOST, C), bf16), ((GHOST, C), bf16),
         ],
-        far, received, joined, near_sums,
+        far, received, joined, kept, near_sums,
         scratch=[pltpu.VMEM((16 * GHOST, C), bf16)],
         name="back_far",
     )
     up, down, over = from_y(message, 1), from_y(message, -1), from_y(over, 2)
-    send, keep, charge, quarter = call(
+    send, keep, charge, early = call(
         charge_back_kernel,
-        [((HALF + C, C), bf16), ((HALF, C), f32), ((C, C), bf16), ((QUARTER, C), bf16)],
+        [((HALF + LOW, C), bf16), ((HALF, C), f32), ((LOW, C), f32), ((PART + 16, C), bf16)],
         message, up, down, over, filt, near, far, near_gain, far_gain, near_rows, far_rows,
-        scratch=[pltpu.VMEM((HALF, C), bf16)],
+        scratch=[pltpu.VMEM((HALF, C), bf16), pltpu.VMEM((C, C), f32)],
         name="charge_back",
     )
     received = swap(send, "dom", 1)
     held, charge, *sends = call(
         tail_spread_kernel,
-        [((ATOMS, C), f32), ((C, C), bf16)] + [((ATOMS + C + QUARTER, C), bf16)] * 3,
-        keep, charge, quarter, received,
+        [((ATOMS, C), f32), ((LOW, C), bf16)] + [((ATOMS + LOW + PART, C), bf16)] * 3,
+        keep, charge, early, received,
         name="tail_spread",
     )
     parts = [swap(values, "dom", 2 * (part + 1)) for part, values in enumerate(sends)]
     raw, charge, grads = call(
         raw_kernel,
-        [((ATOMS, C), bf16), ((C, C), bf16), ((4 * QUARTER, C), bf16)],
-        held, charge, quarter, *parts,
+        [((ATOMS, C), bf16), ((LOW, C), bf16), ((C, C), bf16)],
+        held, charge, early, *parts,
         name="raw",
     )
     parts = [from_y(charge, by) for by in (1, -1, 2)]
-    (feat_grad,) = call(
+    feat_grad, token = call(
         feature_kernel,
-        [((ATOMS, C), bf16)],
+        [((ATOMS, C), bf16), ((8, C), f32)],
         raw, w_charge, own_total, ghost_down, ghost_up, back_down, back_up, up, down,
         name="feature",
     )
     (total,) = call(
-        charge_sum_kernel, [((C + 4 * QUARTER, C), bf16)], charge, *parts, grads, after=[feat_grad], name="charge_sum"
+        charge_sum_kernel, [((LOW + C + 16, C), bf16)], charge, *parts, grads, early, after=[token], name="charge_sum"
     )
     parts = [swap(total, "cell", mask) for mask in (2, 4, 6)]
-    (total,) = call(cell_sum_kernel, [((C + 4 * QUARTER, C), bf16)], total, *parts, name="cell_sum")
-    received = swap(total, "cell", 1)
+    (total,) = call(cell_sum_kernel, [((LOW + C + 16, C), bf16)], total, *parts, name="cell_sum")
+    parts = [swap(total, "dom", 1)] + [swap(total, ("cell", "dom"), DOMS + mask) for mask in (6, 7)]
     charge, message, radial, out = call(
         weights_kernel,
         [((C, C), f32), ((C, C), f32), ((NB, C), f32), ((C, C), f32)],
-        total, received,
+        total, *parts,
         name="weights",
     )
     return updated[None], feat_grad[None], charge, message, radial, out

time: 106 us -> 96.1 us (0.907)
  the two profiles are of different devices: /device:TPU:32 before, /device:TPU:1 now
where the time goes in v3:
time: 96.1 us; the launch traced here: 95.6 us
  starting transfers between devices  47.2 us (49%)
  waiting for transfers between devices  25.4 us (26%)
  Pallas kernels  21.4 us (22%)
    ppermute x22, starting transfers between devices, swap(): return lax.ppermute(values, axis, [(i, i ^ mask) for i in range(count)])  36.8 us
    pallas_call x23, Pallas kernels, call(): pl.pallas_call(run, out_shape=[jax.ShapeDtypeStruct(shape, dtype) for sha...  21.4 us
    ppermute x22, waiting for transfers between devices, swap(): return lax.ppermute(values, axis, [(i, i ^ mask) for i in range(count)])  17.4 us
    ppermute x9, starting transfers between devices, from_y(): lax.ppermute(values, 'dom', [(i, (i + ROW * by) % DOMS) for i in range(DO...  10.4 us
    ppermute x9, waiting for transfers between devices, from_y(): lax.ppermute(values, 'dom', [(i, (i + ROW * by) % DOMS) for i in range(DO...  8.07 us
  transfers between devices with their start and end apart: 31, of which 15 were waited for; matrix products, arithmetic and copies ran while one was open for 0% of the time, Pallas kernels for 17%

profile of v3, /device:TPU:1, one launch (start us, length us, event | category | flops | bytes accessed | tf_op | source)
XLA Modules:
  0.0 95.6 jit_solution(3527175531223907292)
XLA Ops:
  0.6 1.1 %pack.1 = (bf16[144,128]{1,0:T(8,128)(2,1)S(1)}, s32[1,12288]{1,0:T(1,128)S(1)}, s32[1,12288]{1,0:T(1,128)S(1)}, s32[1,12288]{1,0:T(1,128)S(1)}, f32[1,12288]{1,0:T(1,128)S(1)}) custom-call(bf16[128,128]{1,0:T(8,128)(2,1)} %bitcast.6, f32[3,1,128]{2,1,0:T(1,128)} %bitcast.11, s32[1,128]{1,0:T(1,128)} %refs_2_.2, s32[1,32]{1,0:T(1,128)} %refs_3_.7, ...), custom_call_target="tpu_custom_call" | custom-call | bytes 262144 | tf_op jit(solution)/shard_map/pack/pallas_call | solution.py:95
  1.7 5.3 %collective-permute-start.2 = (bf16[144,128]{1,0:T(8,128)(2,1)S(1)}, bf16[144,128]{1,0:T(8,128)(2,1)S(1)}, u32[]{:S(2)}, u32[]{:S(2)}) collective-permute-start(bf16[144,128]{1,0:T(8,128)(2,1)S(1)} %get-tuple-element.64.refs_4_.refs_0_), channel_id=1, source_target_pairs={{0,6},{1,7},{2,4},{3,5},{4,2},{5,3},{6,0},{7,1},{8,14},{9,15},{10,... | collective-permute-start | bytes 110600 | tf_op jit(solution)/shard_map/ppermute | solution.py:462
  7.3 3.2 %edges.4.refs_4_ = f32[1024,192]{1,0:T(8,128)S(1)} custom-call(s32[1,12288]{1,0:T(1,128)S(1)} %get-tuple-element.65.refs_0_, s32[1,12288]{1,0:T(1,128)S(1)} %get-tuple-element.66.refs_1_, s32[1,12288]{1,0:T(1,128)S(1)} %get-tuple-element.67.refs_2_, f32[1,12288]{1,0:T(1,128)S(1)} %get-tuple-element.68.refs_3_, ...), custom_call_target="tpu_custom_call" | custom-call | flops 1610612736 | bytes 262144 | tf_op jit(solution)/shard_map/edges/pallas_call | solution.py:95
  11.1 1.8 %collective-permute-start.3 = (bf16[576,128]{1,0:T(8,128)(2,1)S(1)}, bf16[576,128]{1,0:T(8,128)(2,1)S(1)}, u32[]{:S(2)}, u32[]{:S(2)}) collective-permute-start(bf16[576,128]{1,0:T(8,128)(2,1)S(1)} %gather.1.refs_0_.refs_1_.refs_9_), channel_id=1, source_target_pairs={{0,1},{1,0},{2,3},{3,2},{4,5},{5,4},{6,7},{7,6},{8,9},{9,8},{10,11... | collective-permute-start | bytes 442376 | tf_op jit(solution)/shard_map/ppermute | solution.py:462
  12.9 1.2 %structure_near.1 = (bf16[512,512]{1,0:T(8,128)(2,1)S(1)}, f32[512,128]{1,0:T(8,128)S(1)}, f32[256,128]{1,0:T(8,128)S(1)}, f32[512,128]{1,0:T(8,128)S(1)}) custom-call(bf16[576,128]{1,0:T(8,128)(2,1)S(1)} %gather.1.refs_0_.refs_1_.refs_9_, s32[3,2048]{1,0:T(4,128)S(1)} %copy-done.4, f32[1,128]{1,0:T(1,128)S(1)} %bitcast.10, f32[8,128]{1,0:T(8,128)S(1)} %copy-done.7, ...), custom_call_target="tpu_custom_call" | custom-call | bytes 262144 | tf_op jit(solution)/shard_map/structure_near/pallas_call | solution.py:95
  14.1 1.1 %structure_far.1 = (bf16[512,512]{1,0:T(8,128)(2,1)S(1)}, bf16[512,128]{1,0:T(8,128)(2,1)S(1)}, bf16[576,128]{1,0:T(8,128)(2,1)S(1)}, f32[512,128]{1,0:T(8,128)S...) custom-call(bf16[576,128]{1,0:T(8,128)(2,1)S(1)} %collective-permute-done.3.refs_0_.refs_10_, ...), custom_call_target="tpu_custom_call" | custom-call | bytes 262144 | tf_op jit(solution)/shard_map/structure_far/pallas_call | solution.py:95
  15.2 2.8 %collective-permute-start.5 = (bf16[576,128]{1,0:T(8,128)(2,1)S(1)}, bf16[576,128]{1,0:T(8,128)(2,1)S(1)}, u32[]{:S(2)}, u32[]{:S(2)}) collective-permute-start(bf16[576,128]{1,0:T(8,128)(2,1)S(1)} %get-tuple-element.71.refs_5_), channel_id=1, source_target_pairs={{0,24},{1,25},{2,26},{3,27},{4,28},{5,29},{6,30},{7,31},{8,0},{9,1... | collective-permute-start | bytes 442376 | tf_op jit(solution)/shard_map/ppermute | solution.py:466
  18.0 1.6 %collective-permute-start.6 = (bf16[512,128]{1,0:T(8,128)(2,1)S(1)}, bf16[512,128]{1,0:T(8,128)(2,1)S(1)}, u32[]{:S(2)}, u32[]{:S(2)}) collective-permute-start(bf16[512,128]{1,0:T(8,128)(2,1)S(1)} %get-tuple-element.70.refs_0_), channel_id=1, source_target_pairs={{0,16},{1,17},{2,18},{3,19},{4,20},{5,21},{6,22},{7,23},{8,24},{9,... | collective-permute-start | bytes 393224 | tf_op jit(solution)/shard_map/ppermute | solution.py:466
  19.6 6.4 %edges.5.refs_7_.refs_4_ = f32[1024,192]{1,0:T(8,128)S(1)} custom-call(s32[1,12288]{1,0:T(1,128)S(1)} %get-tuple-element.65.refs_0_, s32[1,12288]{1,0:T(1,128)S(1)} %get-tuple-element.66.refs_1_, s32[1,12288]{1,0:T(1,128)S(1)} %get-tuple-element.67.refs_2_, f32[1,12288]{1,0:T(1,128)S(1)} %get-tuple-element.68.refs_3_, f32[1024,192]{1,0:T(8,128)S(1)} %edges.4.refs_4_, ...), custom_call_target="tpu_custom_call" | custom-call | flops 3221225472 | bytes 262144 | tf_op jit(solution)/shard_map/edges/pallas_call | solution.py:95
  26.5 2.3 %collective-permute-start.7 = (bf16[512,128]{1,0:T(8,128)(2,1)S(1)}, bf16[512,128]{1,0:T(8,128)(2,1)S(1)}, u32[]{:S(2)}, u32[]{:S(2)}) collective-permute-start(bf16[512,128]{1,0:T(8,128)(2,1)S(1)} %get-tuple-element.76.refs_5_), channel_id=1, source_target_pairs={{0,1},{1,0},{2,3},{3,2},{4,5},{5,4},{6,7},{7,6},{8,9},{9,8},{10,11... | collective-permute-start | bytes 393224 | tf_op jit(solution)/shard_map/ppermute | solution.py:462
  30.1 2.6 %collective-permute-start.9 = (bf16[128,128]{1,0:T(8,128)(2,1)S(1)}, bf16[128,128]{1,0:T(8,128)(2,1)S(1)}, u32[]{:S(2)}, u32[]{:S(2)}) collective-permute-start(bf16[128,128]{1,0:T(8,128)(2,1)S(1)} %get-tuple-element.79), channel_id=1, source_target_pairs={{0,4},{1,5},{2,6},{3,7},{4,0},{5,1},{6,2},{7,3},{8,12},{9,13},{10,... | collective-permute-start | bytes 98312 | tf_op jit(solution)/shard_map/ppermute | solution.py:462
  33.5 2.2 %edges.7.refs_6_.refs_9_ = f32[1024,192]{1,0:T(8,128)S(1)} custom-call(s32[1,12288]{1,0:T(1,128)S(1)} %get-tuple-element.65.refs_0_, s32[1,12288]{1,0:T(1,128)S(1)} %get-tuple-element.66.refs_1_, s32[1,12288]{1,0:T(1,128)S(1)} %get-tuple-element.67.refs_2_, f32[1,12288]{1,0:T(1,128)S(1)} %get-tuple-element.68.refs_3_, f32[1024,192]{1,0:T(8,128)S(1)} %edges.6.refs_2_.refs_4_, ...), custom_call_target="tpu_custom_call" | custom-call | flops 1073741824 | bytes 262144 | tf_op jit(solution)/shard_map/edges/pallas_call | solution.py:95
  36.3 1.0 %collective-permute-done.10.refs_3_ = bf16[128,128]{1,0:T(8,128)(2,1)S(1)} collective-permute-done((bf16[128,128]{1,0:T(8,128)(2,1)S(1)}, bf16[128,128]{1,0:T(8,128)(2,1)S(1)}, u32[]{:S(2)}, u32[]{:S(2)}) %collective-permute-start.10) | collective-permute-done | bytes 32800 | tf_op jit(solution)/shard_map/ppermute | solution.py:462
  38.3 1.7 %collective-permute-start.13 = (bf16[272,128]{1,0:T(8,128)(2,1)S(1)}, bf16[272,128]{1,0:T(8,128)(2,1)S(1)}, u32[]{:S(2)}, u32[]{:S(2)}) collective-permute-start(bf16[272,128]{1,0:T(8,128)(2,1)S(1)} %get-tuple-element.93), channel_id=1, source_target_pairs={{0,6},{1,7},{2,4},{3,5},{4,2},{5,3},{6,0},{7,1},{8,14},{9,15},{10,... | collective-permute-start | bytes 208904 | tf_op jit(solution)/shard_map/ppermute | solution.py:462
  42.4 1.6 %collective-permute-done.13.refs_5_ = bf16[272,128]{1,0:T(8,128)(2,1)S(1)} collective-permute-done((bf16[272,128]{1,0:T(8,128)(2,1)S(1)}, bf16[272,128]{1,0:T(8,128)(2,1)S(1)}, u32[]{:S(2)}, u32[]{:S(2)}) %collective-permute-start.13) | collective-permute-done | bytes 69664 | tf_op jit(solution)/shard_map/ppermute | solution.py:462
  44.0 3.4 %collective-permute-start.14 = (bf16[816,128]{1,0:T(8,128)(2,1)S(1)}, bf16[816,128]{1,0:T(8,128)(2,1)S(1)}, u32[]{:S(2)}, u32[]{:S(2)}) collective-permute-start(bf16[816,128]{1,0:T(8,128)(2,1)S(1)} %get-tuple-element.95.refs_1_.refs_2_), channel_id=1, source_target_pairs={{0,1},{1,0},{2,3},{3,2},{4,5},{5,4},{6,7},{7,6},{8,9},{9,8},{10,11... | collective-permute-start | bytes 626696 | tf_op jit(solution)/shard_map/ppermute | solution.py:462
  48.9 1.4 %collective-permute-start.15 = (bf16[624,128]{1,0:T(8,128)(2,1)S(1)}, bf16[624,128]{1,0:T(8,128)(2,1)S(1)}, u32[]{:S(2)}, u32[]{:S(2)}) collective-permute-start(bf16[624,128]{1,0:T(8,128)(2,1)S(1)} %get-tuple-element.97.refs_0_), channel_id=1, source_target_pairs={{0,8},{1,9},{2,10},{3,11},{4,12},{5,13},{6,14},{7,15},{8,16},{9,17... | collective-permute-start | bytes 479240 | tf_op jit(solution)/shard_map/ppermute | solution.py:466
  50.3 1.1 %collective-permute-start.17 = (bf16[560,128]{1,0:T(8,128)(2,1)S(1)}, bf16[560,128]{1,0:T(8,128)(2,1)S(1)}, u32[]{:S(2)}, u32[]{:S(2)}) collective-permute-start(bf16[560,128]{1,0:T(8,128)(2,1)S(1)} %get-tuple-element.98), channel_id=1, source_target_pairs={{0,16},{1,17},{2,18},{3,19},{4,20},{5,21},{6,22},{7,23},{8,24},{9,... | collective-permute-start | bytes 430088 | tf_op jit(solution)/shard_map/ppermute | solution.py:466
  51.5 7.0 %collective-permute-done.17.refs_3_ = bf16[560,128]{1,0:T(8,128)(2,1)S(1)} collective-permute-done((bf16[560,128]{1,0:T(8,128)(2,1)S(1)}, bf16[560,128]{1,0:T(8,128)(2,1)S(1)}, u32[]{:S(2)}, u32[]{:S(2)}) %collective-permute-start.17) | collective-permute-done | bytes 143392 | tf_op jit(solution)/shard_map/ppermute | solution.py:466
  59.2 1.4 %collective-permute-start.18 = (bf16[576,128]{1,0:T(8,128)(2,1)S(1)}, bf16[576,128]{1,0:T(8,128)(2,1)S(1)}, u32[]{:S(2)}, u32[]{:S(2)}) collective-permute-start(bf16[576,128]{1,0:T(8,128)(2,1)S(1)} %get-tuple-element.104), channel_id=1, source_target_pairs={{0,1},{1,0},{2,3},{3,2},{4,5},{5,4},{6,7},{7,6},{8,9},{9,8},{10,11... | collective-permute-start | bytes 442376 | tf_op jit(solution)/shard_map/ppermute | solution.py:462
  60.6 1.0 %collective-permute-done.18.refs_3_ = bf16[576,128]{1,0:T(8,128)(2,1)S(1)} collective-permute-done((bf16[576,128]{1,0:T(8,128)(2,1)S(1)}, bf16[576,128]{1,0:T(8,128)(2,1)S(1)}, u32[]{:S(2)}, u32[]{:S(2)}) %collective-permute-start.18) | collective-permute-done | bytes 147488 | tf_op jit(solution)/shard_map/ppermute | solution.py:462
  62.3 1.5 %collective-permute-start.20 = (bf16[224,128]{1,0:T(8,128)(2,1)S(1)}, bf16[224,128]{1,0:T(8,128)(2,1)S(1)}, u32[]{:S(2)}, u32[]{:S(2)}) collective-permute-start(bf16[224,128]{1,0:T(8,128)(2,1)S(1)} %get-tuple-element.108), channel_id=1, source_target_pairs={{0,4},{1,5},{2,6},{3,7},{4,0},{5,1},{6,2},{7,3},{8,12},{9,13},{10,... | collective-permute-start | bytes 172040 | tf_op jit(solution)/shard_map/ppermute | solution.py:462
  63.8 1.5 %collective-permute-start.21 = (bf16[224,128]{1,0:T(8,128)(2,1)S(1)}, bf16[224,128]{1,0:T(8,128)(2,1)S(1)}, u32[]{:S(2)}, u32[]{:S(2)}) collective-permute-start(bf16[224,128]{1,0:T(8,128)(2,1)S(1)} %get-tuple-element.109), channel_id=1, source_target_pairs={{0,6},{1,7},{2,4},{3,5},{4,2},{5,3},{6,0},{7,1},{8,14},{9,15},{10,... | collective-permute-start | bytes 172040 | tf_op jit(solution)/shard_map/ppermute | solution.py:462
  66.2 2.4 %collective-permute-done.21.refs_5_ = bf16[224,128]{1,0:T(8,128)(2,1)S(1)} collective-permute-done((bf16[224,128]{1,0:T(8,128)(2,1)S(1)}, bf16[224,128]{1,0:T(8,128)(2,1)S(1)}, u32[]{:S(2)}, u32[]{:S(2)}) %collective-permute-start.21) | collective-permute-done | bytes 57376 | tf_op jit(solution)/shard_map/ppermute | solution.py:462
  68.7 1.8 %collective-permute-start.24 = (bf16[64,128]{1,0:T(8,128)(2,1)S(1)}, bf16[64,128]{1,0:T(8,128)(2,1)S(1)}, u32[]{:S(2)}, u32[]{:S(2)}) collective-permute-start(bf16[64,128]{1,0:T(8,128)(2,1)S(1)} %get-tuple-element.115.refs_0_), channel_id=1, source_target_pairs={{0,16},{1,17},{2,18},{3,19},{4,20},{5,21},{6,22},{7,23},{8,24},{9,... | collective-permute-start | bytes 49160 | tf_op jit(solution)/shard_map/ppermute | solution.py:466
  70.7 1.2 %collective-permute-start.22 = (bf16[64,128]{1,0:T(8,128)(2,1)S(1)}, bf16[64,128]{1,0:T(8,128)(2,1)S(1)}, u32[]{:S(2)}, u32[]{:S(2)}) collective-permute-start(bf16[64,128]{1,0:T(8,128)(2,1)S(1)} %get-tuple-element.115.refs_0_), channel_id=1, source_target_pairs={{0,8},{1,9},{2,10},{3,11},{4,12},{5,13},{6,14},{7,15},{8,16},{9,17... | collective-permute-start | bytes 49160 | tf_op jit(solution)/shard_map/ppermute | solution.py:466
  73.4 1.1 %collective-permute-done.22.refs_1_ = bf16[64,128]{1,0:T(8,128)(2,1)S(1)} collective-permute-done((bf16[64,128]{1,0:T(8,128)(2,1)S(1)}, bf16[64,128]{1,0:T(8,128)(2,1)S(1)}, u32[]{:S(2)}, u32[]{:S(2)}) %collective-permute-start.22) | collective-permute-done | bytes 16416 | tf_op jit(solution)/shard_map/ppermute | solution.py:466
  74.5 2.8 %collective-permute-start.27 = (bf16[208,128]{1,0:T(8,128)(2,1)S(1)}, bf16[208,128]{1,0:T(8,128)(2,1)S(1)}, u32[]{:S(2)}, u32[]{:S(2)}) collective-permute-start(bf16[208,128]{1,0:T(8,128)(2,1)S(1)} %charge_sum.1.refs_0_), channel_id=1, source_target_pairs={{0,192},{32,224},{64,128},{96,160},{128,64},{160,96},{192,0},{224,... | collective-permute-start | bytes 159752 | tf_op jit(solution)/shard_map/ppermute | solution.py:462
  79.0 2.8 %collective-permute-done.26.refs_2_ = bf16[208,128]{1,0:T(8,128)(2,1)S(1)} collective-permute-done((bf16[208,128]{1,0:T(8,128)(2,1)S(1)}, bf16[208,128]{1,0:T(8,128)(2,1)S(1)}, u32[]{:S(2)}, u32[]{:S(2)}) %collective-permute-start.26) | collective-permute-done | bytes 53280 | tf_op jit(solution)/shard_map/ppermute | solution.py:462
  81.8 8.2 %collective-permute-start.30 = (bf16[208,128]{1,0:T(8,128)(2,1)S(1)}, bf16[208,128]{1,0:T(8,128)(2,1)S(1)}, u32[]{:S(2)}, u32[]{:S(2)}) collective-permute-start(bf16[208,128]{1,0:T(8,128)(2,1)S(1)} %cell_sum.1.refs_0_), channel_id=1, source_target_pairs={{0,39},{1,38},{2,37},{3,36},{4,35},{5,34},{6,33},{7,32},{8,47},{9,... | collective-permute-start | bytes 159752 | tf_op jit(solution)/shard_map/ppermute | solution.py:462
  90.5 3.1 %collective-permute-done.30.refs_3_ = bf16[208,128]{1,0:T(8,128)(2,1)S(1)} collective-permute-done((bf16[208,128]{1,0:T(8,128)(2,1)S(1)}, bf16[208,128]{1,0:T(8,128)(2,1)S(1)}, u32[]{:S(2)}, u32[]{:S(2)}) %collective-permute-start.30) | collective-permute-done | bytes 53280 | tf_op jit(solution)/shard_map/ppermute | solution.py:462
  93.6 1.3 %collective-permute-done.29.refs_2_ = bf16[208,128]{1,0:T(8,128)(2,1)S(1)} collective-permute-done((bf16[208,128]{1,0:T(8,128)(2,1)S(1)}, bf16[208,128]{1,0:T(8,128)(2,1)S(1)}, u32[]{:S(2)}, u32[]{:S(2)}) %collective-permute-start.29) | collective-permute-done | bytes 53280 | tf_op jit(solution)/shard_map/ppermute | solution.py:462
  (75 shorter events, 15.7 us)
Async XLA Ops:
  1.7 8.9 %collective-permute-start.2 = (bf16[144,128]{1,0:T(8,128)(2,1)S(1)}, bf16[144,128]{1,0:T(8,128)(2,1)S(1)}, u32[]{:S(2)}, u32[]{:S(2)}) collective-permute-start(bf16[144,128]{1,0:T(8,128)(2,1)S(1)} %get-tuple-element.64.refs_4_.refs_0_), channel_id=1, source_target_pairs={{0,6},{1,7},{2,4},{3,5},{4,2},{5,3},{6,0},{7,1},{8,14},{9,15},{10,... | collective-permute-start | bytes 110600 | tf_op jit(solution)/shard_map/ppermute | solution.py:462
  7.0 4.1 %collective-permute-start.1 = (bf16[144,128]{1,0:T(8,128)(2,1)S(1)}, bf16[144,128]{1,0:T(8,128)(2,1)S(1)}, u32[]{:S(2)}, u32[]{:S(2)}) collective-permute-start(bf16[144,128]{1,0:T(8,128)(2,1)S(1)} %get-tuple-element.64.refs_4_.refs_0_), channel_id=1, source_target_pairs={{0,4},{1,5},{2,6},{3,7},{4,0},{5,1},{6,2},{7,3},{8,12},{9,13},{10,... | collective-permute-start | bytes 110600 | tf_op jit(solution)/shard_map/ppermute | solution.py:462
  7.0 4.1 %collective-permute-start = (bf16[144,128]{1,0:T(8,128)(2,1)S(1)}, bf16[144,128]{1,0:T(8,128)(2,1)S(1)}, u32[]{:S(2)}, u32[]{:S(2)}) collective-permute-start(bf16[144,128]{1,0:T(8,128)(2,1)S(1)} %get-tuple-element.64.refs_4_.refs_0_), channel_id=1, source_target_pairs={{0,2},{1,3},{2,0},{3,1},{4,6},{5,7},{6,4},{7,5},{8,10},{9,11},{10,... | collective-permute-start | bytes 110600 | tf_op jit(solution)/shard_map/ppermute | solution.py:462
  10.6 2.3 %copy-start = (bf16[128,128]{1,0:T(8,128)(2,1)S(1)}, bf16[128,128]{1,0:T(8,128)(2,1)}, u32[]{:S(2)}) copy-start(bf16[128,128]{1,0:T(8,128)(2,1)} %refs_1_.3) | copy-start | bytes 98308
  11.1 2.9 %collective-permute-start.3 = (bf16[576,128]{1,0:T(8,128)(2,1)S(1)}, bf16[576,128]{1,0:T(8,128)(2,1)S(1)}, u32[]{:S(2)}, u32[]{:S(2)}) collective-permute-start(bf16[576,128]{1,0:T(8,128)(2,1)S(1)} %gather.1.refs_0_.refs_1_.refs_9_), channel_id=1, source_target_pairs={{0,1},{1,0},{2,3},{3,2},{4,5},{5,4},{6,7},{7,6},{8,9},{9,8},{10,11... | collective-permute-start | bytes 442376 | tf_op jit(solution)/shard_map/ppermute | solution.py:462
  15.2 10.9 %collective-permute-start.5 = (bf16[576,128]{1,0:T(8,128)(2,1)S(1)}, bf16[576,128]{1,0:T(8,128)(2,1)S(1)}, u32[]{:S(2)}, u32[]{:S(2)}) collective-permute-start(bf16[576,128]{1,0:T(8,128)(2,1)S(1)} %get-tuple-element.71.refs_5_), channel_id=1, source_target_pairs={{0,24},{1,25},{2,26},{3,27},{4,28},{5,29},{6,30},{7,31},{8,0},{9,1... | collective-permute-start | bytes 442376 | tf_op jit(solution)/shard_map/ppermute | solution.py:466
  18.0 8.1 %collective-permute-start.4 = (bf16[576,128]{1,0:T(8,128)(2,1)S(1)}, bf16[576,128]{1,0:T(8,128)(2,1)S(1)}, u32[]{:S(2)}, u32[]{:S(2)}) collective-permute-start(bf16[576,128]{1,0:T(8,128)(2,1)S(1)} %get-tuple-element.71.refs_5_), channel_id=1, source_target_pairs={{0,8},{1,9},{2,10},{3,11},{4,12},{5,13},{6,14},{7,15},{8,16},{9,17... | collective-permute-start | bytes 442376 | tf_op jit(solution)/shard_map/ppermute | solution.py:466
  18.0 8.0 %collective-permute-start.6 = (bf16[512,128]{1,0:T(8,128)(2,1)S(1)}, bf16[512,128]{1,0:T(8,128)(2,1)S(1)}, u32[]{:S(2)}, u32[]{:S(2)}) collective-permute-start(bf16[512,128]{1,0:T(8,128)(2,1)S(1)} %get-tuple-element.70.refs_0_), channel_id=1, source_target_pairs={{0,16},{1,17},{2,18},{3,19},{4,20},{5,21},{6,22},{7,23},{8,24},{9,... | collective-permute-start | bytes 393224 | tf_op jit(solution)/shard_map/ppermute | solution.py:466
  26.5 3.3 %collective-permute-start.7 = (bf16[512,128]{1,0:T(8,128)(2,1)S(1)}, bf16[512,128]{1,0:T(8,128)(2,1)S(1)}, u32[]{:S(2)}, u32[]{:S(2)}) collective-permute-start(bf16[512,128]{1,0:T(8,128)(2,1)S(1)} %get-tuple-element.76.refs_5_), channel_id=1, source_target_pairs={{0,1},{1,0},{2,3},{3,2},{4,5},{5,4},{6,7},{7,6},{8,9},{9,8},{10,11... | collective-permute-start | bytes 393224 | tf_op jit(solution)/shard_map/ppermute | solution.py:462
  29.9 6.5 %collective-permute-start.8 = (bf16[128,128]{1,0:T(8,128)(2,1)S(1)}, bf16[128,128]{1,0:T(8,128)(2,1)S(1)}, u32[]{:S(2)}, u32[]{:S(2)}) collective-permute-start(bf16[128,128]{1,0:T(8,128)(2,1)S(1)} %get-tuple-element.78), channel_id=1, source_target_pairs={{0,2},{1,3},{2,0},{3,1},{4,6},{5,7},{6,4},{7,5},{8,10},{9,11},{10,... | collective-permute-start | bytes 98312 | tf_op jit(solution)/shard_map/ppermute | solution.py:462
  30.1 6.2 %collective-permute-start.9 = (bf16[128,128]{1,0:T(8,128)(2,1)S(1)}, bf16[128,128]{1,0:T(8,128)(2,1)S(1)}, u32[]{:S(2)}, u32[]{:S(2)}) collective-permute-start(bf16[128,128]{1,0:T(8,128)(2,1)S(1)} %get-tuple-element.79), channel_id=1, source_target_pairs={{0,4},{1,5},{2,6},{3,7},{4,0},{5,1},{6,2},{7,3},{8,12},{9,13},{10,... | collective-permute-start | bytes 98312 | tf_op jit(solution)/shard_map/ppermute | solution.py:462
  32.8 4.6 %collective-permute-start.10 = (bf16[128,128]{1,0:T(8,128)(2,1)S(1)}, bf16[128,128]{1,0:T(8,128)(2,1)S(1)}, u32[]{:S(2)}, u32[]{:S(2)}) collective-permute-start(bf16[128,128]{1,0:T(8,128)(2,1)S(1)} %get-tuple-element.80), channel_id=1, source_target_pairs={{0,6},{1,7},{2,4},{3,5},{4,2},{5,3},{6,0},{7,1},{8,14},{9,15},{10,... | collective-permute-start | bytes 98312 | tf_op jit(solution)/shard_map/ppermute | solution.py:462
  38.2 4.2 %collective-permute-start.12 = (bf16[272,128]{1,0:T(8,128)(2,1)S(1)}, bf16[272,128]{1,0:T(8,128)(2,1)S(1)}, u32[]{:S(2)}, u32[]{:S(2)}) collective-permute-start(bf16[272,128]{1,0:T(8,128)(2,1)S(1)} %get-tuple-element.92), channel_id=1, source_target_pairs={{0,4},{1,5},{2,6},{3,7},{4,0},{5,1},{6,2},{7,3},{8,12},{9,13},{10,... | collective-permute-start | bytes 208904 | tf_op jit(solution)/shard_map/ppermute | solution.py:462
  38.3 5.7 %collective-permute-start.13 = (bf16[272,128]{1,0:T(8,128)(2,1)S(1)}, bf16[272,128]{1,0:T(8,128)(2,1)S(1)}, u32[]{:S(2)}, u32[]{:S(2)}) collective-permute-start(bf16[272,128]{1,0:T(8,128)(2,1)S(1)} %get-tuple-element.93), channel_id=1, source_target_pairs={{0,6},{1,7},{2,4},{3,5},{4,2},{5,3},{6,0},{7,1},{8,14},{9,15},{10,... | collective-permute-start | bytes 208904 | tf_op jit(solution)/shard_map/ppermute | solution.py:462
  40.0 4.0 %collective-permute-start.11 = (bf16[272,128]{1,0:T(8,128)(2,1)S(1)}, bf16[272,128]{1,0:T(8,128)(2,1)S(1)}, u32[]{:S(2)}, u32[]{:S(2)}) collective-permute-start(bf16[272,128]{1,0:T(8,128)(2,1)S(1)} %get-tuple-element.87.refs_3_), channel_id=1, source_target_pairs={{0,2},{1,3},{2,0},{3,1},{4,6},{5,7},{6,4},{7,5},{8,10},{9,11},{10,... | collective-permute-start | bytes 208904 | tf_op jit(solution)/shard_map/ppermute | solution.py:462
  44.0 4.5 %collective-permute-start.14 = (bf16[816,128]{1,0:T(8,128)(2,1)S(1)}, bf16[816,128]{1,0:T(8,128)(2,1)S(1)}, u32[]{:S(2)}, u32[]{:S(2)}) collective-permute-start(bf16[816,128]{1,0:T(8,128)(2,1)S(1)} %get-tuple-element.95.refs_1_.refs_2_), channel_id=1, source_target_pairs={{0,1},{1,0},{2,3},{3,2},{4,5},{5,4},{6,7},{7,6},{8,9},{9,8},{10,11... | collective-permute-start | bytes 626696 | tf_op jit(solution)/shard_map/ppermute | solution.py:462
  48.8 9.6 %collective-permute-start.16 = (bf16[624,128]{1,0:T(8,128)(2,1)S(1)}, bf16[624,128]{1,0:T(8,128)(2,1)S(1)}, u32[]{:S(2)}, u32[]{:S(2)}) collective-permute-start(bf16[624,128]{1,0:T(8,128)(2,1)S(1)} %get-tuple-element.97.refs_0_), channel_id=1, source_target_pairs={{0,24},{1,25},{2,26},{3,27},{4,28},{5,29},{6,30},{7,31},{8,0},{9,1... | collective-permute-start | bytes 479240 | tf_op jit(solution)/shard_map/ppermute | solution.py:466
  48.9 9.6 %collective-permute-start.15 = (bf16[624,128]{1,0:T(8,128)(2,1)S(1)}, bf16[624,128]{1,0:T(8,128)(2,1)S(1)}, u32[]{:S(2)}, u32[]{:S(2)}) collective-permute-start(bf16[624,128]{1,0:T(8,128)(2,1)S(1)} %get-tuple-element.97.refs_0_), channel_id=1, source_target_pairs={{0,8},{1,9},{2,10},{3,11},{4,12},{5,13},{6,14},{7,15},{8,16},{9,17... | collective-permute-start | bytes 479240 | tf_op jit(solution)/shard_map/ppermute | solution.py:466
  50.3 8.1 %collective-permute-start.17 = (bf16[560,128]{1,0:T(8,128)(2,1)S(1)}, bf16[560,128]{1,0:T(8,128)(2,1)S(1)}, u32[]{:S(2)}, u32[]{:S(2)}) collective-permute-start(bf16[560,128]{1,0:T(8,128)(2,1)S(1)} %get-tuple-element.98), channel_id=1, source_target_pairs={{0,16},{1,17},{2,18},{3,19},{4,20},{5,21},{6,22},{7,23},{8,24},{9,... | collective-permute-start | bytes 430088 | tf_op jit(solution)/shard_map/ppermute | solution.py:466
  59.2 2.4 %collective-permute-start.18 = (bf16[576,128]{1,0:T(8,128)(2,1)S(1)}, bf16[576,128]{1,0:T(8,128)(2,1)S(1)}, u32[]{:S(2)}, u32[]{:S(2)}) collective-permute-start(bf16[576,128]{1,0:T(8,128)(2,1)S(1)} %get-tuple-element.104), channel_id=1, source_target_pairs={{0,1},{1,0},{2,3},{3,2},{4,5},{5,4},{6,7},{7,6},{8,9},{9,8},{10,11... | collective-permute-start | bytes 442376 | tf_op jit(solution)/shard_map/ppermute | solution.py:462
  61.7 3.6 %collective-permute-start.19 = (bf16[224,128]{1,0:T(8,128)(2,1)S(1)}, bf16[224,128]{1,0:T(8,128)(2,1)S(1)}, u32[]{:S(2)}, u32[]{:S(2)}) collective-permute-start(bf16[224,128]{1,0:T(8,128)(2,1)S(1)} %get-tuple-element.107), channel_id=1, source_target_pairs={{0,2},{1,3},{2,0},{3,1},{4,6},{5,7},{6,4},{7,5},{8,10},{9,11},{10,... | collective-permute-start | bytes 172040 | tf_op jit(solution)/shard_map/ppermute | solution.py:462
  62.3 3.9 %collective-permute-start.20 = (bf16[224,128]{1,0:T(8,128)(2,1)S(1)}, bf16[224,128]{1,0:T(8,128)(2,1)S(1)}, u32[]{:S(2)}, u32[]{:S(2)}) collective-permute-start(bf16[224,128]{1,0:T(8,128)(2,1)S(1)} %get-tuple-element.108), channel_id=1, source_target_pairs={{0,4},{1,5},{2,6},{3,7},{4,0},{5,1},{6,2},{7,3},{8,12},{9,13},{10,... | collective-permute-start | bytes 172040 | tf_op jit(solution)/shard_map/ppermute | solution.py:462
  63.8 4.8 %collective-permute-start.21 = (bf16[224,128]{1,0:T(8,128)(2,1)S(1)}, bf16[224,128]{1,0:T(8,128)(2,1)S(1)}, u32[]{:S(2)}, u32[]{:S(2)}) collective-permute-start(bf16[224,128]{1,0:T(8,128)(2,1)S(1)} %get-tuple-element.109), channel_id=1, source_target_pairs={{0,6},{1,7},{2,4},{3,5},{4,2},{5,3},{6,0},{7,1},{8,14},{9,15},{10,... | collective-permute-start | bytes 172040 | tf_op jit(solution)/shard_map/ppermute | solution.py:462
  68.7 4.7 %collective-permute-start.24 = (bf16[64,128]{1,0:T(8,128)(2,1)S(1)}, bf16[64,128]{1,0:T(8,128)(2,1)S(1)}, u32[]{:S(2)}, u32[]{:S(2)}) collective-permute-start(bf16[64,128]{1,0:T(8,128)(2,1)S(1)} %get-tuple-element.115.refs_0_), channel_id=1, source_target_pairs={{0,16},{1,17},{2,18},{3,19},{4,20},{5,21},{6,22},{7,23},{8,24},{9,... | collective-permute-start | bytes 49160 | tf_op jit(solution)/shard_map/ppermute | solution.py:466
  70.5 2.9 %collective-permute-start.23 = (bf16[64,128]{1,0:T(8,128)(2,1)S(1)}, bf16[64,128]{1,0:T(8,128)(2,1)S(1)}, u32[]{:S(2)}, u32[]{:S(2)}) collective-permute-start(bf16[64,128]{1,0:T(8,128)(2,1)S(1)} %get-tuple-element.115.refs_0_), channel_id=1, source_target_pairs={{0,24},{1,25},{2,26},{3,27},{4,28},{5,29},{6,30},{7,31},{8,0},{9,1... | collective-permute-start | bytes 49160 | tf_op jit(solution)/shard_map/ppermute | solution.py:466
  70.7 3.8 %collective-permute-start.22 = (bf16[64,128]{1,0:T(8,128)(2,1)S(1)}, bf16[64,128]{1,0:T(8,128)(2,1)S(1)}, u32[]{:S(2)}, u32[]{:S(2)}) collective-permute-start(bf16[64,128]{1,0:T(8,128)(2,1)S(1)} %get-tuple-element.115.refs_0_), channel_id=1, source_target_pairs={{0,8},{1,9},{2,10},{3,11},{4,12},{5,13},{6,14},{7,15},{8,16},{9,17... | collective-permute-start | bytes 49160 | tf_op jit(solution)/shard_map/ppermute | solution.py:466
  74.5 4.5 %collective-permute-start.27 = (bf16[208,128]{1,0:T(8,128)(2,1)S(1)}, bf16[208,128]{1,0:T(8,128)(2,1)S(1)}, u32[]{:S(2)}, u32[]{:S(2)}) collective-permute-start(bf16[208,128]{1,0:T(8,128)(2,1)S(1)} %charge_sum.1.refs_0_), channel_id=1, source_target_pairs={{0,192},{32,224},{64,128},{96,160},{128,64},{160,96},{192,0},{224,... | collective-permute-start | bytes 159752 | tf_op jit(solution)/shard_map/ppermute | solution.py:462
  77.3 4.5 %collective-permute-start.26 = (bf16[208,128]{1,0:T(8,128)(2,1)S(1)}, bf16[208,128]{1,0:T(8,128)(2,1)S(1)}, u32[]{:S(2)}, u32[]{:S(2)}) collective-permute-start(bf16[208,128]{1,0:T(8,128)(2,1)S(1)} %charge_sum.1.refs_0_), channel_id=1, source_target_pairs={{0,128},{32,160},{64,192},{96,224},{128,0},{160,32},{192,64},{224,... | collective-permute-start | bytes 159752 | tf_op jit(solution)/shard_map/ppermute | solution.py:462
  77.8 4.0 %collective-permute-start.25 = (bf16[208,128]{1,0:T(8,128)(2,1)S(1)}, bf16[208,128]{1,0:T(8,128)(2,1)S(1)}, u32[]{:S(2)}, u32[]{:S(2)}) collective-permute-start(bf16[208,128]{1,0:T(8,128)(2,1)S(1)} %charge_sum.1.refs_0_), channel_id=1, source_target_pairs={{0,64},{32,96},{64,0},{96,32},{128,192},{160,224},{192,128},{224,1... | collective-permute-start | bytes 159752 | tf_op jit(solution)/shard_map/ppermute | solution.py:462
  81.8 11.8 %collective-permute-start.30 = (bf16[208,128]{1,0:T(8,128)(2,1)S(1)}, bf16[208,128]{1,0:T(8,128)(2,1)S(1)}, u32[]{:S(2)}, u32[]{:S(2)}) collective-permute-start(bf16[208,128]{1,0:T(8,128)(2,1)S(1)} %cell_sum.1.refs_0_), channel_id=1, source_target_pairs={{0,39},{1,38},{2,37},{3,36},{4,35},{5,34},{6,33},{7,32},{8,47},{9,... | collective-permute-start | bytes 159752 | tf_op jit(solution)/shard_map/ppermute | solution.py:462
  90.0 4.9 %collective-permute-start.29 = (bf16[208,128]{1,0:T(8,128)(2,1)S(1)}, bf16[208,128]{1,0:T(8,128)(2,1)S(1)}, u32[]{:S(2)}, u32[]{:S(2)}) collective-permute-start(bf16[208,128]{1,0:T(8,128)(2,1)S(1)} %cell_sum.1.refs_0_), channel_id=1, source_target_pairs={{0,38},{1,39},{2,36},{3,37},{4,34},{5,35},{6,32},{7,33},{8,46},{9,... | collective-permute-start | bytes 159752 | tf_op jit(solution)/shard_map/ppermute | solution.py:462
  90.0 4.9 %collective-permute-start.28 = (bf16[208,128]{1,0:T(8,128)(2,1)S(1)}, bf16[208,128]{1,0:T(8,128)(2,1)S(1)}, u32[]{:S(2)}, u32[]{:S(2)}) collective-permute-start(bf16[208,128]{1,0:T(8,128)(2,1)S(1)} %cell_sum.1.refs_0_), channel_id=1, source_target_pairs={{0,1},{1,0},{2,3},{3,2},{4,5},{5,4},{6,7},{7,6},{8,9},{9,8},{10,11... | collective-permute-start | bytes 159752 | tf_op jit(solution)/shard_map/ppermute | solution.py:462
  (10 other events, 17.1 us)

commit v4 on v3

--- a/solution.py
+++ b/solution.py
@@ -27,7 +27,7 @@
 LOW = C // 2
 HALF = ROW * ATOMS // 2
 CHUNK = 1024
-EDGE_STEPS = (3, 6, 1, 2)
+EDGE_STEPS = (5, 7)
 
 cutoff_radius = 6.0
 basis_width = 0.75
@@ -254,28 +254,28 @@
         send[...] = values[ATOMS * (part + 1) : ATOMS * (part + 2)].astype(bf16)
 
 
-def edge_kernel(first, *refs):
-    senders, receivers, live, lengths = refs[:4]
+def edge_kernel(first, count, *refs):
     total, left, right = refs[-3:]
-    step = pl.program_id(0)
-    reach = lengths[...]
-    turn = reach * (0.5 / cutoff_radius)
-    envelope = 0.5 * (horner(COS_TURN, turn * turn) + 1.0) * live[...].astype(f32)
-    centers = 0.5 + basis_width * iota((NB, CHUNK), 0).astype(f32)
-    offset = (reach - centers) * (1.0 / basis_width)
-    weights = (jnp.exp(-offset * offset) * envelope).astype(bf16)
-    atom = iota((ATOMS, CHUNK), 0)
-    onehot = (atom == receivers[...]).astype(f32).astype(bf16)
-    for b in range(NB):
-        left[ATOMS * b : ATOMS * (b + 1), :] = onehot * weights[b : b + 1, :]
-    source = iota((EXT, CHUNK), 0)
-    right[...] = (source == senders[...]).astype(f32).astype(bf16)
-
-    @pl.when(step == 0)
-    def _():
-        total[...] = jnp.zeros_like(total) if first else refs[4][...]
-
-    total[...] += dot_lanes(left[...], right[...])
+    for step in range(first, first + count):
+        senders, receivers, live, reach = (ref[:, CHUNK * step : CHUNK * (step + 1)] for ref in refs[:4])
+        turn = reach * (0.5 / cutoff_radius)
+        envelope = 0.5 * (horner(COS_TURN, turn * turn) + 1.0) * live.astype(f32)
+        centers = 0.5 + basis_width * iota((NB, CHUNK), 0).astype(f32)
+        offset = (reach - centers) * (1.0 / basis_width)
+        weights = (jnp.exp(-offset * offset) * envelope).astype(bf16)
+        atom = iota((ATOMS, CHUNK), 0)
+        onehot = (atom == receivers).astype(f32).astype(bf16)
+        for b in range(NB):
+            left[ATOMS * b : ATOMS * (b + 1), :] = onehot * weights[b : b + 1, :]
+        source = iota((EXT, CHUNK), 0)
+        right[...] = (source == senders).astype(f32).astype(bf16)
+        products = dot_lanes(left[...], right[...])
+        if step > first:
+            total[...] += products
+        elif first:
+            total[...] = refs[4][...] + products
+        else:
+            total[...] = products
 
 
 def aggregate_kernel(feats, below, above, up, down, w_message, operator, w_radial, aggregate, radial_rows, extended):
@@ -446,15 +446,18 @@
     token[...] = total[0:8]
 
 
-def weights_kernel(own, other, own_cell, other_cell, charge, message, radial, out):
-    for first, second, at in ((own, own_cell, core()), (other, other_cell, 1 - core())):
-        total = (first[...].astype(f32) + second[...].astype(f32)) * grad_scale
-        charge[rows_at(at, LOW), :] = total[0:LOW]
+def total_kernel(own, other_cell, total):
+    total[...] = (own[...].astype(f32) + other_cell[...].astype(f32)) * grad_scale
+
+
+def weights_kernel(own, other, charge, message, radial, out):
+    for total, at in ((own, core()), (other, 1 - core())):
+        charge[rows_at(at, LOW), :] = total[0:LOW, :]
         for z in range(4):
             start = LOW + PART * z
-            message[rows_at(2 * z + at, 16), :] = total[start : start + 16]
-            out[rows_at(2 * z + at, 16), :] = total[start + 16 : start + PART]
-        radial[...] = total[LOW + C : LOW + C + NB]
+            message[rows_at(2 * z + at, 16), :] = total[start : start + 16, :]
+            out[rows_at(2 * z + at, 16), :] = total[start + 16 : start + PART, :]
+    radial[...] = own[LOW + C : LOW + C + NB, :]
 
 
 def swap(values, axis, mask):
@@ -489,18 +492,12 @@
     cot = cotangent[0]
 
     def edges(first, count, total, after):
-        spec = pl.BlockSpec((1, CHUNK), lambda e: (0, first + e))
-        whole = pl.BlockSpec((NB * ATOMS, EXT), lambda e: (0, 0))
-        held = [] if total is None else [total]
         (out,) = call(
-            lambda *refs: edge_kernel(total is None, *refs),
+            lambda *refs: edge_kernel(first, count, *refs),
             [((NB * ATOMS, EXT), f32)],
-            *edge_arrays, *held,
+            *edge_arrays, *total,
             scratch=[pltpu.VMEM((NB * ATOMS, CHUNK), bf16), pltpu.VMEM((EXT, CHUNK), bf16)],
             flops=count * 2 * NB * ATOMS * CHUNK * 256,
-            grid=(count,),
-            in_specs=[spec] * 4 + [whole] * len(held),
-            out_specs=[whole],
             after=after,
             name="edges",
         )
@@ -523,7 +520,7 @@
         out_specs=[pl.BlockSpec(memory_space=pltpu.VMEM)] * 5,
         name="pack",
     )
-    operator = edges(0, EDGE_STEPS[0], None, [packed])
+    operator = edges(0, EDGE_STEPS[0], [], [packed])
     (near_rows,) = call(
         gather_kernel,
         [((ROW // 2 * PACK, C), bf16)],
@@ -550,7 +547,7 @@
         name="structure_far",
     )
     up, down, over = from_y(message, 1), from_y(message, -1), from_y(sums, 2)
-    operator = edges(EDGE_STEPS[0], EDGE_STEPS[1], operator, [message])
+    operator = edges(EDGE_STEPS[0], EDGE_STEPS[1], [operator], [message])
     send, keep = call(
         potential_kernel,
         [((HALF, C), bf16), ((HALF, C), f32)],
@@ -559,12 +556,10 @@
         name="potential",
     )
     received = swap(send, "dom", 1)
-    operator = edges(EDGE_STEPS[0] + EDGE_STEPS[1], EDGE_STEPS[2], operator, [send])
     held, *sends = call(
-        spread_kernel, [((ATOMS, C), f32)] + [((ATOMS, C), bf16)] * 3, keep, received, after=[operator], name="spread"
+        spread_kernel, [((ATOMS, C), f32)] + [((ATOMS, C), bf16)] * 3, keep, received, name="spread"
     )
     parts = [swap(values, "dom", 2 * (part + 1)) for part, values in enumerate(sends)]
-    operator = edges(sum(EDGE_STEPS[:3]), EDGE_STEPS[3], operator, [held])
     aggregate, radial_rows, extended = call(
         aggregate_kernel,
         [((ATOMS, C), f32), ((NB * ATOMS, C), f32), ((EXT, C), bf16)],
@@ -637,11 +632,12 @@
     )
     parts = [swap(total, "cell", mask) for mask in (2, 4, 6)]
     (total,) = call(cell_sum_kernel, [((LOW + C + 16, C), bf16)], total, *parts, name="cell_sum")
-    parts = [swap(total, "dom", 1)] + [swap(total, ("cell", "dom"), DOMS + mask) for mask in (6, 7)]
+    received = swap(total, ("cell", "dom"), DOMS + 6)
+    (total,) = call(total_kernel, [((LOW + C + 16, C), f32)], total, received, name="total")
     charge, message, radial, out = call(
         weights_kernel,
         [((C, C), f32), ((C, C), f32), ((NB, C), f32), ((C, C), f32)],
-        total, *parts,
+        total, swap(total, "dom", 1),
         name="weights",
     )
     return updated[None], feat_grad[None], charge, message, radial, out

time: 96.1 us -> 93.8 us (0.976)
  Pallas kernels: 21.4 us -> 16.3 us
  waiting for transfers between devices: 25.4 us -> 27.9 us
    pallas_call x23 -> x22, Pallas kernels: 21.4 us -> 16.3 us  [call(): pl.pallas_call(run, out_shape=[jax.ShapeDtypeStruct(shape, dtype) for sha...]
    ppermute x9, waiting for transfers between devices: 8.07 us -> 9.54 us  [from_y(): lax.ppermute(values, 'dom', [(i, (i + ROW * by) % DOMS) for i in range(DO...]
    ppermute x22 -> x21, starting transfers between devices: 36.8 us -> 38.2 us  [swap(): return lax.ppermute(values, axis, [(i, i ^ mask) for i in range(count)])]
    ppermute x22 -> x21, waiting for transfers between devices: 17.4 us -> 18.4 us  [swap(): return lax.ppermute(values, axis, [(i, i ^ mask) for i in range(count)])]
  transfers between devices with their start and end apart: 31 -> 30, of which waited for: 15 -> 16; matrix products, arithmetic and copies ran while one was open for 0% -> 0% of each run, Pallas kernels for 17% -> 12%
where the time goes in v4:
time: 93.8 us; the launch traced here: 93.5 us
  starting transfers between devices  47.7 us (51%)
  waiting for transfers between devices  27.9 us (30%)
  Pallas kernels  16.3 us (17%)
    ppermute x21, starting transfers between devices, swap(): return lax.ppermute(values, axis, [(i, i ^ mask) for i in range(count)])  38.2 us
    ppermute x21, waiting for transfers between devices, swap(): return lax.ppermute(values, axis, [(i, i ^ mask) for i in range(count)])  18.4 us
    pallas_call x22, Pallas kernels, call(): pl.pallas_call(run, out_shape=[jax.ShapeDtypeStruct(shape, dtype) for sha...  16.3 us
    ppermute x9, waiting for transfers between devices, from_y(): lax.ppermute(values, 'dom', [(i, (i + ROW * by) % DOMS) for i in range(DO...  9.54 us
    ppermute x9, starting transfers between devices, from_y(): lax.ppermute(values, 'dom', [(i, (i + ROW * by) % DOMS) for i in range(DO...  9.54 us
  transfers between devices with their start and end apart: 30, of which 16 were waited for; matrix products, arithmetic and copies ran while one was open for 0% of the time, Pallas kernels for 12%

profile of v4, /device:TPU:1, one launch (start us, length us, event | category | flops | bytes accessed | tf_op | source)
XLA Modules:
  0.0 93.5 jit_solution(18321749804942124600)
XLA Ops:
  0.6 1.1 %pack.1 = (bf16[144,128]{1,0:T(8,128)(2,1)S(1)}, s32[1,12288]{1,0:T(1,128)S(1)}, s32[1,12288]{1,0:T(1,128)S(1)}, s32[1,12288]{1,0:T(1,128)S(1)}, f32[1,12288]{1,0:T(1,128)S(1)}) custom-call(bf16[128,128]{1,0:T(8,128)(2,1)} %bitcast.6, f32[3,1,128]{2,1,0:T(1,128)} %bitcast.11, s32[1,128]{1,0:T(1,128)} %refs_2_.2, s32[1,32]{1,0:T(1,128)} %refs_3_.7, ...), custom_call_target="tpu_custom_call" | custom-call | bytes 262144 | tf_op jit(solution)/shard_map/pack/pallas_call | solution.py:95
  1.7 5.3 %collective-permute-start.2 = (bf16[144,128]{1,0:T(8,128)(2,1)S(1)}, bf16[144,128]{1,0:T(8,128)(2,1)S(1)}, u32[]{:S(2)}, u32[]{:S(2)}) collective-permute-start(bf16[144,128]{1,0:T(8,128)(2,1)S(1)} %get-tuple-element.64.refs_4_.refs_0_), channel_id=1, source_target_pairs={{0,6},{1,7},{2,4},{3,5},{4,2},{5,3},{6,0},{7,1},{8,14},{9,15},{10,... | collective-permute-start | bytes 110600 | tf_op jit(solution)/shard_map/ppermute | solution.py:465
  7.3 3.1 %edges.2.refs_4_ = f32[1024,192]{1,0:T(8,128)S(1)} custom-call(s32[1,12288]{1,0:T(1,128)S(1)} %get-tuple-element.65.refs_0_, s32[1,12288]{1,0:T(1,128)S(1)} %get-tuple-element.66.refs_1_, s32[1,12288]{1,0:T(1,128)S(1)} %get-tuple-element.67.refs_2_, f32[1,12288]{1,0:T(1,128)S(1)} %get-tuple-element.68.refs_3_, ...), custom_call_target="tpu_custom_call" | custom-call | flops 2684354560 | bytes 262144 | tf_op jit(solution)/shard_map/edges/pallas_call | solution.py:95
  11.1 1.8 %collective-permute-start.3 = (bf16[576,128]{1,0:T(8,128)(2,1)S(1)}, bf16[576,128]{1,0:T(8,128)(2,1)S(1)}, u32[]{:S(2)}, u32[]{:S(2)}) collective-permute-start(bf16[576,128]{1,0:T(8,128)(2,1)S(1)} %gather.1.refs_0_.refs_1_.refs_9_), channel_id=1, source_target_pairs={{0,1},{1,0},{2,3},{3,2},{4,5},{5,4},{6,7},{7,6},{8,9},{9,8},{10,11... | collective-permute-start | bytes 442376 | tf_op jit(solution)/shard_map/ppermute | solution.py:465
  12.9 1.2 %structure_near.1 = (bf16[512,512]{1,0:T(8,128)(2,1)S(1)}, f32[512,128]{1,0:T(8,128)S(1)}, f32[256,128]{1,0:T(8,128)S(1)}, f32[512,128]{1,0:T(8,128)S(1)}) custom-call(bf16[576,128]{1,0:T(8,128)(2,1)S(1)} %gather.1.refs_0_.refs_1_.refs_9_, s32[3,2048]{1,0:T(4,128)S(1)} %copy-done.4, f32[1,128]{1,0:T(1,128)S(1)} %bitcast.10, f32[8,128]{1,0:T(8,128)S(1)} %copy-done.7, ...), custom_call_target="tpu_custom_call" | custom-call | bytes 262144 | tf_op jit(solution)/shard_map/structure_near/pallas_call | solution.py:95
  14.1 1.1 %structure_far.1 = (bf16[512,512]{1,0:T(8,128)(2,1)S(1)}, bf16[512,128]{1,0:T(8,128)(2,1)S(1)}, bf16[576,128]{1,0:T(8,128)(2,1)S(1)}, f32[512,128]{1,0:T(8,128)S...) custom-call(bf16[576,128]{1,0:T(8,128)(2,1)S(1)} %collective-permute-done.3.refs_0_.refs_10_, ...), custom_call_target="tpu_custom_call" | custom-call | bytes 262144 | tf_op jit(solution)/shard_map/structure_far/pallas_call | solution.py:95
  15.2 2.8 %collective-permute-start.5 = (bf16[576,128]{1,0:T(8,128)(2,1)S(1)}, bf16[576,128]{1,0:T(8,128)(2,1)S(1)}, u32[]{:S(2)}, u32[]{:S(2)}) collective-permute-start(bf16[576,128]{1,0:T(8,128)(2,1)S(1)} %get-tuple-element.71.refs_5_), channel_id=1, source_target_pairs={{0,24},{1,25},{2,26},{3,27},{4,28},{5,29},{6,30},{7,31},{8,0},{9,1... | collective-permute-start | bytes 442376 | tf_op jit(solution)/shard_map/ppermute | solution.py:469
  18.0 1.6 %collective-permute-start.6 = (bf16[512,128]{1,0:T(8,128)(2,1)S(1)}, bf16[512,128]{1,0:T(8,128)(2,1)S(1)}, u32[]{:S(2)}, u32[]{:S(2)}) collective-permute-start(bf16[512,128]{1,0:T(8,128)(2,1)S(1)} %get-tuple-element.70.refs_0_), channel_id=1, source_target_pairs={{0,16},{1,17},{2,18},{3,19},{4,20},{5,21},{6,22},{7,23},{8,24},{9,... | collective-permute-start | bytes 393224 | tf_op jit(solution)/shard_map/ppermute | solution.py:469
  19.6 4.3 %edges.3.refs_7_.refs_6_.refs_9_ = f32[1024,192]{1,0:T(8,128)S(1)} custom-call(s32[1,12288]{1,0:T(1,128)S(1)} %get-tuple-element.65.refs_0_, s32[1,12288]{1,0:T(1,128)S(1)} %get-tuple-element.66.refs_1_, s32[1,12288]{1,0:T(1,128)S(1)} %get-tuple-element.67.refs_2_, f32[1,12288]{1,0:T(1,128)S(1)} %get-tuple-element.68.refs_3_, f32[1024,192]{1,0:T(8,128)S(1)} %edges.2.refs_4_, ...), custom_call_target="tpu_custom_call" | custom-call | flops 3758096384 | bytes 262144 | tf_op jit(solution)/shard_map/edges/pallas_call | solution.py:95
  23.9 1.6 %collective-permute-done.6.refs_3_ = bf16[512,128]{1,0:T(8,128)(2,1)S(1)} collective-permute-done((bf16[512,128]{1,0:T(8,128)(2,1)S(1)}, bf16[512,128]{1,0:T(8,128)(2,1)S(1)}, u32[]{:S(2)}, u32[]{:S(2)}) %collective-permute-start.6) | collective-permute-done | bytes 131104 | tf_op jit(solution)/shard_map/ppermute | solution.py:469
  26.0 2.8 %collective-permute-start.7 = (bf16[512,128]{1,0:T(8,128)(2,1)S(1)}, bf16[512,128]{1,0:T(8,128)(2,1)S(1)}, u32[]{:S(2)}, u32[]{:S(2)}) collective-permute-start(bf16[512,128]{1,0:T(8,128)(2,1)S(1)} %get-tuple-element.76), channel_id=1, source_target_pairs={{0,1},{1,0},{2,3},{3,2},{4,5},{5,4},{6,7},{7,6},{8,9},{9,8},{10,11... | collective-permute-start | bytes 393224 | tf_op jit(solution)/shard_map/ppermute | solution.py:465
  28.8 1.0 %collective-permute-done.7.refs_1_ = bf16[512,128]{1,0:T(8,128)(2,1)S(1)} collective-permute-done((bf16[512,128]{1,0:T(8,128)(2,1)S(1)}, bf16[512,128]{1,0:T(8,128)(2,1)S(1)}, u32[]{:S(2)}, u32[]{:S(2)}) %collective-permute-start.7) | collective-permute-done | bytes 131104 | tf_op jit(solution)/shard_map/ppermute | solution.py:465
  30.0 2.6 %collective-permute-start.9 = (bf16[128,128]{1,0:T(8,128)(2,1)S(1)}, bf16[128,128]{1,0:T(8,128)(2,1)S(1)}, u32[]{:S(2)}, u32[]{:S(2)}) collective-permute-start(bf16[128,128]{1,0:T(8,128)(2,1)S(1)} %get-tuple-element.79), channel_id=1, source_target_pairs={{0,4},{1,5},{2,6},{3,7},{4,0},{5,1},{6,2},{7,3},{8,12},{9,13},{10,... | collective-permute-start | bytes 98312 | tf_op jit(solution)/shard_map/ppermute | solution.py:465
  34.1 3.2 %collective-permute-done.10.refs_3_ = bf16[128,128]{1,0:T(8,128)(2,1)S(1)} collective-permute-done((bf16[128,128]{1,0:T(8,128)(2,1)S(1)}, bf16[128,128]{1,0:T(8,128)(2,1)S(1)}, u32[]{:S(2)}, u32[]{:S(2)}) %collective-permute-start.10) | collective-permute-done | bytes 32800 | tf_op jit(solution)/shard_map/ppermute | solution.py:465
  38.2 1.0 %collective-permute-start.13 = (bf16[272,128]{1,0:T(8,128)(2,1)S(1)}, bf16[272,128]{1,0:T(8,128)(2,1)S(1)}, u32[]{:S(2)}, u32[]{:S(2)}) collective-permute-start(bf16[272,128]{1,0:T(8,128)(2,1)S(1)} %get-tuple-element.93), channel_id=1, source_target_pairs={{0,6},{1,7},{2,4},{3,5},{4,2},{5,3},{6,0},{7,1},{8,14},{9,15},{10,... | collective-permute-start | bytes 208904 | tf_op jit(solution)/shard_map/ppermute | solution.py:465
  39.2 1.6 %collective-permute-start.11 = (bf16[272,128]{1,0:T(8,128)(2,1)S(1)}, bf16[272,128]{1,0:T(8,128)(2,1)S(1)}, u32[]{:S(2)}, u32[]{:S(2)}) collective-permute-start(bf16[272,128]{1,0:T(8,128)(2,1)S(1)} %get-tuple-element.87.refs_3_), channel_id=1, source_target_pairs={{0,2},{1,3},{2,0},{3,1},{4,6},{5,7},{6,4},{7,5},{8,10},{9,11},{10,... | collective-permute-start | bytes 208904 | tf_op jit(solution)/shard_map/ppermute | solution.py:465
  42.3 1.6 %collective-permute-done.13.refs_5_ = bf16[272,128]{1,0:T(8,128)(2,1)S(1)} collective-permute-done((bf16[272,128]{1,0:T(8,128)(2,1)S(1)}, bf16[272,128]{1,0:T(8,128)(2,1)S(1)}, u32[]{:S(2)}, u32[]{:S(2)}) %collective-permute-start.13) | collective-permute-done | bytes 69664 | tf_op jit(solution)/shard_map/ppermute | solution.py:465
  44.0 3.6 %collective-permute-start.14 = (bf16[816,128]{1,0:T(8,128)(2,1)S(1)}, bf16[816,128]{1,0:T(8,128)(2,1)S(1)}, u32[]{:S(2)}, u32[]{:S(2)}) collective-permute-start(bf16[816,128]{1,0:T(8,128)(2,1)S(1)} %get-tuple-element.95.refs_1_.refs_2_), channel_id=1, source_target_pairs={{0,1},{1,0},{2,3},{3,2},{4,5},{5,4},{6,7},{7,6},{8,9},{9,8},{10,11... | collective-permute-start | bytes 626696 | tf_op jit(solution)/shard_map/ppermute | solution.py:465
  49.0 1.4 %collective-permute-start.15 = (bf16[624,128]{1,0:T(8,128)(2,1)S(1)}, bf16[624,128]{1,0:T(8,128)(2,1)S(1)}, u32[]{:S(2)}, u32[]{:S(2)}) collective-permute-start(bf16[624,128]{1,0:T(8,128)(2,1)S(1)} %get-tuple-element.97.refs_0_), channel_id=1, source_target_pairs={{0,8},{1,9},{2,10},{3,11},{4,12},{5,13},{6,14},{7,15},{8,16},{9,17... | collective-permute-start | bytes 479240 | tf_op jit(solution)/shard_map/ppermute | solution.py:469
  50.8 7.1 %collective-permute-done.17.refs_3_ = bf16[560,128]{1,0:T(8,128)(2,1)S(1)} collective-permute-done((bf16[560,128]{1,0:T(8,128)(2,1)S(1)}, bf16[560,128]{1,0:T(8,128)(2,1)S(1)}, u32[]{:S(2)}, u32[]{:S(2)}) %collective-permute-start.17) | collective-permute-done | bytes 143392 | tf_op jit(solution)/shard_map/ppermute | solution.py:469
  58.6 2.1 %collective-permute-start.18 = (bf16[576,128]{1,0:T(8,128)(2,1)S(1)}, bf16[576,128]{1,0:T(8,128)(2,1)S(1)}, u32[]{:S(2)}, u32[]{:S(2)}) collective-permute-start(bf16[576,128]{1,0:T(8,128)(2,1)S(1)} %get-tuple-element.104), channel_id=1, source_target_pairs={{0,1},{1,0},{2,3},{3,2},{4,5},{5,4},{6,7},{7,6},{8,9},{9,8},{10,11... | collective-permute-start | bytes 442376 | tf_op jit(solution)/shard_map/ppermute | solution.py:465
  60.7 1.0 %collective-permute-done.18.refs_3_ = bf16[576,128]{1,0:T(8,128)(2,1)S(1)} collective-permute-done((bf16[576,128]{1,0:T(8,128)(2,1)S(1)}, bf16[576,128]{1,0:T(8,128)(2,1)S(1)}, u32[]{:S(2)}, u32[]{:S(2)}) %collective-permute-start.18) | collective-permute-done | bytes 147488 | tf_op jit(solution)/shard_map/ppermute | solution.py:465
  62.2 1.4 %collective-permute-start.20 = (bf16[224,128]{1,0:T(8,128)(2,1)S(1)}, bf16[224,128]{1,0:T(8,128)(2,1)S(1)}, u32[]{:S(2)}, u32[]{:S(2)}) collective-permute-start(bf16[224,128]{1,0:T(8,128)(2,1)S(1)} %get-tuple-element.108), channel_id=1, source_target_pairs={{0,4},{1,5},{2,6},{3,7},{4,0},{5,1},{6,2},{7,3},{8,12},{9,13},{10,... | collective-permute-start | bytes 172040 | tf_op jit(solution)/shard_map/ppermute | solution.py:465
  63.5 1.9 %collective-permute-start.21 = (bf16[224,128]{1,0:T(8,128)(2,1)S(1)}, bf16[224,128]{1,0:T(8,128)(2,1)S(1)}, u32[]{:S(2)}, u32[]{:S(2)}) collective-permute-start(bf16[224,128]{1,0:T(8,128)(2,1)S(1)} %get-tuple-element.109), channel_id=1, source_target_pairs={{0,6},{1,7},{2,4},{3,5},{4,2},{5,3},{6,0},{7,1},{8,14},{9,15},{10,... | collective-permute-start | bytes 172040 | tf_op jit(solution)/shard_map/ppermute | solution.py:465
  66.2 2.5 %collective-permute-done.21.refs_5_ = bf16[224,128]{1,0:T(8,128)(2,1)S(1)} collective-permute-done((bf16[224,128]{1,0:T(8,128)(2,1)S(1)}, bf16[224,128]{1,0:T(8,128)(2,1)S(1)}, u32[]{:S(2)}, u32[]{:S(2)}) %collective-permute-start.21) | collective-permute-done | bytes 57376 | tf_op jit(solution)/shard_map/ppermute | solution.py:465
  68.7 1.8 %collective-permute-start.24 = (bf16[64,128]{1,0:T(8,128)(2,1)S(1)}, bf16[64,128]{1,0:T(8,128)(2,1)S(1)}, u32[]{:S(2)}, u32[]{:S(2)}) collective-permute-start(bf16[64,128]{1,0:T(8,128)(2,1)S(1)} %get-tuple-element.115.refs_0_), channel_id=1, source_target_pairs={{0,16},{1,17},{2,18},{3,19},{4,20},{5,21},{6,22},{7,23},{8,24},{9,... | collective-permute-start | bytes 49160 | tf_op jit(solution)/shard_map/ppermute | solution.py:469
  70.5 1.5 %collective-permute-start.22 = (bf16[64,128]{1,0:T(8,128)(2,1)S(1)}, bf16[64,128]{1,0:T(8,128)(2,1)S(1)}, u32[]{:S(2)}, u32[]{:S(2)}) collective-permute-start(bf16[64,128]{1,0:T(8,128)(2,1)S(1)} %get-tuple-element.115.refs_0_), channel_id=1, source_target_pairs={{0,8},{1,9},{2,10},{3,11},{4,12},{5,13},{6,14},{7,15},{8,16},{9,17... | collective-permute-start | bytes 49160 | tf_op jit(solution)/shard_map/ppermute | solution.py:469
  74.3 2.6 %collective-permute-start.27 = (bf16[208,128]{1,0:T(8,128)(2,1)S(1)}, bf16[208,128]{1,0:T(8,128)(2,1)S(1)}, u32[]{:S(2)}, u32[]{:S(2)}) collective-permute-start(bf16[208,128]{1,0:T(8,128)(2,1)S(1)} %charge_sum.1.refs_0_), channel_id=1, source_target_pairs={{0,192},{32,224},{64,128},{96,160},{128,64},{160,96},{192,0},{224,... | collective-permute-start | bytes 159752 | tf_op jit(solution)/shard_map/ppermute | solution.py:465
  78.6 2.8 %collective-permute-done.26.refs_2_ = bf16[208,128]{1,0:T(8,128)(2,1)S(1)} collective-permute-done((bf16[208,128]{1,0:T(8,128)(2,1)S(1)}, bf16[208,128]{1,0:T(8,128)(2,1)S(1)}, u32[]{:S(2)}, u32[]{:S(2)}) %collective-permute-start.26) | collective-permute-done | bytes 53280 | tf_op jit(solution)/shard_map/ppermute | solution.py:465
  81.4 3.0 %collective-permute-start.28 = (bf16[208,128]{1,0:T(8,128)(2,1)S(1)}, bf16[208,128]{1,0:T(8,128)(2,1)S(1)}, u32[]{:S(2)}, u32[]{:S(2)}) collective-permute-start(bf16[208,128]{1,0:T(8,128)(2,1)S(1)} %cell_sum.1.refs_0_), channel_id=1, source_target_pairs={{0,38},{1,39},{2,36},{3,37},{4,34},{5,35},{6,32},{7,33},{8,46},{9,... | collective-permute-start | bytes 159752 | tf_op jit(solution)/shard_map/ppermute | solution.py:465
  84.4 1.5 %collective-permute-done.28.refs_1_ = bf16[208,128]{1,0:T(8,128)(2,1)S(1)} collective-permute-done((bf16[208,128]{1,0:T(8,128)(2,1)S(1)}, bf16[208,128]{1,0:T(8,128)(2,1)S(1)}, u32[]{:S(2)}, u32[]{:S(2)}) %collective-permute-start.28) | collective-permute-done | bytes 53280 | tf_op jit(solution)/shard_map/ppermute | solution.py:465
  86.0 5.9 %collective-permute-start.29 = (f32[208,128]{1,0:T(8,128)S(1)}, f32[208,128]{1,0:T(8,128)S(1)}, u32[]{:S(2)}, u32[]{:S(2)}) collective-permute-start(f32[208,128]{1,0:T(8,128)S(1)} %total.1.refs_0_), channel_id=1, source_target_pairs={{0,1},{1,0},{2,3},{3,2},{4,5},{5,4},{6,7},{7,6},{8,9},{9,8},{10,11... | collective-permute-start | bytes 319496 | tf_op jit(solution)/shard_map/ppermute | solution.py:465
  (72 shorter events, 15.1 us)
Async XLA Ops:
  1.7 8.8 %collective-permute-start.2 = (bf16[144,128]{1,0:T(8,128)(2,1)S(1)}, bf16[144,128]{1,0:T(8,128)(2,1)S(1)}, u32[]{:S(2)}, u32[]{:S(2)}) collective-permute-start(bf16[144,128]{1,0:T(8,128)(2,1)S(1)} %get-tuple-element.64.refs_4_.refs_0_), channel_id=1, source_target_pairs={{0,6},{1,7},{2,4},{3,5},{4,2},{5,3},{6,0},{7,1},{8,14},{9,15},{10,... | collective-permute-start | bytes 110600 | tf_op jit(solution)/shard_map/ppermute | solution.py:465
  7.0 4.1 %collective-permute-start.1 = (bf16[144,128]{1,0:T(8,128)(2,1)S(1)}, bf16[144,128]{1,0:T(8,128)(2,1)S(1)}, u32[]{:S(2)}, u32[]{:S(2)}) collective-permute-start(bf16[144,128]{1,0:T(8,128)(2,1)S(1)} %get-tuple-element.64.refs_4_.refs_0_), channel_id=1, source_target_pairs={{0,4},{1,5},{2,6},{3,7},{4,0},{5,1},{6,2},{7,3},{8,12},{9,13},{10,... | collective-permute-start | bytes 110600 | tf_op jit(solution)/shard_map/ppermute | solution.py:465
  7.0 4.1 %collective-permute-start = (bf16[144,128]{1,0:T(8,128)(2,1)S(1)}, bf16[144,128]{1,0:T(8,128)(2,1)S(1)}, u32[]{:S(2)}, u32[]{:S(2)}) collective-permute-start(bf16[144,128]{1,0:T(8,128)(2,1)S(1)} %get-tuple-element.64.refs_4_.refs_0_), channel_id=1, source_target_pairs={{0,2},{1,3},{2,0},{3,1},{4,6},{5,7},{6,4},{7,5},{8,10},{9,11},{10,... | collective-permute-start | bytes 110600 | tf_op jit(solution)/shard_map/ppermute | solution.py:465
  11.1 2.9 %collective-permute-start.3 = (bf16[576,128]{1,0:T(8,128)(2,1)S(1)}, bf16[576,128]{1,0:T(8,128)(2,1)S(1)}, u32[]{:S(2)}, u32[]{:S(2)}) collective-permute-start(bf16[576,128]{1,0:T(8,128)(2,1)S(1)} %gather.1.refs_0_.refs_1_.refs_9_), channel_id=1, source_target_pairs={{0,1},{1,0},{2,3},{3,2},{4,5},{5,4},{6,7},{7,6},{8,9},{9,8},{10,11... | collective-permute-start | bytes 442376 | tf_op jit(solution)/shard_map/ppermute | solution.py:465
  15.2 10.3 %collective-permute-start.5 = (bf16[576,128]{1,0:T(8,128)(2,1)S(1)}, bf16[576,128]{1,0:T(8,128)(2,1)S(1)}, u32[]{:S(2)}, u32[]{:S(2)}) collective-permute-start(bf16[576,128]{1,0:T(8,128)(2,1)S(1)} %get-tuple-element.71.refs_5_), channel_id=1, source_target_pairs={{0,24},{1,25},{2,26},{3,27},{4,28},{5,29},{6,30},{7,31},{8,0},{9,1... | collective-permute-start | bytes 442376 | tf_op jit(solution)/shard_map/ppermute | solution.py:469
  18.0 7.5 %collective-permute-start.4 = (bf16[576,128]{1,0:T(8,128)(2,1)S(1)}, bf16[576,128]{1,0:T(8,128)(2,1)S(1)}, u32[]{:S(2)}, u32[]{:S(2)}) collective-permute-start(bf16[576,128]{1,0:T(8,128)(2,1)S(1)} %get-tuple-element.71.refs_5_), channel_id=1, source_target_pairs={{0,8},{1,9},{2,10},{3,11},{4,12},{5,13},{6,14},{7,15},{8,16},{9,17... | collective-permute-start | bytes 442376 | tf_op jit(solution)/shard_map/ppermute | solution.py:469
  18.0 7.5 %collective-permute-start.6 = (bf16[512,128]{1,0:T(8,128)(2,1)S(1)}, bf16[512,128]{1,0:T(8,128)(2,1)S(1)}, u32[]{:S(2)}, u32[]{:S(2)}) collective-permute-start(bf16[512,128]{1,0:T(8,128)(2,1)S(1)} %get-tuple-element.70.refs_0_), channel_id=1, source_target_pairs={{0,16},{1,17},{2,18},{3,19},{4,20},{5,21},{6,22},{7,23},{8,24},{9,... | collective-permute-start | bytes 393224 | tf_op jit(solution)/shard_map/ppermute | solution.py:469
  26.0 3.8 %collective-permute-start.7 = (bf16[512,128]{1,0:T(8,128)(2,1)S(1)}, bf16[512,128]{1,0:T(8,128)(2,1)S(1)}, u32[]{:S(2)}, u32[]{:S(2)}) collective-permute-start(bf16[512,128]{1,0:T(8,128)(2,1)S(1)} %get-tuple-element.76), channel_id=1, source_target_pairs={{0,1},{1,0},{2,3},{3,2},{4,5},{5,4},{6,7},{7,6},{8,9},{9,8},{10,11... | collective-permute-start | bytes 393224 | tf_op jit(solution)/shard_map/ppermute | solution.py:465
  29.9 4.3 %collective-permute-start.8 = (bf16[128,128]{1,0:T(8,128)(2,1)S(1)}, bf16[128,128]{1,0:T(8,128)(2,1)S(1)}, u32[]{:S(2)}, u32[]{:S(2)}) collective-permute-start(bf16[128,128]{1,0:T(8,128)(2,1)S(1)} %get-tuple-element.78), channel_id=1, source_target_pairs={{0,2},{1,3},{2,0},{3,1},{4,6},{5,7},{6,4},{7,5},{8,10},{9,11},{10,... | collective-permute-start | bytes 98312 | tf_op jit(solution)/shard_map/ppermute | solution.py:465
  30.0 4.1 %collective-permute-start.9 = (bf16[128,128]{1,0:T(8,128)(2,1)S(1)}, bf16[128,128]{1,0:T(8,128)(2,1)S(1)}, u32[]{:S(2)}, u32[]{:S(2)}) collective-permute-start(bf16[128,128]{1,0:T(8,128)(2,1)S(1)} %get-tuple-element.79), channel_id=1, source_target_pairs={{0,4},{1,5},{2,6},{3,7},{4,0},{5,1},{6,2},{7,3},{8,12},{9,13},{10,... | collective-permute-start | bytes 98312 | tf_op jit(solution)/shard_map/ppermute | solution.py:465
  32.7 4.7 %collective-permute-start.10 = (bf16[128,128]{1,0:T(8,128)(2,1)S(1)}, bf16[128,128]{1,0:T(8,128)(2,1)S(1)}, u32[]{:S(2)}, u32[]{:S(2)}) collective-permute-start(bf16[128,128]{1,0:T(8,128)(2,1)S(1)} %get-tuple-element.80), channel_id=1, source_target_pairs={{0,6},{1,7},{2,4},{3,5},{4,2},{5,3},{6,0},{7,1},{8,14},{9,15},{10,... | collective-permute-start | bytes 98312 | tf_op jit(solution)/shard_map/ppermute | solution.py:465
  33.5 3.8 %copy-start.3 = (bf16[128,128]{1,0:T(8,128)(2,1)S(1)}, bf16[128,128]{1,0:T(8,128)(2,1)}, u32[]{:S(2)}) copy-start(bf16[128,128]{1,0:T(8,128)(2,1)} %refs_2_.3) | copy-start | bytes 98308
  33.5 3.8 %copy-start.5 = (bf16[1,128,128]{2,1,0:T(8,128)(2,1)S(1)}, bf16[1,128,128]{2,1,0:T(8,128)(2,1)}, u32[]{:S(2)}) copy-start(bf16[1,128,128]{2,1,0:T(8,128)(2,1)} %param.33) | copy-start | bytes 98308
  38.1 4.2 %collective-permute-start.12 = (bf16[272,128]{1,0:T(8,128)(2,1)S(1)}, bf16[272,128]{1,0:T(8,128)(2,1)S(1)}, u32[]{:S(2)}, u32[]{:S(2)}) collective-permute-start(bf16[272,128]{1,0:T(8,128)(2,1)S(1)} %get-tuple-element.92), channel_id=1, source_target_pairs={{0,4},{1,5},{2,6},{3,7},{4,0},{5,1},{6,2},{7,3},{8,12},{9,13},{10,... | collective-permute-start | bytes 208904 | tf_op jit(solution)/shard_map/ppermute | solution.py:465
  38.2 5.7 %collective-permute-start.13 = (bf16[272,128]{1,0:T(8,128)(2,1)S(1)}, bf16[272,128]{1,0:T(8,128)(2,1)S(1)}, u32[]{:S(2)}, u32[]{:S(2)}) collective-permute-start(bf16[272,128]{1,0:T(8,128)(2,1)S(1)} %get-tuple-element.93), channel_id=1, source_target_pairs={{0,6},{1,7},{2,4},{3,5},{4,2},{5,3},{6,0},{7,1},{8,14},{9,15},{10,... | collective-permute-start | bytes 208904 | tf_op jit(solution)/shard_map/ppermute | solution.py:465
  39.2 4.7 %collective-permute-start.11 = (bf16[272,128]{1,0:T(8,128)(2,1)S(1)}, bf16[272,128]{1,0:T(8,128)(2,1)S(1)}, u32[]{:S(2)}, u32[]{:S(2)}) collective-permute-start(bf16[272,128]{1,0:T(8,128)(2,1)S(1)} %get-tuple-element.87.refs_3_), channel_id=1, source_target_pairs={{0,2},{1,3},{2,0},{3,1},{4,6},{5,7},{6,4},{7,5},{8,10},{9,11},{10,... | collective-permute-start | bytes 208904 | tf_op jit(solution)/shard_map/ppermute | solution.py:465
  44.0 4.7 %collective-permute-start.14 = (bf16[816,128]{1,0:T(8,128)(2,1)S(1)}, bf16[816,128]{1,0:T(8,128)(2,1)S(1)}, u32[]{:S(2)}, u32[]{:S(2)}) collective-permute-start(bf16[816,128]{1,0:T(8,128)(2,1)S(1)} %get-tuple-element.95.refs_1_.refs_2_), channel_id=1, source_target_pairs={{0,1},{1,0},{2,3},{3,2},{4,5},{5,4},{6,7},{7,6},{8,9},{9,8},{10,11... | collective-permute-start | bytes 626696 | tf_op jit(solution)/shard_map/ppermute | solution.py:465
  48.9 8.9 %collective-permute-start.16 = (bf16[624,128]{1,0:T(8,128)(2,1)S(1)}, bf16[624,128]{1,0:T(8,128)(2,1)S(1)}, u32[]{:S(2)}, u32[]{:S(2)}) collective-permute-start(bf16[624,128]{1,0:T(8,128)(2,1)S(1)} %get-tuple-element.97.refs_0_), channel_id=1, source_target_pairs={{0,24},{1,25},{2,26},{3,27},{4,28},{5,29},{6,30},{7,31},{8,0},{9,1... | collective-permute-start | bytes 479240 | tf_op jit(solution)/shard_map/ppermute | solution.py:469
  49.0 8.8 %collective-permute-start.15 = (bf16[624,128]{1,0:T(8,128)(2,1)S(1)}, bf16[624,128]{1,0:T(8,128)(2,1)S(1)}, u32[]{:S(2)}, u32[]{:S(2)}) collective-permute-start(bf16[624,128]{1,0:T(8,128)(2,1)S(1)} %get-tuple-element.97.refs_0_), channel_id=1, source_target_pairs={{0,8},{1,9},{2,10},{3,11},{4,12},{5,13},{6,14},{7,15},{8,16},{9,17... | collective-permute-start | bytes 479240 | tf_op jit(solution)/shard_map/ppermute | solution.py:469
  50.4 7.4 %collective-permute-start.17 = (bf16[560,128]{1,0:T(8,128)(2,1)S(1)}, bf16[560,128]{1,0:T(8,128)(2,1)S(1)}, u32[]{:S(2)}, u32[]{:S(2)}) collective-permute-start(bf16[560,128]{1,0:T(8,128)(2,1)S(1)} %get-tuple-element.98), channel_id=1, source_target_pairs={{0,16},{1,17},{2,18},{3,19},{4,20},{5,21},{6,22},{7,23},{8,24},{9,... | collective-permute-start | bytes 430088 | tf_op jit(solution)/shard_map/ppermute | solution.py:469
  58.6 3.1 %collective-permute-start.18 = (bf16[576,128]{1,0:T(8,128)(2,1)S(1)}, bf16[576,128]{1,0:T(8,128)(2,1)S(1)}, u32[]{:S(2)}, u32[]{:S(2)}) collective-permute-start(bf16[576,128]{1,0:T(8,128)(2,1)S(1)} %get-tuple-element.104), channel_id=1, source_target_pairs={{0,1},{1,0},{2,3},{3,2},{4,5},{5,4},{6,7},{7,6},{8,9},{9,8},{10,11... | collective-permute-start | bytes 442376 | tf_op jit(solution)/shard_map/ppermute | solution.py:465
  61.8 3.6 %collective-permute-start.19 = (bf16[224,128]{1,0:T(8,128)(2,1)S(1)}, bf16[224,128]{1,0:T(8,128)(2,1)S(1)}, u32[]{:S(2)}, u32[]{:S(2)}) collective-permute-start(bf16[224,128]{1,0:T(8,128)(2,1)S(1)} %get-tuple-element.107), channel_id=1, source_target_pairs={{0,2},{1,3},{2,0},{3,1},{4,6},{5,7},{6,4},{7,5},{8,10},{9,11},{10,... | collective-permute-start | bytes 172040 | tf_op jit(solution)/shard_map/ppermute | solution.py:465
  62.2 4.0 %collective-permute-start.20 = (bf16[224,128]{1,0:T(8,128)(2,1)S(1)}, bf16[224,128]{1,0:T(8,128)(2,1)S(1)}, u32[]{:S(2)}, u32[]{:S(2)}) collective-permute-start(bf16[224,128]{1,0:T(8,128)(2,1)S(1)} %get-tuple-element.108), channel_id=1, source_target_pairs={{0,4},{1,5},{2,6},{3,7},{4,0},{5,1},{6,2},{7,3},{8,12},{9,13},{10,... | collective-permute-start | bytes 172040 | tf_op jit(solution)/shard_map/ppermute | solution.py:465
  63.5 5.1 %collective-permute-start.21 = (bf16[224,128]{1,0:T(8,128)(2,1)S(1)}, bf16[224,128]{1,0:T(8,128)(2,1)S(1)}, u32[]{:S(2)}, u32[]{:S(2)}) collective-permute-start(bf16[224,128]{1,0:T(8,128)(2,1)S(1)} %get-tuple-element.109), channel_id=1, source_target_pairs={{0,6},{1,7},{2,4},{3,5},{4,2},{5,3},{6,0},{7,1},{8,14},{9,15},{10,... | collective-permute-start | bytes 172040 | tf_op jit(solution)/shard_map/ppermute | solution.py:465
  68.7 4.7 %collective-permute-start.24 = (bf16[64,128]{1,0:T(8,128)(2,1)S(1)}, bf16[64,128]{1,0:T(8,128)(2,1)S(1)}, u32[]{:S(2)}, u32[]{:S(2)}) collective-permute-start(bf16[64,128]{1,0:T(8,128)(2,1)S(1)} %get-tuple-element.115.refs_0_), channel_id=1, source_target_pairs={{0,16},{1,17},{2,18},{3,19},{4,20},{5,21},{6,22},{7,23},{8,24},{9,... | collective-permute-start | bytes 49160 | tf_op jit(solution)/shard_map/ppermute | solution.py:469
  70.5 2.9 %collective-permute-start.23 = (bf16[64,128]{1,0:T(8,128)(2,1)S(1)}, bf16[64,128]{1,0:T(8,128)(2,1)S(1)}, u32[]{:S(2)}, u32[]{:S(2)}) collective-permute-start(bf16[64,128]{1,0:T(8,128)(2,1)S(1)} %get-tuple-element.115.refs_0_), channel_id=1, source_target_pairs={{0,24},{1,25},{2,26},{3,27},{4,28},{5,29},{6,30},{7,31},{8,0},{9,1... | collective-permute-start | bytes 49160 | tf_op jit(solution)/shard_map/ppermute | solution.py:469
  70.5 3.8 %collective-permute-start.22 = (bf16[64,128]{1,0:T(8,128)(2,1)S(1)}, bf16[64,128]{1,0:T(8,128)(2,1)S(1)}, u32[]{:S(2)}, u32[]{:S(2)}) collective-permute-start(bf16[64,128]{1,0:T(8,128)(2,1)S(1)} %get-tuple-element.115.refs_0_), channel_id=1, source_target_pairs={{0,8},{1,9},{2,10},{3,11},{4,12},{5,13},{6,14},{7,15},{8,16},{9,17... | collective-permute-start | bytes 49160 | tf_op jit(solution)/shard_map/ppermute | solution.py:469
  74.3 4.3 %collective-permute-start.27 = (bf16[208,128]{1,0:T(8,128)(2,1)S(1)}, bf16[208,128]{1,0:T(8,128)(2,1)S(1)}, u32[]{:S(2)}, u32[]{:S(2)}) collective-permute-start(bf16[208,128]{1,0:T(8,128)(2,1)S(1)} %charge_sum.1.refs_0_), channel_id=1, source_target_pairs={{0,192},{32,224},{64,128},{96,160},{128,64},{160,96},{192,0},{224,... | collective-permute-start | bytes 159752 | tf_op jit(solution)/shard_map/ppermute | solution.py:465
  76.9 4.5 %collective-permute-start.26 = (bf16[208,128]{1,0:T(8,128)(2,1)S(1)}, bf16[208,128]{1,0:T(8,128)(2,1)S(1)}, u32[]{:S(2)}, u32[]{:S(2)}) collective-permute-start(bf16[208,128]{1,0:T(8,128)(2,1)S(1)} %charge_sum.1.refs_0_), channel_id=1, source_target_pairs={{0,128},{32,160},{64,192},{96,224},{128,0},{160,32},{192,64},{224,... | collective-permute-start | bytes 159752 | tf_op jit(solution)/shard_map/ppermute | solution.py:465
  77.4 4.0 %collective-permute-start.25 = (bf16[208,128]{1,0:T(8,128)(2,1)S(1)}, bf16[208,128]{1,0:T(8,128)(2,1)S(1)}, u32[]{:S(2)}, u32[]{:S(2)}) collective-permute-start(bf16[208,128]{1,0:T(8,128)(2,1)S(1)} %charge_sum.1.refs_0_), channel_id=1, source_target_pairs={{0,64},{32,96},{64,0},{96,32},{128,192},{160,224},{192,128},{224,1... | collective-permute-start | bytes 159752 | tf_op jit(solution)/shard_map/ppermute | solution.py:465
  81.4 4.5 %collective-permute-start.28 = (bf16[208,128]{1,0:T(8,128)(2,1)S(1)}, bf16[208,128]{1,0:T(8,128)(2,1)S(1)}, u32[]{:S(2)}, u32[]{:S(2)}) collective-permute-start(bf16[208,128]{1,0:T(8,128)(2,1)S(1)} %cell_sum.1.refs_0_), channel_id=1, source_target_pairs={{0,38},{1,39},{2,36},{3,37},{4,34},{5,35},{6,32},{7,33},{8,46},{9,... | collective-permute-start | bytes 159752 | tf_op jit(solution)/shard_map/ppermute | solution.py:465
  86.0 6.8 %collective-permute-start.29 = (f32[208,128]{1,0:T(8,128)S(1)}, f32[208,128]{1,0:T(8,128)S(1)}, u32[]{:S(2)}, u32[]{:S(2)}) collective-permute-start(f32[208,128]{1,0:T(8,128)S(1)} %total.1.refs_0_), channel_id=1, source_target_pairs={{0,1},{1,0},{2,3},{3,2},{4,5},{5,4},{6,7},{7,6},{8,9},{9,8},{10,11... | collective-permute-start | bytes 319496 | tf_op jit(solution)/shard_map/ppermute | solution.py:465
  (9 other events, 20.8 us)

commit v5 on v4

--- a/solution.py
+++ b/solution.py
@@ -24,7 +24,8 @@
 PACK = ATOMS + 16
 QUARTER = 64
 PART = QUARTER // 2
-LOW = C // 2
+NEAR = ROW // 2 * PACK
+COLUMN = 4
 HALF = ROW * ATOMS // 2
 CHUNK = 1024
 EDGE_STEPS = (5, 7)
@@ -116,7 +117,8 @@
 
 
 def z_at(part, count):
-    return rows_at((place_in_row() // 2) ^ part, count)
+    quarter = (place_in_row() // 2) ^ (3 * lax.rem(lax.axis_index("cell"), 2))
+    return rows_at(quarter ^ part, count)
 
 
 def core():
@@ -138,7 +140,7 @@
     ]
     for copy in copies:
         copy.start()
-    for copy in copies:
+    for copy in copies[: len(near)]:
         copy.wait()
     packed[0:ATOMS, :] = whole[...]
     at = iota((16, ATOMS), 0)
@@ -153,6 +155,8 @@
     tail[10:11, 0:GHOST] = indices[0].astype(f32)
     tail[11:12, 0:GHOST] = indices[1].astype(f32)
     packed[ATOMS:PACK, :] = tail[...].astype(bf16)
+    for copy in copies[len(near) :]:
+        copy.wait()
 
 
 def gather_kernel(own, near, across, corner, out):
@@ -207,14 +211,15 @@
 
 def structure_far_kernel(
     packed, near, near_sums, waves, species_gain, w_charge,
-    table, sums, message, gain, below, above, charges, joined,
+    table, sums, message_up, message_down, gain, below, above, charges, joined,
 ):
     tables_of(packed, wave_lanes(waves), species_gain, w_charge, table, gain, charges)
     total = (near_sums[...] + dot(table[...], charges[...])).astype(bf16)
     sums[...] = total
-    message[0 : 2 * KB, :] = total
-    joined[0 : PACK * ROW // 2, :] = near[...]
-    joined[PACK * ROW // 2 :, :] = packed[...]
+    message_up[0 : 2 * KB, :] = total
+    message_down[0 : 2 * KB, :] = total
+    joined[0:NEAR, :] = near[...]
+    joined[NEAR:, :] = packed[...]
     place = place_in_row()
     atom = iota((ATOMS, GHOST), 0).astype(f32)
 
@@ -226,8 +231,49 @@
 
     below[...] = ghosts((place + ROW - 1) % ROW, 10)
     above[...] = ghosts((place + 1) % ROW, 11)
-    message[2 * KB : 2 * KB + GHOST, :] = ghosts(ROW - 1, 10)
-    message[2 * KB + GHOST :, :] = ghosts(0, 11)
+    message_up[2 * KB :, :] = ghosts(ROW - 1, 10)
+    message_down[2 * KB :, :] = ghosts(0, 11)
+
+
+def copy_kernel(rows, out):
+    out[...] = rows[...]
+
+
+def pair_kernel(own, other, out):
+    out[0:NEAR, :] = own[...]
+    out[NEAR:, :] = other[...]
+
+
+def collect_kernel(pair, other, out):
+    mine = lax.axis_index("dom") // ROW
+    for at, rows, half in ((mine, pair, 0), (mine ^ 1, pair, 1), (mine ^ 3, other, 0), (mine ^ 2, other, 1)):
+        out[rows_at(at, NEAR), :] = rows[NEAR * half : NEAR * (half + 1), :]
+
+
+def column_tables_kernel(packed, waves, species_gain, table, gain, turned):
+    mine = waves[:, pl.ds(pl.multiple_of(place_in_row() * KB, KB), KB)].astype(f32)
+    at = iota((16, KB), 0)
+    kind_at = iota((8, ATOMS), 0).astype(f32)
+    for j in range(COLUMN * ROW // 2):
+        tail = packed[PACK * j + ATOMS : PACK * (j + 1), :]
+        turned[:, ATOMS * j : ATOMS * (j + 1)] = packed[PACK * j : PACK * j + ATOMS, :].T
+        span = slice(ATOMS * j, ATOMS * (j + 1))
+        turns = jnp.zeros((ATOMS, KB), f32)
+        for axis in range(3):
+            chosen = (at == axis) | (at == axis + 3) | (at == axis + 6)
+            turns = turns + dot_rows(tail, chosen.astype(f32).astype(bf16)) * mine[axis : axis + 1, :]
+        turns = turns - jnp.round(turns)
+        square = turns * turns
+        table[span, 0:KB] = horner(COS_TURN, square).astype(bf16)
+        table[span, KB : 2 * KB] = (turns * horner(SIN_TURN, square)).astype(bf16)
+        onehot = (tail.astype(f32)[9:10, :] == kind_at).astype(f32)
+        gain[span, :] = lax.dot_general(
+            onehot,
+            species_gain[...],
+            (((0,), (0,)), ((), ())),
+            precision=lax.Precision.HIGHEST,
+            preferred_element_type=f32,
+        )
 
 
 def column_sum(own, up, down, over, span):
@@ -281,9 +327,8 @@
 def aggregate_kernel(feats, below, above, up, down, w_message, operator, w_radial, aggregate, radial_rows, extended):
     place = place_in_row()
     extended[0:ATOMS, :] = feats[...]
-    first, last = 2 * KB, 2 * KB + GHOST
-    extended[ATOMS : ATOMS + GHOST, :] = jnp.where(place == 0, up[first:last, :], below[...])
-    extended[ATOMS + GHOST :, :] = jnp.where(place == ROW - 1, down[last:, :], above[...])
+    extended[ATOMS : ATOMS + GHOST, :] = jnp.where(place == 0, up[2 * KB :, :], below[...])
+    extended[ATOMS + GHOST :, :] = jnp.where(place == ROW - 1, down[2 * KB :, :], above[...])
     rows = dot(extended[...], w_message[...]).astype(bf16)
     high, low = split(operator[...])
     products = dot(high, rows) + dot(low, rows)
@@ -358,12 +403,14 @@
     sums[...] = dot(table[...], joined[0:HALF, :])
 
 
-def back_far_kernel(table, received, joined, kept, near_sums, message, over, back_down, back_up, ghosts):
+def back_far_kernel(
+    table, received, joined, kept, near_sums, message_up, message_down, over, back_down, back_up, ghosts
+):
     total = (near_sums[...] + dot(table[...], received[0:HALF, :])).astype(bf16)
     ends = HALF + 8 * GHOST
     part = (kept[...] + received[ends : ends + PART, :].astype(f32)).astype(bf16)
     radial = (joined[ends + PART :, :].astype(f32) + received[ends + PART :, :].astype(f32)).astype(bf16)
-    for target in (message, over):
+    for target in (message_up, message_down, over):
         target[0 : 2 * KB, :] = total
         target[2 * KB : 2 * KB + PART, :] = part
         target[2 * KB + PART : 2 * KB + PART + 16, :] = radial
@@ -378,86 +425,72 @@
     back_down[...] = returned((place + ROW - 1) % ROW, 1)
     back_up[...] = returned((place + 1) % ROW, 0)
     first = 2 * KB + PART + 16
-    message[first : first + GHOST, :] = returned(ROW - 1, 1)
-    message[first + GHOST :, :] = returned(0, 0)
-
-
-def charge_back_kernel(
-    own, up, down, over, filt, near, far, near_gain, far_gain, near_rows, far_rows,
-    send, keep, charge, early, rounded, sums,
-):
-    field = field_of(column_sum(own, up, down, over, slice(0, 2 * KB)), filt, inv_waves * inv_atoms)
+    message_up[first:, :] = returned(ROW - 1, 1)
+    message_down[first:, :] = returned(0, 0)
+
+
+def charge_back_kernel(own, up, down, over, filt, near, far, near_gain, far_gain, send, keep, early, field):
+    field[...] = field_of(column_sum(own, up, down, over, slice(0, 2 * KB)), filt, inv_waves * inv_atoms)
     early[...] = column_sum(own, up, down, over, slice(2 * KB, 2 * KB + PART + 16)).astype(bf16)
-    send[0:HALF, :] = (dot_rows(far[...], field) * far_gain[...]).astype(bf16)
-    values = dot_rows(near[...], field) * near_gain[...]
-    keep[...] = values
-    rounded[...] = values.astype(bf16)
+    send[...] = (dot_rows(far[...], field[...]) * far_gain[...]).astype(bf16)
+    keep[...] = dot_rows(near[...], field[...]) * near_gain[...]
+
+
+def charge_kernel(field, early, near_table, near_gain, near_rows, far_table, far_gain, far_rows, message):
     total = jnp.zeros((C, C), f32)
-    for j in range(ROW // 2):
-        rows, atoms = slice(PACK * j, PACK * j + ATOMS), slice(ATOMS * j, ATOMS * (j + 1))
-        total = total + dot_rows(near_rows[rows, :], rounded[atoms, :])
-        total = total + dot_rows(far_rows[rows, :], send[atoms, :])
-    sums[...] = total
-    charge[...] = sums[rows_at(core(), LOW), :]
-    send[HALF:, :] = sums[rows_at(1 - core(), LOW), :].astype(bf16)
-
-
-def tail_spread_kernel(held, charge, early, received, own, charge_out, *sends):
-    values = held[...] + received[0:HALF, :].astype(f32)
-    total = (charge[...] + received[HALF:, :].astype(f32)).astype(bf16)
+    for table, gain, rows in ((near_table, near_gain, near_rows), (far_table, far_gain, far_rows)):
+        total = total + dot(rows[...], (dot(table[...], field[...]) * gain[...]).astype(bf16))
+    message[0:C, :] = total.astype(bf16)
+    message[C:, :] = early[...]
+
+
+def tail_spread_kernel(held, received, mine, other, own, grads, *sends):
+    values = held[...] + received[...].astype(f32)
+    total = (mine[...].astype(f32) + other[...].astype(f32)).astype(bf16)
     own[...] = values[0:ATOMS]
-    charge_out[...] = total
+    grads[...] = total
     for part, send in enumerate(sends):
         send[0:ATOMS, :] = values[ATOMS * (part + 1) : ATOMS * (part + 2)].astype(bf16)
-        send[ATOMS : ATOMS + LOW, :] = total
-        send[ATOMS + LOW :, :] = early[0:PART, :]
-
-
-def raw_kernel(held, charge, early, near, across, corner, raw, charge_out, grads):
+        send[ATOMS:, :] = total[0 : C + PART]
+
+
+def raw_kernel(held, grads, near, across, corner, raw, message):
     rows = slice(0, ATOMS)
     raw[...] = tree(held[...], near[rows, :], across[rows, :], corner[rows, :]).astype(bf16)
-    rows = slice(ATOMS, ATOMS + LOW)
-    charge_out[...] = tree(charge[...], near[rows, :], across[rows, :], corner[rows, :]).astype(bf16)
-    grads[z_at(0, PART), :] = early[0:PART, :]
+    rows = slice(ATOMS, ATOMS + C)
+    message[0:C, :] = tree(grads[0:C, :], near[rows, :], across[rows, :], corner[rows, :]).astype(bf16)
+    quarters = message.at[C : 2 * C]
+    quarters[z_at(0, PART), :] = grads[C : C + PART, :]
     for part, received in ((1, near), (2, across), (3, corner)):
-        grads[z_at(part, PART), :] = received[ATOMS + LOW :, :]
-
-
-def charge_sum_kernel(own, up, down, over, grads, early, out):
-    out[0:LOW, :] = column_sum(own, up, down, over, slice(0, LOW)).astype(bf16)
-    out[LOW : LOW + C, :] = grads[...]
-    out[LOW + C :, :] = early[PART:, :]
+        quarters[z_at(part, PART), :] = received[ATOMS + C :, :]
+    message[2 * C :, :] = grads[C + PART :, :]
 
 
 def cell_sum_kernel(own, near, across, corner, out):
-    out[...] = tree(own[...], near[...], across[...], corner[...]).astype(bf16)
+    out[...] = tree(own[...], near[...], across[...], corner[...]) * grad_scale
 
 
 def feature_kernel(raw, w_charge, own, downs, ups, back_down, back_up, up, down, out, token):
     place = place_in_row()
-    first, last = 2 * KB + PART + 16, 2 * KB + PART + 16 + GHOST
-    returned = jnp.where(place == 0, up[first:last, :], back_down[...])
+    first = 2 * KB + PART + 16
+    returned = jnp.where(place == 0, up[first:, :], back_down[...])
     total = own[...] + dot_lanes(raw[...], w_charge[...])
     atom = iota((ATOMS, GHOST), 0)
     total = total + dot((atom == downs[...]).astype(f32).astype(bf16), returned)
-    returned = jnp.where(place == ROW - 1, down[last:, :], back_up[...])
+    returned = jnp.where(place == ROW - 1, down[first:, :], back_up[...])
     total = total + dot((atom == ups[...]).astype(f32).astype(bf16), returned)
     out[...] = total.astype(bf16)
     token[...] = total[0:8]
 
 
-def total_kernel(own, other_cell, total):
-    total[...] = (own[...].astype(f32) + other_cell[...].astype(f32)) * grad_scale
-
-
 def weights_kernel(own, other, charge, message, radial, out):
+    charge[...] = own[0:C, :] + other[0:C, :]
     for total, at in ((own, core()), (other, 1 - core())):
-        charge[rows_at(at, LOW), :] = total[0:LOW, :]
         for z in range(4):
-            start = LOW + PART * z
+            start = C + PART * z
             message[rows_at(2 * z + at, 16), :] = total[start : start + 16, :]
             out[rows_at(2 * z + at, 16), :] = total[start + 16 : start + PART, :]
-    radial[...] = own[LOW + C : LOW + C + NB, :]
+    radial[...] = own[2 * C : 2 * C + NB, :]
 
 
 def swap(values, axis, mask):
@@ -536,23 +569,25 @@
         scratch=[pltpu.VMEM((HALF, C), bf16)],
         name="structure_near",
     )
-    far, sums, message, far_gain, below, above = call(
+    far, sums, message_up, message_down, far_gain, below, above = call(
         structure_far_kernel,
         [
-            ((2 * KB, HALF), bf16), ((2 * KB, C), bf16), ((2 * KB + 2 * GHOST, C), bf16), ((HALF, C), f32),
-            ((GHOST, C), bf16), ((GHOST, C), bf16),
+            ((2 * KB, HALF), bf16), ((2 * KB, C), bf16), ((2 * KB + GHOST, C), bf16), ((2 * KB + GHOST, C), bf16),
+            ((HALF, C), f32), ((GHOST, C), bf16), ((GHOST, C), bf16),
         ],
         far_rows, near_rows, near_sums, wave_vectors, species_gain, w_charge,
         scratch=[pltpu.VMEM((HALF, C), bf16), pltpu.VMEM((ROW * PACK, C), bf16)],
         name="structure_far",
     )
-    up, down, over = from_y(message, 1), from_y(message, -1), from_y(sums, 2)
-    operator = edges(EDGE_STEPS[0], EDGE_STEPS[1], [operator], [message])
+    up, down, over = from_y(message_up, 1), from_y(message_down, -1), from_y(sums, 2)
+    operator = edges(EDGE_STEPS[0], EDGE_STEPS[1], [operator], [message_up])
+    (own_near,) = call(copy_kernel, [((NEAR, C), bf16)], near_rows, after=[operator], name="copy")
+    other_near = swap(own_near, "dom", 8)
     send, keep = call(
         potential_kernel,
         [((HALF, C), bf16), ((HALF, C), f32)],
         sums, up, down, over, filt, near, far,
-        after=[operator],
+        after=[own_near],
         name="potential",
     )
     received = swap(send, "dom", 1)
@@ -566,6 +601,10 @@
         own_rows, below, above, up, down, w_message, operator, w_radial,
         name="aggregate",
     )
+    (pair,) = call(
+        pair_kernel, [((2 * NEAR, C), bf16)], own_near, other_near, after=[aggregate], name="pair"
+    )
+    other_pair = swap(pair, "dom", 24)
     act, own_total, back_rows, quarter, radial, *sends = call(
         update_kernel,
         [((ATOMS, C), bf16), ((ATOMS, C), f32), ((EXT, C), bf16), ((QUARTER, C), f32), ((16, C), bf16)]
@@ -588,52 +627,65 @@
     )
     received = swap(joined, "dom", 1)
     (near_sums,) = call(back_near_kernel, [((2 * KB, C), f32)], near, joined, name="back_near")
-    message, over, back_down, back_up = call(
+    message_up, message_down, over, back_down, back_up = call(
         back_far_kernel,
         [
-            ((2 * KB + PART + 16 + 2 * GHOST, C), bf16), ((2 * KB + PART + 16, C), bf16),
+            ((2 * KB + PART + 16 + GHOST, C), bf16), ((2 * KB + PART + 16 + GHOST, C), bf16),
+            ((2 * KB + PART + 16, C), bf16),
             ((GHOST, C), bf16), ((GHOST, C), bf16),
         ],
         far, received, joined, kept, near_sums,
         scratch=[pltpu.VMEM((16 * GHOST, C), bf16)],
         name="back_far",
     )
-    up, down, over = from_y(message, 1), from_y(message, -1), from_y(over, 2)
-    send, keep, charge, early = call(
+    (near_column,) = call(
+        collect_kernel, [((COLUMN * NEAR, C), bf16)], pair, other_pair, after=[over], name="collect"
+    )
+    far_column = swap(near_column, "dom", 1)
+    column_shapes = [((COLUMN * HALF, 2 * KB), bf16), ((COLUMN * HALF, C), f32), ((C, COLUMN * HALF), bf16)]
+    near_table, near_column_gain, near_turned = call(
+        column_tables_kernel, column_shapes, near_column, wave_vectors, species_gain, after=[over], name="near_tables"
+    )
+    far_table, far_column_gain, far_turned = call(
+        column_tables_kernel, column_shapes, far_column, wave_vectors, species_gain, after=[over], name="far_tables"
+    )
+    sums = over
+    up, down, over = from_y(message_up, 1), from_y(message_down, -1), from_y(over, 2)
+    send, keep, early, field = call(
         charge_back_kernel,
-        [((HALF + LOW, C), bf16), ((HALF, C), f32), ((LOW, C), f32), ((PART + 16, C), bf16)],
-        message, up, down, over, filt, near, far, near_gain, far_gain, near_rows, far_rows,
-        scratch=[pltpu.VMEM((HALF, C), bf16), pltpu.VMEM((C, C), f32)],
+        [((HALF, C), bf16), ((HALF, C), f32), ((PART + 16, C), bf16), ((2 * KB, C), bf16)],
+        sums, up, down, over, filt, near, far, near_gain, far_gain,
+        after=[near_column_gain, far_column_gain],
         name="charge_back",
     )
     received = swap(send, "dom", 1)
-    held, charge, *sends = call(
+    (message,) = call(
+        charge_kernel,
+        [((C + PART + 16, C), bf16)],
+        field, early, near_table, near_column_gain, near_turned, far_table, far_column_gain, far_turned,
+        after=[send],
+        name="charge",
+    )
+    other = swap(message, ("cell", "dom"), DOMS + 6)
+    held, grads, *sends = call(
         tail_spread_kernel,
-        [((ATOMS, C), f32), ((LOW, C), bf16)] + [((ATOMS + LOW + PART, C), bf16)] * 3,
-        keep, charge, early, received,
+        [((ATOMS, C), f32), ((C + PART + 16, C), bf16)] + [((ATOMS + C + PART, C), bf16)] * 3,
+        keep, received, message, other,
         name="tail_spread",
     )
     parts = [swap(values, "dom", 2 * (part + 1)) for part, values in enumerate(sends)]
-    raw, charge, grads = call(
-        raw_kernel,
-        [((ATOMS, C), bf16), ((LOW, C), bf16), ((C, C), bf16)],
-        held, charge, early, *parts,
-        name="raw",
-    )
-    parts = [from_y(charge, by) for by in (1, -1, 2)]
+    raw, message = call(
+        raw_kernel, [((ATOMS, C), bf16), ((2 * C + 16, C), bf16)], held, grads, *parts, name="raw"
+    )
+    parts = [swap(message, "cell", mask) for mask in (2, 4, 6)]
     feat_grad, token = call(
         feature_kernel,
         [((ATOMS, C), bf16), ((8, C), f32)],
         raw, w_charge, own_total, ghost_down, ghost_up, back_down, back_up, up, down,
+        after=[message],
         name="feature",
     )
-    (total,) = call(
-        charge_sum_kernel, [((LOW + C + 16, C), bf16)], charge, *parts, grads, early, after=[token], name="charge_sum"
-    )
-    parts = [swap(total, "cell", mask) for mask in (2, 4, 6)]
-    (total,) = call(cell_sum_kernel, [((LOW + C + 16, C), bf16)], total, *parts, name="cell_sum")
-    received = swap(total, ("cell", "dom"), DOMS + 6)
-    (total,) = call(total_kernel, [((LOW + C + 16, C), f32)], total, received, name="total")
+    (total,) = call(cell_sum_kernel, [((2 * C + 16, C), f32)], message, *parts, after=[token], name="cell_sum")
     charge, message, radial, out = call(
         weights_kernel,
         [((C, C), f32), ((C, C), f32), ((NB, C), f32), ((C, C), f32)],

time: 93.8 us -> 89.8 us (0.957)
  waiting for transfers between devices: 27.9 us -> 17.9 us
  Pallas kernels: 16.3 us -> 23.3 us
    ppermute x9 -> x6, waiting for transfers between devices: 9.54 us -> 2.14 us  [from_y(): lax.ppermute(values, 'dom', [(i, (i + ROW * by) % DOMS) for i in range(DO...]
    pallas_call x22 -> x26, Pallas kernels: 16.3 us -> 23.3 us  [call(): pl.pallas_call(run, out_shape=[jax.ShapeDtypeStruct(shape, dtype) for sha...]
    ppermute x21 -> x24, waiting for transfers between devices: 18.4 us -> 15.7 us  [swap(): return lax.ppermute(values, axis, [(i, i ^ mask) for i in range(count)])]
    ppermute x9 -> x6, starting transfers between devices: 9.54 us -> 7.71 us  [from_y(): lax.ppermute(values, 'dom', [(i, (i + ROW * by) % DOMS) for i in range(DO...]
    ppermute x21 -> x24, starting transfers between devices: 38.2 us -> 39.8 us  [swap(): return lax.ppermute(values, axis, [(i, i ^ mask) for i in range(count)])]
  transfers between devices with their start and end apart: 30 -> 30, of which waited for: 16 -> 14; matrix products, arithmetic and copies ran while one was open for 0% -> 0% of each run, Pallas kernels for 12% -> 21%
where the time goes in v5:
time: 89.8 us; the launch traced here: 89.6 us
  starting transfers between devices  47.5 us (53%)
  Pallas kernels  23.3 us (26%)
  waiting for transfers between devices  17.9 us (20%)
  between operations  0.9 us (1%)
    ppermute x24, starting transfers between devices, swap(): return lax.ppermute(values, axis, [(i, i ^ mask) for i in range(count)])  39.8 us
    pallas_call x26, Pallas kernels, call(): pl.pallas_call(run, out_shape=[jax.ShapeDtypeStruct(shape, dtype) for sha...  23.3 us
    ppermute x24, waiting for transfers between devices, swap(): return lax.ppermute(values, axis, [(i, i ^ mask) for i in range(count)])  15.7 us
    ppermute x6, starting transfers between devices, from_y(): lax.ppermute(values, 'dom', [(i, (i + ROW * by) % DOMS) for i in range(DO...  7.71 us
    ppermute x6, waiting for transfers between devices, from_y(): lax.ppermute(values, 'dom', [(i, (i + ROW * by) % DOMS) for i in range(DO...  2.14 us
  transfers between devices with their start and end apart: 30, of which 14 were waited for; matrix products, arithmetic and copies ran while one was open for 0% of the time, Pallas kernels for 21%

profile of v5, /device:TPU:1, one launch (start us, length us, event | category | flops | bytes accessed | tf_op | source)
XLA Modules:
  0.0 89.6 jit_solution(12762718679577505841)
XLA Ops:
  1.7 2.6 %collective-permute-start = (bf16[144,128]{1,0:T(8,128)(2,1)S(1)}, bf16[144,128]{1,0:T(8,128)(2,1)S(1)}, u32[]{:S(2)}, u32[]{:S(2)}) collective-permute-start(bf16[144,128]{1,0:T(8,128)(2,1)S(1)} %get-tuple-element.71.refs_4_.refs_0_), channel_id=1, source_target_pairs={{0,2},{1,3},{2,0},{3,1},{4,6},{5,7},{6,4},{7,5},{8,10},{9,11},{10,... | collective-permute-start | bytes 110600 | tf_op jit(solution)/shard_map/ppermute | solution.py:498
  4.2 3.0 %collective-permute-start.1 = (bf16[144,128]{1,0:T(8,128)(2,1)S(1)}, bf16[144,128]{1,0:T(8,128)(2,1)S(1)}, u32[]{:S(2)}, u32[]{:S(2)}) collective-permute-start(bf16[144,128]{1,0:T(8,128)(2,1)S(1)} %get-tuple-element.71.refs_4_.refs_0_), channel_id=1, source_target_pairs={{0,4},{1,5},{2,6},{3,7},{4,0},{5,1},{6,2},{7,3},{8,12},{9,13},{10,... | collective-permute-start | bytes 110600 | tf_op jit(solution)/shard_map/ppermute | solution.py:498
  7.2 3.1 %edges.2.refs_4_ = f32[1024,192]{1,0:T(8,128)S(1)} custom-call(s32[1,12288]{1,0:T(1,128)S(1)} %get-tuple-element.72.refs_0_, s32[1,12288]{1,0:T(1,128)S(1)} %get-tuple-element.73.refs_1_, s32[1,12288]{1,0:T(1,128)S(1)} %get-tuple-element.74.refs_2_, f32[1,12288]{1,0:T(1,128)S(1)} %get-tuple-element.75.refs_3_, ...), custom_call_target="tpu_custom_call" | custom-call | flops 2684354560 | bytes 262144 | tf_op jit(solution)/shard_map/edges/pallas_call | solution.py:96
  10.4 1.4 %collective-permute-done.2.refs_3_ = bf16[144,128]{1,0:T(8,128)(2,1)S(1)} collective-permute-done((bf16[144,128]{1,0:T(8,128)(2,1)S(1)}, bf16[144,128]{1,0:T(8,128)(2,1)S(1)}, u32[]{:S(2)}, u32[]{:S(2)}) %collective-permute-start.2) | collective-permute-done | bytes 36896 | tf_op jit(solution)/shard_map/ppermute | solution.py:498
  11.8 2.5 %collective-permute-start.3 = (bf16[576,128]{1,0:T(8,128)(2,1)S(1)}, bf16[576,128]{1,0:T(8,128)(2,1)S(1)}, u32[]{:S(2)}, u32[]{:S(2)}) collective-permute-start(bf16[576,128]{1,0:T(8,128)(2,1)S(1)} %gather.1.refs_0_.refs_1_), channel_id=1, source_target_pairs={{0,1},{1,0},{2,3},{3,2},{4,5},{5,4},{6,7},{7,6},{8,9},{9,8},{10,11... | collective-permute-start | bytes 442376 | tf_op jit(solution)/shard_map/ppermute | solution.py:498
  14.3 1.2 %structure_near.1 = (bf16[512,512]{1,0:T(8,128)(2,1)S(1)}, f32[512,128]{1,0:T(8,128)S(1)}, f32[256,128]{1,0:T(8,128)S(1)}, f32[512,128]{1,0:T(8,128)S(1)}) custom-call(bf16[576,128]{1,0:T(8,128)(2,1)S(1)} %gather.1.refs_0_.refs_1_, s32[3,2048]{1,0:T(4,128)S(1)} %copy-done, f32[1,128]{1,0:T(1,128)S(1)} %bitcast.10, f32[8,128]{1,0:T(8,128)S(1)} %copy-done.5, ...), custom_call_target="tpu_custom_call" | custom-call | bytes 262144 | tf_op jit(solution)/shard_map/structure_near/pallas_call | solution.py:96
  16.6 1.4 %collective-permute-start.4 = (bf16[544,128]{1,0:T(8,128)(2,1)S(1)}, bf16[544,128]{1,0:T(8,128)(2,1)S(1)}, u32[]{:S(2)}, u32[]{:S(2)}) collective-permute-start(bf16[544,128]{1,0:T(8,128)(2,1)S(1)} %get-tuple-element.78.refs_5_), channel_id=1, source_target_pairs={{0,8},{1,9},{2,10},{3,11},{4,12},{5,13},{6,14},{7,15},{8,16},{9,17... | collective-permute-start | bytes 417800 | tf_op jit(solution)/shard_map/ppermute | solution.py:502
  18.0 1.5 %collective-permute-start.5 = (bf16[544,128]{1,0:T(8,128)(2,1)S(1)}, bf16[544,128]{1,0:T(8,128)(2,1)S(1)}, u32[]{:S(2)}, u32[]{:S(2)}) collective-permute-start(bf16[544,128]{1,0:T(8,128)(2,1)S(1)} %get-tuple-element.79), channel_id=1, source_target_pairs={{0,24},{1,25},{2,26},{3,27},{4,28},{5,29},{6,30},{7,31},{8,0},{9,1... | collective-permute-start | bytes 417800 | tf_op jit(solution)/shard_map/ppermute | solution.py:502
  19.5 1.6 %collective-permute-start.6 = (bf16[512,128]{1,0:T(8,128)(2,1)S(1)}, bf16[512,128]{1,0:T(8,128)(2,1)S(1)}, u32[]{:S(2)}, u32[]{:S(2)}) collective-permute-start(bf16[512,128]{1,0:T(8,128)(2,1)S(1)} %get-tuple-element.77.refs_0_), channel_id=1, source_target_pairs={{0,16},{1,17},{2,18},{3,19},{4,20},{5,21},{6,22},{7,23},{8,24},{9,... | collective-permute-start | bytes 393224 | tf_op jit(solution)/shard_map/ppermute | solution.py:502
  21.1 4.3 %edges.3.refs_1_.refs_6_.refs_9_ = f32[1024,192]{1,0:T(8,128)S(1)} custom-call(s32[1,12288]{1,0:T(1,128)S(1)} %get-tuple-element.72.refs_0_, s32[1,12288]{1,0:T(1,128)S(1)} %get-tuple-element.73.refs_1_, s32[1,12288]{1,0:T(1,128)S(1)} %get-tuple-element.74.refs_2_, f32[1,12288]{1,0:T(1,128)S(1)} %get-tuple-element.75.refs_3_, f32[1024,192]{1,0:T(8,128)S(1)} %edges.2.refs_4_, ...), custom_call_target="tpu_custom_call" | custom-call | flops 3758096384 | bytes 262144 | tf_op jit(solution)/shard_map/edges/pallas_call | solution.py:96
  25.4 1.6 %collective-permute-done.6.refs_3_ = bf16[512,128]{1,0:T(8,128)(2,1)S(1)} collective-permute-done((bf16[512,128]{1,0:T(8,128)(2,1)S(1)}, bf16[512,128]{1,0:T(8,128)(2,1)S(1)}, u32[]{:S(2)}, u32[]{:S(2)}) %collective-permute-start.6) | collective-permute-done | bytes 131104 | tf_op jit(solution)/shard_map/ppermute | solution.py:502
  30.7 2.6 %collective-permute-start.9 = (bf16[128,128]{1,0:T(8,128)(2,1)S(1)}, bf16[128,128]{1,0:T(8,128)(2,1)S(1)}, u32[]{:S(2)}, u32[]{:S(2)}) collective-permute-start(bf16[128,128]{1,0:T(8,128)(2,1)S(1)} %get-tuple-element.87), channel_id=1, source_target_pairs={{0,4},{1,5},{2,6},{3,7},{4,0},{5,1},{6,2},{7,3},{8,12},{9,13},{10,... | collective-permute-start | bytes 98312 | tf_op jit(solution)/shard_map/ppermute | solution.py:498
  34.1 1.7 %collective-permute-start.19 = (bf16[1152,128]{1,0:T(8,128)(2,1)S(1)}, bf16[1152,128]{1,0:T(8,128)(2,1)S(1)}, u32[]{:S(2)}, u32[]{:S(2)}) collective-permute-start(bf16[1152,128]{1,0:T(8,128)(2,1)S(1)} %pair.1.refs_0_), channel_id=1, source_target_pairs={{0,24},{1,25},{2,26},{3,27},{4,28},{5,29},{6,30},{7,31},{8,16},{9,... | collective-permute-start | bytes 884744 | tf_op jit(solution)/shard_map/ppermute | solution.py:498
  38.0 2.1 %collective-permute-start.13 = (bf16[272,128]{1,0:T(8,128)(2,1)S(1)}, bf16[272,128]{1,0:T(8,128)(2,1)S(1)}, u32[]{:S(2)}, u32[]{:S(2)}) collective-permute-start(bf16[272,128]{1,0:T(8,128)(2,1)S(1)} %get-tuple-element.101), channel_id=1, source_target_pairs={{0,6},{1,7},{2,4},{3,5},{4,2},{5,3},{6,0},{7,1},{8,14},{9,15},{10,... | collective-permute-start | bytes 208904 | tf_op jit(solution)/shard_map/ppermute | solution.py:498
  41.3 2.2 %collective-permute-done.13.refs_5_ = bf16[272,128]{1,0:T(8,128)(2,1)S(1)} collective-permute-done((bf16[272,128]{1,0:T(8,128)(2,1)S(1)}, bf16[272,128]{1,0:T(8,128)(2,1)S(1)}, u32[]{:S(2)}, u32[]{:S(2)}) %collective-permute-start.13) | collective-permute-done | bytes 69664 | tf_op jit(solution)/shard_map/ppermute | solution.py:498
  43.5 3.3 %collective-permute-start.14 = (bf16[816,128]{1,0:T(8,128)(2,1)S(1)}, bf16[816,128]{1,0:T(8,128)(2,1)S(1)}, u32[]{:S(2)}, u32[]{:S(2)}) collective-permute-start(bf16[816,128]{1,0:T(8,128)(2,1)S(1)} %get-tuple-element.103.refs_1_.refs_2_), channel_id=1, source_target_pairs={{0,1},{1,0},{2,3},{3,2},{4,5},{5,4},{6,7},{7,6},{8,9},{9,8},{10,11... | collective-permute-start | bytes 626696 | tf_op jit(solution)/shard_map/ppermute | solution.py:498
  49.7 1.8 %collective-permute-start.16 = (bf16[592,128]{1,0:T(8,128)(2,1)S(1)}, bf16[592,128]{1,0:T(8,128)(2,1)S(1)}, u32[]{:S(2)}, u32[]{:S(2)}) collective-permute-start(bf16[592,128]{1,0:T(8,128)(2,1)S(1)} %get-tuple-element.107), channel_id=1, source_target_pairs={{0,24},{1,25},{2,26},{3,27},{4,28},{5,29},{6,30},{7,31},{8,0},{9,1... | collective-permute-start | bytes 454664 | tf_op jit(solution)/shard_map/ppermute | solution.py:502
  52.1 2.7 %near_tables.1 = (bf16[2048,512]{1,0:T(8,128)(2,1)S(1)}, f32[2048,128]{1,0:T(8,128)S(1)}, bf16[128,2048]{1,0:T(8,128)(2,1)S(1)}) custom-call(bf16[2304,128]{1,0:T(8,128)(2,1)S(1)} %collect.1.refs_0_, s32[3,2048]{1,0:T(4,128)S(1)} %copy-done, f32[8,128]{1,0:T(8,128)S(1)} %copy-done.5, bf16[560,128]{1,0:T(8,128)(2,1)S(1)} %get-tuple-element.105.refs_2_.refs_3_.refs_0_), custom_call_target="tpu_custom_call" | custom-call | bytes 262144 | tf_op jit(solution)/shard_map/near_tables/pallas_call | solution.py:96
  54.8 2.8 %far_tables.1 = (bf16[2048,512]{1,0:T(8,128)(2,1)S(1)}, f32[2048,128]{1,0:T(8,128)S(1)}, bf16[128,2048]{1,0:T(8,128)(2,1)S(1)}) custom-call(bf16[2304,128]{1,0:T(8,128)(2,1)S(1)} %collective-permute-done.20.refs_0_, s32[3,2048]{1,0:T(4,128)S(1)} %copy-done, f32[8,128]{1,0:T(8,128)S(1)} %copy-done.5, ...), custom_call_target="tpu_custom_call" | custom-call | bytes 262144 | tf_op jit(solution)/shard_map/far_tables/pallas_call | solution.py:96
  58.6 1.5 %collective-permute-start.21 = (bf16[512,128]{1,0:T(8,128)(2,1)S(1)}, bf16[512,128]{1,0:T(8,128)(2,1)S(1)}, u32[]{:S(2)}, u32[]{:S(2)}) collective-permute-start(bf16[512,128]{1,0:T(8,128)(2,1)S(1)} %get-tuple-element.113.refs_8_), channel_id=1, source_target_pairs={{0,1},{1,0},{2,3},{3,2},{4,5},{5,4},{6,7},{7,6},{8,9},{9,8},{10,11... | collective-permute-start | bytes 393224 | tf_op jit(solution)/shard_map/ppermute | solution.py:498
  60.1 1.6 %charge.1.refs_2_ = bf16[176,128]{1,0:T(8,128)(2,1)S(1)} custom-call(bf16[512,128]{1,0:T(8,128)(2,1)S(1)} %get-tuple-element.114.refs_0_, bf16[48,128]{1,0:T(8,128)(2,1)S(1)} %get-tuple-element.115.refs_1_, bf16[2048,512]{1,0:T(8,128)(2,1)S(1)} %get-tuple-element.116.refs_2_, f32[2048,128]{1,0:T(8,128)S(1)} %get-tuple-element.110.refs_9_.refs_3_, ...), custom_call_target="tpu_custom_call" | custom-call | bytes 262144 | tf_op jit(solution)/shard_map/charge/pallas_call | solution.py:96
  61.7 2.9 %collective-permute-start.22 = (bf16[176,128]{1,0:T(8,128)(2,1)S(1)}, bf16[176,128]{1,0:T(8,128)(2,1)S(1)}, u32[]{:S(2)}, u32[]{:S(2)}) collective-permute-start(bf16[176,128]{1,0:T(8,128)(2,1)S(1)} %charge.1.refs_2_), channel_id=1, source_target_pairs={{0,38},{1,39},{2,36},{3,37},{4,34},{5,35},{6,32},{7,33},{8,46},{9,... | collective-permute-start | bytes 135176 | tf_op jit(solution)/shard_map/ppermute | solution.py:498
  64.7 1.9 %collective-permute-done.22.refs_3_ = bf16[176,128]{1,0:T(8,128)(2,1)S(1)} collective-permute-done((bf16[176,128]{1,0:T(8,128)(2,1)S(1)}, bf16[176,128]{1,0:T(8,128)(2,1)S(1)}, u32[]{:S(2)}, u32[]{:S(2)}) %collective-permute-start.22) | collective-permute-done | bytes 45088 | tf_op jit(solution)/shard_map/ppermute | solution.py:498
  66.6 1.8 %collective-permute-start.23 = (bf16[288,128]{1,0:T(8,128)(2,1)S(1)}, bf16[288,128]{1,0:T(8,128)(2,1)S(1)}, u32[]{:S(2)}, u32[]{:S(2)}) collective-permute-start(bf16[288,128]{1,0:T(8,128)(2,1)S(1)} %get-tuple-element.122), channel_id=1, source_target_pairs={{0,2},{1,3},{2,0},{3,1},{4,6},{5,7},{6,4},{7,5},{8,10},{9,11},{10,... | collective-permute-start | bytes 221192 | tf_op jit(solution)/shard_map/ppermute | solution.py:498
  69.2 1.4 %collective-permute-start.25 = (bf16[288,128]{1,0:T(8,128)(2,1)S(1)}, bf16[288,128]{1,0:T(8,128)(2,1)S(1)}, u32[]{:S(2)}, u32[]{:S(2)}) collective-permute-start(bf16[288,128]{1,0:T(8,128)(2,1)S(1)} %get-tuple-element.124), channel_id=1, source_target_pairs={{0,6},{1,7},{2,4},{3,5},{4,2},{5,3},{6,0},{7,1},{8,14},{9,15},{10,... | collective-permute-start | bytes 221192 | tf_op jit(solution)/shard_map/ppermute | solution.py:498
  70.6 2.7 %collective-permute-done.24.refs_3_ = bf16[288,128]{1,0:T(8,128)(2,1)S(1)} collective-permute-done((bf16[288,128]{1,0:T(8,128)(2,1)S(1)}, bf16[288,128]{1,0:T(8,128)(2,1)S(1)}, u32[]{:S(2)}, u32[]{:S(2)}) %collective-permute-start.24) | collective-permute-done | bytes 73760 | tf_op jit(solution)/shard_map/ppermute | solution.py:498
  73.3 1.7 %collective-permute-done.25.refs_4_ = bf16[288,128]{1,0:T(8,128)(2,1)S(1)} collective-permute-done((bf16[288,128]{1,0:T(8,128)(2,1)S(1)}, bf16[288,128]{1,0:T(8,128)(2,1)S(1)}, u32[]{:S(2)}, u32[]{:S(2)}) %collective-permute-start.25) | collective-permute-done | bytes 73760 | tf_op jit(solution)/shard_map/ppermute | solution.py:498
  75.0 1.3 %collective-permute-start.26 = (bf16[272,128]{1,0:T(8,128)(2,1)S(1)}, bf16[272,128]{1,0:T(8,128)(2,1)S(1)}, u32[]{:S(2)}, u32[]{:S(2)}) collective-permute-start(bf16[272,128]{1,0:T(8,128)(2,1)S(1)} %get-tuple-element.129.refs_9_.refs_0_), channel_id=1, source_target_pairs={{0,64},{32,96},{64,0},{96,32},{128,192},{160,224},{192,128},{224,1... | collective-permute-start | bytes 208904 | tf_op jit(solution)/shard_map/ppermute | solution.py:498
  76.3 2.4 %collective-permute-start.27 = (bf16[272,128]{1,0:T(8,128)(2,1)S(1)}, bf16[272,128]{1,0:T(8,128)(2,1)S(1)}, u32[]{:S(2)}, u32[]{:S(2)}) collective-permute-start(bf16[272,128]{1,0:T(8,128)(2,1)S(1)} %get-tuple-element.129.refs_9_.refs_0_), channel_id=1, source_target_pairs={{0,128},{32,160},{64,192},{96,224},{128,0},{160,32},{192,64},{224,... | collective-permute-start | bytes 208904 | tf_op jit(solution)/shard_map/ppermute | solution.py:498
  79.7 1.4 %collective-permute-done.27.refs_2_ = bf16[272,128]{1,0:T(8,128)(2,1)S(1)} collective-permute-done((bf16[272,128]{1,0:T(8,128)(2,1)S(1)}, bf16[272,128]{1,0:T(8,128)(2,1)S(1)}, u32[]{:S(2)}, u32[]{:S(2)}) %collective-permute-start.27) | collective-permute-done | bytes 69664 | tf_op jit(solution)/shard_map/ppermute | solution.py:498
  81.2 1.9 %collective-permute-done.28.refs_3_ = bf16[272,128]{1,0:T(8,128)(2,1)S(1)} collective-permute-done((bf16[272,128]{1,0:T(8,128)(2,1)S(1)}, bf16[272,128]{1,0:T(8,128)(2,1)S(1)}, u32[]{:S(2)}, u32[]{:S(2)}) %collective-permute-start.28) | collective-permute-done | bytes 69664 | tf_op jit(solution)/shard_map/ppermute | solution.py:498
  83.1 4.8 %collective-permute-start.29 = (f32[272,128]{1,0:T(8,128)S(1)}, f32[272,128]{1,0:T(8,128)S(1)}, u32[]{:S(2)}, u32[]{:S(2)}) collective-permute-start(f32[272,128]{1,0:T(8,128)S(1)} %cell_sum.1.refs_0_), channel_id=1, source_target_pairs={{0,1},{1,0},{2,3},{3,2},{4,5},{5,4},{6,7},{7,6},{8,9},{9,8},{10,11... | collective-permute-start | bytes 417800 | tf_op jit(solution)/shard_map/ppermute | solution.py:498
  (76 shorter events, 18.0 us)
Async XLA Ops:
  1.7 8.7 %collective-permute-start = (bf16[144,128]{1,0:T(8,128)(2,1)S(1)}, bf16[144,128]{1,0:T(8,128)(2,1)S(1)}, u32[]{:S(2)}, u32[]{:S(2)}) collective-permute-start(bf16[144,128]{1,0:T(8,128)(2,1)S(1)} %get-tuple-element.71.refs_4_.refs_0_), channel_id=1, source_target_pairs={{0,2},{1,3},{2,0},{3,1},{4,6},{5,7},{6,4},{7,5},{8,10},{9,11},{10,... | collective-permute-start | bytes 110600 | tf_op jit(solution)/shard_map/ppermute | solution.py:498
  4.2 6.1 %collective-permute-start.1 = (bf16[144,128]{1,0:T(8,128)(2,1)S(1)}, bf16[144,128]{1,0:T(8,128)(2,1)S(1)}, u32[]{:S(2)}, u32[]{:S(2)}) collective-permute-start(bf16[144,128]{1,0:T(8,128)(2,1)S(1)} %get-tuple-element.71.refs_4_.refs_0_), channel_id=1, source_target_pairs={{0,4},{1,5},{2,6},{3,7},{4,0},{5,1},{6,2},{7,3},{8,12},{9,13},{10,... | collective-permute-start | bytes 110600 | tf_op jit(solution)/shard_map/ppermute | solution.py:498
  7.2 4.6 %collective-permute-start.2 = (bf16[144,128]{1,0:T(8,128)(2,1)S(1)}, bf16[144,128]{1,0:T(8,128)(2,1)S(1)}, u32[]{:S(2)}, u32[]{:S(2)}) collective-permute-start(bf16[144,128]{1,0:T(8,128)(2,1)S(1)} %get-tuple-element.71.refs_4_.refs_0_), channel_id=1, source_target_pairs={{0,6},{1,7},{2,4},{3,5},{4,2},{5,3},{6,0},{7,1},{8,14},{9,15},{10,... | collective-permute-start | bytes 110600 | tf_op jit(solution)/shard_map/ppermute | solution.py:498
  11.8 3.7 %collective-permute-start.3 = (bf16[576,128]{1,0:T(8,128)(2,1)S(1)}, bf16[576,128]{1,0:T(8,128)(2,1)S(1)}, u32[]{:S(2)}, u32[]{:S(2)}) collective-permute-start(bf16[576,128]{1,0:T(8,128)(2,1)S(1)} %gather.1.refs_0_.refs_1_), channel_id=1, source_target_pairs={{0,1},{1,0},{2,3},{3,2},{4,5},{5,4},{6,7},{7,6},{8,9},{9,8},{10,11... | collective-permute-start | bytes 442376 | tf_op jit(solution)/shard_map/ppermute | solution.py:498
  16.6 10.4 %collective-permute-start.4 = (bf16[544,128]{1,0:T(8,128)(2,1)S(1)}, bf16[544,128]{1,0:T(8,128)(2,1)S(1)}, u32[]{:S(2)}, u32[]{:S(2)}) collective-permute-start(bf16[544,128]{1,0:T(8,128)(2,1)S(1)} %get-tuple-element.78.refs_5_), channel_id=1, source_target_pairs={{0,8},{1,9},{2,10},{3,11},{4,12},{5,13},{6,14},{7,15},{8,16},{9,17... | collective-permute-start | bytes 417800 | tf_op jit(solution)/shard_map/ppermute | solution.py:502
  18.0 9.1 %collective-permute-start.5 = (bf16[544,128]{1,0:T(8,128)(2,1)S(1)}, bf16[544,128]{1,0:T(8,128)(2,1)S(1)}, u32[]{:S(2)}, u32[]{:S(2)}) collective-permute-start(bf16[544,128]{1,0:T(8,128)(2,1)S(1)} %get-tuple-element.79), channel_id=1, source_target_pairs={{0,24},{1,25},{2,26},{3,27},{4,28},{5,29},{6,30},{7,31},{8,0},{9,1... | collective-permute-start | bytes 417800 | tf_op jit(solution)/shard_map/ppermute | solution.py:502
  19.5 7.5 %collective-permute-start.6 = (bf16[512,128]{1,0:T(8,128)(2,1)S(1)}, bf16[512,128]{1,0:T(8,128)(2,1)S(1)}, u32[]{:S(2)}, u32[]{:S(2)}) collective-permute-start(bf16[512,128]{1,0:T(8,128)(2,1)S(1)} %get-tuple-element.77.refs_0_), channel_id=1, source_target_pairs={{0,16},{1,17},{2,18},{3,19},{4,20},{5,21},{6,22},{7,23},{8,24},{9,... | collective-permute-start | bytes 393224 | tf_op jit(solution)/shard_map/ppermute | solution.py:502
  27.6 2.1 %collective-permute-start.7 = (bf16[512,128]{1,0:T(8,128)(2,1)S(1)}, bf16[512,128]{1,0:T(8,128)(2,1)S(1)}, u32[]{:S(2)}, u32[]{:S(2)}) collective-permute-start(bf16[512,128]{1,0:T(8,128)(2,1)S(1)} %get-tuple-element.84), channel_id=1, source_target_pairs={{0,1},{1,0},{2,3},{3,2},{4,5},{5,4},{6,7},{7,6},{8,9},{9,8},{10,11... | collective-permute-start | bytes 393224 | tf_op jit(solution)/shard_map/ppermute | solution.py:498
  28.7 5.4 %collective-permute-start.18 = (bf16[576,128]{1,0:T(8,128)(2,1)S(1)}, bf16[576,128]{1,0:T(8,128)(2,1)S(1)}, u32[]{:S(2)}, u32[]{:S(2)}) collective-permute-start(bf16[576,128]{1,0:T(8,128)(2,1)S(1)} %copy.24.refs_7_.refs_0_), channel_id=1, source_target_pairs={{0,8},{1,9},{2,10},{3,11},{4,12},{5,13},{6,14},{7,15},{8,0},{9,1},... | collective-permute-start | bytes 442376 | tf_op jit(solution)/shard_map/ppermute | solution.py:498
  29.7 6.1 %collective-permute-start.10 = (bf16[128,128]{1,0:T(8,128)(2,1)S(1)}, bf16[128,128]{1,0:T(8,128)(2,1)S(1)}, u32[]{:S(2)}, u32[]{:S(2)}) collective-permute-start(bf16[128,128]{1,0:T(8,128)(2,1)S(1)} %get-tuple-element.88), channel_id=1, source_target_pairs={{0,6},{1,7},{2,4},{3,5},{4,2},{5,3},{6,0},{7,1},{8,14},{9,15},{10,... | collective-permute-start | bytes 98312 | tf_op jit(solution)/shard_map/ppermute | solution.py:498
  30.7 5.0 %collective-permute-start.8 = (bf16[128,128]{1,0:T(8,128)(2,1)S(1)}, bf16[128,128]{1,0:T(8,128)(2,1)S(1)}, u32[]{:S(2)}, u32[]{:S(2)}) collective-permute-start(bf16[128,128]{1,0:T(8,128)(2,1)S(1)} %get-tuple-element.86), channel_id=1, source_target_pairs={{0,2},{1,3},{2,0},{3,1},{4,6},{5,7},{6,4},{7,5},{8,10},{9,11},{10,... | collective-permute-start | bytes 98312 | tf_op jit(solution)/shard_map/ppermute | solution.py:498
  30.7 5.0 %collective-permute-start.9 = (bf16[128,128]{1,0:T(8,128)(2,1)S(1)}, bf16[128,128]{1,0:T(8,128)(2,1)S(1)}, u32[]{:S(2)}, u32[]{:S(2)}) collective-permute-start(bf16[128,128]{1,0:T(8,128)(2,1)S(1)} %get-tuple-element.87), channel_id=1, source_target_pairs={{0,4},{1,5},{2,6},{3,7},{4,0},{5,1},{6,2},{7,3},{8,12},{9,13},{10,... | collective-permute-start | bytes 98312 | tf_op jit(solution)/shard_map/ppermute | solution.py:498
  34.1 14.2 %collective-permute-start.19 = (bf16[1152,128]{1,0:T(8,128)(2,1)S(1)}, bf16[1152,128]{1,0:T(8,128)(2,1)S(1)}, u32[]{:S(2)}, u32[]{:S(2)}) collective-permute-start(bf16[1152,128]{1,0:T(8,128)(2,1)S(1)} %pair.1.refs_0_), channel_id=1, source_target_pairs={{0,24},{1,25},{2,26},{3,27},{4,28},{5,29},{6,30},{7,31},{8,16},{9,... | collective-permute-start | bytes 884744 | tf_op jit(solution)/shard_map/ppermute | solution.py:498
  36.6 4.4 %collective-permute-start.11 = (bf16[272,128]{1,0:T(8,128)(2,1)S(1)}, bf16[272,128]{1,0:T(8,128)(2,1)S(1)}, u32[]{:S(2)}, u32[]{:S(2)}) collective-permute-start(bf16[272,128]{1,0:T(8,128)(2,1)S(1)} %get-tuple-element.95.refs_3_), channel_id=1, source_target_pairs={{0,2},{1,3},{2,0},{3,1},{4,6},{5,7},{6,4},{7,5},{8,10},{9,11},{10,... | collective-permute-start | bytes 208904 | tf_op jit(solution)/shard_map/ppermute | solution.py:498
  37.0 4.4 %collective-permute-start.12 = (bf16[272,128]{1,0:T(8,128)(2,1)S(1)}, bf16[272,128]{1,0:T(8,128)(2,1)S(1)}, u32[]{:S(2)}, u32[]{:S(2)}) collective-permute-start(bf16[272,128]{1,0:T(8,128)(2,1)S(1)} %get-tuple-element.100), channel_id=1, source_target_pairs={{0,4},{1,5},{2,6},{3,7},{4,0},{5,1},{6,2},{7,3},{8,12},{9,13},{10,... | collective-permute-start | bytes 208904 | tf_op jit(solution)/shard_map/ppermute | solution.py:498
  38.0 5.5 %collective-permute-start.13 = (bf16[272,128]{1,0:T(8,128)(2,1)S(1)}, bf16[272,128]{1,0:T(8,128)(2,1)S(1)}, u32[]{:S(2)}, u32[]{:S(2)}) collective-permute-start(bf16[272,128]{1,0:T(8,128)(2,1)S(1)} %get-tuple-element.101), channel_id=1, source_target_pairs={{0,6},{1,7},{2,4},{3,5},{4,2},{5,3},{6,0},{7,1},{8,14},{9,15},{10,... | collective-permute-start | bytes 208904 | tf_op jit(solution)/shard_map/ppermute | solution.py:498
  43.5 4.4 %collective-permute-start.14 = (bf16[816,128]{1,0:T(8,128)(2,1)S(1)}, bf16[816,128]{1,0:T(8,128)(2,1)S(1)}, u32[]{:S(2)}, u32[]{:S(2)}) collective-permute-start(bf16[816,128]{1,0:T(8,128)(2,1)S(1)} %get-tuple-element.103.refs_1_.refs_2_), channel_id=1, source_target_pairs={{0,1},{1,0},{2,3},{3,2},{4,5},{5,4},{6,7},{7,6},{8,9},{9,8},{10,11... | collective-permute-start | bytes 626696 | tf_op jit(solution)/shard_map/ppermute | solution.py:498
  48.3 6.5 %collective-permute-start.20 = (bf16[2304,128]{1,0:T(8,128)(2,1)S(1)}, bf16[2304,128]{1,0:T(8,128)(2,1)S(1)}, u32[]{:S(2)}, u32[]{:S(2)}) collective-permute-start(bf16[2304,128]{1,0:T(8,128)(2,1)S(1)} %collect.1.refs_0_), channel_id=1, source_target_pairs={{0,1},{1,0},{2,3},{3,2},{4,5},{5,4},{6,7},{7,6},{8,9},{9,8},{10,11... | collective-permute-start | bytes 1769480 | tf_op jit(solution)/shard_map/ppermute | solution.py:498
  48.8 9.3 %collective-permute-start.15 = (bf16[592,128]{1,0:T(8,128)(2,1)S(1)}, bf16[592,128]{1,0:T(8,128)(2,1)S(1)}, u32[]{:S(2)}, u32[]{:S(2)}) collective-permute-start(bf16[592,128]{1,0:T(8,128)(2,1)S(1)} %get-tuple-element.106), channel_id=1, source_target_pairs={{0,8},{1,9},{2,10},{3,11},{4,12},{5,13},{6,14},{7,15},{8,16},{9,17... | collective-permute-start | bytes 454664 | tf_op jit(solution)/shard_map/ppermute | solution.py:502
  49.7 8.4 %collective-permute-start.16 = (bf16[592,128]{1,0:T(8,128)(2,1)S(1)}, bf16[592,128]{1,0:T(8,128)(2,1)S(1)}, u32[]{:S(2)}, u32[]{:S(2)}) collective-permute-start(bf16[592,128]{1,0:T(8,128)(2,1)S(1)} %get-tuple-element.107), channel_id=1, source_target_pairs={{0,24},{1,25},{2,26},{3,27},{4,28},{5,29},{6,30},{7,31},{8,0},{9,1... | collective-permute-start | bytes 454664 | tf_op jit(solution)/shard_map/ppermute | solution.py:502
  51.5 6.6 %collective-permute-start.17 = (bf16[560,128]{1,0:T(8,128)(2,1)S(1)}, bf16[560,128]{1,0:T(8,128)(2,1)S(1)}, u32[]{:S(2)}, u32[]{:S(2)}) collective-permute-start(bf16[560,128]{1,0:T(8,128)(2,1)S(1)} %get-tuple-element.105.refs_2_.refs_3_.refs_0_), channel_id=1, source_target_pairs={{0,16},{1,17},{2,18},{3,19},{4,20},{5,21},{6,22},{7,23},{8,24},{9,... | collective-permute-start | bytes 430088 | tf_op jit(solution)/shard_map/ppermute | solution.py:502
  58.6 7.9 %collective-permute-start.21 = (bf16[512,128]{1,0:T(8,128)(2,1)S(1)}, bf16[512,128]{1,0:T(8,128)(2,1)S(1)}, u32[]{:S(2)}, u32[]{:S(2)}) collective-permute-start(bf16[512,128]{1,0:T(8,128)(2,1)S(1)} %get-tuple-element.113.refs_8_), channel_id=1, source_target_pairs={{0,1},{1,0},{2,3},{3,2},{4,5},{5,4},{6,7},{7,6},{8,9},{9,8},{10,11... | collective-permute-start | bytes 393224 | tf_op jit(solution)/shard_map/ppermute | solution.py:498
  60.1 18.8 %copy-start.8 = (s32[1,32]{1,0:T(1,128)S(1)}, s32[1,32]{1,0:T(1,128)}, u32[]{:S(2)}) copy-start(s32[1,32]{1,0:T(1,128)} %refs_3_.7) | copy-start | bytes 388
  60.1 18.8 %copy-start.9 = (s32[1,32]{1,0:T(1,128)S(1)}, s32[1,32]{1,0:T(1,128)}, u32[]{:S(2)}) copy-start(s32[1,32]{1,0:T(1,128)} %refs_4_.7) | copy-start | bytes 388
  61.7 4.8 %collective-permute-start.22 = (bf16[176,128]{1,0:T(8,128)(2,1)S(1)}, bf16[176,128]{1,0:T(8,128)(2,1)S(1)}, u32[]{:S(2)}, u32[]{:S(2)}) collective-permute-start(bf16[176,128]{1,0:T(8,128)(2,1)S(1)} %charge.1.refs_2_), channel_id=1, source_target_pairs={{0,38},{1,39},{2,36},{3,37},{4,34},{5,35},{6,32},{7,33},{8,46},{9,... | collective-permute-start | bytes 135176 | tf_op jit(solution)/shard_map/ppermute | solution.py:498
  66.6 4.0 %collective-permute-start.23 = (bf16[288,128]{1,0:T(8,128)(2,1)S(1)}, bf16[288,128]{1,0:T(8,128)(2,1)S(1)}, u32[]{:S(2)}, u32[]{:S(2)}) collective-permute-start(bf16[288,128]{1,0:T(8,128)(2,1)S(1)} %get-tuple-element.122), channel_id=1, source_target_pairs={{0,2},{1,3},{2,0},{3,1},{4,6},{5,7},{6,4},{7,5},{8,10},{9,11},{10,... | collective-permute-start | bytes 221192 | tf_op jit(solution)/shard_map/ppermute | solution.py:498
  68.4 4.9 %collective-permute-start.24 = (bf16[288,128]{1,0:T(8,128)(2,1)S(1)}, bf16[288,128]{1,0:T(8,128)(2,1)S(1)}, u32[]{:S(2)}, u32[]{:S(2)}) collective-permute-start(bf16[288,128]{1,0:T(8,128)(2,1)S(1)} %get-tuple-element.123), channel_id=1, source_target_pairs={{0,4},{1,5},{2,6},{3,7},{4,0},{5,1},{6,2},{7,3},{8,12},{9,13},{10,... | collective-permute-start | bytes 221192 | tf_op jit(solution)/shard_map/ppermute | solution.py:498
  69.2 5.7 %collective-permute-start.25 = (bf16[288,128]{1,0:T(8,128)(2,1)S(1)}, bf16[288,128]{1,0:T(8,128)(2,1)S(1)}, u32[]{:S(2)}, u32[]{:S(2)}) collective-permute-start(bf16[288,128]{1,0:T(8,128)(2,1)S(1)} %get-tuple-element.124), channel_id=1, source_target_pairs={{0,6},{1,7},{2,4},{3,5},{4,2},{5,3},{6,0},{7,1},{8,14},{9,15},{10,... | collective-permute-start | bytes 221192 | tf_op jit(solution)/shard_map/ppermute | solution.py:498
  75.0 4.7 %collective-permute-start.26 = (bf16[272,128]{1,0:T(8,128)(2,1)S(1)}, bf16[272,128]{1,0:T(8,128)(2,1)S(1)}, u32[]{:S(2)}, u32[]{:S(2)}) collective-permute-start(bf16[272,128]{1,0:T(8,128)(2,1)S(1)} %get-tuple-element.129.refs_9_.refs_0_), channel_id=1, source_target_pairs={{0,64},{32,96},{64,0},{96,32},{128,192},{160,224},{192,128},{224,1... | collective-permute-start | bytes 208904 | tf_op jit(solution)/shard_map/ppermute | solution.py:498
  76.3 4.9 %collective-permute-start.27 = (bf16[272,128]{1,0:T(8,128)(2,1)S(1)}, bf16[272,128]{1,0:T(8,128)(2,1)S(1)}, u32[]{:S(2)}, u32[]{:S(2)}) collective-permute-start(bf16[272,128]{1,0:T(8,128)(2,1)S(1)} %get-tuple-element.129.refs_9_.refs_0_), channel_id=1, source_target_pairs={{0,128},{32,160},{64,192},{96,224},{128,0},{160,32},{192,64},{224,... | collective-permute-start | bytes 208904 | tf_op jit(solution)/shard_map/ppermute | solution.py:498
  78.7 4.4 %collective-permute-start.28 = (bf16[272,128]{1,0:T(8,128)(2,1)S(1)}, bf16[272,128]{1,0:T(8,128)(2,1)S(1)}, u32[]{:S(2)}, u32[]{:S(2)}) collective-permute-start(bf16[272,128]{1,0:T(8,128)(2,1)S(1)} %get-tuple-element.129.refs_9_.refs_0_), channel_id=1, source_target_pairs={{0,192},{32,224},{64,128},{96,160},{128,64},{160,96},{192,0},{224,... | collective-permute-start | bytes 208904 | tf_op jit(solution)/shard_map/ppermute | solution.py:498
  83.1 5.8 %collective-permute-start.29 = (f32[272,128]{1,0:T(8,128)S(1)}, f32[272,128]{1,0:T(8,128)S(1)}, u32[]{:S(2)}, u32[]{:S(2)}) collective-permute-start(f32[272,128]{1,0:T(8,128)S(1)} %cell_sum.1.refs_0_), channel_id=1, source_target_pairs={{0,1},{1,0},{2,3},{3,2},{4,5},{5,4},{6,7},{7,6},{8,9},{9,8},{10,11... | collective-permute-start | bytes 417800 | tf_op jit(solution)/shard_map/ppermute | solution.py:498
  (9 other events, 69.4 us)

commit v6 on v5

--- a/solution.py
+++ b/solution.py
@@ -56,6 +56,25 @@
     -12.471244745942547,
 )
 
+MIX = (
+    (1.25563, -0.56805, 0.251163, -0.11939, 0.059896, -0.030538, 0.014724, -0.005361),
+    (-0.56805, 1.647472, -0.773752, 0.355088, -0.172104, 0.085726, -0.040753, 0.014724),
+    (0.251163, -0.773752, 1.767661, -0.8374, 0.386766, -0.185002, 0.085726, -0.030538),
+    (-0.11939, 0.355088, -0.8374, 1.801205, -0.851469, 0.386766, -0.172104, 0.059896),
+    (0.059896, -0.172104, 0.386766, -0.851469, 1.801205, -0.8374, 0.355088, -0.11939),
+    (-0.030538, 0.085726, -0.185002, 0.386766, -0.8374, 1.767661, -0.773752, 0.251163),
+    (0.014724, -0.040753, 0.085726, -0.172104, 0.355088, -0.773752, 1.647472, -0.56805),
+    (-0.005361, 0.014724, -0.030538, 0.059896, -0.11939, 0.251163, -0.56805, 1.25563),
+    (0.943774626, 0.330363768, 0.0119126827, 0.00237723804, -0.00100488116, 0.000442211757, -0.000188380319, 6.26400104e-05),
+    (0.330363768, 0.879800949, 0.341632643, 0.00920268838, 0.00330706128, -0.00137507484, 0.000571783509, -0.000188380319),
+    (0.0119126827, 0.341632643, 0.874756301, 0.343305856, 0.00862722425, 0.0034955942, -0.00137507484, 0.000442211757),
+    (0.00237723804, 0.00920268838, 0.343305856, 0.87403504, 0.343551294, 0.00862722425, 0.00330706128, -0.00100488116),
+    (-0.00100488116, 0.00330706128, 0.00862722425, 0.343551294, 0.87403504, 0.343305856, 0.00920268838, 0.00237723804),
+    (0.000442211757, -0.00137507484, 0.0034955942, 0.00862722425, 0.343305856, 0.874756301, 0.341632643, 0.0119126827),
+    (-0.000188380319, 0.000571783509, -0.00137507484, 0.00330706128, 0.00920268838, 0.341632643, 0.879800949, 0.330363768),
+    (6.26400104e-05, -0.000188380319, 0.000442211757, -0.00100488116, 0.00237723804, 0.0119126827, 0.330363768, 0.943774626),
+)
+
 
 def horner(coefficients, x):
     total = jnp.full_like(x, coefficients[-1])
@@ -70,6 +89,19 @@
 
 def dot(left, right):
     return jnp.dot(left, right, preferred_element_type=f32)
+
+
+def mixed(table, values):
+    at = iota((NB, C), 0)
+    total = None
+    for j in range(NB):
+        column = jnp.full((NB, C), table[0][j], f32)
+        for b in range(1, NB):
+            column = jnp.where(at == b, table[b][j], column)
+        column = jnp.concatenate([column] * (values.shape[1] // C), axis=1)
+        part = column * values[j : j + 1, :]
+        total = part if total is None else total + part
+    return total
 
 
 def dot_rows(left, right):
@@ -308,7 +340,7 @@
         envelope = 0.5 * (horner(COS_TURN, turn * turn) + 1.0) * live.astype(f32)
         centers = 0.5 + basis_width * iota((NB, CHUNK), 0).astype(f32)
         offset = (reach - centers) * (1.0 / basis_width)
-        weights = (jnp.exp(-offset * offset) * envelope).astype(bf16)
+        weights = (mixed(MIX[:NB], jnp.exp(-offset * offset)) * envelope).astype(bf16)
         atom = iota((ATOMS, CHUNK), 0)
         onehot = (atom == receivers).astype(f32).astype(bf16)
         for b in range(NB):
@@ -333,9 +365,10 @@
     high, low = split(operator[...])
     products = dot(high, rows) + dot(low, rows)
     radial_rows[...] = products
+    weights = mixed(MIX[NB:], w_radial[...])
     total = jnp.zeros((ATOMS, C), f32)
     for b in range(NB):
-        total = total + w_radial[b : b + 1, :] * products[ATOMS * b : ATOMS * (b + 1)]
+        total = total + weights[b : b + 1, :] * products[ATOMS * b : ATOMS * (b + 1)]
     aggregate[...] = total * edge_scale
 
 
@@ -349,9 +382,11 @@
     grad = grad_act * sig * (1.0 + preact * (1.0 - sig))
     rounded = grad.astype(bf16)
     grad = grad * edge_scale
-    stacked = jnp.concatenate([w_radial[b : b + 1, :] * grad for b in range(NB)], axis=0).astype(bf16)
+    weights = mixed(MIX[NB:], w_radial[...])
+    stacked = split(jnp.concatenate([weights[b : b + 1, :] * grad for b in range(NB)], axis=0))
     high, low = split(operator[...])
-    grad_msg = (dot_rows(high, stacked) + dot_rows(low, stacked)).astype(bf16)
+    products = dot_rows(high, jnp.concatenate(stacked, axis=1))
+    grad_msg = (products[:, :C] + products[:, C:] + dot_rows(low, stacked[0])).astype(bf16)
     grad_rows = dot_lanes(grad_msg, w_message[...])
     own_total[...] = cotangent[...].astype(f32) + grad_rows[:ATOMS]
     own_rows[0:ATOMS, :] = rounded
@@ -363,12 +398,12 @@
     for t in range(ROW):
         grads[PART * t : PART * t + 16, :] = grad_message[16 * t : 16 * (t + 1)]
         grads[PART * t + 16 : PART * (t + 1), :] = grad_out[16 * t : 16 * (t + 1)]
-    at = iota((16, C), 0)
-    tail = jnp.zeros((16, C), f32)
+    at = iota((NB, C), 0)
+    tail = jnp.zeros((NB, C), f32)
     for b in range(NB):
         part = jnp.sum(grad * radial_rows[ATOMS * b : ATOMS * (b + 1), :], axis=0, keepdims=True)
         tail = jnp.where(at == b, part, tail)
-    tail = tail.astype(bf16)
+    tail = jnp.concatenate([mixed(MIX[NB:], tail), jnp.zeros((NB, C), f32)], axis=0).astype(bf16)
     own_radial[...] = tail
     own_quarter[...] = grads[z_at(0, QUARTER), :]
     for part, send in ((1, send_near), (2, send_across), (3, send_corner)):

time: 89.8 us -> 89.8 us (level)
  transfers between devices with their start and end apart: 30 -> 30, of which waited for: 14 -> 14; matrix products, arithmetic and copies ran while one was open for 0% -> 0% of each run, Pallas kernels for 21% -> 22%
where the time goes in v6:
time: 89.8 us; the launch traced here: 89.6 us
  starting transfers between devices  47.5 us (53%)
  Pallas kernels  23.3 us (26%)
  waiting for transfers between devices  17.8 us (20%)
  between operations  0.9 us (1%)
    ppermute x24, starting transfers between devices, swap(): return lax.ppermute(values, axis, [(i, i ^ mask) for i in range(count)])  39.8 us
    pallas_call x26, Pallas kernels, call(): pl.pallas_call(run, out_shape=[jax.ShapeDtypeStruct(shape, dtype) for sha...  23.3 us
    ppermute x24, waiting for transfers between devices, swap(): return lax.ppermute(values, axis, [(i, i ^ mask) for i in range(count)])  15.7 us
    ppermute x6, starting transfers between devices, from_y(): lax.ppermute(values, 'dom', [(i, (i + ROW * by) % DOMS) for i in range(DO...  7.71 us
    ppermute x6, waiting for transfers between devices, from_y(): lax.ppermute(values, 'dom', [(i, (i + ROW * by) % DOMS) for i in range(DO...  2.1 us
  transfers between devices with their start and end apart: 30, of which 14 were waited for; matrix products, arithmetic and copies ran while one was open for 0% of the time, Pallas kernels for 22%

profile of v6, /device:TPU:1, one launch (start us, length us, event | category | flops | bytes accessed | tf_op | source)
XLA Modules:
  0.0 89.6 jit_solution(4406062361392819088)
XLA Ops:
  1.7 2.6 %collective-permute-start = (bf16[144,128]{1,0:T(8,128)(2,1)S(1)}, bf16[144,128]{1,0:T(8,128)(2,1)S(1)}, u32[]{:S(2)}, u32[]{:S(2)}) collective-permute-start(bf16[144,128]{1,0:T(8,128)(2,1)S(1)} %get-tuple-element.71.refs_4_.refs_0_), channel_id=1, source_target_pairs={{0,2},{1,3},{2,0},{3,1},{4,6},{5,7},{6,4},{7,5},{8,10},{9,11},{10,... | collective-permute-start | bytes 110600 | tf_op jit(solution)/shard_map/ppermute | solution.py:533
  4.2 3.0 %collective-permute-start.1 = (bf16[144,128]{1,0:T(8,128)(2,1)S(1)}, bf16[144,128]{1,0:T(8,128)(2,1)S(1)}, u32[]{:S(2)}, u32[]{:S(2)}) collective-permute-start(bf16[144,128]{1,0:T(8,128)(2,1)S(1)} %get-tuple-element.71.refs_4_.refs_0_), channel_id=1, source_target_pairs={{0,4},{1,5},{2,6},{3,7},{4,0},{5,1},{6,2},{7,3},{8,12},{9,13},{10,... | collective-permute-start | bytes 110600 | tf_op jit(solution)/shard_map/ppermute | solution.py:533
  7.2 3.1 %edges.2.refs_4_ = f32[1024,192]{1,0:T(8,128)S(1)} custom-call(s32[1,12288]{1,0:T(1,128)S(1)} %get-tuple-element.72.refs_0_, s32[1,12288]{1,0:T(1,128)S(1)} %get-tuple-element.73.refs_1_, s32[1,12288]{1,0:T(1,128)S(1)} %get-tuple-element.74.refs_2_, f32[1,12288]{1,0:T(1,128)S(1)} %get-tuple-element.75.refs_3_, ...), custom_call_target="tpu_custom_call" | custom-call | flops 2684354560 | bytes 262144 | tf_op jit(solution)/shard_map/edges/pallas_call | solution.py:128
  10.4 1.4 %collective-permute-done.2.refs_3_ = bf16[144,128]{1,0:T(8,128)(2,1)S(1)} collective-permute-done((bf16[144,128]{1,0:T(8,128)(2,1)S(1)}, bf16[144,128]{1,0:T(8,128)(2,1)S(1)}, u32[]{:S(2)}, u32[]{:S(2)}) %collective-permute-start.2) | collective-permute-done | bytes 36896 | tf_op jit(solution)/shard_map/ppermute | solution.py:533
  11.8 2.5 %collective-permute-start.3 = (bf16[576,128]{1,0:T(8,128)(2,1)S(1)}, bf16[576,128]{1,0:T(8,128)(2,1)S(1)}, u32[]{:S(2)}, u32[]{:S(2)}) collective-permute-start(bf16[576,128]{1,0:T(8,128)(2,1)S(1)} %gather.1.refs_0_.refs_1_), channel_id=1, source_target_pairs={{0,1},{1,0},{2,3},{3,2},{4,5},{5,4},{6,7},{7,6},{8,9},{9,8},{10,11... | collective-permute-start | bytes 442376 | tf_op jit(solution)/shard_map/ppermute | solution.py:533
  14.3 1.2 %structure_near.1 = (bf16[512,512]{1,0:T(8,128)(2,1)S(1)}, f32[512,128]{1,0:T(8,128)S(1)}, f32[256,128]{1,0:T(8,128)S(1)}, f32[512,128]{1,0:T(8,128)S(1)}) custom-call(bf16[576,128]{1,0:T(8,128)(2,1)S(1)} %gather.1.refs_0_.refs_1_, s32[3,2048]{1,0:T(4,128)S(1)} %copy-done, f32[1,128]{1,0:T(1,128)S(1)} %bitcast.10, f32[8,128]{1,0:T(8,128)S(1)} %copy-done.5, ...), custom_call_target="tpu_custom_call" | custom-call | bytes 262144 | tf_op jit(solution)/shard_map/structure_near/pallas_call | solution.py:128
  16.6 1.4 %collective-permute-start.4 = (bf16[544,128]{1,0:T(8,128)(2,1)S(1)}, bf16[544,128]{1,0:T(8,128)(2,1)S(1)}, u32[]{:S(2)}, u32[]{:S(2)}) collective-permute-start(bf16[544,128]{1,0:T(8,128)(2,1)S(1)} %get-tuple-element.78.refs_5_), channel_id=1, source_target_pairs={{0,8},{1,9},{2,10},{3,11},{4,12},{5,13},{6,14},{7,15},{8,16},{9,17... | collective-permute-start | bytes 417800 | tf_op jit(solution)/shard_map/ppermute | solution.py:537
  18.0 1.5 %collective-permute-start.5 = (bf16[544,128]{1,0:T(8,128)(2,1)S(1)}, bf16[544,128]{1,0:T(8,128)(2,1)S(1)}, u32[]{:S(2)}, u32[]{:S(2)}) collective-permute-start(bf16[544,128]{1,0:T(8,128)(2,1)S(1)} %get-tuple-element.79), channel_id=1, source_target_pairs={{0,24},{1,25},{2,26},{3,27},{4,28},{5,29},{6,30},{7,31},{8,0},{9,1... | collective-permute-start | bytes 417800 | tf_op jit(solution)/shard_map/ppermute | solution.py:537
  19.5 1.6 %collective-permute-start.6 = (bf16[512,128]{1,0:T(8,128)(2,1)S(1)}, bf16[512,128]{1,0:T(8,128)(2,1)S(1)}, u32[]{:S(2)}, u32[]{:S(2)}) collective-permute-start(bf16[512,128]{1,0:T(8,128)(2,1)S(1)} %get-tuple-element.77.refs_0_), channel_id=1, source_target_pairs={{0,16},{1,17},{2,18},{3,19},{4,20},{5,21},{6,22},{7,23},{8,24},{9,... | collective-permute-start | bytes 393224 | tf_op jit(solution)/shard_map/ppermute | solution.py:537
  21.1 4.3 %edges.3.refs_1_.refs_6_.refs_9_ = f32[1024,192]{1,0:T(8,128)S(1)} custom-call(s32[1,12288]{1,0:T(1,128)S(1)} %get-tuple-element.72.refs_0_, s32[1,12288]{1,0:T(1,128)S(1)} %get-tuple-element.73.refs_1_, s32[1,12288]{1,0:T(1,128)S(1)} %get-tuple-element.74.refs_2_, f32[1,12288]{1,0:T(1,128)S(1)} %get-tuple-element.75.refs_3_, f32[1024,192]{1,0:T(8,128)S(1)} %edges.2.refs_4_, ...), custom_call_target="tpu_custom_call" | custom-call | flops 3758096384 | bytes 262144 | tf_op jit(solution)/shard_map/edges/pallas_call | solution.py:128
  25.5 1.6 %collective-permute-done.6.refs_3_ = bf16[512,128]{1,0:T(8,128)(2,1)S(1)} collective-permute-done((bf16[512,128]{1,0:T(8,128)(2,1)S(1)}, bf16[512,128]{1,0:T(8,128)(2,1)S(1)}, u32[]{:S(2)}, u32[]{:S(2)}) %collective-permute-start.6) | collective-permute-done | bytes 131104 | tf_op jit(solution)/shard_map/ppermute | solution.py:537
  30.7 2.6 %collective-permute-start.9 = (bf16[128,128]{1,0:T(8,128)(2,1)S(1)}, bf16[128,128]{1,0:T(8,128)(2,1)S(1)}, u32[]{:S(2)}, u32[]{:S(2)}) collective-permute-start(bf16[128,128]{1,0:T(8,128)(2,1)S(1)} %get-tuple-element.87), channel_id=1, source_target_pairs={{0,4},{1,5},{2,6},{3,7},{4,0},{5,1},{6,2},{7,3},{8,12},{9,13},{10,... | collective-permute-start | bytes 98312 | tf_op jit(solution)/shard_map/ppermute | solution.py:533
  34.1 1.7 %collective-permute-start.19 = (bf16[1152,128]{1,0:T(8,128)(2,1)S(1)}, bf16[1152,128]{1,0:T(8,128)(2,1)S(1)}, u32[]{:S(2)}, u32[]{:S(2)}) collective-permute-start(bf16[1152,128]{1,0:T(8,128)(2,1)S(1)} %pair.1.refs_0_), channel_id=1, source_target_pairs={{0,24},{1,25},{2,26},{3,27},{4,28},{5,29},{6,30},{7,31},{8,16},{9,... | collective-permute-start | bytes 884744 | tf_op jit(solution)/shard_map/ppermute | solution.py:533
  38.1 2.1 %collective-permute-start.13 = (bf16[272,128]{1,0:T(8,128)(2,1)S(1)}, bf16[272,128]{1,0:T(8,128)(2,1)S(1)}, u32[]{:S(2)}, u32[]{:S(2)}) collective-permute-start(bf16[272,128]{1,0:T(8,128)(2,1)S(1)} %get-tuple-element.101), channel_id=1, source_target_pairs={{0,6},{1,7},{2,4},{3,5},{4,2},{5,3},{6,0},{7,1},{8,14},{9,15},{10,... | collective-permute-start | bytes 208904 | tf_op jit(solution)/shard_map/ppermute | solution.py:533
  41.3 2.2 %collective-permute-done.13.refs_5_ = bf16[272,128]{1,0:T(8,128)(2,1)S(1)} collective-permute-done((bf16[272,128]{1,0:T(8,128)(2,1)S(1)}, bf16[272,128]{1,0:T(8,128)(2,1)S(1)}, u32[]{:S(2)}, u32[]{:S(2)}) %collective-permute-start.13) | collective-permute-done | bytes 69664 | tf_op jit(solution)/shard_map/ppermute | solution.py:533
  43.5 3.3 %collective-permute-start.14 = (bf16[816,128]{1,0:T(8,128)(2,1)S(1)}, bf16[816,128]{1,0:T(8,128)(2,1)S(1)}, u32[]{:S(2)}, u32[]{:S(2)}) collective-permute-start(bf16[816,128]{1,0:T(8,128)(2,1)S(1)} %get-tuple-element.103.refs_1_.refs_2_), channel_id=1, source_target_pairs={{0,1},{1,0},{2,3},{3,2},{4,5},{5,4},{6,7},{7,6},{8,9},{9,8},{10,11... | collective-permute-start | bytes 626696 | tf_op jit(solution)/shard_map/ppermute | solution.py:533
  49.7 1.8 %collective-permute-start.16 = (bf16[592,128]{1,0:T(8,128)(2,1)S(1)}, bf16[592,128]{1,0:T(8,128)(2,1)S(1)}, u32[]{:S(2)}, u32[]{:S(2)}) collective-permute-start(bf16[592,128]{1,0:T(8,128)(2,1)S(1)} %get-tuple-element.107), channel_id=1, source_target_pairs={{0,24},{1,25},{2,26},{3,27},{4,28},{5,29},{6,30},{7,31},{8,0},{9,1... | collective-permute-start | bytes 454664 | tf_op jit(solution)/shard_map/ppermute | solution.py:537
  52.1 2.7 %near_tables.1 = (bf16[2048,512]{1,0:T(8,128)(2,1)S(1)}, f32[2048,128]{1,0:T(8,128)S(1)}, bf16[128,2048]{1,0:T(8,128)(2,1)S(1)}) custom-call(bf16[2304,128]{1,0:T(8,128)(2,1)S(1)} %collect.1.refs_0_, s32[3,2048]{1,0:T(4,128)S(1)} %copy-done, f32[8,128]{1,0:T(8,128)S(1)} %copy-done.5, bf16[560,128]{1,0:T(8,128)(2,1)S(1)} %get-tuple-element.105.refs_2_.refs_3_.refs_0_), custom_call_target="tpu_custom_call" | custom-call | bytes 262144 | tf_op jit(solution)/shard_map/near_tables/pallas_call | solution.py:128
  54.8 2.8 %far_tables.1 = (bf16[2048,512]{1,0:T(8,128)(2,1)S(1)}, f32[2048,128]{1,0:T(8,128)S(1)}, bf16[128,2048]{1,0:T(8,128)(2,1)S(1)}) custom-call(bf16[2304,128]{1,0:T(8,128)(2,1)S(1)} %collective-permute-done.20.refs_0_, s32[3,2048]{1,0:T(4,128)S(1)} %copy-done, f32[8,128]{1,0:T(8,128)S(1)} %copy-done.5, ...), custom_call_target="tpu_custom_call" | custom-call | bytes 262144 | tf_op jit(solution)/shard_map/far_tables/pallas_call | solution.py:128
  58.6 1.5 %collective-permute-start.21 = (bf16[512,128]{1,0:T(8,128)(2,1)S(1)}, bf16[512,128]{1,0:T(8,128)(2,1)S(1)}, u32[]{:S(2)}, u32[]{:S(2)}) collective-permute-start(bf16[512,128]{1,0:T(8,128)(2,1)S(1)} %get-tuple-element.113.refs_8_), channel_id=1, source_target_pairs={{0,1},{1,0},{2,3},{3,2},{4,5},{5,4},{6,7},{7,6},{8,9},{9,8},{10,11... | collective-permute-start | bytes 393224 | tf_op jit(solution)/shard_map/ppermute | solution.py:533
  60.1 1.6 %charge.1.refs_2_ = bf16[176,128]{1,0:T(8,128)(2,1)S(1)} custom-call(bf16[512,128]{1,0:T(8,128)(2,1)S(1)} %get-tuple-element.114.refs_0_, bf16[48,128]{1,0:T(8,128)(2,1)S(1)} %get-tuple-element.115.refs_1_, bf16[2048,512]{1,0:T(8,128)(2,1)S(1)} %get-tuple-element.116.refs_2_, f32[2048,128]{1,0:T(8,128)S(1)} %get-tuple-element.110.refs_9_.refs_3_, ...), custom_call_target="tpu_custom_call" | custom-call | bytes 262144 | tf_op jit(solution)/shard_map/charge/pallas_call | solution.py:128
  61.7 2.9 %collective-permute-start.22 = (bf16[176,128]{1,0:T(8,128)(2,1)S(1)}, bf16[176,128]{1,0:T(8,128)(2,1)S(1)}, u32[]{:S(2)}, u32[]{:S(2)}) collective-permute-start(bf16[176,128]{1,0:T(8,128)(2,1)S(1)} %charge.1.refs_2_), channel_id=1, source_target_pairs={{0,38},{1,39},{2,36},{3,37},{4,34},{5,35},{6,32},{7,33},{8,46},{9,... | collective-permute-start | bytes 135176 | tf_op jit(solution)/shard_map/ppermute | solution.py:533
  64.7 1.9 %collective-permute-done.22.refs_3_ = bf16[176,128]{1,0:T(8,128)(2,1)S(1)} collective-permute-done((bf16[176,128]{1,0:T(8,128)(2,1)S(1)}, bf16[176,128]{1,0:T(8,128)(2,1)S(1)}, u32[]{:S(2)}, u32[]{:S(2)}) %collective-permute-start.22) | collective-permute-done | bytes 45088 | tf_op jit(solution)/shard_map/ppermute | solution.py:533
  66.6 1.8 %collective-permute-start.23 = (bf16[288,128]{1,0:T(8,128)(2,1)S(1)}, bf16[288,128]{1,0:T(8,128)(2,1)S(1)}, u32[]{:S(2)}, u32[]{:S(2)}) collective-permute-start(bf16[288,128]{1,0:T(8,128)(2,1)S(1)} %get-tuple-element.122), channel_id=1, source_target_pairs={{0,2},{1,3},{2,0},{3,1},{4,6},{5,7},{6,4},{7,5},{8,10},{9,11},{10,... | collective-permute-start | bytes 221192 | tf_op jit(solution)/shard_map/ppermute | solution.py:533
  69.2 1.4 %collective-permute-start.25 = (bf16[288,128]{1,0:T(8,128)(2,1)S(1)}, bf16[288,128]{1,0:T(8,128)(2,1)S(1)}, u32[]{:S(2)}, u32[]{:S(2)}) collective-permute-start(bf16[288,128]{1,0:T(8,128)(2,1)S(1)} %get-tuple-element.124), channel_id=1, source_target_pairs={{0,6},{1,7},{2,4},{3,5},{4,2},{5,3},{6,0},{7,1},{8,14},{9,15},{10,... | collective-permute-start | bytes 221192 | tf_op jit(solution)/shard_map/ppermute | solution.py:533
  70.6 2.7 %collective-permute-done.24.refs_3_ = bf16[288,128]{1,0:T(8,128)(2,1)S(1)} collective-permute-done((bf16[288,128]{1,0:T(8,128)(2,1)S(1)}, bf16[288,128]{1,0:T(8,128)(2,1)S(1)}, u32[]{:S(2)}, u32[]{:S(2)}) %collective-permute-start.24) | collective-permute-done | bytes 73760 | tf_op jit(solution)/shard_map/ppermute | solution.py:533
  73.3 1.7 %collective-permute-done.25.refs_4_ = bf16[288,128]{1,0:T(8,128)(2,1)S(1)} collective-permute-done((bf16[288,128]{1,0:T(8,128)(2,1)S(1)}, bf16[288,128]{1,0:T(8,128)(2,1)S(1)}, u32[]{:S(2)}, u32[]{:S(2)}) %collective-permute-start.25) | collective-permute-done | bytes 73760 | tf_op jit(solution)/shard_map/ppermute | solution.py:533
  75.0 1.3 %collective-permute-start.26 = (bf16[272,128]{1,0:T(8,128)(2,1)S(1)}, bf16[272,128]{1,0:T(8,128)(2,1)S(1)}, u32[]{:S(2)}, u32[]{:S(2)}) collective-permute-start(bf16[272,128]{1,0:T(8,128)(2,1)S(1)} %get-tuple-element.129.refs_9_.refs_0_), channel_id=1, source_target_pairs={{0,64},{32,96},{64,0},{96,32},{128,192},{160,224},{192,128},{224,1... | collective-permute-start | bytes 208904 | tf_op jit(solution)/shard_map/ppermute | solution.py:533
  76.3 2.4 %collective-permute-start.27 = (bf16[272,128]{1,0:T(8,128)(2,1)S(1)}, bf16[272,128]{1,0:T(8,128)(2,1)S(1)}, u32[]{:S(2)}, u32[]{:S(2)}) collective-permute-start(bf16[272,128]{1,0:T(8,128)(2,1)S(1)} %get-tuple-element.129.refs_9_.refs_0_), channel_id=1, source_target_pairs={{0,128},{32,160},{64,192},{96,224},{128,0},{160,32},{192,64},{224,... | collective-permute-start | bytes 208904 | tf_op jit(solution)/shard_map/ppermute | solution.py:533
  79.7 1.4 %collective-permute-done.27.refs_2_ = bf16[272,128]{1,0:T(8,128)(2,1)S(1)} collective-permute-done((bf16[272,128]{1,0:T(8,128)(2,1)S(1)}, bf16[272,128]{1,0:T(8,128)(2,1)S(1)}, u32[]{:S(2)}, u32[]{:S(2)}) %collective-permute-start.27) | collective-permute-done | bytes 69664 | tf_op jit(solution)/shard_map/ppermute | solution.py:533
  81.2 1.9 %collective-permute-done.28.refs_3_ = bf16[272,128]{1,0:T(8,128)(2,1)S(1)} collective-permute-done((bf16[272,128]{1,0:T(8,128)(2,1)S(1)}, bf16[272,128]{1,0:T(8,128)(2,1)S(1)}, u32[]{:S(2)}, u32[]{:S(2)}) %collective-permute-start.28) | collective-permute-done | bytes 69664 | tf_op jit(solution)/shard_map/ppermute | solution.py:533
  83.1 4.8 %collective-permute-start.29 = (f32[272,128]{1,0:T(8,128)S(1)}, f32[272,128]{1,0:T(8,128)S(1)}, u32[]{:S(2)}, u32[]{:S(2)}) collective-permute-start(f32[272,128]{1,0:T(8,128)S(1)} %cell_sum.1.refs_0_), channel_id=1, source_target_pairs={{0,1},{1,0},{2,3},{3,2},{4,5},{5,4},{6,7},{7,6},{8,9},{9,8},{10,11... | collective-permute-start | bytes 417800 | tf_op jit(solution)/shard_map/ppermute | solution.py:533
  (76 shorter events, 18.1 us)
Async XLA Ops:
  1.7 8.7 %collective-permute-start = (bf16[144,128]{1,0:T(8,128)(2,1)S(1)}, bf16[144,128]{1,0:T(8,128)(2,1)S(1)}, u32[]{:S(2)}, u32[]{:S(2)}) collective-permute-start(bf16[144,128]{1,0:T(8,128)(2,1)S(1)} %get-tuple-element.71.refs_4_.refs_0_), channel_id=1, source_target_pairs={{0,2},{1,3},{2,0},{3,1},{4,6},{5,7},{6,4},{7,5},{8,10},{9,11},{10,... | collective-permute-start | bytes 110600 | tf_op jit(solution)/shard_map/ppermute | solution.py:533
  4.2 6.2 %collective-permute-start.1 = (bf16[144,128]{1,0:T(8,128)(2,1)S(1)}, bf16[144,128]{1,0:T(8,128)(2,1)S(1)}, u32[]{:S(2)}, u32[]{:S(2)}) collective-permute-start(bf16[144,128]{1,0:T(8,128)(2,1)S(1)} %get-tuple-element.71.refs_4_.refs_0_), channel_id=1, source_target_pairs={{0,4},{1,5},{2,6},{3,7},{4,0},{5,1},{6,2},{7,3},{8,12},{9,13},{10,... | collective-permute-start | bytes 110600 | tf_op jit(solution)/shard_map/ppermute | solution.py:533
  7.2 4.6 %collective-permute-start.2 = (bf16[144,128]{1,0:T(8,128)(2,1)S(1)}, bf16[144,128]{1,0:T(8,128)(2,1)S(1)}, u32[]{:S(2)}, u32[]{:S(2)}) collective-permute-start(bf16[144,128]{1,0:T(8,128)(2,1)S(1)} %get-tuple-element.71.refs_4_.refs_0_), channel_id=1, source_target_pairs={{0,6},{1,7},{2,4},{3,5},{4,2},{5,3},{6,0},{7,1},{8,14},{9,15},{10,... | collective-permute-start | bytes 110600 | tf_op jit(solution)/shard_map/ppermute | solution.py:533
  11.8 3.7 %collective-permute-start.3 = (bf16[576,128]{1,0:T(8,128)(2,1)S(1)}, bf16[576,128]{1,0:T(8,128)(2,1)S(1)}, u32[]{:S(2)}, u32[]{:S(2)}) collective-permute-start(bf16[576,128]{1,0:T(8,128)(2,1)S(1)} %gather.1.refs_0_.refs_1_), channel_id=1, source_target_pairs={{0,1},{1,0},{2,3},{3,2},{4,5},{5,4},{6,7},{7,6},{8,9},{9,8},{10,11... | collective-permute-start | bytes 442376 | tf_op jit(solution)/shard_map/ppermute | solution.py:533
  16.6 10.4 %collective-permute-start.4 = (bf16[544,128]{1,0:T(8,128)(2,1)S(1)}, bf16[544,128]{1,0:T(8,128)(2,1)S(1)}, u32[]{:S(2)}, u32[]{:S(2)}) collective-permute-start(bf16[544,128]{1,0:T(8,128)(2,1)S(1)} %get-tuple-element.78.refs_5_), channel_id=1, source_target_pairs={{0,8},{1,9},{2,10},{3,11},{4,12},{5,13},{6,14},{7,15},{8,16},{9,17... | collective-permute-start | bytes 417800 | tf_op jit(solution)/shard_map/ppermute | solution.py:537
  18.0 9.1 %collective-permute-start.5 = (bf16[544,128]{1,0:T(8,128)(2,1)S(1)}, bf16[544,128]{1,0:T(8,128)(2,1)S(1)}, u32[]{:S(2)}, u32[]{:S(2)}) collective-permute-start(bf16[544,128]{1,0:T(8,128)(2,1)S(1)} %get-tuple-element.79), channel_id=1, source_target_pairs={{0,24},{1,25},{2,26},{3,27},{4,28},{5,29},{6,30},{7,31},{8,0},{9,1... | collective-permute-start | bytes 417800 | tf_op jit(solution)/shard_map/ppermute | solution.py:537
  19.5 7.5 %collective-permute-start.6 = (bf16[512,128]{1,0:T(8,128)(2,1)S(1)}, bf16[512,128]{1,0:T(8,128)(2,1)S(1)}, u32[]{:S(2)}, u32[]{:S(2)}) collective-permute-start(bf16[512,128]{1,0:T(8,128)(2,1)S(1)} %get-tuple-element.77.refs_0_), channel_id=1, source_target_pairs={{0,16},{1,17},{2,18},{3,19},{4,20},{5,21},{6,22},{7,23},{8,24},{9,... | collective-permute-start | bytes 393224 | tf_op jit(solution)/shard_map/ppermute | solution.py:537
  27.6 2.1 %collective-permute-start.7 = (bf16[512,128]{1,0:T(8,128)(2,1)S(1)}, bf16[512,128]{1,0:T(8,128)(2,1)S(1)}, u32[]{:S(2)}, u32[]{:S(2)}) collective-permute-start(bf16[512,128]{1,0:T(8,128)(2,1)S(1)} %get-tuple-element.84), channel_id=1, source_target_pairs={{0,1},{1,0},{2,3},{3,2},{4,5},{5,4},{6,7},{7,6},{8,9},{9,8},{10,11... | collective-permute-start | bytes 393224 | tf_op jit(solution)/shard_map/ppermute | solution.py:533
  28.7 5.4 %collective-permute-start.18 = (bf16[576,128]{1,0:T(8,128)(2,1)S(1)}, bf16[576,128]{1,0:T(8,128)(2,1)S(1)}, u32[]{:S(2)}, u32[]{:S(2)}) collective-permute-start(bf16[576,128]{1,0:T(8,128)(2,1)S(1)} %copy.24.refs_7_.refs_0_), channel_id=1, source_target_pairs={{0,8},{1,9},{2,10},{3,11},{4,12},{5,13},{6,14},{7,15},{8,0},{9,1},... | collective-permute-start | bytes 442376 | tf_op jit(solution)/shard_map/ppermute | solution.py:533
  29.7 6.1 %collective-permute-start.10 = (bf16[128,128]{1,0:T(8,128)(2,1)S(1)}, bf16[128,128]{1,0:T(8,128)(2,1)S(1)}, u32[]{:S(2)}, u32[]{:S(2)}) collective-permute-start(bf16[128,128]{1,0:T(8,128)(2,1)S(1)} %get-tuple-element.88), channel_id=1, source_target_pairs={{0,6},{1,7},{2,4},{3,5},{4,2},{5,3},{6,0},{7,1},{8,14},{9,15},{10,... | collective-permute-start | bytes 98312 | tf_op jit(solution)/shard_map/ppermute | solution.py:533
  30.7 5.0 %collective-permute-start.8 = (bf16[128,128]{1,0:T(8,128)(2,1)S(1)}, bf16[128,128]{1,0:T(8,128)(2,1)S(1)}, u32[]{:S(2)}, u32[]{:S(2)}) collective-permute-start(bf16[128,128]{1,0:T(8,128)(2,1)S(1)} %get-tuple-element.86), channel_id=1, source_target_pairs={{0,2},{1,3},{2,0},{3,1},{4,6},{5,7},{6,4},{7,5},{8,10},{9,11},{10,... | collective-permute-start | bytes 98312 | tf_op jit(solution)/shard_map/ppermute | solution.py:533
  30.7 5.0 %collective-permute-start.9 = (bf16[128,128]{1,0:T(8,128)(2,1)S(1)}, bf16[128,128]{1,0:T(8,128)(2,1)S(1)}, u32[]{:S(2)}, u32[]{:S(2)}) collective-permute-start(bf16[128,128]{1,0:T(8,128)(2,1)S(1)} %get-tuple-element.87), channel_id=1, source_target_pairs={{0,4},{1,5},{2,6},{3,7},{4,0},{5,1},{6,2},{7,3},{8,12},{9,13},{10,... | collective-permute-start | bytes 98312 | tf_op jit(solution)/shard_map/ppermute | solution.py:533
  34.1 14.2 %collective-permute-start.19 = (bf16[1152,128]{1,0:T(8,128)(2,1)S(1)}, bf16[1152,128]{1,0:T(8,128)(2,1)S(1)}, u32[]{:S(2)}, u32[]{:S(2)}) collective-permute-start(bf16[1152,128]{1,0:T(8,128)(2,1)S(1)} %pair.1.refs_0_), channel_id=1, source_target_pairs={{0,24},{1,25},{2,26},{3,27},{4,28},{5,29},{6,30},{7,31},{8,16},{9,... | collective-permute-start | bytes 884744 | tf_op jit(solution)/shard_map/ppermute | solution.py:533
  36.6 4.4 %collective-permute-start.11 = (bf16[272,128]{1,0:T(8,128)(2,1)S(1)}, bf16[272,128]{1,0:T(8,128)(2,1)S(1)}, u32[]{:S(2)}, u32[]{:S(2)}) collective-permute-start(bf16[272,128]{1,0:T(8,128)(2,1)S(1)} %get-tuple-element.95.refs_3_), channel_id=1, source_target_pairs={{0,2},{1,3},{2,0},{3,1},{4,6},{5,7},{6,4},{7,5},{8,10},{9,11},{10,... | collective-permute-start | bytes 208904 | tf_op jit(solution)/shard_map/ppermute | solution.py:533
  37.0 4.4 %collective-permute-start.12 = (bf16[272,128]{1,0:T(8,128)(2,1)S(1)}, bf16[272,128]{1,0:T(8,128)(2,1)S(1)}, u32[]{:S(2)}, u32[]{:S(2)}) collective-permute-start(bf16[272,128]{1,0:T(8,128)(2,1)S(1)} %get-tuple-element.100), channel_id=1, source_target_pairs={{0,4},{1,5},{2,6},{3,7},{4,0},{5,1},{6,2},{7,3},{8,12},{9,13},{10,... | collective-permute-start | bytes 208904 | tf_op jit(solution)/shard_map/ppermute | solution.py:533
  38.1 5.5 %collective-permute-start.13 = (bf16[272,128]{1,0:T(8,128)(2,1)S(1)}, bf16[272,128]{1,0:T(8,128)(2,1)S(1)}, u32[]{:S(2)}, u32[]{:S(2)}) collective-permute-start(bf16[272,128]{1,0:T(8,128)(2,1)S(1)} %get-tuple-element.101), channel_id=1, source_target_pairs={{0,6},{1,7},{2,4},{3,5},{4,2},{5,3},{6,0},{7,1},{8,14},{9,15},{10,... | collective-permute-start | bytes 208904 | tf_op jit(solution)/shard_map/ppermute | solution.py:533
  43.5 4.4 %collective-permute-start.14 = (bf16[816,128]{1,0:T(8,128)(2,1)S(1)}, bf16[816,128]{1,0:T(8,128)(2,1)S(1)}, u32[]{:S(2)}, u32[]{:S(2)}) collective-permute-start(bf16[816,128]{1,0:T(8,128)(2,1)S(1)} %get-tuple-element.103.refs_1_.refs_2_), channel_id=1, source_target_pairs={{0,1},{1,0},{2,3},{3,2},{4,5},{5,4},{6,7},{7,6},{8,9},{9,8},{10,11... | collective-permute-start | bytes 626696 | tf_op jit(solution)/shard_map/ppermute | solution.py:533
  48.4 6.5 %collective-permute-start.20 = (bf16[2304,128]{1,0:T(8,128)(2,1)S(1)}, bf16[2304,128]{1,0:T(8,128)(2,1)S(1)}, u32[]{:S(2)}, u32[]{:S(2)}) collective-permute-start(bf16[2304,128]{1,0:T(8,128)(2,1)S(1)} %collect.1.refs_0_), channel_id=1, source_target_pairs={{0,1},{1,0},{2,3},{3,2},{4,5},{5,4},{6,7},{7,6},{8,9},{9,8},{10,11... | collective-permute-start | bytes 1769480 | tf_op jit(solution)/shard_map/ppermute | solution.py:533
  48.8 9.3 %collective-permute-start.15 = (bf16[592,128]{1,0:T(8,128)(2,1)S(1)}, bf16[592,128]{1,0:T(8,128)(2,1)S(1)}, u32[]{:S(2)}, u32[]{:S(2)}) collective-permute-start(bf16[592,128]{1,0:T(8,128)(2,1)S(1)} %get-tuple-element.106), channel_id=1, source_target_pairs={{0,8},{1,9},{2,10},{3,11},{4,12},{5,13},{6,14},{7,15},{8,16},{9,17... | collective-permute-start | bytes 454664 | tf_op jit(solution)/shard_map/ppermute | solution.py:537
  49.7 8.4 %collective-permute-start.16 = (bf16[592,128]{1,0:T(8,128)(2,1)S(1)}, bf16[592,128]{1,0:T(8,128)(2,1)S(1)}, u32[]{:S(2)}, u32[]{:S(2)}) collective-permute-start(bf16[592,128]{1,0:T(8,128)(2,1)S(1)} %get-tuple-element.107), channel_id=1, source_target_pairs={{0,24},{1,25},{2,26},{3,27},{4,28},{5,29},{6,30},{7,31},{8,0},{9,1... | collective-permute-start | bytes 454664 | tf_op jit(solution)/shard_map/ppermute | solution.py:537
  51.5 6.6 %collective-permute-start.17 = (bf16[560,128]{1,0:T(8,128)(2,1)S(1)}, bf16[560,128]{1,0:T(8,128)(2,1)S(1)}, u32[]{:S(2)}, u32[]{:S(2)}) collective-permute-start(bf16[560,128]{1,0:T(8,128)(2,1)S(1)} %get-tuple-element.105.refs_2_.refs_3_.refs_0_), channel_id=1, source_target_pairs={{0,16},{1,17},{2,18},{3,19},{4,20},{5,21},{6,22},{7,23},{8,24},{9,... | collective-permute-start | bytes 430088 | tf_op jit(solution)/shard_map/ppermute | solution.py:537
  58.6 8.0 %collective-permute-start.21 = (bf16[512,128]{1,0:T(8,128)(2,1)S(1)}, bf16[512,128]{1,0:T(8,128)(2,1)S(1)}, u32[]{:S(2)}, u32[]{:S(2)}) collective-permute-start(bf16[512,128]{1,0:T(8,128)(2,1)S(1)} %get-tuple-element.113.refs_8_), channel_id=1, source_target_pairs={{0,1},{1,0},{2,3},{3,2},{4,5},{5,4},{6,7},{7,6},{8,9},{9,8},{10,11... | collective-permute-start | bytes 393224 | tf_op jit(solution)/shard_map/ppermute | solution.py:533
  60.1 18.8 %copy-start.8 = (s32[1,32]{1,0:T(1,128)S(1)}, s32[1,32]{1,0:T(1,128)}, u32[]{:S(2)}) copy-start(s32[1,32]{1,0:T(1,128)} %refs_3_.7) | copy-start | bytes 388
  60.1 18.8 %copy-start.9 = (s32[1,32]{1,0:T(1,128)S(1)}, s32[1,32]{1,0:T(1,128)}, u32[]{:S(2)}) copy-start(s32[1,32]{1,0:T(1,128)} %refs_4_.7) | copy-start | bytes 388
  61.7 4.9 %collective-permute-start.22 = (bf16[176,128]{1,0:T(8,128)(2,1)S(1)}, bf16[176,128]{1,0:T(8,128)(2,1)S(1)}, u32[]{:S(2)}, u32[]{:S(2)}) collective-permute-start(bf16[176,128]{1,0:T(8,128)(2,1)S(1)} %charge.1.refs_2_), channel_id=1, source_target_pairs={{0,38},{1,39},{2,36},{3,37},{4,34},{5,35},{6,32},{7,33},{8,46},{9,... | collective-permute-start | bytes 135176 | tf_op jit(solution)/shard_map/ppermute | solution.py:533
  66.6 3.9 %collective-permute-start.23 = (bf16[288,128]{1,0:T(8,128)(2,1)S(1)}, bf16[288,128]{1,0:T(8,128)(2,1)S(1)}, u32[]{:S(2)}, u32[]{:S(2)}) collective-permute-start(bf16[288,128]{1,0:T(8,128)(2,1)S(1)} %get-tuple-element.122), channel_id=1, source_target_pairs={{0,2},{1,3},{2,0},{3,1},{4,6},{5,7},{6,4},{7,5},{8,10},{9,11},{10,... | collective-permute-start | bytes 221192 | tf_op jit(solution)/shard_map/ppermute | solution.py:533
  68.4 4.9 %collective-permute-start.24 = (bf16[288,128]{1,0:T(8,128)(2,1)S(1)}, bf16[288,128]{1,0:T(8,128)(2,1)S(1)}, u32[]{:S(2)}, u32[]{:S(2)}) collective-permute-start(bf16[288,128]{1,0:T(8,128)(2,1)S(1)} %get-tuple-element.123), channel_id=1, source_target_pairs={{0,4},{1,5},{2,6},{3,7},{4,0},{5,1},{6,2},{7,3},{8,12},{9,13},{10,... | collective-permute-start | bytes 221192 | tf_op jit(solution)/shard_map/ppermute | solution.py:533
  69.2 5.7 %collective-permute-start.25 = (bf16[288,128]{1,0:T(8,128)(2,1)S(1)}, bf16[288,128]{1,0:T(8,128)(2,1)S(1)}, u32[]{:S(2)}, u32[]{:S(2)}) collective-permute-start(bf16[288,128]{1,0:T(8,128)(2,1)S(1)} %get-tuple-element.124), channel_id=1, source_target_pairs={{0,6},{1,7},{2,4},{3,5},{4,2},{5,3},{6,0},{7,1},{8,14},{9,15},{10,... | collective-permute-start | bytes 221192 | tf_op jit(solution)/shard_map/ppermute | solution.py:533
  75.0 4.7 %collective-permute-start.26 = (bf16[272,128]{1,0:T(8,128)(2,1)S(1)}, bf16[272,128]{1,0:T(8,128)(2,1)S(1)}, u32[]{:S(2)}, u32[]{:S(2)}) collective-permute-start(bf16[272,128]{1,0:T(8,128)(2,1)S(1)} %get-tuple-element.129.refs_9_.refs_0_), channel_id=1, source_target_pairs={{0,64},{32,96},{64,0},{96,32},{128,192},{160,224},{192,128},{224,1... | collective-permute-start | bytes 208904 | tf_op jit(solution)/shard_map/ppermute | solution.py:533
  76.3 4.9 %collective-permute-start.27 = (bf16[272,128]{1,0:T(8,128)(2,1)S(1)}, bf16[272,128]{1,0:T(8,128)(2,1)S(1)}, u32[]{:S(2)}, u32[]{:S(2)}) collective-permute-start(bf16[272,128]{1,0:T(8,128)(2,1)S(1)} %get-tuple-element.129.refs_9_.refs_0_), channel_id=1, source_target_pairs={{0,128},{32,160},{64,192},{96,224},{128,0},{160,32},{192,64},{224,... | collective-permute-start | bytes 208904 | tf_op jit(solution)/shard_map/ppermute | solution.py:533
  78.7 4.4 %collective-permute-start.28 = (bf16[272,128]{1,0:T(8,128)(2,1)S(1)}, bf16[272,128]{1,0:T(8,128)(2,1)S(1)}, u32[]{:S(2)}, u32[]{:S(2)}) collective-permute-start(bf16[272,128]{1,0:T(8,128)(2,1)S(1)} %get-tuple-element.129.refs_9_.refs_0_), channel_id=1, source_target_pairs={{0,192},{32,224},{64,128},{96,160},{128,64},{160,96},{192,0},{224,... | collective-permute-start | bytes 208904 | tf_op jit(solution)/shard_map/ppermute | solution.py:533
  83.1 5.8 %collective-permute-start.29 = (f32[272,128]{1,0:T(8,128)S(1)}, f32[272,128]{1,0:T(8,128)S(1)}, u32[]{:S(2)}, u32[]{:S(2)}) collective-permute-start(f32[272,128]{1,0:T(8,128)S(1)} %cell_sum.1.refs_0_), channel_id=1, source_target_pairs={{0,1},{1,0},{2,3},{3,2},{4,5},{5,4},{6,7},{7,6},{8,9},{9,8},{10,11... | collective-permute-start | bytes 417800 | tf_op jit(solution)/shard_map/ppermute | solution.py:533
  (9 other events, 69.4 us)

commit v7 on v6

--- a/solution.py
+++ b/solution.py
@@ -89,6 +89,20 @@
 
 def dot(left, right):
     return jnp.dot(left, right, preferred_element_type=f32)
+
+
+def thirds(values):
+    rest = jnp.concatenate([values, jnp.zeros_like(values)], axis=0)
+    parts = []
+    for _ in range(3):
+        parts.append(rest.astype(bf16))
+        rest = rest - parts[-1].astype(f32)
+    return parts
+
+
+def pick(onehot, parts):
+    chosen = onehot.astype(bf16)
+    return dot_rows(chosen, parts[0]) + dot_rows(chosen, parts[1]) + dot_rows(chosen, parts[2])
 
 
 def mixed(table, values):
@@ -208,18 +222,13 @@
 
 
 def tables_of(packed, lanes, species_gain, w_charge, table, gain, charges):
-    kind_at = iota((8, ATOMS), 0).astype(f32)
+    kind_at = iota((16, ATOMS), 0).astype(f32)
+    gains = thirds(species_gain[...])
     for j in range(ROW // 2):
         rows = packed[PACK * j : PACK * j + ATOMS, :]
         tail = packed[PACK * j + ATOMS : PACK * (j + 1), :].astype(f32)
         onehot = (tail[9:10, :] == kind_at).astype(f32)
-        own_gain = lax.dot_general(
-            onehot,
-            species_gain[...],
-            (((0,), (0,)), ((), ())),
-            precision=lax.Precision.HIGHEST,
-            preferred_element_type=f32,
-        )
+        own_gain = pick(onehot, gains)
         span = slice(ATOMS * j, ATOMS * (j + 1))
         gain[span, :] = own_gain
         charges[span, :] = (dot(rows, w_charge[...]) * own_gain).astype(bf16)
@@ -241,9 +250,17 @@
     sums[...] = dot(table[...], charges[...])
 
 
+def ghosts(joined, owner, row):
+    atom = iota((ATOMS, GHOST), 0).astype(f32)
+    start = at_block(place_in_row() ^ owner, PACK)
+    rows = joined[pl.ds(start, ATOMS), :]
+    tail = joined[pl.ds(pl.multiple_of(start + ATOMS, 16), 16), :].astype(f32)
+    return dot_rows((atom == tail[row : row + 1, 0:GHOST]).astype(f32).astype(bf16), rows).astype(bf16)
+
+
 def structure_far_kernel(
     packed, near, near_sums, waves, species_gain, w_charge,
-    table, sums, message_up, message_down, gain, below, above, charges, joined,
+    table, sums, message_up, message_down, gain, joined, charges,
 ):
     tables_of(packed, wave_lanes(waves), species_gain, w_charge, table, gain, charges)
     total = (near_sums[...] + dot(table[...], charges[...])).astype(bf16)
@@ -252,23 +269,15 @@
     message_down[0 : 2 * KB, :] = total
     joined[0:NEAR, :] = near[...]
     joined[NEAR:, :] = packed[...]
+    message_up[2 * KB :, :] = ghosts(joined, ROW - 1, 10)
+    message_down[2 * KB :, :] = ghosts(joined, 0, 11)
+
+
+def copy_kernel(rows, joined, out, below, above):
+    out[...] = rows[...]
     place = place_in_row()
-    atom = iota((ATOMS, GHOST), 0).astype(f32)
-
-    def ghosts(owner, row):
-        start = at_block(place ^ owner, PACK)
-        rows = joined[pl.ds(start, ATOMS), :]
-        tail = joined[pl.ds(pl.multiple_of(start + ATOMS, 16), 16), :].astype(f32)
-        return dot_rows((atom == tail[row : row + 1, 0:GHOST]).astype(f32).astype(bf16), rows).astype(bf16)
-
-    below[...] = ghosts((place + ROW - 1) % ROW, 10)
-    above[...] = ghosts((place + 1) % ROW, 11)
-    message_up[2 * KB :, :] = ghosts(ROW - 1, 10)
-    message_down[2 * KB :, :] = ghosts(0, 11)
-
-
-def copy_kernel(rows, out):
-    out[...] = rows[...]
+    below[...] = ghosts(joined, (place + ROW - 1) % ROW, 10)
+    above[...] = ghosts(joined, (place + 1) % ROW, 11)
 
 
 def pair_kernel(own, other, out):
@@ -285,7 +294,8 @@
 def column_tables_kernel(packed, waves, species_gain, table, gain, turned):
     mine = waves[:, pl.ds(pl.multiple_of(place_in_row() * KB, KB), KB)].astype(f32)
     at = iota((16, KB), 0)
-    kind_at = iota((8, ATOMS), 0).astype(f32)
+    kind_at = iota((16, ATOMS), 0).astype(f32)
+    gains = thirds(species_gain[...])
     for j in range(COLUMN * ROW // 2):
         tail = packed[PACK * j + ATOMS : PACK * (j + 1), :]
         turned[:, ATOMS * j : ATOMS * (j + 1)] = packed[PACK * j : PACK * j + ATOMS, :].T
@@ -299,13 +309,7 @@
         table[span, 0:KB] = horner(COS_TURN, square).astype(bf16)
         table[span, KB : 2 * KB] = (turns * horner(SIN_TURN, square)).astype(bf16)
         onehot = (tail.astype(f32)[9:10, :] == kind_at).astype(f32)
-        gain[span, :] = lax.dot_general(
-            onehot,
-            species_gain[...],
-            (((0,), (0,)), ((), ())),
-            precision=lax.Precision.HIGHEST,
-            preferred_element_type=f32,
-        )
+        gain[span, :] = pick(onehot, gains)
 
 
 def column_sum(own, up, down, over, span):
@@ -604,19 +608,25 @@
         scratch=[pltpu.VMEM((HALF, C), bf16)],
         name="structure_near",
     )
-    far, sums, message_up, message_down, far_gain, below, above = call(
+    far, sums, message_up, message_down, far_gain, joined_rows = call(
         structure_far_kernel,
         [
             ((2 * KB, HALF), bf16), ((2 * KB, C), bf16), ((2 * KB + GHOST, C), bf16), ((2 * KB + GHOST, C), bf16),
-            ((HALF, C), f32), ((GHOST, C), bf16), ((GHOST, C), bf16),
+            ((HALF, C), f32), ((ROW * PACK, C), bf16),
         ],
         far_rows, near_rows, near_sums, wave_vectors, species_gain, w_charge,
-        scratch=[pltpu.VMEM((HALF, C), bf16), pltpu.VMEM((ROW * PACK, C), bf16)],
+        scratch=[pltpu.VMEM((HALF, C), bf16)],
         name="structure_far",
     )
     up, down, over = from_y(message_up, 1), from_y(message_down, -1), from_y(sums, 2)
     operator = edges(EDGE_STEPS[0], EDGE_STEPS[1], [operator], [message_up])
-    (own_near,) = call(copy_kernel, [((NEAR, C), bf16)], near_rows, after=[operator], name="copy")
+    own_near, below, above = call(
+        copy_kernel,
+        [((NEAR, C), bf16), ((GHOST, C), bf16), ((GHOST, C), bf16)],
+        near_rows, joined_rows,
+        after=[operator],
+        name="copy",
+    )
     other_near = swap(own_near, "dom", 8)
     send, keep = call(
         potential_kernel,

time: 89.8 us -> 89.7 us (level)
  transfers between devices with their start and end apart: 30 -> 30, of which waited for: 14 -> 14; matrix products, arithmetic and copies ran while one was open for 0% -> 0% of each run, Pallas kernels for 22% -> 21%
where the time goes in v7:
time: 89.7 us; the launch traced here: 89.5 us
  starting transfers between devices  47.6 us (53%)
  Pallas kernels  23.2 us (26%)
  waiting for transfers between devices  17.9 us (20%)
    ppermute x24, starting transfers between devices, swap(): return lax.ppermute(values, axis, [(i, i ^ mask) for i in range(count)])  39.9 us
    pallas_call x26, Pallas kernels, call(): pl.pallas_call(run, out_shape=[jax.ShapeDtypeStruct(shape, dtype) for sha...  23.2 us
    ppermute x24, waiting for transfers between devices, swap(): return lax.ppermute(values, axis, [(i, i ^ mask) for i in range(count)])  15.7 us
    ppermute x6, starting transfers between devices, from_y(): lax.ppermute(values, 'dom', [(i, (i + ROW * by) % DOMS) for i in range(DO...  7.7 us
    ppermute x6, waiting for transfers between devices, from_y(): lax.ppermute(values, 'dom', [(i, (i + ROW * by) % DOMS) for i in range(DO...  2.13 us
  transfers between devices with their start and end apart: 30, of which 14 were waited for; matrix products, arithmetic and copies ran while one was open for 0% of the time, Pallas kernels for 21%

profile of v7, /device:TPU:1, one launch (start us, length us, event | category | flops | bytes accessed | tf_op | source)
XLA Modules:
  0.0 89.5 jit_solution(1434170379044873959)
XLA Ops:
  1.7 2.6 %collective-permute-start = (bf16[144,128]{1,0:T(8,128)(2,1)S(1)}, bf16[144,128]{1,0:T(8,128)(2,1)S(1)}, u32[]{:S(2)}, u32[]{:S(2)}) collective-permute-start(bf16[144,128]{1,0:T(8,128)(2,1)S(1)} %get-tuple-element.73.refs_4_.refs_0_), channel_id=1, source_target_pairs={{0,2},{1,3},{2,0},{3,1},{4,6},{5,7},{6,4},{7,5},{8,10},{9,11},{10,... | collective-permute-start | bytes 110600 | tf_op jit(solution)/shard_map/ppermute | solution.py:537
  4.2 3.0 %collective-permute-start.1 = (bf16[144,128]{1,0:T(8,128)(2,1)S(1)}, bf16[144,128]{1,0:T(8,128)(2,1)S(1)}, u32[]{:S(2)}, u32[]{:S(2)}) collective-permute-start(bf16[144,128]{1,0:T(8,128)(2,1)S(1)} %get-tuple-element.73.refs_4_.refs_0_), channel_id=1, source_target_pairs={{0,4},{1,5},{2,6},{3,7},{4,0},{5,1},{6,2},{7,3},{8,12},{9,13},{10,... | collective-permute-start | bytes 110600 | tf_op jit(solution)/shard_map/ppermute | solution.py:537
  7.2 3.1 %edges.2.refs_4_ = f32[1024,192]{1,0:T(8,128)S(1)} custom-call(s32[1,12288]{1,0:T(1,128)S(1)} %get-tuple-element.74.refs_0_, s32[1,12288]{1,0:T(1,128)S(1)} %get-tuple-element.75.refs_1_, s32[1,12288]{1,0:T(1,128)S(1)} %get-tuple-element.76.refs_2_, f32[1,12288]{1,0:T(1,128)S(1)} %get-tuple-element.77.refs_3_, ...), custom_call_target="tpu_custom_call" | custom-call | flops 2684354560 | bytes 262144 | tf_op jit(solution)/shard_map/edges/pallas_call | solution.py:142
  10.4 1.4 %collective-permute-done.2.refs_3_ = bf16[144,128]{1,0:T(8,128)(2,1)S(1)} collective-permute-done((bf16[144,128]{1,0:T(8,128)(2,1)S(1)}, bf16[144,128]{1,0:T(8,128)(2,1)S(1)}, u32[]{:S(2)}, u32[]{:S(2)}) %collective-permute-start.2) | collective-permute-done | bytes 36896 | tf_op jit(solution)/shard_map/ppermute | solution.py:537
  11.8 2.5 %collective-permute-start.3 = (bf16[576,128]{1,0:T(8,128)(2,1)S(1)}, bf16[576,128]{1,0:T(8,128)(2,1)S(1)}, u32[]{:S(2)}, u32[]{:S(2)}) collective-permute-start(bf16[576,128]{1,0:T(8,128)(2,1)S(1)} %gather.1.refs_0_.refs_1_), channel_id=1, source_target_pairs={{0,1},{1,0},{2,3},{3,2},{4,5},{5,4},{6,7},{7,6},{8,9},{9,8},{10,11... | collective-permute-start | bytes 442376 | tf_op jit(solution)/shard_map/ppermute | solution.py:537
  14.3 1.1 %structure_near.1 = (bf16[512,512]{1,0:T(8,128)(2,1)S(1)}, f32[512,128]{1,0:T(8,128)S(1)}, f32[256,128]{1,0:T(8,128)S(1)}, f32[512,128]{1,0:T(8,128)S(1)}) custom-call(bf16[576,128]{1,0:T(8,128)(2,1)S(1)} %gather.1.refs_0_.refs_1_, s32[3,2048]{1,0:T(4,128)S(1)} %copy-done, f32[1,128]{1,0:T(1,128)S(1)} %bitcast.10, f32[8,128]{1,0:T(8,128)S(1)} %copy-done.5, ...), custom_call_target="tpu_custom_call" | custom-call | bytes 262144 | tf_op jit(solution)/shard_map/structure_near/pallas_call | solution.py:142
  16.5 1.4 %collective-permute-start.4 = (bf16[544,128]{1,0:T(8,128)(2,1)S(1)}, bf16[544,128]{1,0:T(8,128)(2,1)S(1)}, u32[]{:S(2)}, u32[]{:S(2)}) collective-permute-start(bf16[544,128]{1,0:T(8,128)(2,1)S(1)} %get-tuple-element.80.refs_5_), channel_id=1, source_target_pairs={{0,8},{1,9},{2,10},{3,11},{4,12},{5,13},{6,14},{7,15},{8,16},{9,17... | collective-permute-start | bytes 417800 | tf_op jit(solution)/shard_map/ppermute | solution.py:541
  17.9 1.5 %collective-permute-start.5 = (bf16[544,128]{1,0:T(8,128)(2,1)S(1)}, bf16[544,128]{1,0:T(8,128)(2,1)S(1)}, u32[]{:S(2)}, u32[]{:S(2)}) collective-permute-start(bf16[544,128]{1,0:T(8,128)(2,1)S(1)} %get-tuple-element.81), channel_id=1, source_target_pairs={{0,24},{1,25},{2,26},{3,27},{4,28},{5,29},{6,30},{7,31},{8,0},{9,1... | collective-permute-start | bytes 417800 | tf_op jit(solution)/shard_map/ppermute | solution.py:541
  19.4 1.6 %collective-permute-start.6 = (bf16[512,128]{1,0:T(8,128)(2,1)S(1)}, bf16[512,128]{1,0:T(8,128)(2,1)S(1)}, u32[]{:S(2)}, u32[]{:S(2)}) collective-permute-start(bf16[512,128]{1,0:T(8,128)(2,1)S(1)} %get-tuple-element.79.refs_0_), channel_id=1, source_target_pairs={{0,16},{1,17},{2,18},{3,19},{4,20},{5,21},{6,22},{7,23},{8,24},{9,... | collective-permute-start | bytes 393224 | tf_op jit(solution)/shard_map/ppermute | solution.py:541
  21.0 4.3 %edges.3.refs_2_.refs_6_.refs_9_ = f32[1024,192]{1,0:T(8,128)S(1)} custom-call(s32[1,12288]{1,0:T(1,128)S(1)} %get-tuple-element.74.refs_0_, s32[1,12288]{1,0:T(1,128)S(1)} %get-tuple-element.75.refs_1_, s32[1,12288]{1,0:T(1,128)S(1)} %get-tuple-element.76.refs_2_, f32[1,12288]{1,0:T(1,128)S(1)} %get-tuple-element.77.refs_3_, f32[1024,192]{1,0:T(8,128)S(1)} %edges.2.refs_4_, ...), custom_call_target="tpu_custom_call" | custom-call | flops 3758096384 | bytes 262144 | tf_op jit(solution)/shard_map/edges/pallas_call | solution.py:142
  25.6 1.4 %collective-permute-done.6.refs_3_ = bf16[512,128]{1,0:T(8,128)(2,1)S(1)} collective-permute-done((bf16[512,128]{1,0:T(8,128)(2,1)S(1)}, bf16[512,128]{1,0:T(8,128)(2,1)S(1)}, u32[]{:S(2)}, u32[]{:S(2)}) %collective-permute-start.6) | collective-permute-done | bytes 131104 | tf_op jit(solution)/shard_map/ppermute | solution.py:541
  30.7 2.6 %collective-permute-start.9 = (bf16[128,128]{1,0:T(8,128)(2,1)S(1)}, bf16[128,128]{1,0:T(8,128)(2,1)S(1)}, u32[]{:S(2)}, u32[]{:S(2)}) collective-permute-start(bf16[128,128]{1,0:T(8,128)(2,1)S(1)} %get-tuple-element.91), channel_id=1, source_target_pairs={{0,4},{1,5},{2,6},{3,7},{4,0},{5,1},{6,2},{7,3},{8,12},{9,13},{10,... | collective-permute-start | bytes 98312 | tf_op jit(solution)/shard_map/ppermute | solution.py:537
  34.0 1.6 %collective-permute-start.19 = (bf16[1152,128]{1,0:T(8,128)(2,1)S(1)}, bf16[1152,128]{1,0:T(8,128)(2,1)S(1)}, u32[]{:S(2)}, u32[]{:S(2)}) collective-permute-start(bf16[1152,128]{1,0:T(8,128)(2,1)S(1)} %pair.1.refs_0_), channel_id=1, source_target_pairs={{0,24},{1,25},{2,26},{3,27},{4,28},{5,29},{6,30},{7,31},{8,16},{9,... | collective-permute-start | bytes 884744 | tf_op jit(solution)/shard_map/ppermute | solution.py:537
  38.0 2.1 %collective-permute-start.13 = (bf16[272,128]{1,0:T(8,128)(2,1)S(1)}, bf16[272,128]{1,0:T(8,128)(2,1)S(1)}, u32[]{:S(2)}, u32[]{:S(2)}) collective-permute-start(bf16[272,128]{1,0:T(8,128)(2,1)S(1)} %get-tuple-element.105), channel_id=1, source_target_pairs={{0,6},{1,7},{2,4},{3,5},{4,2},{5,3},{6,0},{7,1},{8,14},{9,15},{10,... | collective-permute-start | bytes 208904 | tf_op jit(solution)/shard_map/ppermute | solution.py:537
  41.3 2.2 %collective-permute-done.13.refs_5_ = bf16[272,128]{1,0:T(8,128)(2,1)S(1)} collective-permute-done((bf16[272,128]{1,0:T(8,128)(2,1)S(1)}, bf16[272,128]{1,0:T(8,128)(2,1)S(1)}, u32[]{:S(2)}, u32[]{:S(2)}) %collective-permute-start.13) | collective-permute-done | bytes 69664 | tf_op jit(solution)/shard_map/ppermute | solution.py:537
  43.5 3.3 %collective-permute-start.14 = (bf16[816,128]{1,0:T(8,128)(2,1)S(1)}, bf16[816,128]{1,0:T(8,128)(2,1)S(1)}, u32[]{:S(2)}, u32[]{:S(2)}) collective-permute-start(bf16[816,128]{1,0:T(8,128)(2,1)S(1)} %get-tuple-element.107.refs_1_.refs_2_), channel_id=1, source_target_pairs={{0,1},{1,0},{2,3},{3,2},{4,5},{5,4},{6,7},{7,6},{8,9},{9,8},{10,11... | collective-permute-start | bytes 626696 | tf_op jit(solution)/shard_map/ppermute | solution.py:537
  49.6 1.8 %collective-permute-start.16 = (bf16[592,128]{1,0:T(8,128)(2,1)S(1)}, bf16[592,128]{1,0:T(8,128)(2,1)S(1)}, u32[]{:S(2)}, u32[]{:S(2)}) collective-permute-start(bf16[592,128]{1,0:T(8,128)(2,1)S(1)} %get-tuple-element.111), channel_id=1, source_target_pairs={{0,24},{1,25},{2,26},{3,27},{4,28},{5,29},{6,30},{7,31},{8,0},{9,1... | collective-permute-start | bytes 454664 | tf_op jit(solution)/shard_map/ppermute | solution.py:541
  52.0 2.6 %near_tables.1 = (bf16[2048,512]{1,0:T(8,128)(2,1)S(1)}, f32[2048,128]{1,0:T(8,128)S(1)}, bf16[128,2048]{1,0:T(8,128)(2,1)S(1)}) custom-call(bf16[2304,128]{1,0:T(8,128)(2,1)S(1)} %collect.1.refs_0_, s32[3,2048]{1,0:T(4,128)S(1)} %copy-done, f32[8,128]{1,0:T(8,128)S(1)} %copy-done.5, bf16[560,128]{1,0:T(8,128)(2,1)S(1)} %get-tuple-element.109.refs_2_.refs_3_.refs_0_), custom_call_target="tpu_custom_call" | custom-call | bytes 262144 | tf_op jit(solution)/shard_map/near_tables/pallas_call | solution.py:142
  54.6 2.6 %far_tables.1 = (bf16[2048,512]{1,0:T(8,128)(2,1)S(1)}, f32[2048,128]{1,0:T(8,128)S(1)}, bf16[128,2048]{1,0:T(8,128)(2,1)S(1)}) custom-call(bf16[2304,128]{1,0:T(8,128)(2,1)S(1)} %collective-permute-done.20.refs_0_, s32[3,2048]{1,0:T(4,128)S(1)} %copy-done, f32[8,128]{1,0:T(8,128)S(1)} %copy-done.5, ...), custom_call_target="tpu_custom_call" | custom-call | bytes 262144 | tf_op jit(solution)/shard_map/far_tables/pallas_call | solution.py:142
  58.5 1.5 %collective-permute-start.21 = (bf16[512,128]{1,0:T(8,128)(2,1)S(1)}, bf16[512,128]{1,0:T(8,128)(2,1)S(1)}, u32[]{:S(2)}, u32[]{:S(2)}) collective-permute-start(bf16[512,128]{1,0:T(8,128)(2,1)S(1)} %get-tuple-element.117.refs_8_), channel_id=1, source_target_pairs={{0,1},{1,0},{2,3},{3,2},{4,5},{5,4},{6,7},{7,6},{8,9},{9,8},{10,11... | collective-permute-start | bytes 393224 | tf_op jit(solution)/shard_map/ppermute | solution.py:537
  60.1 1.6 %charge.1.refs_2_ = bf16[176,128]{1,0:T(8,128)(2,1)S(1)} custom-call(bf16[512,128]{1,0:T(8,128)(2,1)S(1)} %get-tuple-element.118.refs_0_, bf16[48,128]{1,0:T(8,128)(2,1)S(1)} %get-tuple-element.119.refs_1_, bf16[2048,512]{1,0:T(8,128)(2,1)S(1)} %get-tuple-element.120.refs_2_, f32[2048,128]{1,0:T(8,128)S(1)} %get-tuple-element.114.refs_9_.refs_3_, ...), custom_call_target="tpu_custom_call" | custom-call | bytes 262144 | tf_op jit(solution)/shard_map/charge/pallas_call | solution.py:142
  61.6 2.9 %collective-permute-start.22 = (bf16[176,128]{1,0:T(8,128)(2,1)S(1)}, bf16[176,128]{1,0:T(8,128)(2,1)S(1)}, u32[]{:S(2)}, u32[]{:S(2)}) collective-permute-start(bf16[176,128]{1,0:T(8,128)(2,1)S(1)} %charge.1.refs_2_), channel_id=1, source_target_pairs={{0,38},{1,39},{2,36},{3,37},{4,34},{5,35},{6,32},{7,33},{8,46},{9,... | collective-permute-start | bytes 135176 | tf_op jit(solution)/shard_map/ppermute | solution.py:537
  64.6 1.9 %collective-permute-done.22.refs_3_ = bf16[176,128]{1,0:T(8,128)(2,1)S(1)} collective-permute-done((bf16[176,128]{1,0:T(8,128)(2,1)S(1)}, bf16[176,128]{1,0:T(8,128)(2,1)S(1)}, u32[]{:S(2)}, u32[]{:S(2)}) %collective-permute-start.22) | collective-permute-done | bytes 45088 | tf_op jit(solution)/shard_map/ppermute | solution.py:537
  66.5 1.8 %collective-permute-start.23 = (bf16[288,128]{1,0:T(8,128)(2,1)S(1)}, bf16[288,128]{1,0:T(8,128)(2,1)S(1)}, u32[]{:S(2)}, u32[]{:S(2)}) collective-permute-start(bf16[288,128]{1,0:T(8,128)(2,1)S(1)} %get-tuple-element.126), channel_id=1, source_target_pairs={{0,2},{1,3},{2,0},{3,1},{4,6},{5,7},{6,4},{7,5},{8,10},{9,11},{10,... | collective-permute-start | bytes 221192 | tf_op jit(solution)/shard_map/ppermute | solution.py:537
  69.1 1.4 %collective-permute-start.25 = (bf16[288,128]{1,0:T(8,128)(2,1)S(1)}, bf16[288,128]{1,0:T(8,128)(2,1)S(1)}, u32[]{:S(2)}, u32[]{:S(2)}) collective-permute-start(bf16[288,128]{1,0:T(8,128)(2,1)S(1)} %get-tuple-element.128), channel_id=1, source_target_pairs={{0,6},{1,7},{2,4},{3,5},{4,2},{5,3},{6,0},{7,1},{8,14},{9,15},{10,... | collective-permute-start | bytes 221192 | tf_op jit(solution)/shard_map/ppermute | solution.py:537
  70.5 2.7 %collective-permute-done.24.refs_3_ = bf16[288,128]{1,0:T(8,128)(2,1)S(1)} collective-permute-done((bf16[288,128]{1,0:T(8,128)(2,1)S(1)}, bf16[288,128]{1,0:T(8,128)(2,1)S(1)}, u32[]{:S(2)}, u32[]{:S(2)}) %collective-permute-start.24) | collective-permute-done | bytes 73760 | tf_op jit(solution)/shard_map/ppermute | solution.py:537
  73.2 1.7 %collective-permute-done.25.refs_4_ = bf16[288,128]{1,0:T(8,128)(2,1)S(1)} collective-permute-done((bf16[288,128]{1,0:T(8,128)(2,1)S(1)}, bf16[288,128]{1,0:T(8,128)(2,1)S(1)}, u32[]{:S(2)}, u32[]{:S(2)}) %collective-permute-start.25) | collective-permute-done | bytes 73760 | tf_op jit(solution)/shard_map/ppermute | solution.py:537
  74.9 1.3 %collective-permute-start.26 = (bf16[272,128]{1,0:T(8,128)(2,1)S(1)}, bf16[272,128]{1,0:T(8,128)(2,1)S(1)}, u32[]{:S(2)}, u32[]{:S(2)}) collective-permute-start(bf16[272,128]{1,0:T(8,128)(2,1)S(1)} %get-tuple-element.133.refs_9_.refs_0_), channel_id=1, source_target_pairs={{0,64},{32,96},{64,0},{96,32},{128,192},{160,224},{192,128},{224,1... | collective-permute-start | bytes 208904 | tf_op jit(solution)/shard_map/ppermute | solution.py:537
  76.2 2.5 %collective-permute-start.27 = (bf16[272,128]{1,0:T(8,128)(2,1)S(1)}, bf16[272,128]{1,0:T(8,128)(2,1)S(1)}, u32[]{:S(2)}, u32[]{:S(2)}) collective-permute-start(bf16[272,128]{1,0:T(8,128)(2,1)S(1)} %get-tuple-element.133.refs_9_.refs_0_), channel_id=1, source_target_pairs={{0,128},{32,160},{64,192},{96,224},{128,0},{160,32},{192,64},{224,... | collective-permute-start | bytes 208904 | tf_op jit(solution)/shard_map/ppermute | solution.py:537
  79.6 1.4 %collective-permute-done.27.refs_2_ = bf16[272,128]{1,0:T(8,128)(2,1)S(1)} collective-permute-done((bf16[272,128]{1,0:T(8,128)(2,1)S(1)}, bf16[272,128]{1,0:T(8,128)(2,1)S(1)}, u32[]{:S(2)}, u32[]{:S(2)}) %collective-permute-start.27) | collective-permute-done | bytes 69664 | tf_op jit(solution)/shard_map/ppermute | solution.py:537
  81.1 1.9 %collective-permute-done.28.refs_3_ = bf16[272,128]{1,0:T(8,128)(2,1)S(1)} collective-permute-done((bf16[272,128]{1,0:T(8,128)(2,1)S(1)}, bf16[272,128]{1,0:T(8,128)(2,1)S(1)}, u32[]{:S(2)}, u32[]{:S(2)}) %collective-permute-start.28) | collective-permute-done | bytes 69664 | tf_op jit(solution)/shard_map/ppermute | solution.py:537
  83.1 4.8 %collective-permute-start.29 = (f32[272,128]{1,0:T(8,128)S(1)}, f32[272,128]{1,0:T(8,128)S(1)}, u32[]{:S(2)}, u32[]{:S(2)}) collective-permute-start(f32[272,128]{1,0:T(8,128)S(1)} %cell_sum.1.refs_0_), channel_id=1, source_target_pairs={{0,1},{1,0},{2,3},{3,2},{4,5},{5,4},{6,7},{7,6},{8,9},{9,8},{10,11... | collective-permute-start | bytes 417800 | tf_op jit(solution)/shard_map/ppermute | solution.py:537
  (76 shorter events, 18.5 us)
Async XLA Ops:
  1.7 8.7 %collective-permute-start = (bf16[144,128]{1,0:T(8,128)(2,1)S(1)}, bf16[144,128]{1,0:T(8,128)(2,1)S(1)}, u32[]{:S(2)}, u32[]{:S(2)}) collective-permute-start(bf16[144,128]{1,0:T(8,128)(2,1)S(1)} %get-tuple-element.73.refs_4_.refs_0_), channel_id=1, source_target_pairs={{0,2},{1,3},{2,0},{3,1},{4,6},{5,7},{6,4},{7,5},{8,10},{9,11},{10,... | collective-permute-start | bytes 110600 | tf_op jit(solution)/shard_map/ppermute | solution.py:537
  4.2 6.2 %collective-permute-start.1 = (bf16[144,128]{1,0:T(8,128)(2,1)S(1)}, bf16[144,128]{1,0:T(8,128)(2,1)S(1)}, u32[]{:S(2)}, u32[]{:S(2)}) collective-permute-start(bf16[144,128]{1,0:T(8,128)(2,1)S(1)} %get-tuple-element.73.refs_4_.refs_0_), channel_id=1, source_target_pairs={{0,4},{1,5},{2,6},{3,7},{4,0},{5,1},{6,2},{7,3},{8,12},{9,13},{10,... | collective-permute-start | bytes 110600 | tf_op jit(solution)/shard_map/ppermute | solution.py:537
  7.2 4.6 %collective-permute-start.2 = (bf16[144,128]{1,0:T(8,128)(2,1)S(1)}, bf16[144,128]{1,0:T(8,128)(2,1)S(1)}, u32[]{:S(2)}, u32[]{:S(2)}) collective-permute-start(bf16[144,128]{1,0:T(8,128)(2,1)S(1)} %get-tuple-element.73.refs_4_.refs_0_), channel_id=1, source_target_pairs={{0,6},{1,7},{2,4},{3,5},{4,2},{5,3},{6,0},{7,1},{8,14},{9,15},{10,... | collective-permute-start | bytes 110600 | tf_op jit(solution)/shard_map/ppermute | solution.py:537
  11.8 3.6 %collective-permute-start.3 = (bf16[576,128]{1,0:T(8,128)(2,1)S(1)}, bf16[576,128]{1,0:T(8,128)(2,1)S(1)}, u32[]{:S(2)}, u32[]{:S(2)}) collective-permute-start(bf16[576,128]{1,0:T(8,128)(2,1)S(1)} %gather.1.refs_0_.refs_1_), channel_id=1, source_target_pairs={{0,1},{1,0},{2,3},{3,2},{4,5},{5,4},{6,7},{7,6},{8,9},{9,8},{10,11... | collective-permute-start | bytes 442376 | tf_op jit(solution)/shard_map/ppermute | solution.py:537
  16.5 10.4 %collective-permute-start.4 = (bf16[544,128]{1,0:T(8,128)(2,1)S(1)}, bf16[544,128]{1,0:T(8,128)(2,1)S(1)}, u32[]{:S(2)}, u32[]{:S(2)}) collective-permute-start(bf16[544,128]{1,0:T(8,128)(2,1)S(1)} %get-tuple-element.80.refs_5_), channel_id=1, source_target_pairs={{0,8},{1,9},{2,10},{3,11},{4,12},{5,13},{6,14},{7,15},{8,16},{9,17... | collective-permute-start | bytes 417800 | tf_op jit(solution)/shard_map/ppermute | solution.py:541
  17.9 9.0 %collective-permute-start.5 = (bf16[544,128]{1,0:T(8,128)(2,1)S(1)}, bf16[544,128]{1,0:T(8,128)(2,1)S(1)}, u32[]{:S(2)}, u32[]{:S(2)}) collective-permute-start(bf16[544,128]{1,0:T(8,128)(2,1)S(1)} %get-tuple-element.81), channel_id=1, source_target_pairs={{0,24},{1,25},{2,26},{3,27},{4,28},{5,29},{6,30},{7,31},{8,0},{9,1... | collective-permute-start | bytes 417800 | tf_op jit(solution)/shard_map/ppermute | solution.py:541
  19.4 7.5 %collective-permute-start.6 = (bf16[512,128]{1,0:T(8,128)(2,1)S(1)}, bf16[512,128]{1,0:T(8,128)(2,1)S(1)}, u32[]{:S(2)}, u32[]{:S(2)}) collective-permute-start(bf16[512,128]{1,0:T(8,128)(2,1)S(1)} %get-tuple-element.79.refs_0_), channel_id=1, source_target_pairs={{0,16},{1,17},{2,18},{3,19},{4,20},{5,21},{6,22},{7,23},{8,24},{9,... | collective-permute-start | bytes 393224 | tf_op jit(solution)/shard_map/ppermute | solution.py:541
  27.5 2.1 %collective-permute-start.7 = (bf16[512,128]{1,0:T(8,128)(2,1)S(1)}, bf16[512,128]{1,0:T(8,128)(2,1)S(1)}, u32[]{:S(2)}, u32[]{:S(2)}) collective-permute-start(bf16[512,128]{1,0:T(8,128)(2,1)S(1)} %get-tuple-element.88), channel_id=1, source_target_pairs={{0,1},{1,0},{2,3},{3,2},{4,5},{5,4},{6,7},{7,6},{8,9},{9,8},{10,11... | collective-permute-start | bytes 393224 | tf_op jit(solution)/shard_map/ppermute | solution.py:537
  28.6 5.4 %collective-permute-start.18 = (bf16[576,128]{1,0:T(8,128)(2,1)S(1)}, bf16[576,128]{1,0:T(8,128)(2,1)S(1)}, u32[]{:S(2)}, u32[]{:S(2)}) collective-permute-start(bf16[576,128]{1,0:T(8,128)(2,1)S(1)} %get-tuple-element.86.refs_7_.refs_0_), channel_id=1, source_target_pairs={{0,8},{1,9},{2,10},{3,11},{4,12},{5,13},{6,14},{7,15},{8,0},{9,1},... | collective-permute-start | bytes 442376 | tf_op jit(solution)/shard_map/ppermute | solution.py:537
  29.6 6.1 %collective-permute-start.10 = (bf16[128,128]{1,0:T(8,128)(2,1)S(1)}, bf16[128,128]{1,0:T(8,128)(2,1)S(1)}, u32[]{:S(2)}, u32[]{:S(2)}) collective-permute-start(bf16[128,128]{1,0:T(8,128)(2,1)S(1)} %get-tuple-element.92), channel_id=1, source_target_pairs={{0,6},{1,7},{2,4},{3,5},{4,2},{5,3},{6,0},{7,1},{8,14},{9,15},{10,... | collective-permute-start | bytes 98312 | tf_op jit(solution)/shard_map/ppermute | solution.py:537
  30.6 5.0 %collective-permute-start.8 = (bf16[128,128]{1,0:T(8,128)(2,1)S(1)}, bf16[128,128]{1,0:T(8,128)(2,1)S(1)}, u32[]{:S(2)}, u32[]{:S(2)}) collective-permute-start(bf16[128,128]{1,0:T(8,128)(2,1)S(1)} %get-tuple-element.90), channel_id=1, source_target_pairs={{0,2},{1,3},{2,0},{3,1},{4,6},{5,7},{6,4},{7,5},{8,10},{9,11},{10,... | collective-permute-start | bytes 98312 | tf_op jit(solution)/shard_map/ppermute | solution.py:537
  30.7 5.0 %collective-permute-start.9 = (bf16[128,128]{1,0:T(8,128)(2,1)S(1)}, bf16[128,128]{1,0:T(8,128)(2,1)S(1)}, u32[]{:S(2)}, u32[]{:S(2)}) collective-permute-start(bf16[128,128]{1,0:T(8,128)(2,1)S(1)} %get-tuple-element.91), channel_id=1, source_target_pairs={{0,4},{1,5},{2,6},{3,7},{4,0},{5,1},{6,2},{7,3},{8,12},{9,13},{10,... | collective-permute-start | bytes 98312 | tf_op jit(solution)/shard_map/ppermute | solution.py:537
  34.0 14.2 %collective-permute-start.19 = (bf16[1152,128]{1,0:T(8,128)(2,1)S(1)}, bf16[1152,128]{1,0:T(8,128)(2,1)S(1)}, u32[]{:S(2)}, u32[]{:S(2)}) collective-permute-start(bf16[1152,128]{1,0:T(8,128)(2,1)S(1)} %pair.1.refs_0_), channel_id=1, source_target_pairs={{0,24},{1,25},{2,26},{3,27},{4,28},{5,29},{6,30},{7,31},{8,16},{9,... | collective-permute-start | bytes 884744 | tf_op jit(solution)/shard_map/ppermute | solution.py:537
  36.5 4.4 %collective-permute-start.11 = (bf16[272,128]{1,0:T(8,128)(2,1)S(1)}, bf16[272,128]{1,0:T(8,128)(2,1)S(1)}, u32[]{:S(2)}, u32[]{:S(2)}) collective-permute-start(bf16[272,128]{1,0:T(8,128)(2,1)S(1)} %get-tuple-element.99.refs_3_), channel_id=1, source_target_pairs={{0,2},{1,3},{2,0},{3,1},{4,6},{5,7},{6,4},{7,5},{8,10},{9,11},{10,... | collective-permute-start | bytes 208904 | tf_op jit(solution)/shard_map/ppermute | solution.py:537
  36.9 4.4 %collective-permute-start.12 = (bf16[272,128]{1,0:T(8,128)(2,1)S(1)}, bf16[272,128]{1,0:T(8,128)(2,1)S(1)}, u32[]{:S(2)}, u32[]{:S(2)}) collective-permute-start(bf16[272,128]{1,0:T(8,128)(2,1)S(1)} %get-tuple-element.104), channel_id=1, source_target_pairs={{0,4},{1,5},{2,6},{3,7},{4,0},{5,1},{6,2},{7,3},{8,12},{9,13},{10,... | collective-permute-start | bytes 208904 | tf_op jit(solution)/shard_map/ppermute | solution.py:537
  38.0 5.5 %collective-permute-start.13 = (bf16[272,128]{1,0:T(8,128)(2,1)S(1)}, bf16[272,128]{1,0:T(8,128)(2,1)S(1)}, u32[]{:S(2)}, u32[]{:S(2)}) collective-permute-start(bf16[272,128]{1,0:T(8,128)(2,1)S(1)} %get-tuple-element.105), channel_id=1, source_target_pairs={{0,6},{1,7},{2,4},{3,5},{4,2},{5,3},{6,0},{7,1},{8,14},{9,15},{10,... | collective-permute-start | bytes 208904 | tf_op jit(solution)/shard_map/ppermute | solution.py:537
  43.5 4.4 %collective-permute-start.14 = (bf16[816,128]{1,0:T(8,128)(2,1)S(1)}, bf16[816,128]{1,0:T(8,128)(2,1)S(1)}, u32[]{:S(2)}, u32[]{:S(2)}) collective-permute-start(bf16[816,128]{1,0:T(8,128)(2,1)S(1)} %get-tuple-element.107.refs_1_.refs_2_), channel_id=1, source_target_pairs={{0,1},{1,0},{2,3},{3,2},{4,5},{5,4},{6,7},{7,6},{8,9},{9,8},{10,11... | collective-permute-start | bytes 626696 | tf_op jit(solution)/shard_map/ppermute | solution.py:537
  48.3 6.3 %collective-permute-start.20 = (bf16[2304,128]{1,0:T(8,128)(2,1)S(1)}, bf16[2304,128]{1,0:T(8,128)(2,1)S(1)}, u32[]{:S(2)}, u32[]{:S(2)}) collective-permute-start(bf16[2304,128]{1,0:T(8,128)(2,1)S(1)} %collect.1.refs_0_), channel_id=1, source_target_pairs={{0,1},{1,0},{2,3},{3,2},{4,5},{5,4},{6,7},{7,6},{8,9},{9,8},{10,11... | collective-permute-start | bytes 1769480 | tf_op jit(solution)/shard_map/ppermute | solution.py:537
  48.7 9.3 %collective-permute-start.15 = (bf16[592,128]{1,0:T(8,128)(2,1)S(1)}, bf16[592,128]{1,0:T(8,128)(2,1)S(1)}, u32[]{:S(2)}, u32[]{:S(2)}) collective-permute-start(bf16[592,128]{1,0:T(8,128)(2,1)S(1)} %get-tuple-element.110), channel_id=1, source_target_pairs={{0,8},{1,9},{2,10},{3,11},{4,12},{5,13},{6,14},{7,15},{8,16},{9,17... | collective-permute-start | bytes 454664 | tf_op jit(solution)/shard_map/ppermute | solution.py:541
  49.6 8.4 %collective-permute-start.16 = (bf16[592,128]{1,0:T(8,128)(2,1)S(1)}, bf16[592,128]{1,0:T(8,128)(2,1)S(1)}, u32[]{:S(2)}, u32[]{:S(2)}) collective-permute-start(bf16[592,128]{1,0:T(8,128)(2,1)S(1)} %get-tuple-element.111), channel_id=1, source_target_pairs={{0,24},{1,25},{2,26},{3,27},{4,28},{5,29},{6,30},{7,31},{8,0},{9,1... | collective-permute-start | bytes 454664 | tf_op jit(solution)/shard_map/ppermute | solution.py:541
  51.4 6.6 %collective-permute-start.17 = (bf16[560,128]{1,0:T(8,128)(2,1)S(1)}, bf16[560,128]{1,0:T(8,128)(2,1)S(1)}, u32[]{:S(2)}, u32[]{:S(2)}) collective-permute-start(bf16[560,128]{1,0:T(8,128)(2,1)S(1)} %get-tuple-element.109.refs_2_.refs_3_.refs_0_), channel_id=1, source_target_pairs={{0,16},{1,17},{2,18},{3,19},{4,20},{5,21},{6,22},{7,23},{8,24},{9,... | collective-permute-start | bytes 430088 | tf_op jit(solution)/shard_map/ppermute | solution.py:541
  58.5 8.0 %collective-permute-start.21 = (bf16[512,128]{1,0:T(8,128)(2,1)S(1)}, bf16[512,128]{1,0:T(8,128)(2,1)S(1)}, u32[]{:S(2)}, u32[]{:S(2)}) collective-permute-start(bf16[512,128]{1,0:T(8,128)(2,1)S(1)} %get-tuple-element.117.refs_8_), channel_id=1, source_target_pairs={{0,1},{1,0},{2,3},{3,2},{4,5},{5,4},{6,7},{7,6},{8,9},{9,8},{10,11... | collective-permute-start | bytes 393224 | tf_op jit(solution)/shard_map/ppermute | solution.py:537
  60.1 18.8 %copy-start.8 = (s32[1,32]{1,0:T(1,128)S(1)}, s32[1,32]{1,0:T(1,128)}, u32[]{:S(2)}) copy-start(s32[1,32]{1,0:T(1,128)} %refs_3_.7) | copy-start | bytes 388
  60.1 18.8 %copy-start.9 = (s32[1,32]{1,0:T(1,128)S(1)}, s32[1,32]{1,0:T(1,128)}, u32[]{:S(2)}) copy-start(s32[1,32]{1,0:T(1,128)} %refs_4_.7) | copy-start | bytes 388
  61.6 4.8 %collective-permute-start.22 = (bf16[176,128]{1,0:T(8,128)(2,1)S(1)}, bf16[176,128]{1,0:T(8,128)(2,1)S(1)}, u32[]{:S(2)}, u32[]{:S(2)}) collective-permute-start(bf16[176,128]{1,0:T(8,128)(2,1)S(1)} %charge.1.refs_2_), channel_id=1, source_target_pairs={{0,38},{1,39},{2,36},{3,37},{4,34},{5,35},{6,32},{7,33},{8,46},{9,... | collective-permute-start | bytes 135176 | tf_op jit(solution)/shard_map/ppermute | solution.py:537
  66.5 4.0 %collective-permute-start.23 = (bf16[288,128]{1,0:T(8,128)(2,1)S(1)}, bf16[288,128]{1,0:T(8,128)(2,1)S(1)}, u32[]{:S(2)}, u32[]{:S(2)}) collective-permute-start(bf16[288,128]{1,0:T(8,128)(2,1)S(1)} %get-tuple-element.126), channel_id=1, source_target_pairs={{0,2},{1,3},{2,0},{3,1},{4,6},{5,7},{6,4},{7,5},{8,10},{9,11},{10,... | collective-permute-start | bytes 221192 | tf_op jit(solution)/shard_map/ppermute | solution.py:537
  68.3 4.9 %collective-permute-start.24 = (bf16[288,128]{1,0:T(8,128)(2,1)S(1)}, bf16[288,128]{1,0:T(8,128)(2,1)S(1)}, u32[]{:S(2)}, u32[]{:S(2)}) collective-permute-start(bf16[288,128]{1,0:T(8,128)(2,1)S(1)} %get-tuple-element.127), channel_id=1, source_target_pairs={{0,4},{1,5},{2,6},{3,7},{4,0},{5,1},{6,2},{7,3},{8,12},{9,13},{10,... | collective-permute-start | bytes 221192 | tf_op jit(solution)/shard_map/ppermute | solution.py:537
  69.1 5.7 %collective-permute-start.25 = (bf16[288,128]{1,0:T(8,128)(2,1)S(1)}, bf16[288,128]{1,0:T(8,128)(2,1)S(1)}, u32[]{:S(2)}, u32[]{:S(2)}) collective-permute-start(bf16[288,128]{1,0:T(8,128)(2,1)S(1)} %get-tuple-element.128), channel_id=1, source_target_pairs={{0,6},{1,7},{2,4},{3,5},{4,2},{5,3},{6,0},{7,1},{8,14},{9,15},{10,... | collective-permute-start | bytes 221192 | tf_op jit(solution)/shard_map/ppermute | solution.py:537
  74.9 4.7 %collective-permute-start.26 = (bf16[272,128]{1,0:T(8,128)(2,1)S(1)}, bf16[272,128]{1,0:T(8,128)(2,1)S(1)}, u32[]{:S(2)}, u32[]{:S(2)}) collective-permute-start(bf16[272,128]{1,0:T(8,128)(2,1)S(1)} %get-tuple-element.133.refs_9_.refs_0_), channel_id=1, source_target_pairs={{0,64},{32,96},{64,0},{96,32},{128,192},{160,224},{192,128},{224,1... | collective-permute-start | bytes 208904 | tf_op jit(solution)/shard_map/ppermute | solution.py:537
  76.2 4.9 %collective-permute-start.27 = (bf16[272,128]{1,0:T(8,128)(2,1)S(1)}, bf16[272,128]{1,0:T(8,128)(2,1)S(1)}, u32[]{:S(2)}, u32[]{:S(2)}) collective-permute-start(bf16[272,128]{1,0:T(8,128)(2,1)S(1)} %get-tuple-element.133.refs_9_.refs_0_), channel_id=1, source_target_pairs={{0,128},{32,160},{64,192},{96,224},{128,0},{160,32},{192,64},{224,... | collective-permute-start | bytes 208904 | tf_op jit(solution)/shard_map/ppermute | solution.py:537
  78.6 4.4 %collective-permute-start.28 = (bf16[272,128]{1,0:T(8,128)(2,1)S(1)}, bf16[272,128]{1,0:T(8,128)(2,1)S(1)}, u32[]{:S(2)}, u32[]{:S(2)}) collective-permute-start(bf16[272,128]{1,0:T(8,128)(2,1)S(1)} %get-tuple-element.133.refs_9_.refs_0_), channel_id=1, source_target_pairs={{0,192},{32,224},{64,128},{96,160},{128,64},{160,96},{192,0},{224,... | collective-permute-start | bytes 208904 | tf_op jit(solution)/shard_map/ppermute | solution.py:537
  83.1 5.8 %collective-permute-start.29 = (f32[272,128]{1,0:T(8,128)S(1)}, f32[272,128]{1,0:T(8,128)S(1)}, u32[]{:S(2)}, u32[]{:S(2)}) collective-permute-start(f32[272,128]{1,0:T(8,128)S(1)} %cell_sum.1.refs_0_), channel_id=1, source_target_pairs={{0,1},{1,0},{2,3},{3,2},{4,5},{5,4},{6,7},{7,6},{8,9},{9,8},{10,11... | collective-permute-start | bytes 417800 | tf_op jit(solution)/shard_map/ppermute | solution.py:537
  (9 other events, 69.4 us)
